TPU v7x, 256 devices: a whole 4x4x8 slice. The times are simulated.
256 devices in a mesh: fact: 8 (over z), dim: 32 (over y, x, core).
Axes of the slice: x: 4, y: 4, z: 8, core: 2. Of those that a mesh axis runs over, the one named last changes fastest.
Arguments:
- facts: bfloat16 [32768, 512], P(('fact', 'dim')), may hold values from -6 to 6
- dims: bfloat16 [32768, 512], P(('fact', 'dim')), may hold values from -6 to 6
- tiles: bfloat16 [8192, 128, 128], P(('fact', 'dim')), may hold values from -0.125 to 0.125
- links: int32 [8192, 2], P(('fact', 'dim')), may hold values from 0 to 255, as said below
- link_count: int32 [256], P(('fact', 'dim')), may hold values from 8 to 32, as said below
- block_table: int32 [256], replicated, may hold values from 0 to 2
- w_self: bfloat16 [512, 512], replicated, may hold values from -0.25 to 0.25
- w_tables: bfloat16 [3, 512, 512], replicated, may hold values from -0.25 to 0.25
- cot: bfloat16 [32768, 512], P(('fact', 'dim')), may hold values from -6 to 6
Outputs:
- fact_out: bfloat16 [32768, 512], P(('fact', 'dim'))
- grad_dims: float32 [32768, 512], P(('fact', 'dim'))
- grad_w_self: float32 [512, 512], replicated
- grad_w_tables: float32 [3, 512, 512], replicated
Inputs may be any that keep to these rules, and one draw needn't show every extreme that they name: On device k = f * 32 + d (f, d its fact and dim indices), links[l,0] is a fact block among those of rows f * 128 * 32 to (f + 1) * 128 * 32 - 1, and links[l,1] is a dimension block held by a device with dim index d, i.e. links[l,1] % 32 == d. Slots beyond the device's count hold such indices too and are padding. `link_count`: some device has all 32 slots live and some device exactly 8.
All inputs are finite; a program needn't handle non-finite values.
Results may differ from a plain program's by a relative error of at most 0.017.
Values may be sent and summed in bfloat16 or wider, within the bound.
No kernel may reach another device: no remote copies, remote signals or barrier semaphores. Data moves between devices by JAX's collectives and lax.ppermute only.
A program may use at most 64 MiB of HBM per device.

v0:
```python
import math

import jax
import jax.numpy as jnp
from jax import lax
from jax.sharding import PartitionSpec as P


def project_rows(rows, row_table, w_tables):
    acc = jnp.zeros((rows.shape[0], w_tables.shape[2]), jnp.float32)
    for table in range(w_tables.shape[0]):
        term = jnp.dot(rows, w_tables[table], preferred_element_type=jnp.float32)
        acc = acc + jnp.where(row_table[:, None] == table, term, jnp.float32(0.0))
    return acc.astype(jnp.bfloat16)


def lookup_tables(global_blocks, block_table):
    every = jnp.arange(block_table.shape[0], dtype=jnp.int32)
    match = global_blocks[:, None] == every[None, :]
    return jnp.sum(jnp.where(match, block_table[None, :], 0), axis=1)


def body(facts, dims, tiles, links, link_count, block_table, w_self, w_tables, cot):
    n_fact = lax.axis_size("fact")
    n_dim = lax.axis_size("dim")
    fact_pos = lax.axis_index("fact")
    dim_pos = lax.axis_index("dim")
    block = tiles.shape[1]
    width = facts.shape[1]
    rows_own = facts.shape[0]
    dim_own = dims.shape[0]
    link_slots = tiles.shape[0]
    tables = w_tables.shape[0]
    shard_rows = rows_own * n_dim
    panel_rows = dim_own * n_fact
    per_owner = dim_own // block
    own_blocks = (fact_pos * n_dim + dim_pos) * per_owner + jnp.arange(per_owner, dtype=jnp.int32)
    own_row_table = jnp.repeat(lookup_tables(own_blocks, block_table), block)
    panel_local = jnp.arange(n_fact * per_owner, dtype=jnp.int32)
    panel_blocks_global = (
        panel_local // per_owner * n_dim + dim_pos
    ) * per_owner + panel_local % per_owner
    panel_row_table = jnp.repeat(lookup_tables(panel_blocks_global, block_table), block)
    panel = project_rows(
        lax.all_gather(dims, "fact", axis=0, tiled=True), panel_row_table, w_tables
    )
    fact_blk = links[:, 0] - fact_pos * (shard_rows // block)
    global_dim = links[:, 1]
    holder = global_dim // per_owner // n_dim
    dim_blk = holder * per_owner + global_dim % per_owner
    live = (jnp.arange(link_slots, dtype=jnp.int32) < link_count[0]).astype(jnp.float32)
    group = math.gcd(link_slots, 32)
    steps_count = link_slots // group
    tile_groups = tiles.reshape(steps_count, group, block, block)
    fact_groups = fact_blk.reshape(steps_count, group)
    dim_groups = dim_blk.reshape(steps_count, group)
    live_groups = live.reshape(steps_count, group)
    panel_blocks = panel.reshape(panel_rows // block, block, width)

    def forward_step(acc, xs):
        tile, fact_ids, dim_ids, alive = xs
        contrib = jnp.einsum(
            "lij,ljd->lid", tile, panel_blocks[dim_ids], preferred_element_type=jnp.float32
        )
        return (acc.at[fact_ids].add(contrib * alive[:, None, None]), None)

    start_fwd = jnp.zeros((shard_rows // block, block, width), jnp.float32)
    partial_value, _ = lax.scan(
        forward_step, start_fwd, (tile_groups, fact_groups, dim_groups, live_groups)
    )
    agg = lax.psum_scatter(
        partial_value.reshape(shard_rows, width).astype(jnp.bfloat16),
        "dim",
        scatter_dimension=0,
        tiled=True,
    ).astype(jnp.float32)
    pre = jnp.dot(facts, w_self, preferred_element_type=jnp.float32) + agg
    fact_out = jax.nn.silu(pre).astype(jnp.bfloat16)
    sig = jax.nn.sigmoid(pre)
    grad_pre = (cot.astype(jnp.float32) * sig * (1.0 + pre * (1.0 - sig))).astype(jnp.bfloat16)
    total_facts = rows_own * n_fact * n_dim
    total_dims = dim_own * n_fact * n_dim
    grad_self = lax.dot_general(
        facts, grad_pre, (((0,), (0,)), ((), ())), preferred_element_type=jnp.float32
    ) * total_facts ** (-0.5)
    shard_grad = lax.all_gather(grad_pre, "dim", axis=0, tiled=True)
    grad_blocks = shard_grad.reshape(shard_rows // block, block, width)

    def backward_step(acc, xs):
        tile, fact_ids, dim_ids, alive = xs
        contrib = jnp.einsum(
            "lji,ljd->lid", tile, grad_blocks[fact_ids], preferred_element_type=jnp.float32
        )
        return (acc.at[dim_ids].add(contrib * alive[:, None, None]), None)

    start_bwd = jnp.zeros((panel_rows // block, block, width), jnp.float32)
    panel_grad, _ = lax.scan(
        backward_step, start_bwd, (tile_groups, fact_groups, dim_groups, live_groups)
    )
    own_grad = lax.psum_scatter(
        panel_grad.reshape(panel_rows, width).astype(jnp.bfloat16),
        "fact",
        scatter_dimension=0,
        tiled=True,
    )
    grad_dims = jnp.zeros((dim_own, width), jnp.float32)
    table_grads = []
    for table in range(tables):
        term = lax.dot_general(
            own_grad, w_tables[table], (((1,), (1,)), ((), ())), preferred_element_type=jnp.float32
        )
        grad_dims = grad_dims + jnp.where(own_row_table[:, None] == table, term, jnp.float32(0.0))
        masked = jnp.where(own_row_table[:, None] == table, dims, jnp.zeros_like(dims))
        table_grads.append(
            lax.dot_general(
                masked, own_grad, (((0,), (0,)), ((), ())), preferred_element_type=jnp.float32
            )
            * total_dims ** (-0.5)
        )
    grad_tab = jnp.stack(table_grads)
    grad_self, grad_tab = lax.psum((grad_self, grad_tab), ("fact", "dim"))
    return (fact_out, grad_dims, grad_self, grad_tab)


def solution(mesh):
    placed = (
        P(("fact", "dim"), None),
        P(("fact", "dim"), None),
        P(("fact", "dim"), None, None),
        P(("fact", "dim"), None),
        P(("fact", "dim")),
        P(),
        P(),
        P(),
        P(("fact", "dim"), None),
    )
    return jax.shard_map(
        body,
        mesh=mesh,
        in_specs=placed,
        out_specs=(P(("fact", "dim"), None), P(("fact", "dim"), None), P(), P()),
        check_vma=False,
    )
```

profile of v0, /device:TPU:1, one launch (start us, length us, event | category | flops | bytes accessed | tf_op | source)
XLA Modules:
  0.0 607.1 jit_solution(12641887231790719428)
XLA Ops:
  7.2 0.0 all-gather.3.cloned.1.call-start
  7.2 0.7 all-gather.3.cloned.1.call-update
  7.9 0.0 reduce-scatter.3.cloned.1.call-start
  8.6 0.8 fusion.31
  9.4 0.9 select_reduce_fusion
  10.3 0.1 broadcast_bitcast_fusion.2
  10.4 0.1 broadcast_bitcast_fusion
  10.4 36.8 %all-gather.3.cloned.1.call-done = bf16[1024,512]{1,0:T(8,128)(2,1)} async-done(((bf16[128,512]{1,0:T(8,128)(2,1)}), bf16[1024,512]{1,0:T(8,128)(2,1)}) %all-gather.3.cloned.1.call-update) | async-done | bytes 1048592 | tf_op jit(solution)/shard_map/all_gather | solution.py:45
  47.3 2.1 fusion.12
  49.4 1.7 fusion.9
  51.2 2.4 add_convert_fusion
  53.5 2.8 gather_fusion
  56.3 7.1 %multiply_bitcast_fusion.1 = f32[32,128,512]{1,2,0:T(8,128)} fusion(f32[32]{0:T(128)S(1)} %compare_convert_fusion, bf16[32,128,512]{2,1,0:T(8,128)(2,1)} %gather_fusion, bf16[32,128,128]{2,1,0:T(8,128)(2,1)S(1)} %copy-done), kind=kOutput, calls=%fused_computation.5 | convolution fusion | flops 538968064 | bytes 13631616 | tf_op jit(solution)/shard_map/while/body/eval_jaxpr/lij,ljd->lid/dot_general | solution.py:62
  63.4 9.0 %copy.22 = f32[32,128,512]{2,1,0:T(8,128)} copy(f32[32,128,512]{1,2,0:T(8,128)} %multiply_bitcast_fusion.1) | data formatting | bytes 16777216 | tf_op jit(solution)/shard_map/while/body/eval_jaxpr/mul | solution.py:65
  72.4 4.3 broadcast_in_dim.107
  76.7 18.6 %scatter_fusion = f32[32,128,512]{2,1,0:T(8,128)} fusion(f32[32,128,512]{2,1,0:T(8,128)} %broadcast_in_dim.107, s32[32]{0:T(128)S(1)} %get-tuple-element.63, f32[32,128,512]{2,1,0:T(8,128)} %copy.22), kind=kCustom, calls=%fused_computation.2 | custom fusion | flops 2097152 | bytes 25165952 | tf_op jit(solution)/shard_map/while/body/eval_jaxpr/scatter-add | solution.py:65
  95.3 6.0 convert_element_type.32
  101.3 0.0 reduce-scatter.3.cloned.1.call-update
  101.3 0.0 all-gather.5.cloned.1.call-start
  101.4 91.7 %reduce-scatter.3.cloned.1.call-done = bf16[128,512]{1,0:T(8,128)(2,1)} async-done(((bf16[4096,512]{1,0:T(8,128)(2,1)}), bf16[128,512]{1,0:T(8,128)(2,1)}) %reduce-scatter.3.cloned.1.call-update) | async-done | bytes 131088 | tf_op jit(solution)/shard_map/reduce_scatter | solution.py:71
  193.1 1.9 multiply_convert_fusion
  195.0 0.0 all-gather.5.cloned.1.call-update
  195.0 0.0 reduce-scatter.5.cloned.1.call-start
  195.1 54.0 %all-gather.5.cloned.1.call-done = bf16[4096,512]{1,0:T(8,128)(2,1)} async-done(((bf16[128,512]{1,0:T(8,128)(2,1)}), bf16[4096,512]{1,0:T(8,128)(2,1)}) %all-gather.5.cloned.1.call-update) | async-done | bytes 4194320 | tf_op jit(solution)/shard_map/all_gather | solution.py:86
  249.1 5.0 gather_fusion.1
  254.1 7.0 %multiply_bitcast_fusion = f32[32,128,512]{1,2,0:T(8,128)} fusion(f32[32]{0:T(128)S(1)} %compare_convert_fusion, bf16[32,128,512]{2,1,0:T(8,128)(2,1)} %gather_fusion.1, bf16[32,128,128]{2,1,0:T(8,128)(2,1)S(1)} %copy-done), kind=kOutput, calls=%fused_computation.4 | convolution fusion | flops 538968064 | bytes 13631616 | tf_op jit(solution)/shard_map/while/body/eval_jaxpr/lji,ljd->lid/dot_general | solution.py:91
  261.1 9.0 %copy.24 = f32[32,128,512]{2,1,0:T(8,128)} copy(f32[32,128,512]{1,2,0:T(8,128)} %multiply_bitcast_fusion) | data formatting | bytes 16777216 | tf_op jit(solution)/shard_map/while/body/eval_jaxpr/mul | solution.py:94
  270.1 0.2 broadcast_in_dim.119
  270.4 11.8 %scatter_fusion.1 = f32[8,128,512]{2,1,0:T(8,128)S(1)} fusion(f32[8,128,512]{2,1,0:T(8,128)S(1)} %broadcast_in_dim.119, s32[32]{0:T(128)S(1)} %get-tuple-element.62, f32[32,128,512]{2,1,0:T(8,128)} %copy.24), kind=kCustom, calls=%fused_computation.3 | custom fusion | flops 2097152 | bytes 25165952 | tf_op jit(solution)/shard_map/while/body/eval_jaxpr/scatter-add | solution.py:94
  282.2 1.1 convert_element_type.38
  283.3 0.0 reduce-scatter.5.cloned.1.call-update
  283.4 0.0 all-reduce.3.cloned.1.call-start
  283.4 0.6 fusion.29
  286.0 1.3 fusion.3
  287.3 28.9 %reduce-scatter.5.cloned.1.call-done = bf16[128,512]{1,0:T(8,128)(2,1)} async-done(((bf16[1024,512]{1,0:T(8,128)(2,1)}), bf16[128,512]{1,0:T(8,128)(2,1)}) %reduce-scatter.5.cloned.1.call-update) | async-done | bytes 131088 | tf_op jit(solution)/shard_map/reduce_scatter | solution.py:100
  316.2 1.2 fusion
  317.5 1.2 fusion.1
  318.7 1.2 fusion.2
  319.9 2.0 pad_maximum_fusion
  321.9 0.0 all-reduce.3.cloned.1.call-update
  321.9 0.9 copy-done.2
  322.8 0.6 copy-done.3
  323.4 0.3 convolution_select_fusion.1
  323.7 0.3 fusion.4
  324.0 1.0 fusion.5
  325.0 269.1 %all-reduce.3.cloned.1.call-done = (f32[512,512]{0,1:T(8,128)}, f32[3,512,512]{2,1,0:T(8,128)}) async-done(((f32[512,512]{0,1:T(8,128)}, f32[3,512,512]{2,1,0:T(8,128)}), (f32[512,512]{0,1:T(8,128)}, f32[3,512,512]{2,1,0:T(8,128)})) %all-reduce.3.cloned.1.call-update) | async-done | bytes 4194320 | tf_op jit(solution)/shard_map/psum | solution.py:121
  594.1 2.5 copy.25
  596.7 3.9 copy.33
  (25 shorter events, 0.1 us)
Async XLA Ops:
  7.2 49.2 %copy-start = (bf16[32,128,128]{2,1,0:T(8,128)(2,1)S(1)}, bf16[32,128,128]{2,1,0:T(8,128)(2,1)}, u32[]{:S(2)}) copy-start(bf16[32,128,128]{2,1,0:T(8,128)(2,1)} %param.11) | copy-start | bytes 3145732
  7.2 40.1 %all-gather.3.cloned.1.call-start = ((), (), s32[]{:S(2)}) async-start(), calls=%async_computation.2 | async-start | bytes 1179648 | tf_op jit(solution)/shard_map/all_gather | solution.py:45
  7.9 185.2 %reduce-scatter.3.cloned.1.call-start = ((), (), s32[]{:S(2)}) async-start(), calls=%async_computation.3 | async-start | bytes 4325376 | tf_op jit(solution)/shard_map/reduce_scatter | solution.py:71
  47.3 2.2 copy-start.4
  101.3 91.8 %copy-start.7 = (bf16[128,512]{1,0:T(8,128)(2,1)S(1)}, bf16[128,512]{1,0:T(8,128)(2,1)}, u32[]{:S(2)}) copy-start(bf16[128,512]{1,0:T(8,128)(2,1)} %param.9) | copy-start | bytes 393220
  101.3 91.8 %copy-start.9 = (bf16[512,512]{1,0:T(8,128)(2,1)S(1)}, bf16[512,512]{1,0:T(8,128)(2,1)}, u32[]{:S(2)}) copy-start(bf16[512,512]{1,0:T(8,128)(2,1)} %param.15) | copy-start | bytes 1572868
  101.3 91.8 %copy-start.10 = (bf16[128,512]{1,0:T(8,128)(2,1)S(1)}, bf16[128,512]{1,0:T(8,128)(2,1)}, u32[]{:S(2)}) copy-start(bf16[128,512]{1,0:T(8,128)(2,1)} %param.17) | copy-start | bytes 393220
  101.3 147.8 %all-gather.5.cloned.1.call-start = ((), (), s32[]{:S(2)}) async-start(), calls=%async_computation.4 | async-start | bytes 4325376 | tf_op jit(solution)/shard_map/all_gather | solution.py:86
  195.0 121.2 %reduce-scatter.5.cloned.1.call-start = ((), (), s32[]{:S(2)}) async-start(), calls=%async_computation.5 | async-start | bytes 1179648 | tf_op jit(solution)/shard_map/reduce_scatter | solution.py:100
  282.2 1.2 copy-start.8
  282.2 3.8 copy-start.6
  282.2 34.0 %copy-start.5 = (bf16[128,512]{1,0:T(8,128)(2,1)S(1)}, bf16[128,512]{1,0:T(8,128)(2,1)}, u32[]{:S(2)}) copy-start(bf16[128,512]{1,0:T(8,128)(2,1)} %param.10) | copy-start | bytes 393220
  283.4 310.8 %all-reduce.3.cloned.1.call-start = ((), (), s32[]{:S(2)}) async-start(), calls=%async_computation.6 | async-start | bytes 8388608 | tf_op jit(solution)/shard_map/psum | solution.py:121
  321.9 0.9 copy-start.2
  321.9 1.5 copy-start.3
  596.7 4.0 copy-start.1
Sparse Core Ops, SparseCore 0:
  9.8 37.4 all-gather.2
  101.4 91.5 reduce-scatter.2
  196.5 52.5 all-gather.4
  283.5 32.7 reduce-scatter.4
  323.2 270.8 all-reduce.2
where the time goes:
time: 609 us; the launch traced here: 607 us
  waiting for transfers between devices  481 us (79%)
  other arithmetic  41.7 us (7%)
  local copies, waits for them, and re-layouts  38.5 us (6%)
  matrix products  28.9 us (5%)
  between operations  16.5 us (3%)
    psum x1, waiting for transfers between devices, body(): grad_self, grad_tab = lax.psum((grad_self, grad_tab), ('fact', 'dim'))  269 us
    reduce_scatter x1, waiting for transfers between devices, body(): lax.psum_scatter(partial_value.reshape(shard_rows, width).astype(jnp.bflo...  91.7 us
    all_gather x1, waiting for transfers between devices, body(): shard_grad = lax.all_gather(grad_pre, 'dim', axis=0, tiled=True)  54 us
    all_gather x1, waiting for transfers between devices, body(): lax.all_gather(dims, 'fact', axis=0, tiled=True)  36.8 us
    reduce_scatter x1, waiting for transfers between devices, body(): lax.psum_scatter(panel_grad.reshape(panel_rows, width).astype(jnp.bfloat1...  28.9 us
    scatter-add x1, other arithmetic, forward_step(): return (acc.at[fact_ids].add(contrib * alive[:, None, None]), None)  18.6 us
  transfers between devices with their start and end apart: 5, of which 5 were waited for; matrix products, arithmetic and copies ran while one was open for 1% of the time, Pallas kernels for 0%

commit v1 on v0

v1 whole, which is shorter than its diff:
```python
import jax
import jax.numpy as jnp
from jax import lax
from jax.experimental import pallas as pl
from jax.experimental.pallas import tpu as pltpu
from jax.sharding import PartitionSpec as P

F32 = jnp.float32
BF16 = jnp.bfloat16
VMEM = pl.BlockSpec(memory_space=pltpu.VMEM)
SMEM = pl.BlockSpec(memory_space=pltpu.SMEM)
PARAMS = pltpu.CompilerParams(vmem_limit_bytes=48 * 1024 * 1024)


def call(kernel, out_shape, in_specs, scratch=(), flops=0, moved=0):
    return pl.pallas_call(
        kernel,
        out_shape=out_shape,
        in_specs=in_specs,
        out_specs=jax.tree.map(lambda _: VMEM, out_shape),
        scratch_shapes=list(scratch),
        compiler_params=PARAMS,
        cost_estimate=pl.CostEstimate(flops=flops, bytes_accessed=moved, transcendentals=0),
    )


def forward_kernel(place, links_own, links_sib, table, dims_own, dims_sib, w, tiles_own, tiles_sib, out, proj, acc):
    dim_pos, core = place[1], place[2]
    holders, n_dim = dims_own.shape[0], table.shape[0] // dims_own.shape[0]
    sides = ((dims_own, links_own, tiles_own, dim_pos), (dims_sib, links_sib, tiles_sib, dim_pos + 1 - 2 * core))
    for side, (dims, _, _, column) in enumerate(sides):
        for h in range(holders):
            kind = table[h * n_dim + column]
            proj[side * holders + h] = jnp.dot(dims[h], w[kind], preferred_element_type=F32).astype(BF16)
    acc[...] = jnp.zeros_like(acc)
    for side, (_, links, tiles, _) in enumerate(sides):

        def step(slot, carry, side=side, links=links, tiles=tiles):
            target, holder = links[2 * slot], links[2 * slot + 1]

            @pl.when(lax.rem(target, 2) == core)
            def _():
                chip = lax.div(target, 2)
                acc[chip] += jnp.dot(tiles[slot], proj[side * holders + holder], preferred_element_type=F32)

            return carry

        lax.fori_loop(0, tiles.shape[0], step, 0)
    out[...] = acc[...].astype(BF16)


def middle_kernel(parts, facts, w, cot, fact_out, spread):
    pre = jnp.dot(facts[...], w[...], preferred_element_type=F32)
    agg = parts[0].astype(F32)
    for chip in range(1, parts.shape[0]):
        agg = agg + parts[chip].astype(F32)
    pre = pre + agg
    sig = jax.nn.sigmoid(pre)
    fact_out[...] = (pre * sig).astype(BF16)
    grad = cot[...].astype(F32) * sig * (1.0 + pre * (1.0 - sig))
    turned = grad.T.astype(BF16)
    for chip in range(spread.shape[0]):
        spread[chip] = turned


def backward_kernel(place, links_own, links_sib, grads, facts, tiles_own, tiles_sib, own, sib, acc, weight):
    core, chip_pos = place[2], place[3]
    holders = acc.shape[0] // 2
    acc[...] = jnp.zeros_like(acc)
    for side, (links, tiles) in enumerate(((links_own, tiles_own), (links_sib, tiles_sib))):

        def step(slot, carry, side=side, links=links, tiles=tiles):
            target, holder = links[2 * slot], links[2 * slot + 1]

            @pl.when(lax.rem(target, 2) == core)
            def _():
                at = side * holders + holder
                acc[at] += jnp.dot(grads[lax.div(target, 2)], tiles[slot], preferred_element_type=F32)

            return carry

        lax.fori_loop(0, tiles.shape[0], step, 0)
    chips = grads.shape[0]
    piece = weight.shape[0]
    half = piece // 2
    first = pl.multiple_of(chip_pos * piece, piece)
    total = jnp.zeros(weight.shape, F32)
    for chip in range(chips):
        total = total + jnp.dot(grads[chip, pl.ds(first, piece), :], facts[chip], preferred_element_type=F32)
    weight[...] = total
    for out, base, row, kind in ((own, 0, core * half, F32), (sib, holders, (1 - core) * half, BF16)):
        for z in range(8):
            for h in range(holders):
                out[z, h * 64 : (h + 1) * 64, :] = acc[base + h, z * 64 : (z + 1) * 64, :].astype(kind)
            rows = pl.ds(pl.multiple_of(row + (z % 2) * 8, 8), 8)
            mine = weight[rows, (z // 2) * 128 : (z // 2 + 1) * 128]
            out[z, 512:528, :] = jnp.concatenate([mine, jnp.zeros_like(mine)], axis=0).astype(kind)


def slice_kernel(place, table, parts, dims, tab, gsum, self_piece, tacc):
    dim_pos = place[1]
    holders = dims.shape[0]
    n_dim = table.shape[0] // holders
    total = parts[0].astype(F32)
    for z in range(1, parts.shape[0]):
        total = total + parts[z].astype(F32)
    self_piece[...] = total[512:520]
    tacc[...] = jnp.zeros_like(tacc)
    for h in range(holders):
        rounded = total[h * 64 : (h + 1) * 64].astype(BF16)
        gsum[h] = rounded
        kind = table[h * n_dim + dim_pos]
        tacc[kind] += jnp.dot(rounded, dims[h], preferred_element_type=F32)
    for q in range(4):
        for t in range(3):
            at = q * 192 + t * 64
            tab[at : at + 64, :] = tacc[t, :, q * 128 : (q + 1) * 128].astype(BF16)


def pack_kernel(parts, gsum, self_piece, out):
    total = jnp.sum(parts[...].astype(F32), axis=0)
    piece = jnp.concatenate([total, self_piece[...]], axis=0).astype(BF16)
    for z in range(out.shape[0]):
        out[z, 0:64, :] = gsum[z]
        out[z, 64:96, :] = piece


def final_kernel(place, own, sib, grad_self, grad_tab):
    even = place[2] == 0
    scale = F32(32768.0**-0.5)

    def block(d, z):
        mine, other = own[d // 2, z].astype(F32), sib[d // 2, z].astype(F32)
        return jnp.where(even, mine, other) if d % 2 == 0 else jnp.where(even, other, mine)

    for q in range(4):
        rows = []
        for pair in range(4):
            halves = []
            for z in (2 * pair, 2 * pair + 1):
                parts = [block(d, z)[0:24] for d in range(8 * q, 8 * q + 8)]
                halves.append(jnp.concatenate(parts, axis=0))
            for t in range(3):
                both = jnp.concatenate([x[t * 64 : (t + 1) * 64] for x in halves], axis=0)
                grad_tab[t, q * 128 : (q + 1) * 128, pair * 128 : (pair + 1) * 128] = both.T * scale
        for d in range(32):
            rows += [block(d, 2 * q)[24:32], block(d, 2 * q + 1)[24:32]]
        for part in range(4):
            both = jnp.concatenate(rows[part * 16 : (part + 1) * 16], axis=0)
            grad_self[q * 128 : (q + 1) * 128, part * 128 : (part + 1) * 128] = both.T * scale


def body(facts, dims, tiles, links, link_count, block_table, w_self, w_tables, cot):
    n_fact = lax.axis_size("fact")
    n_dim = lax.axis_size("dim")
    fact_pos = lax.axis_index("fact")
    dim_pos = lax.axis_index("dim")
    chips = n_dim // 2
    same = [[2 * m + core for m in range(chips)] for core in range(2)]
    pair = [(d, d ^ 1) for d in range(n_dim)]
    rows, width = dims.shape
    slots, block, _ = tiles.shape
    place = jnp.stack([fact_pos, dim_pos, dim_pos % 2, dim_pos // 2]).astype(jnp.int32)

    def swap(x):
        return lax.ppermute(x, "dim", pair)

    def by_chip(x):
        return lax.all_to_all(x, "dim", 0, 0, tiled=True, axis_index_groups=same)

    def by_fact(x):
        return lax.all_to_all(x, "fact", 0, 0, tiled=True)

    live = jnp.arange(slots, dtype=jnp.int32) < link_count[0]
    target = jnp.where(live, links[:, 0] - fact_pos * n_dim, -1)
    links_own = jnp.stack([target, links[:, 1] // n_dim], axis=1).reshape(-1)
    links_sib = swap(links_own)
    tiles_sib = swap(tiles)
    facts_all = lax.all_gather(facts, "dim", axis=0, axis_index_groups=same)
    dims_own = by_fact(jnp.broadcast_to(dims[None], (n_fact, rows, width)))
    dims_sib = swap(dims_own)

    partial = call(
        forward_kernel,
        jax.ShapeDtypeStruct((chips, block, width), BF16),
        [SMEM] * 4 + [VMEM] * 5,
        [pltpu.VMEM((2 * n_fact, rows, width), BF16), pltpu.VMEM((chips, block, width), F32)],
        flops=2 * slots * block * block * width + 4 * n_fact * rows * width * width,
        moved=8 << 20,
    )(place, links_own, links_sib, block_table, dims_own, dims_sib, w_tables, tiles, tiles_sib)
    parts = by_chip(partial)

    fact_out, spread = call(
        middle_kernel,
        (jax.ShapeDtypeStruct((block, width), BF16), jax.ShapeDtypeStruct((chips, width, block), BF16)),
        [VMEM] * 4,
        flops=2 * block * width * width,
        moved=5 << 20,
    )(parts, facts, w_self, cot)
    grads = by_chip(spread)

    own, sib = call(
        backward_kernel,
        (jax.ShapeDtypeStruct((n_fact, 528, 128), F32), jax.ShapeDtypeStruct((n_fact, 528, 128), BF16)),
        [SMEM] * 3 + [VMEM] * 4,
        [pltpu.VMEM((2 * n_fact, width, block), F32), pltpu.VMEM((width // chips, width), F32)],
        flops=2 * slots * block * block * width,
        moved=9 << 20,
    )(place, links_own, links_sib, grads, facts_all, tiles, tiles_sib)
    slices = by_fact((own + swap(sib).astype(F32)).astype(BF16))

    tab, gsum, self_piece = call(
        slice_kernel,
        (
            jax.ShapeDtypeStruct((768, 128), BF16),
            jax.ShapeDtypeStruct((n_fact, 64, 128), BF16),
            jax.ShapeDtypeStruct((8, 128), F32),
        ),
        [SMEM] * 2 + [VMEM] * 2,
        [pltpu.VMEM((3, 64, width), F32)],
        flops=2 * n_fact * 64 * 128 * width,
        moved=3 << 20,
    )(place, block_table, slices, dims_own)
    tab = lax.all_to_all(tab.reshape(n_dim, 24, 128), "dim", 0, 0, tiled=True)
    packed = call(
        pack_kernel, jax.ShapeDtypeStruct((n_fact, 96, 128), BF16), [VMEM] * 3, moved=1 << 19
    )(tab, gsum, self_piece)
    packed = by_fact(packed)
    pieces_own = by_chip(jnp.broadcast_to(packed[None, :, 64:, :], (chips, n_fact, 32, 128)))
    pieces_sib = swap(pieces_own)

    turned = packed[:, :64, :].reshape(width, rows)
    kind = lax.dynamic_index_in_dim(block_table, fact_pos * n_dim + dim_pos, keepdims=False)
    weight = lax.dynamic_index_in_dim(w_tables, kind, keepdims=False)
    grad_dims = lax.dot_general(turned, weight, (((0,), (1,)), ((), ())), preferred_element_type=F32)

    grad_self, grad_tab = call(
        final_kernel,
        (jax.ShapeDtypeStruct((width, width), F32), jax.ShapeDtypeStruct((3, width, width), F32)),
        [SMEM] + [VMEM] * 2,
        moved=6 << 20,
    )(place, pieces_own, pieces_sib)
    return (fact_out, grad_dims, grad_self, grad_tab)


def solution(mesh):
    split = P(("fact", "dim"), None)
    return jax.shard_map(
        body,
        mesh=mesh,
        in_specs=(split, split, P(("fact", "dim"), None, None), split, P(("fact", "dim")), P(), P(), P(), split),
        out_specs=(split, split, P(), P()),
        check_vma=False,
    )
```

time: 609 us -> 263 us (0.43)
  waiting for transfers between devices: 481 us -> 99.6 us
  blocking collectives: 0 us -> 83 us
  other arithmetic: 41.7 us -> 1.92 us
  local copies, waits for them, and re-layouts: 38.5 us -> 9.54 us
  matrix products: 28.9 us -> 2.06 us
  starting transfers between devices: 0.2 us -> 26.4 us
  Pallas kernels: 0 us -> 22 us
    psum x1 -> x0, waiting for transfers between devices: 269 us -> none  [body(): grad_self, grad_tab = lax.psum((grad_self, grad_tab), ('fact', 'dim'))]
    reduce_scatter x2 -> x0, waiting for transfers between devices: 121 us -> none  [the longest x1 91.7 us: body(): lax.psum_scatter(partial_value.reshape(shard_rows, width).astype(jnp.bflo...]
    all_to_all x0 -> x4, blocking collectives: none -> 83 us  [the longest x2 51.7 us: by_fact(): return lax.all_to_all(x, 'fact', 0, 0, tiled=True)]
    all_to_all x0 -> x3, waiting for transfers between devices: none -> 57.8 us  [the longest x2 29.7 us: by_chip(): return lax.all_to_all(x, 'dim', 0, 0, tiled=True, axis_index_groups=same)]
    all_gather x2 -> x1, waiting for transfers between devices: 90.8 us -> 37.4 us  [body(): facts_all = lax.all_gather(facts, 'dim', axis=0, axis_index_groups=same)]
    scatter-add x2 -> x0, other arithmetic: 30.4 us -> none  [the longest x1 18.6 us: forward_step(): return (acc.at[fact_ids].add(contrib * alive[:, None, None]), None)]
    dot_general x13 -> x1, matrix products: 28.9 us -> 2.06 us  [body(): lax.dot_general(turned, weight, (((0,), (1,)), ((), ())), preferred_eleme...]
    pallas_call x0 -> x6, Pallas kernels: none -> 22 us  [the longest x1 8.61 us: body(): call(forward_kernel, jax.ShapeDtypeStruct((chips, block, width), BF16), [...]
  transfers between devices with their start and end apart: 5 -> 9, of which waited for: 5 -> 6; matrix products, arithmetic and copies ran while one was open for 1% -> 1% of each run, Pallas kernels for 0% -> 0%
where the time goes in v1:
time: 263 us; the launch traced here: 261 us
  waiting for transfers between devices  99.6 us (38%)
  blocking collectives  83 us (32%)
  starting transfers between devices  26.4 us (10%)
  Pallas kernels  22 us (8%)
  between operations  16.8 us (6%)
  local copies, waits for them, and re-layouts  9.54 us (4%)
    all_to_all x2, blocking collectives, by_fact(): return lax.all_to_all(x, 'fact', 0, 0, tiled=True)  51.7 us
    all_gather x1, waiting for transfers between devices, body(): facts_all = lax.all_gather(facts, 'dim', axis=0, axis_index_groups=same)  37.4 us
    all_to_all x2, waiting for transfers between devices, by_chip(): return lax.all_to_all(x, 'dim', 0, 0, tiled=True, axis_index_groups=same)  29.7 us
    all_to_all x1, waiting for transfers between devices, by_fact(): return lax.all_to_all(x, 'fact', 0, 0, tiled=True)  28.1 us
    all_to_all x1, blocking collectives, by_chip(): return lax.all_to_all(x, 'dim', 0, 0, tiled=True, axis_index_groups=same)  18.9 us
    all_to_all x1, blocking collectives, body(): tab = lax.all_to_all(tab.reshape(n_dim, 24, 128), 'dim', 0, 0, tiled=True)  12.4 us
    all_to_all x2, starting transfers between devices, by_chip(): return lax.all_to_all(x, 'dim', 0, 0, tiled=True, axis_index_groups=same)  11.5 us
    all_to_all x1, starting transfers between devices, by_fact(): return lax.all_to_all(x, 'fact', 0, 0, tiled=True)  9.01 us
  transfers between devices with their start and end apart: 9, of which 6 were waited for; matrix products, arithmetic and copies ran while one was open for 1% of the time, Pallas kernels for 0%

profile of v1, /device:TPU:1, one launch (start us, length us, event | category | flops | bytes accessed | tf_op | source)
XLA Modules:
  0.0 261.2 jit_solution(13977228310772313525)
XLA Ops:
  7.2 0.0 copy-start
  7.2 0.0 copy-start.10
  7.2 0.0 copy-start.9
  7.2 2.0 broadcast_in_dim.9
  9.2 9.0 %all-to-all-start = ((bf16[8,128,512]{2,1,0:T(8,128)(2,1)}), bf16[8,128,512]{2,1,0:T(8,128)(2,1)S(1)}, u32[]{:S(2)}, u32[]{:S(2)}) async-start(bf16[8,128,512]{2,1,0:T(8,128)(2,1)} %broadcast_in_dim.9), calls=%async_computation | async-start | bytes 2097152 | tf_op jit(solution)/shard_map/all_to_all | solution.py:172
  18.3 0.0 copy-done
  18.3 1.0 collective-permute-start.2
  19.3 28.1 %all-to-all-done.dims_own.dims = bf16[8,128,512]{2,1,0:T(8,128)(2,1)S(1)} async-done(((bf16[8,128,512]{2,1,0:T(8,128)(2,1)}), bf16[8,128,512]{2,1,0:T(8,128)(2,1)S(1)}, u32[]{:S(2)}, u32[]{:S(2)}) %all-to-all-start) | async-done | bytes 1048608 | tf_op jit(solution)/shard_map/all_to_all | solution.py:172
  47.5 0.5 collective-permute-start.1
  48.6 0.0 copy-done.10
  48.6 0.1 copy.14
  48.7 0.1 reshape.26.links_own
  48.8 0.1 collective-permute-start
  49.0 0.1 pad_add_fusion.1.place
  49.0 1.2 collective-permute-done.links_sib
  50.2 0.0 collective-permute-done.2.tiles_sib
  50.2 0.1 collective-permute-done.1.dims_sib
  50.4 0.0 copy-done.9
  50.4 1.7 copy-done.4
  52.0 8.6 %shard_map.120 = bf16[16,128,512]{2,1,0:T(8,128)(2,1)} custom-call(s32[4]{0:T(128)S(1)} %pad_add_fusion.1.place, s32[64]{0:T(128)S(1)} %reshape.26.links_own, s32[64]{0:T(128)S(1)} %collective-permute-done.links_sib, s32[256]{0:T(256)S(1)} %copy-done.9, bf16[8,128,512]{2,1,0:T(8,128)(2,1)S(1)} %all-to-all-done.dims_own.dims, ...), custom_call_target="tpu_custom_call" | custom-call | flops 1610612736 | bytes 8388608 | tf_op jit(solution)/shard_map/pallas_call | solution.py:183
  60.7 7.3 %all-to-all-start.1 = ((bf16[16,128,512]{2,1,0:T(8,128)(2,1)}), bf16[16,128,512]{2,1,0:T(8,128)(2,1)S(1)}, u32[]{:S(2)}, u32[]{:S(2)}) async-start(bf16[16,128,512]{2,1,0:T(8,128)(2,1)} %shard_map.120), calls=%async_computation.1 | async-start | bytes 4194304 | tf_op jit(solution)/shard_map/all_to_all | solution.py:169
  68.0 0.0 all-gather.3.cloned.1.call-start
  68.0 0.7 all-gather.3.cloned.1.call-update
  68.7 29.7 %all-to-all-done.1.parts = bf16[16,128,512]{2,1,0:T(8,128)(2,1)S(1)} async-done(((bf16[16,128,512]{2,1,0:T(8,128)(2,1)}), bf16[16,128,512]{2,1,0:T(8,128)(2,1)S(1)}, u32[]{:S(2)}, u32[]{:S(2)}) %all-to-all-start.1) | async-done | bytes 2097184 | tf_op jit(solution)/shard_map/all_to_all | solution.py:169
  98.4 0.0 copy-done.6
  98.4 1.0 copy-done.7
  99.4 1.1 shard_map.121
  100.6 1.3 copy-done.5
  101.9 4.2 %all-to-all-start.2 = ((bf16[16,512,128]{2,1,0:T(8,128)(2,1)}), bf16[16,512,128]{2,1,0:T(8,128)(2,1)S(1)}, u32[]{:S(2)}, u32[]{:S(2)}) async-start(bf16[16,512,128]{2,1,0:T(8,128)(2,1)} %copy-done.5), calls=%async_computation.2 | async-start | bytes 4194304 | tf_op jit(solution)/shard_map/all_to_all | solution.py:169
  106.1 37.4 %all-gather.3.cloned.1.call-done = bf16[2048,512]{1,0:T(8,128)(2,1)} async-done(((bf16[128,512]{1,0:T(8,128)(2,1)}), bf16[2048,512]{1,0:T(8,128)(2,1)}) %all-gather.3.cloned.1.call-update) | async-done | bytes 2097168 | tf_op jit(solution)/shard_map/all_gather | solution.py:179
  143.5 0.0 all-to-all-done.2.grads
  143.5 1.2 copy-done.1
  144.8 1.2 copy-done.3
  146.0 8.1 %shard_map.122 = (f32[8,528,128]{2,1,0:T(8,128)}, bf16[8,528,128]{2,1,0:T(8,128)(2,1)S(1)}) custom-call(s32[4]{0:T(128)S(1)} %pad_add_fusion.1.place, s32[64]{0:T(128)S(1)} %reshape.26.links_own, s32[64]{0:T(128)S(1)} %collective-permute-done.links_sib, bf16[16,512,128]{2,1,0:T(8,128)(2,1)S(1)} %all-to-all-done.2.grads, bf16[16,128,512]{2,1,0:T(8,128)(2,1)} %bitcast.15, ...), custom_call_target="tpu_custom_call" | custom-call | flops 536870912 | bytes 9437184 | tf_op jit(solution)/shard_map/pallas_call | solution.py:202
  154.1 2.2 collective-permute-start.3
  156.2 2.3 collective-permute-done.3
  158.6 1.8 add_convert_fusion
  160.4 38.4 %all_to_all.35.parts = bf16[8,528,128]{2,1,0:T(8,128)(2,1)S(1)} all-to-all(bf16[8,528,128]{2,1,0:T(8,128)(2,1)S(1)} %add_convert_fusion), channel_id=1, replica_groups=mesh['fact'=8,'dim'=32] {'fact'}, dimensions={0} | all-to-all | bytes 2162688 | tf_op jit(solution)/shard_map/all_to_all | solution.py:172
  198.8 0.9 shard_map.123
  199.7 12.4 %all_to_all.36.parts = bf16[32,24,128]{2,1,0:T(8,128)(2,1)S(1)} all-to-all(bf16[32,24,128]{2,1,0:T(8,128)(2,1)S(1)} %bitcast.14), channel_id=1, replica_groups=mesh['fact'=8,'dim'=32] {'dim'}, dimensions={0} | all-to-all | bytes 393216 | tf_op jit(solution)/shard_map/all_to_all | solution.py:224
  212.2 13.3 %all_to_all.37 = bf16[8,96,128]{2,1,0:T(8,128)(2,1)S(1)} all-to-all(bf16[8,96,128]{2,1,0:T(8,128)(2,1)S(1)} %shard_map.124), channel_id=1, replica_groups=mesh['fact'=8,'dim'=32] {'fact'}, dimensions={0} | all-to-all | bytes 393216 | tf_op jit(solution)/shard_map/all_to_all | solution.py:172
  225.5 0.2 broadcast_in_dim.18
  225.7 18.9 %all_to_all.38.own = bf16[16,8,32,128]{3,2,1,0:T(8,128)(2,1)S(1)} all-to-all(bf16[16,8,32,128]{3,2,1,0:T(8,128)(2,1)S(1)} %broadcast_in_dim.18), channel_id=1, replica_groups={{0,2,4,6,8,10,12,14,16,18,20,22,24,26,28,30},{1,3,5,7,9,11,13,15,17,19,..., dimensions={0} | all-to-all | bytes 2097152 | tf_op jit(solution)/shard_map/all_to_all | solution.py:169
  244.6 2.0 collective-permute-start.4
  246.6 0.6 dynamic_slice.8
  249.1 2.1 fusion
  251.2 0.0 collective-permute-done.4.sib
  251.2 3.2 %shard_map.125 = (f32[512,512]{1,0:T(8,128)}, f32[3,512,512]{2,1,0:T(8,128)}) custom-call(s32[4]{0:T(128)S(1)} %pad_add_fusion.1.place, bf16[16,8,32,128]{3,2,1,0:T(8,128)(2,1)S(1)} %all_to_all.38.own, bf16[16,8,32,128]{3,2,1,0:T(8,128)(2,1)S(1)} %collective-permute-done.4.sib), custom_call_target="tpu_custom_call" | custom-call | bytes 6291456 | tf_op jit(solution)/shard_map/pallas_call | solution.py:237
  (15 shorter events, 0.1 us)
Async XLA Ops:
  7.2 11.1 %copy-start = (bf16[32,128,128]{2,1,0:T(8,128)(2,1)S(1)}, bf16[32,128,128]{2,1,0:T(8,128)(2,1)}, u32[]{:S(2)}) copy-start(bf16[32,128,128]{2,1,0:T(8,128)(2,1)} %tiles_own.3) | copy-start | bytes 3145732
  7.2 41.4 %copy-start.10 = (s32[32,2]{0,1:T(2,128)S(1)}, s32[32,2]{0,1:T(2,128)}, u32[]{:S(2)}) copy-start(s32[32,2]{0,1:T(2,128)} %param.12) | copy-start | bytes 772
  7.2 43.2 %copy-start.9 = (s32[256]{0:T(256)S(1)}, s32[256]{0:T(256)}, u32[]{:S(2)}) copy-start(s32[256]{0:T(256)} %table.3) | copy-start | bytes 3076
  9.2 38.2 %all-to-all-start = ((bf16[8,128,512]{2,1,0:T(8,128)(2,1)}), bf16[8,128,512]{2,1,0:T(8,128)(2,1)S(1)}, u32[]{:S(2)}, u32[]{:S(2)}) async-start(bf16[8,128,512]{2,1,0:T(8,128)(2,1)} %broadcast_in_dim.9), calls=%async_computation | async-start | bytes 2097152 | tf_op jit(solution)/shard_map/all_to_all | solution.py:172
  18.3 32.0 %collective-permute-start.2 = (bf16[32,128,128]{2,1,0:T(8,128)(2,1)S(1)}, bf16[32,128,128]{2,1,0:T(8,128)(2,1)S(1)}, u32[]{:S(2)}, u32[]{:S(2)}) collective-permute-start(bf16[32,128,128]{2,1,0:T(8,128)(2,1)S(1)} %copy-done), channel_id=1, source_target_pairs={{0,1},{1,0},{2,3},{3,2},{4,5},{5,4},{6,7},{7,6},{8,9},{9,8},{10,11... | collective-permute-start | bytes 3145736 | tf_op jit(solution)/shard_map/ppermute | solution.py:166
  47.5 2.9 %collective-permute-start.1 = (bf16[8,128,512]{2,1,0:T(8,128)(2,1)S(1)}, bf16[8,128,512]{2,1,0:T(8,128)(2,1)}, u32[]{:S(2)}, u32[]{:S(2)}) collective-permute-start(bf16[8,128,512]{2,1,0:T(8,128)(2,1)S(1)} %all-to-all-done.dims_own.dims), channel_id=1, source_target_pairs={{0,1},{1,0},{2,3},{3,2},{4,5},{5,4},{6,7},{7,6},{8,9},{9,8},{10,11... | collective-permute-start | bytes 3145736 | tf_op jit(solution)/shard_map/ppermute | solution.py:166
  48.8 1.4 collective-permute-start
  50.2 10.4 %copy-start.2 = (bf16[32,128,128]{2,1,0:T(8,128)(2,1)}, bf16[32,128,128]{2,1,0:T(8,128)(2,1)S(1)}, u32[]{:S(2)}) copy-start(bf16[32,128,128]{2,1,0:T(8,128)(2,1)S(1)} %collective-permute-done.2.tiles_sib) | copy-start | bytes 3145732
  50.4 1.7 copy-start.4
  60.6 37.7 %copy-start.6 = (bf16[128,512]{1,0:T(8,128)(2,1)S(1)}, bf16[128,512]{1,0:T(8,128)(2,1)}, u32[]{:S(2)}) copy-start(bf16[128,512]{1,0:T(8,128)(2,1)} %facts.1) | copy-start | bytes 393220
  60.6 37.7 %copy-start.8 = (bf16[128,512]{1,0:T(8,128)(2,1)S(1)}, bf16[128,512]{1,0:T(8,128)(2,1)}, u32[]{:S(2)}) copy-start(bf16[128,512]{1,0:T(8,128)(2,1)} %cot.1) | copy-start | bytes 393220
  60.7 37.7 %all-to-all-start.1 = ((bf16[16,128,512]{2,1,0:T(8,128)(2,1)}), bf16[16,128,512]{2,1,0:T(8,128)(2,1)S(1)}, u32[]{:S(2)}, u32[]{:S(2)}) async-start(bf16[16,128,512]{2,1,0:T(8,128)(2,1)} %shard_map.120), calls=%async_computation.1 | async-start | bytes 4194304 | tf_op jit(solution)/shard_map/all_to_all | solution.py:169
  68.0 75.6 %all-gather.3.cloned.1.call-start = ((), (), s32[]{:S(2)}) async-start(), calls=%async_computation.7 | async-start | bytes 2228224 | tf_op jit(solution)/shard_map/all_gather | solution.py:179
  98.4 1.0 copy-start.7
  100.6 1.3 copy-start.5
  101.9 41.6 %all-to-all-start.2 = ((bf16[16,512,128]{2,1,0:T(8,128)(2,1)}), bf16[16,512,128]{2,1,0:T(8,128)(2,1)S(1)}, u32[]{:S(2)}, u32[]{:S(2)}) async-start(bf16[16,512,128]{2,1,0:T(8,128)(2,1)} %copy-done.5), calls=%async_computation.2 | async-start | bytes 4194304 | tf_op jit(solution)/shard_map/all_to_all | solution.py:169
  143.5 1.2 copy-start.1
  144.7 1.2 copy-start.3
  154.1 4.5 %collective-permute-start.3 = (bf16[8,528,128]{2,1,0:T(8,128)(2,1)S(1)}, bf16[8,528,128]{2,1,0:T(8,128)(2,1)S(1)}, u32[]{:S(2)}, u32[]{:S(2)}) collective-permute-start(bf16[8,528,128]{2,1,0:T(8,128)(2,1)S(1)} %get-tuple-element.16), channel_id=1, source_target_pairs={{0,1},{1,0},{2,3},{3,2},{4,5},{5,4},{6,7},{7,6},{8,9},{9,8},{10,11... | collective-permute-start | bytes 3244040 | tf_op jit(solution)/shard_map/ppermute | solution.py:166
  244.6 6.6 %collective-permute-start.4 = (bf16[16,8,32,128]{3,2,1,0:T(8,128)(2,1)S(1)}, bf16[16,8,32,128]{3,2,1,0:T(8,128)(2,1)S(1)}, u32[]{:S(2)}, u32[]{:S(2)}) collective-permute-start(bf16[16,8,32,128]{3,2,1,0:T(8,128)(2,1)S(1)} %all_to_all.38.own), channel_id=1, source_target_pairs={{0,1},{1,0},{2,3},{3,2},{4,5},{5,4},{6,7},{7,6},{8,9},{9,8},{10,11... | collective-permute-start | bytes 3145736 | tf_op jit(solution)/shard_map/ppermute | solution.py:166
Sparse Core Ops, SparseCore 0:
  71.2 72.2 all-gather.2

commit v2 on v1

v2 whole, which is shorter than its diff:
```python
import jax
import jax.numpy as jnp
from jax import lax
from jax.experimental import pallas as pl
from jax.experimental.pallas import tpu as pltpu
from jax.sharding import PartitionSpec as P

F32 = jnp.float32
BF16 = jnp.bfloat16
VMEM = pl.BlockSpec(memory_space=pltpu.VMEM)
SMEM = pl.BlockSpec(memory_space=pltpu.SMEM)
PARAMS = pltpu.CompilerParams(vmem_limit_bytes=24 * 1024 * 1024)
UNROLL = 2


def call(kernel, out_shape, in_specs, scratch=(), flops=0, moved=0):
    return pl.pallas_call(
        kernel,
        out_shape=out_shape,
        in_specs=in_specs,
        out_specs=jax.tree.map(lambda _: VMEM, out_shape),
        scratch_shapes=list(scratch),
        compiler_params=PARAMS,
        cost_estimate=pl.CostEstimate(flops=flops, bytes_accessed=moved, transcendentals=0),
    )


def project_kernel(place, table, dims, w, out):
    out[...] = jnp.dot(dims[...], w[0], preferred_element_type=F32).astype(BF16)


def project(place, table, dims, w):
    rows, width = dims.shape
    n_dim = table.shape[0] // 8
    return pl.pallas_call(
        project_kernel,
        out_shape=jax.ShapeDtypeStruct((rows, width), BF16),
        grid_spec=pltpu.PrefetchScalarGridSpec(
            num_scalar_prefetch=2,
            grid=(1,),
            in_specs=[
                pl.BlockSpec((rows, width), lambda i, place, table: (0, 0)),
                pl.BlockSpec((1, width, width), lambda i, place, table: (table[place[0] * n_dim + place[1]], 0, 0)),
            ],
            out_specs=pl.BlockSpec((rows, width), lambda i, place, table: (0, 0)),
        ),
        compiler_params=PARAMS,
        cost_estimate=pl.CostEstimate(flops=2 * rows * width * width, bytes_accessed=1 << 20, transcendentals=0),
    )(place, table, dims, w)


def decode(code):
    return code & 31, (code >> 5) & 7, code >> 8


def forward_kernel(place, lists, counts, *refs):
    panels, (facts_t, tiles_own, tiles_sib, out, panel, acc) = (refs[:9], refs[9:18]), refs[18:]
    fact_pos = place[0]
    half = panels[0][7].shape[0]
    for side in range(2):
        for at, shift in enumerate((0, -1, 1, -2, 2, -3, 3)):
            panel[side * 8 + ((fact_pos + shift) & 7)] = panels[side][at][...]
        far = side * 8 + ((fact_pos + 4) & 7)
        panel[far, 0:half, :] = panels[side][7][...]
        panel[far, half : 2 * half, :] = panels[side][8][...]
    acc[...] = jnp.zeros_like(acc)
    for side, tiles in enumerate((tiles_own, tiles_sib)):

        def step(i, carry, side=side, tiles=tiles):
            found = []
            for u in range(UNROLL):
                slot, holder, chip = decode(lists[side * 32 + i * UNROLL + u])
                found.append((chip, jnp.dot(tiles[slot], panel[side * 8 + holder], preferred_element_type=F32)))
            for chip, value in found:
                acc[chip] += value
            return carry

        lax.fori_loop(0, (counts[side] + UNROLL - 1) // UNROLL, step, 0)
    for chip in range(out.shape[0]):
        for q in range(4):
            out[chip, q * 128 : (q + 1) * 128, :] = acc[chip, :, q * 128 : (q + 1) * 128].astype(BF16)
        out[chip, 512:544, :] = facts_t[chip]


def middle_kernel(parts, facts, w, cot, fact_out, spread, facts_t):
    pre = jnp.dot(facts[...], w[...], preferred_element_type=F32)
    aggs = []
    for q in range(4):
        agg = parts[0, q * 128 : (q + 1) * 128, :].astype(F32)
        for chip in range(1, parts.shape[0]):
            agg = agg + parts[chip, q * 128 : (q + 1) * 128, :].astype(F32)
        aggs.append(agg)
    pre = pre + jnp.concatenate(aggs, axis=1)
    sig = jax.nn.sigmoid(pre)
    fact_out[...] = (pre * sig).astype(BF16)
    grad = cot[...].astype(F32) * sig * (1.0 + pre * (1.0 - sig))
    turned = grad.T.astype(BF16)
    for chip in range(spread.shape[0]):
        spread[chip] = turned
        facts_t[chip] = parts[chip, 512:544, :]


def backward_kernel(place, lists, counts, grads, facts_t, tiles_own, tiles_sib, own, sib, acc, weight):
    core = place[2]
    holders = 8
    acc[...] = jnp.zeros_like(acc)
    for side, tiles in enumerate((tiles_own, tiles_sib)):

        def step(i, carry, side=side, tiles=tiles):
            found = []
            for u in range(UNROLL):
                slot, holder, chip = decode(lists[side * 32 + i * UNROLL + u])
                at = jnp.where(chip == 16, 16, side * holders + holder)
                value = jnp.dot(grads[jnp.minimum(chip, 15)], tiles[slot], preferred_element_type=F32)
                found.append((at, value))
            for at, value in found:
                acc[at] += value
            return carry

        lax.fori_loop(0, (counts[side] + UNROLL - 1) // UNROLL, step, 0)
    half = weight.shape[0] // 2
    total = jnp.zeros(weight.shape, F32)
    for chip in range(grads.shape[0]):
        total = total + lax.dot_general(
            facts_t[chip], grads[chip], (((1,), (1,)), ((), ())), preferred_element_type=F32
        )
    weight[...] = total
    for out, base, row, kind in ((own, 0, core * half, F32), (sib, holders, (1 - core) * half, BF16)):
        for z in range(8):
            for h in range(holders):
                out[z, h * 64 : (h + 1) * 64, :] = acc[base + h, z * 64 : (z + 1) * 64, :].astype(kind)
            rows = pl.ds(pl.multiple_of(row + (z % 2) * 8, 8), 8)
            mine = weight[rows, (z // 2) * 128 : (z // 2 + 1) * 128]
            out[z, 512:528, :] = jnp.concatenate([mine, jnp.zeros_like(mine)], axis=0).astype(kind)


def slice_kernel(place, table, parts, dims, tab, gsum, self_piece, tacc):
    dim_pos = place[1]
    holders = dims.shape[0]
    n_dim = table.shape[0] // holders
    total = parts[0].astype(F32)
    for z in range(1, parts.shape[0]):
        total = total + parts[z].astype(F32)
    self_piece[...] = total[512:520]
    tacc[...] = jnp.zeros_like(tacc)
    for h in range(holders):
        rounded = total[h * 64 : (h + 1) * 64].astype(BF16)
        gsum[h] = rounded
        kind = table[h * n_dim + dim_pos]
        tacc[kind] += jnp.dot(rounded, dims[h], preferred_element_type=F32)
    for q in range(4):
        for t in range(3):
            at = q * 192 + t * 64
            tab[at : at + 64, :] = tacc[t, :, q * 128 : (q + 1) * 128].astype(BF16)


def pack_kernel(parts, gsum, self_piece, out):
    total = jnp.sum(parts[...].astype(F32), axis=0)
    piece = jnp.concatenate([total, self_piece[...]], axis=0).astype(BF16)
    for z in range(out.shape[0]):
        out[z, 0:64, :] = gsum[z]
        out[z, 64:96, :] = piece


def final_kernel(place, table, own, sib, packed, w, grad_dims, grad_self, grad_tab):
    even = place[2] == 0
    scale = F32(32768.0**-0.5)
    kind = table[place[0] * 32 + place[1]]
    turned = packed[:, 0:64, :].astype(F32).reshape(512, 128)
    grad_dims[...] = lax.dot_general(
        turned.T.astype(BF16), w[kind], (((1,), (1,)), ((), ())), preferred_element_type=F32
    )

    def block(d, z):
        mine, other = own[d // 2, z].astype(F32), sib[d // 2, z].astype(F32)
        return (jnp.where(even, mine, other) if d % 2 == 0 else jnp.where(even, other, mine)) * scale

    for q in range(4):
        for pair in range(4):
            halves = []
            for z in (2 * pair, 2 * pair + 1):
                every = [block(d, z) for d in range(8 * q, 8 * q + 8)]
                halves.append(jnp.concatenate([x[0:24] for x in every], axis=0))
                for at, x in enumerate(every):
                    row = (8 * q + at) * 16 + (z % 2) * 8
                    grad_self[row : row + 8, pair * 128 : (pair + 1) * 128] = x[24:32]
            for t in range(3):
                both = jnp.concatenate([x[t * 64 : (t + 1) * 64] for x in halves], axis=0)
                grad_tab[t, q * 128 : (q + 1) * 128, pair * 128 : (pair + 1) * 128] = both.T


def compact(codes, active):
    at = jnp.arange(codes.shape[0], dtype=jnp.int32)
    place_of = jnp.sum(jnp.where(active[None, :] & (at[None, :] < at[:, None]), 1, 0), axis=1)
    hit = active[:, None] & (place_of[:, None] == at[None, :])
    listed = jnp.sum(jnp.where(hit, codes[:, None] - (16 << 8), 0), axis=0) + (16 << 8)
    return listed, jnp.sum(active.astype(jnp.int32))


def body(facts, dims, tiles, links, link_count, block_table, w_self, w_tables, cot):
    n_fact = lax.axis_size("fact")
    n_dim = lax.axis_size("dim")
    fact_pos = lax.axis_index("fact")
    dim_pos = lax.axis_index("dim")
    chips = n_dim // 2
    same = [[2 * m + core for m in range(chips)] for core in range(2)]
    pair = [(d, d ^ 1) for d in range(n_dim)]
    rows, width = dims.shape
    slots, block, _ = tiles.shape
    core = dim_pos & 1
    place = jnp.stack([fact_pos, dim_pos, core, dim_pos >> 1]).astype(jnp.int32)

    def swap(x):
        return lax.ppermute(x, "dim", pair)

    def shift(x, by):
        return lax.ppermute(x, "fact", [(i, (i + by) % n_fact) for i in range(n_fact)])

    def by_chip(x):
        return lax.all_to_all(x, "dim", 0, 0, tiled=True, axis_index_groups=same)

    def by_fact(x):
        return lax.all_to_all(x, "fact", 0, 0, tiled=True)

    mine = project(place, block_table, dims, w_tables)
    pieces, up, down = [mine], mine, mine
    for _ in range(3):
        up, down = shift(up, 1), shift(down, -1)
        pieces += [up, down]
    pieces += [shift(up[: rows // 2], 1), shift(down[rows // 2 :], -1)]
    pieces_sib = [swap(x) for x in pieces]

    live = jnp.arange(slots, dtype=jnp.int32) < link_count[0]
    target = links[:, 0] - fact_pos * n_dim
    codes_own = jnp.arange(slots, dtype=jnp.int32) + ((links[:, 1] // n_dim) << 5) + ((target >> 1) << 8)
    keys_own = jnp.where(live, 2 * codes_own + (target & 1), -1)
    keys_sib = swap(keys_own)
    tiles_sib = swap(tiles)
    found = [compact(x >> 1, (x >= 0) & ((x & 1) == core)) for x in (keys_own, keys_sib)]
    lists = jnp.concatenate([x[0] for x in found])
    counts = jnp.stack([x[1] for x in found])
    facts_t = facts.T.reshape(chips, width // chips, block)

    partial = call(
        forward_kernel,
        jax.ShapeDtypeStruct((chips, 544, 128), BF16),
        [SMEM] * 3 + [VMEM] * 21,
        [pltpu.VMEM((2 * n_fact, rows, width), BF16), pltpu.VMEM((chips + 1, block, width), F32)],
        flops=2 * slots * block * block * width,
        moved=8 << 20,
    )(place, lists, counts, *pieces, *pieces_sib, facts_t, tiles, tiles_sib)
    late_dims, partial = lax.optimization_barrier((dims, partial))
    dims_all = lax.all_gather(late_dims, "fact", axis=0)
    parts = by_chip(partial)

    fact_out, spread, facts_t = call(
        middle_kernel,
        (
            jax.ShapeDtypeStruct((block, width), BF16),
            jax.ShapeDtypeStruct((chips, width, block), BF16),
            jax.ShapeDtypeStruct((chips, width // chips, block), BF16),
        ),
        [VMEM] * 4,
        flops=2 * block * width * width,
        moved=5 << 20,
    )(parts, facts, w_self, cot)
    grads, dims_all = lax.optimization_barrier((by_chip(spread), dims_all))

    own, sib = call(
        backward_kernel,
        (jax.ShapeDtypeStruct((n_fact, 528, 128), F32), jax.ShapeDtypeStruct((n_fact, 528, 128), BF16)),
        [SMEM] * 3 + [VMEM] * 4,
        [pltpu.VMEM((2 * n_fact + 1, width, block), F32), pltpu.VMEM((width // chips, width), F32)],
        flops=2 * slots * block * block * width,
        moved=9 << 20,
    )(place, lists, counts, grads, facts_t, tiles, tiles_sib)
    slices = by_fact((own + swap(sib).astype(F32)).astype(BF16))

    tab, gsum, self_piece = call(
        slice_kernel,
        (
            jax.ShapeDtypeStruct((768, 128), BF16),
            jax.ShapeDtypeStruct((n_fact, 64, 128), BF16),
            jax.ShapeDtypeStruct((8, 128), F32),
        ),
        [SMEM] * 2 + [VMEM] * 2,
        [pltpu.VMEM((3, 64, width), F32)],
        flops=2 * n_fact * 64 * 128 * width,
        moved=3 << 20,
    )(place, block_table, slices, dims_all)
    tab = lax.all_to_all(tab.reshape(n_dim, 24, 128), "dim", 0, 0, tiled=True)
    packed = call(
        pack_kernel, jax.ShapeDtypeStruct((n_fact, 96, 128), BF16), [VMEM] * 3, moved=1 << 19
    )(tab, gsum, self_piece)
    packed = by_fact(packed)
    pieces_own = by_chip(jnp.broadcast_to(packed[None, :, 64:, :], (chips, n_fact, 32, 128)))
    pieces_sib = swap(pieces_own)

    grad_dims, grad_self, grad_tab = call(
        final_kernel,
        (
            jax.ShapeDtypeStruct((rows, width), F32),
            jax.ShapeDtypeStruct((width, width), F32),
            jax.ShapeDtypeStruct((3, width, width), F32),
        ),
        [SMEM] * 2 + [VMEM] * 4,
        moved=8 << 20,
    )(place, block_table, pieces_own, pieces_sib, packed, w_tables)
    return (fact_out, grad_dims, grad_self, grad_tab)


def solution(mesh):
    split = P(("fact", "dim"), None)
    return jax.shard_map(
        body,
        mesh=mesh,
        in_specs=(split, split, P(("fact", "dim"), None, None), split, P(("fact", "dim")), P(), P(), P(), split),
        out_specs=(split, split, P(), P()),
        check_vma=False,
    )
```

time: 263 us -> 239 us (0.909)
  waiting for transfers between devices: 99.6 us -> 44.2 us
  blocking collectives: 83 us -> 116 us
  starting transfers between devices: 26.4 us -> 37.2 us
  Pallas kernels: 22 us -> 12.9 us
  other arithmetic: 1.92 us -> 5.02 us
  local copies, waits for them, and re-layouts: 9.54 us -> 6.81 us
    all_to_all x1 -> x2, blocking collectives: 18.9 us -> 54.4 us  [by_chip(): return lax.all_to_all(x, 'dim', 0, 0, tiled=True, axis_index_groups=same)]
    all_to_all x2 -> x1, waiting for transfers between devices: 29.7 us -> 0.01 us  [by_chip(): return lax.all_to_all(x, 'dim', 0, 0, tiled=True, axis_index_groups=same)]
    all_to_all x1 -> x0, waiting for transfers between devices: 28.1 us -> none  [by_fact(): return lax.all_to_all(x, 'fact', 0, 0, tiled=True)]
    ppermute x5 -> x13, starting transfers between devices: 5.77 us -> 21.7 us  [swap(): return lax.ppermute(x, 'dim', pair)]
    ppermute x0 -> x8, starting transfers between devices: none -> 11.7 us  [shift(): lax.ppermute(x, 'fact', [(i, (i + by) % n_fact) for i in range(n_fact)])]
    all_to_all x1 -> x0, starting transfers between devices: 9.01 us -> none  [by_fact(): return lax.all_to_all(x, 'fact', 0, 0, tiled=True)]
    all_to_all x2 -> x1, starting transfers between devices: 11.5 us -> 3.72 us  [by_chip(): return lax.all_to_all(x, 'dim', 0, 0, tiled=True, axis_index_groups=same)]
    all_to_all x2, blocking collectives: 51.7 us -> 46 us  [by_fact(): return lax.all_to_all(x, 'fact', 0, 0, tiled=True)]
  transfers between devices with their start and end apart: 9 -> 23, of which waited for: 6 -> 7; matrix products, arithmetic and copies ran while one was open for 1% -> 2% of each run, Pallas kernels for 0% -> 0%
where the time goes in v2:
time: 239 us; the launch traced here: 237 us
  blocking collectives  116 us (49%)
  waiting for transfers between devices  44.2 us (18%)
  starting transfers between devices  37.2 us (16%)
  between operations  14.9 us (6%)
  Pallas kernels  12.9 us (5%)
  local copies, waits for them, and re-layouts  6.81 us (3%)
  other arithmetic  5.02 us (2%)
    all_to_all x2, blocking collectives, by_chip(): return lax.all_to_all(x, 'dim', 0, 0, tiled=True, axis_index_groups=same)  54.4 us
    all_to_all x2, blocking collectives, by_fact(): return lax.all_to_all(x, 'fact', 0, 0, tiled=True)  46 us
    all_gather x1, waiting for transfers between devices, body(): dims_all = lax.all_gather(late_dims, 'fact', axis=0)  35.2 us
    ppermute x13, starting transfers between devices, swap(): return lax.ppermute(x, 'dim', pair)  21.7 us
    all_to_all x1, blocking collectives, body(): tab = lax.all_to_all(tab.reshape(n_dim, 24, 128), 'dim', 0, 0, tiled=True)  16.1 us
    ppermute x8, starting transfers between devices, shift(): lax.ppermute(x, 'fact', [(i, (i + by) % n_fact) for i in range(n_fact)])  11.7 us
    unnamed x26, local copies, waits for them, and re-layouts  5.58 us
    ppermute x13, waiting for transfers between devices, swap(): return lax.ppermute(x, 'dim', pair)  5.47 us
  transfers between devices with their start and end apart: 23, of which 7 were waited for; matrix products, arithmetic and copies ran while one was open for 2% of the time, Pallas kernels for 0%

profile of v2, /device:TPU:1, one launch (start us, length us, event | category | flops | bytes accessed | tf_op | source)
XLA Modules:
  0.0 237.5 jit_solution(15614569425871243934)
XLA Ops:
  7.3 1.4 copy-done
  8.7 0.9 copy-done.9
  9.6 0.7 copy-done.11
  10.2 0.8 shard_map.120.refs_0_
  11.0 3.3 %collective-permute-start.9 = (bf16[128,512]{1,0:T(8,128)(2,1)S(1)}, bf16[128,512]{1,0:T(8,128)(2,1)S(1)}, u32[]{:S(2)}, u32[]{:S(2)}) collective-permute-start(bf16[128,512]{1,0:T(8,128)(2,1)S(1)} %shard_map.120.refs_0_), channel_id=1, source_target_pairs={{0,1},{1,0},{2,3},{3,2},{4,5},{5,4},{6,7},{7,6},{8,9},{9,8},{10,11... | collective-permute-start | bytes 393224 | tf_op jit(solution)/shard_map/ppermute | solution.py:214
  14.4 3.9 %collective-permute-start.2 = (bf16[128,512]{1,0:T(8,128)(2,1)S(1)}, bf16[128,512]{1,0:T(8,128)(2,1)S(1)}, u32[]{:S(2)}, u32[]{:S(2)}) collective-permute-start(bf16[128,512]{1,0:T(8,128)(2,1)S(1)} %shard_map.120.refs_0_), channel_id=1, source_target_pairs={{0,224},{32,0},{64,32},{96,64},{128,96},{160,128},{192,160},{224,1... | collective-permute-start | bytes 393224 | tf_op jit(solution)/shard_map/ppermute | solution.py:217
  18.9 1.4 convert_reduce_fusion.1
  20.3 0.4 collective-permute-start
  20.6 0.2 collective-permute-start.18
  20.8 0.8 and_bitcast_fusion
  21.6 0.1 select_reduce_fusion.3
  21.7 1.0 copy.14
  22.8 2.9 %collective-permute-start.4 = (bf16[128,512]{1,0:T(8,128)(2,1)S(1)}, bf16[128,512]{1,0:T(8,128)(2,1)S(1)}, u32[]{:S(2)}, u32[]{:S(2)}) collective-permute-start(bf16[128,512]{1,0:T(8,128)(2,1)S(1)} %collective-permute-done.2.refs_2_), channel_id=1, source_target_pairs={{0,224},{32,0},{64,32},{96,64},{128,96},{160,128},{192,160},{224,1... | collective-permute-start | bytes 393224 | tf_op jit(solution)/shard_map/ppermute | solution.py:217
  25.7 0.6 convert_reduce_fusion
  26.4 1.7 collective-permute-done.4.refs_4_
  28.1 3.4 %collective-permute-start.6 = (bf16[128,512]{1,0:T(8,128)(2,1)S(1)}, bf16[128,512]{1,0:T(8,128)(2,1)S(1)}, u32[]{:S(2)}, u32[]{:S(2)}) collective-permute-start(bf16[128,512]{1,0:T(8,128)(2,1)S(1)} %collective-permute-done.4.refs_4_), channel_id=1, source_target_pairs={{0,224},{32,0},{64,32},{96,64},{128,96},{160,128},{192,160},{224,1... | collective-permute-start | bytes 393224 | tf_op jit(solution)/shard_map/ppermute | solution.py:217
  31.7 1.7 collective-permute-start.11
  33.5 2.1 collective-permute-start.13
  35.6 0.9 collective-permute-done.5.refs_5_
  36.5 2.8 %collective-permute-start.12 = (bf16[128,512]{1,0:T(8,128)(2,1)S(1)}, bf16[128,512]{1,0:T(8,128)(2,1)S(1)}, u32[]{:S(2)}, u32[]{:S(2)}) collective-permute-start(bf16[128,512]{1,0:T(8,128)(2,1)S(1)} %collective-permute-done.3.refs_3_), channel_id=1, source_target_pairs={{0,1},{1,0},{2,3},{3,2},{4,5},{5,4},{6,7},{7,6},{8,9},{9,8},{10,11... | collective-permute-start | bytes 393224 | tf_op jit(solution)/shard_map/ppermute | solution.py:214
  39.4 1.4 collective-permute-start.7
  40.9 0.6 collective-permute-start.15
  41.5 1.4 pad_add_fusion.2.counts
  42.9 0.2 collective-permute-done.8.refs_8_
  43.1 0.8 collective-permute-start.17
  43.9 1.5 collective-permute-start.16
  45.5 0.8 collective-permute-done.16.refs_16_
  46.3 3.0 %shard_map.121 = bf16[16,544,128]{2,1,0:T(8,128)(2,1)S(1)} custom-call(s32[4]{0:T(128)S(1)} %pad_add_fusion.place, s32[64]{0:T(128)S(1)} %pad_add_fusion.1.lists, s32[2]{0:T(128)S(1)} %pad_add_fusion.2.counts, bf16[128,512]{1,0:T(8,128)(2,1)S(1)} %shard_map.120.refs_0_, bf16[128,512]{1,0:T(8,128)(2,1)S(1)} %collective-permute-done.1.refs_1_, ...), custom_call_target="tpu_custom_call" | custom-call | flops 536870912 | bytes 8388608 | tf_op jit(solution)/shard_map/pallas_call | solution.py:244
  49.4 35.4 %all_to_all.30.parts = bf16[16,544,128]{2,1,0:T(8,128)(2,1)S(1)} all-to-all(bf16[16,544,128]{2,1,0:T(8,128)(2,1)S(1)} %shard_map.121), channel_id=1, replica_groups={{0,2,4,6,8,10,12,14,16,18,20,22,24,26,28,30},{1,3,5,7,9,11,13,15,17,19,..., dimensions={0} | all-to-all | bytes 4456448 | tf_op jit(solution)/shard_map/all_to_all | solution.py:220
  84.8 1.2 shard_map.122
  85.9 1.3 copy-done.5
  87.3 3.7 %all-to-all-start.1 = ((bf16[16,512,128]{2,1,0:T(8,128)(2,1)}), bf16[16,512,128]{2,1,0:T(8,128)(2,1)S(1)}, u32[]{:S(2)}, u32[]{:S(2)}) async-start(bf16[16,512,128]{2,1,0:T(8,128)(2,1)} %copy-done.5), calls=%async_computation.1 | async-start | bytes 4194304 | tf_op jit(solution)/shard_map/all_to_all | solution.py:220
  91.0 0.7 all-gather.3.cloned.1.call-update
  91.7 35.2 %all-gather.3.cloned.1.call-done = bf16[1024,512]{1,0:T(8,128)(2,1)} async-done(((bf16[128,512]{1,0:T(8,128)(2,1)}), bf16[1024,512]{1,0:T(8,128)(2,1)}) %all-gather.3.cloned.1.call-update) | async-done | bytes 1048592 | tf_op jit(solution)/shard_map/all_gather | solution.py:253
  127.0 1.2 copy-done.4
  128.2 3.7 %shard_map.123 = (f32[8,528,128]{2,1,0:T(8,128)S(1)}, bf16[8,528,128]{2,1,0:T(8,128)(2,1)S(1)}) custom-call(s32[4]{0:T(128)S(1)} %pad_add_fusion.place, s32[64]{0:T(128)S(1)} %pad_add_fusion.1.lists, s32[2]{0:T(128)S(1)} %pad_add_fusion.2.counts, bf16[16,512,128]{2,1,0:T(8,128)(2,1)S(1)} %all-to-all-done.1.grads, ...), custom_call_target="tpu_custom_call" | custom-call | flops 536870912 | bytes 9437184 | tf_op jit(solution)/shard_map/pallas_call | solution.py:269
  131.9 6.3 %collective-permute-start.19 = (bf16[8,528,128]{2,1,0:T(8,128)(2,1)S(1)}, bf16[8,528,128]{2,1,0:T(8,128)(2,1)S(1)}, u32[]{:S(2)}, u32[]{:S(2)}) collective-permute-start(bf16[8,528,128]{2,1,0:T(8,128)(2,1)S(1)} %get-tuple-element.26), channel_id=1, source_target_pairs={{0,1},{1,0},{2,3},{3,2},{4,5},{5,4},{6,7},{7,6},{8,9},{9,8},{10,11... | collective-permute-start | bytes 3244040 | tf_op jit(solution)/shard_map/ppermute | solution.py:214
  138.1 2.3 collective-permute-done.19
  140.5 0.3 add_convert_fusion
  140.7 32.5 %all_to_all.31.parts = bf16[8,528,128]{2,1,0:T(8,128)(2,1)S(1)} all-to-all(bf16[8,528,128]{2,1,0:T(8,128)(2,1)S(1)} %add_convert_fusion), channel_id=1, replica_groups=mesh['fact'=8,'dim'=32] {'fact'}, dimensions={0} | all-to-all | bytes 2162688 | tf_op jit(solution)/shard_map/all_to_all | solution.py:223
  173.3 0.9 shard_map.124
  174.2 16.1 %all_to_all.32.parts = bf16[32,24,128]{2,1,0:T(8,128)(2,1)S(1)} all-to-all(bf16[32,24,128]{2,1,0:T(8,128)(2,1)S(1)} %bitcast.43), channel_id=1, replica_groups=mesh['fact'=8,'dim'=32] {'dim'}, dimensions={0} | all-to-all | bytes 393216 | tf_op jit(solution)/shard_map/all_to_all | solution.py:291
  190.3 13.5 %all_to_all.33.packed = bf16[8,96,128]{2,1,0:T(8,128)(2,1)S(1)} all-to-all(bf16[8,96,128]{2,1,0:T(8,128)(2,1)S(1)} %shard_map.125), channel_id=1, replica_groups=mesh['fact'=8,'dim'=32] {'fact'}, dimensions={0} | all-to-all | bytes 393216 | tf_op jit(solution)/shard_map/all_to_all | solution.py:223
  203.8 0.2 broadcast_in_dim.55
  204.0 18.9 %all_to_all.34.own = bf16[16,8,32,128]{3,2,1,0:T(8,128)(2,1)S(1)} all-to-all(bf16[16,8,32,128]{3,2,1,0:T(8,128)(2,1)S(1)} %broadcast_in_dim.55), channel_id=1, replica_groups={{0,2,4,6,8,10,12,14,16,18,20,22,24,26,28,30},{1,3,5,7,9,11,13,15,17,19,..., dimensions={0} | all-to-all | bytes 2097152 | tf_op jit(solution)/shard_map/all_to_all | solution.py:220
  222.9 2.0 collective-permute-start.20
  224.9 2.3 collective-permute-done.20.sib
  227.2 3.4 %shard_map.126 = (f32[128,512]{1,0:T(8,128)}, f32[512,512]{1,0:T(8,128)}, f32[3,512,512]{2,1,0:T(8,128)}) custom-call(s32[4]{0:T(128)S(1)} %pad_add_fusion.place, s32[256]{0:T(256)S(1)} %copy-done.12, bf16[16,8,32,128]{3,2,1,0:T(8,128)(2,1)S(1)} %all_to_all.34.own, bf16[16,8,32,128]{3,2,1,0:T(8,128)(2,1)S(1)} %collective-permute-done.20.sib, ...), custom_call_target="tpu_custom_call" | custom-call | bytes 8388608 | tf_op jit(solution)/shard_map/pallas_call | solution.py:299
  (55 shorter events, 1.0 us)
Async XLA Ops:
  7.2 1.4 copy-start
  8.7 0.9 copy-start.9
  9.6 0.7 copy-start.11
  10.2 36.1 %copy-start.2 = (bf16[32,128,128]{2,1,0:T(8,128)(2,1)S(1)}, bf16[32,128,128]{2,1,0:T(8,128)(2,1)}, u32[]{:S(2)}) copy-start(bf16[32,128,128]{2,1,0:T(8,128)(2,1)} %tiles_own.1) | copy-start | bytes 3145732
  11.0 22.4 %collective-permute-start.9 = (bf16[128,512]{1,0:T(8,128)(2,1)S(1)}, bf16[128,512]{1,0:T(8,128)(2,1)S(1)}, u32[]{:S(2)}, u32[]{:S(2)}) collective-permute-start(bf16[128,512]{1,0:T(8,128)(2,1)S(1)} %shard_map.120.refs_0_), channel_id=1, source_target_pairs={{0,1},{1,0},{2,3},{3,2},{4,5},{5,4},{6,7},{7,6},{8,9},{9,8},{10,11... | collective-permute-start | bytes 393224 | tf_op jit(solution)/shard_map/ppermute | solution.py:214
  14.4 8.5 %collective-permute-start.2 = (bf16[128,512]{1,0:T(8,128)(2,1)S(1)}, bf16[128,512]{1,0:T(8,128)(2,1)S(1)}, u32[]{:S(2)}, u32[]{:S(2)}) collective-permute-start(bf16[128,512]{1,0:T(8,128)(2,1)S(1)} %shard_map.120.refs_0_), channel_id=1, source_target_pairs={{0,224},{32,0},{64,32},{96,64},{128,96},{160,128},{192,160},{224,1... | collective-permute-start | bytes 393224 | tf_op jit(solution)/shard_map/ppermute | solution.py:217
  18.2 7.5 %collective-permute-start.1 = (bf16[128,512]{1,0:T(8,128)(2,1)S(1)}, bf16[128,512]{1,0:T(8,128)(2,1)S(1)}, u32[]{:S(2)}, u32[]{:S(2)}) collective-permute-start(bf16[128,512]{1,0:T(8,128)(2,1)S(1)} %shard_map.120.refs_0_), channel_id=1, source_target_pairs={{0,32},{32,64},{64,96},{96,128},{128,160},{160,192},{192,224},{224... | collective-permute-start | bytes 393224 | tf_op jit(solution)/shard_map/ppermute | solution.py:217
  20.3 5.4 %collective-permute-start = (s32[32]{0:T(128)S(1)}, s32[32]{0:T(128)S(1)}, u32[]{:S(2)}, u32[]{:S(2)}) collective-permute-start(s32[32]{0:T(128)S(1)} %get-tuple-element.36), channel_id=1, source_target_pairs={{0,1},{1,0},{2,3},{3,2},{4,5},{5,4},{6,7},{7,6},{8,9},{9,8},{10,11... | collective-permute-start | bytes 392 | tf_op jit(solution)/shard_map/ppermute | solution.py:214
  20.6 25.7 %collective-permute-start.18 = (bf16[32,128,128]{2,1,0:T(8,128)(2,1)}, bf16[32,128,128]{2,1,0:T(8,128)(2,1)S(1)}, u32[]{:S(2)}, u32[]{:S(2)}) collective-permute-start(bf16[32,128,128]{2,1,0:T(8,128)(2,1)} %tiles_own.1), channel_id=1, source_target_pairs={{0,1},{1,0},{2,3},{3,2},{4,5},{5,4},{6,7},{7,6},{8,9},{9,8},{10,11... | collective-permute-start | bytes 3145736 | tf_op jit(solution)/shard_map/ppermute | solution.py:214
  22.8 5.2 %collective-permute-start.4 = (bf16[128,512]{1,0:T(8,128)(2,1)S(1)}, bf16[128,512]{1,0:T(8,128)(2,1)S(1)}, u32[]{:S(2)}, u32[]{:S(2)}) collective-permute-start(bf16[128,512]{1,0:T(8,128)(2,1)S(1)} %collective-permute-done.2.refs_2_), channel_id=1, source_target_pairs={{0,224},{32,0},{64,32},{96,64},{128,96},{160,128},{192,160},{224,1... | collective-permute-start | bytes 393224 | tf_op jit(solution)/shard_map/ppermute | solution.py:217
  25.7 5.8 %collective-permute-start.3 = (bf16[128,512]{1,0:T(8,128)(2,1)S(1)}, bf16[128,512]{1,0:T(8,128)(2,1)S(1)}, u32[]{:S(2)}, u32[]{:S(2)}) collective-permute-start(bf16[128,512]{1,0:T(8,128)(2,1)S(1)} %collective-permute-done.1.refs_1_), channel_id=1, source_target_pairs={{0,32},{32,64},{64,96},{96,128},{128,160},{160,192},{192,224},{224... | collective-permute-start | bytes 393224 | tf_op jit(solution)/shard_map/ppermute | solution.py:217
  28.1 5.5 %collective-permute-start.6 = (bf16[128,512]{1,0:T(8,128)(2,1)S(1)}, bf16[128,512]{1,0:T(8,128)(2,1)S(1)}, u32[]{:S(2)}, u32[]{:S(2)}) collective-permute-start(bf16[128,512]{1,0:T(8,128)(2,1)S(1)} %collective-permute-done.4.refs_4_), channel_id=1, source_target_pairs={{0,224},{32,0},{64,32},{96,64},{128,96},{160,128},{192,160},{224,1... | collective-permute-start | bytes 393224 | tf_op jit(solution)/shard_map/ppermute | solution.py:217
  31.5 5.0 %collective-permute-start.5 = (bf16[128,512]{1,0:T(8,128)(2,1)S(1)}, bf16[128,512]{1,0:T(8,128)(2,1)S(1)}, u32[]{:S(2)}, u32[]{:S(2)}) collective-permute-start(bf16[128,512]{1,0:T(8,128)(2,1)S(1)} %collective-permute-done.3.refs_3_), channel_id=1, source_target_pairs={{0,32},{32,64},{64,96},{96,128},{128,160},{160,192},{192,224},{224... | collective-permute-start | bytes 393224 | tf_op jit(solution)/shard_map/ppermute | solution.py:217
  31.7 7.6 %collective-permute-start.11 = (bf16[128,512]{1,0:T(8,128)(2,1)S(1)}, bf16[128,512]{1,0:T(8,128)(2,1)S(1)}, u32[]{:S(2)}, u32[]{:S(2)}) collective-permute-start(bf16[128,512]{1,0:T(8,128)(2,1)S(1)} %collective-permute-done.2.refs_2_), channel_id=1, source_target_pairs={{0,1},{1,0},{2,3},{3,2},{4,5},{5,4},{6,7},{7,6},{8,9},{9,8},{10,11... | collective-permute-start | bytes 393224 | tf_op jit(solution)/shard_map/ppermute | solution.py:214
  33.4 6.0 %collective-permute-start.10 = (bf16[128,512]{1,0:T(8,128)(2,1)S(1)}, bf16[128,512]{1,0:T(8,128)(2,1)S(1)}, u32[]{:S(2)}, u32[]{:S(2)}) collective-permute-start(bf16[128,512]{1,0:T(8,128)(2,1)S(1)} %collective-permute-done.1.refs_1_), channel_id=1, source_target_pairs={{0,1},{1,0},{2,3},{3,2},{4,5},{5,4},{6,7},{7,6},{8,9},{9,8},{10,11... | collective-permute-start | bytes 393224 | tf_op jit(solution)/shard_map/ppermute | solution.py:214
  33.5 7.3 %collective-permute-start.13 = (bf16[128,512]{1,0:T(8,128)(2,1)S(1)}, bf16[128,512]{1,0:T(8,128)(2,1)S(1)}, u32[]{:S(2)}, u32[]{:S(2)}) collective-permute-start(bf16[128,512]{1,0:T(8,128)(2,1)S(1)} %collective-permute-done.4.refs_4_), channel_id=1, source_target_pairs={{0,1},{1,0},{2,3},{3,2},{4,5},{5,4},{6,7},{7,6},{8,9},{9,8},{10,11... | collective-permute-start | bytes 393224 | tf_op jit(solution)/shard_map/ppermute | solution.py:214
  36.5 4.9 %collective-permute-start.12 = (bf16[128,512]{1,0:T(8,128)(2,1)S(1)}, bf16[128,512]{1,0:T(8,128)(2,1)S(1)}, u32[]{:S(2)}, u32[]{:S(2)}) collective-permute-start(bf16[128,512]{1,0:T(8,128)(2,1)S(1)} %collective-permute-done.3.refs_3_), channel_id=1, source_target_pairs={{0,1},{1,0},{2,3},{3,2},{4,5},{5,4},{6,7},{7,6},{8,9},{9,8},{10,11... | collective-permute-start | bytes 393224 | tf_op jit(solution)/shard_map/ppermute | solution.py:214
  39.3 3.8 %collective-permute-start.8 = (bf16[64,512]{1,0:T(8,128)(2,1)S(1)}, bf16[64,512]{1,0:T(8,128)(2,1)S(1)}, u32[]{:S(2)}, u32[]{:S(2)}) collective-permute-start(bf16[64,512]{1,0:T(8,128)(2,1)S(1)} %slice.21), channel_id=1, source_target_pairs={{0,224},{32,0},{64,32},{96,64},{128,96},{160,128},{192,160},{224,1... | collective-permute-start | bytes 196616 | tf_op jit(solution)/shard_map/ppermute | solution.py:217
  39.4 4.5 %collective-permute-start.7 = (bf16[64,512]{1,0:T(8,128)(2,1)S(1)}, bf16[64,512]{1,0:T(8,128)(2,1)S(1)}, u32[]{:S(2)}, u32[]{:S(2)}) collective-permute-start(bf16[64,512]{1,0:T(8,128)(2,1)S(1)} %slice.20), channel_id=1, source_target_pairs={{0,32},{32,64},{64,96},{96,128},{128,160},{160,192},{192,224},{224... | collective-permute-start | bytes 196616 | tf_op jit(solution)/shard_map/ppermute | solution.py:217
  40.9 5.4 %collective-permute-start.15 = (bf16[128,512]{1,0:T(8,128)(2,1)S(1)}, bf16[128,512]{1,0:T(8,128)(2,1)S(1)}, u32[]{:S(2)}, u32[]{:S(2)}) collective-permute-start(bf16[128,512]{1,0:T(8,128)(2,1)S(1)} %collective-permute-done.6.refs_6_), channel_id=1, source_target_pairs={{0,1},{1,0},{2,3},{3,2},{4,5},{5,4},{6,7},{7,6},{8,9},{9,8},{10,11... | collective-permute-start | bytes 393224 | tf_op jit(solution)/shard_map/ppermute | solution.py:214
  41.5 4.9 %collective-permute-start.14 = (bf16[128,512]{1,0:T(8,128)(2,1)S(1)}, bf16[128,512]{1,0:T(8,128)(2,1)S(1)}, u32[]{:S(2)}, u32[]{:S(2)}) collective-permute-start(bf16[128,512]{1,0:T(8,128)(2,1)S(1)} %collective-permute-done.5.refs_5_), channel_id=1, source_target_pairs={{0,1},{1,0},{2,3},{3,2},{4,5},{5,4},{6,7},{7,6},{8,9},{9,8},{10,11... | collective-permute-start | bytes 393224 | tf_op jit(solution)/shard_map/ppermute | solution.py:214
  43.1 2.3 collective-permute-start.17
  43.9 2.4 %collective-permute-start.16 = (bf16[64,512]{1,0:T(8,128)(2,1)S(1)}, bf16[64,512]{1,0:T(8,128)(2,1)S(1)}, u32[]{:S(2)}, u32[]{:S(2)}) collective-permute-start(bf16[64,512]{1,0:T(8,128)(2,1)S(1)} %collective-permute-done.7.refs_7_), channel_id=1, source_target_pairs={{0,1},{1,0},{2,3},{3,2},{4,5},{5,4},{6,7},{7,6},{8,9},{9,8},{10,11... | collective-permute-start | bytes 196616 | tf_op jit(solution)/shard_map/ppermute | solution.py:214
  46.3 3.0 %copy-start.3 = (bf16[32,128,128]{2,1,0:T(8,128)(2,1)}, bf16[32,128,128]{2,1,0:T(8,128)(2,1)S(1)}, u32[]{:S(2)}) copy-start(bf16[32,128,128]{2,1,0:T(8,128)(2,1)S(1)} %collective-permute-done.18.refs_20_.tiles_sib) | copy-start | bytes 3145732
  49.3 35.5 %copy-start.7 = (bf16[128,512]{1,0:T(8,128)(2,1)S(1)}, bf16[128,512]{1,0:T(8,128)(2,1)}, u32[]{:S(2)}) copy-start(bf16[128,512]{1,0:T(8,128)(2,1)} %facts.1) | copy-start | bytes 393220
  49.3 35.5 %copy-start.8 = (bf16[512,512]{1,0:T(8,128)(2,1)S(1)}, bf16[512,512]{1,0:T(8,128)(2,1)}, u32[]{:S(2)}) copy-start(bf16[512,512]{1,0:T(8,128)(2,1)} %w.4) | copy-start | bytes 1572868
  49.3 35.4 %copy-start.10 = (bf16[128,512]{1,0:T(8,128)(2,1)S(1)}, bf16[128,512]{1,0:T(8,128)(2,1)}, u32[]{:S(2)}) copy-start(bf16[128,512]{1,0:T(8,128)(2,1)} %cot.1) | copy-start | bytes 393220
  85.9 1.3 copy-start.5
  87.3 39.7 %all-to-all-start.1 = ((bf16[16,512,128]{2,1,0:T(8,128)(2,1)}), bf16[16,512,128]{2,1,0:T(8,128)(2,1)S(1)}, u32[]{:S(2)}, u32[]{:S(2)}) async-start(bf16[16,512,128]{2,1,0:T(8,128)(2,1)} %copy-done.5), calls=%async_computation.1 | async-start | bytes 4194304 | tf_op jit(solution)/shard_map/all_to_all | solution.py:220
  91.0 36.0 %all-gather.3.cloned.1.call-start = ((), (), s32[]{:S(2)}) async-start(), calls=%async_computation.6 | async-start | bytes 1179648 | tf_op jit(solution)/shard_map/all_gather | solution.py:253
  127.0 1.2 copy-start.4
  131.9 8.6 %collective-permute-start.19 = (bf16[8,528,128]{2,1,0:T(8,128)(2,1)S(1)}, bf16[8,528,128]{2,1,0:T(8,128)(2,1)S(1)}, u32[]{:S(2)}, u32[]{:S(2)}) collective-permute-start(bf16[8,528,128]{2,1,0:T(8,128)(2,1)S(1)} %get-tuple-element.26), channel_id=1, source_target_pairs={{0,1},{1,0},{2,3},{3,2},{4,5},{5,4},{6,7},{7,6},{8,9},{9,8},{10,11... | collective-permute-start | bytes 3244040 | tf_op jit(solution)/shard_map/ppermute | solution.py:214
  140.7 32.5 %copy-start.6 = (bf16[1024,512]{1,0:T(8,128)(2,1)S(1)}, bf16[1024,512]{1,0:T(8,128)(2,1)}, u32[]{:S(2)}) copy-start(bf16[1024,512]{1,0:T(8,128)(2,1)} %all-gather.3.cloned.1.call-done) | copy-start | bytes 3145732
  140.7 32.5 %copy-start.12 = (s32[256]{0:T(256)S(1)}, s32[256]{0:T(256)}, u32[]{:S(2)}) copy-start(s32[256]{0:T(256)} %table.5) | copy-start | bytes 3076
  190.3 36.9 %copy-start.1 = (bf16[3,512,512]{2,1,0:T(8,128)(2,1)S(1)}, bf16[3,512,512]{2,1,0:T(8,128)(2,1)}, u32[]{:S(2)}) copy-start(bf16[3,512,512]{2,1,0:T(8,128)(2,1)} %w.5) | copy-start | bytes 4718596
  222.9 4.3 %collective-permute-start.20 = (bf16[16,8,32,128]{3,2,1,0:T(8,128)(2,1)S(1)}, bf16[16,8,32,128]{3,2,1,0:T(8,128)(2,1)S(1)}, u32[]{:S(2)}, u32[]{:S(2)}) collective-permute-start(bf16[16,8,32,128]{3,2,1,0:T(8,128)(2,1)S(1)} %all_to_all.34.own), channel_id=1, source_target_pairs={{0,1},{1,0},{2,3},{3,2},{4,5},{5,4},{6,7},{7,6},{8,9},{9,8},{10,11... | collective-permute-start | bytes 3145736 | tf_op jit(solution)/shard_map/ppermute | solution.py:214
Sparse Core Ops, SparseCore 0:
  93.6 33.2 all-gather.2

commit v3 on v2

v3 whole, which is shorter than its diff:
```python
import jax
import jax.numpy as jnp
from jax import lax
from jax.experimental import pallas as pl
from jax.experimental.pallas import tpu as pltpu
from jax.sharding import PartitionSpec as P

F32 = jnp.float32
BF16 = jnp.bfloat16
VMEM = pl.BlockSpec(memory_space=pltpu.VMEM)
SMEM = pl.BlockSpec(memory_space=pltpu.SMEM)
PARAMS = pltpu.CompilerParams(vmem_limit_bytes=24 * 1024 * 1024)
UNROLL = 2


ORDER = (0, -1, 1, -2, 2, -3, 3)
EARLY = 5
LIST = 40


def call(kernel, out_shape, in_specs, scratch=(), flops=0, moved=0, out_specs=None):
    return pl.pallas_call(
        kernel,
        out_shape=out_shape,
        in_specs=in_specs,
        out_specs=jax.tree.map(lambda _: VMEM, out_shape) if out_specs is None else out_specs,
        scratch_shapes=list(scratch),
        compiler_params=PARAMS,
        cost_estimate=pl.CostEstimate(flops=flops, bytes_accessed=moved, transcendentals=0),
    )


def decode(code):
    return code & 31, (code >> 5) & 7, code >> 8


def column_kind(place, table, side, h):
    dim_pos = place[1]
    return table[h * 32 + (dim_pos if side == 0 else dim_pos + 1 - 2 * place[2])]


def prepare_kernel(place, table, links_own, links_sib, count_own, count_sib, facts, w, *refs):
    early, (lists, counts, proj, facts_t) = refs[: 2 * EARLY], refs[2 * EARLY :]
    fact_pos, core = place[0], place[2]
    for side, (links, count) in enumerate(((links_own, count_own), (links_sib, count_sib))):
        n = jnp.int32(0)
        for slot in range(32):
            target = links[slot, 0] - fact_pos * 32
            lists[side * LIST + n] = slot + ((links[slot, 1] >> 5) << 5) + ((target >> 1) << 8)
            n = n + jnp.where((slot < count[0]) & ((target & 1) == core), 1, 0)
        lists[side * LIST + n] = 16 << 8
        counts[side] = n
    for side in range(2):
        for at, shift in enumerate(ORDER[:EARLY]):
            kind = column_kind(place, table, side, (fact_pos + shift) & 7)
            value = jnp.dot(early[side * EARLY + at][...], w[kind], preferred_element_type=F32)
            proj[side * EARLY + at] = value.astype(BF16)
    facts_t[...] = facts[...].astype(F32).T.astype(BF16)


def forward_kernel(place, table, lists, counts, proj, *refs):
    late = 9 - EARLY
    sides, (w, facts_t, tiles_own, tiles_sib, out, panel, acc) = (refs[:late], refs[late : 2 * late]), refs[2 * late :]
    fact_pos = place[0]
    for side, pieces in enumerate(sides):
        for at, shift in enumerate(ORDER[:EARLY]):
            panel[side * 8 + ((fact_pos + shift) & 7)] = proj[side * EARLY + at]
        blocks = [x[...] for x in pieces[:-2]] + [jnp.concatenate([pieces[-2][...], pieces[-1][...]], axis=0)]
        for shift, rows in zip(ORDER[EARLY:] + (4,), blocks):
            h = (fact_pos + shift) & 7
            value = jnp.dot(rows, w[column_kind(place, table, side, h)], preferred_element_type=F32)
            panel[side * 8 + h] = value.astype(BF16)
    acc[...] = jnp.zeros_like(acc)
    for side, tiles in enumerate((tiles_own, tiles_sib)):

        def step(i, carry, side=side, tiles=tiles):
            found = []
            for u in range(UNROLL):
                slot, holder, chip = decode(lists[side * LIST + i * UNROLL + u])
                found.append((chip, jnp.dot(tiles[slot], panel[side * 8 + holder], preferred_element_type=F32)))
            for chip, value in found:
                acc[chip] += value
            return carry

        lax.fori_loop(0, (counts[side] + UNROLL - 1) // UNROLL, step, 0)
    for chip in range(out.shape[0]):
        for q in range(4):
            out[chip, q * 128 : (q + 1) * 128, :] = acc[chip, :, q * 128 : (q + 1) * 128].astype(BF16)
        out[chip, 512:544, :] = facts_t[chip * 32 : (chip + 1) * 32, :]


def middle_kernel(parts, facts, w, cot, fact_out, spread, facts_t):
    pre = jnp.dot(facts[...], w[...], preferred_element_type=F32)
    aggs = []
    for q in range(4):
        agg = parts[0, q * 128 : (q + 1) * 128, :].astype(F32)
        for chip in range(1, parts.shape[0]):
            agg = agg + parts[chip, q * 128 : (q + 1) * 128, :].astype(F32)
        aggs.append(agg)
    pre = pre + jnp.concatenate(aggs, axis=1)
    sig = jax.nn.sigmoid(pre)
    fact_out[...] = (pre * sig).astype(BF16)
    grad = cot[...].astype(F32) * sig * (1.0 + pre * (1.0 - sig))
    turned = grad.T.astype(BF16)
    for chip in range(spread.shape[0]):
        spread[chip] = turned
        facts_t[chip] = parts[chip, 512:544, :]


def backward_kernel(place, lists, counts, grads, facts_t, tiles_own, tiles_sib, keep, give, acc, weight):
    core = place[2]
    acc[...] = jnp.zeros_like(acc)
    for side, tiles in enumerate((tiles_own, tiles_sib)):
        base = 8 * (core if side == 0 else 1 - core)

        def step(i, carry, side=side, tiles=tiles, base=base):
            found = []
            for u in range(UNROLL):
                slot, holder, chip = decode(lists[side * LIST + i * UNROLL + u])
                at = jnp.where(chip == 16, 16, base + holder)
                value = jnp.dot(grads[jnp.minimum(chip, 15)], tiles[slot], preferred_element_type=F32)
                found.append((at, value))
            for at, value in found:
                acc[at] += value
            return carry

        lax.fori_loop(0, (counts[side] + UNROLL - 1) // UNROLL, step, 0)
    half = weight.shape[0] // 2
    total = jnp.zeros(weight.shape, F32)
    for chip in range(grads.shape[0]):
        total = total + lax.dot_general(
            facts_t[chip], grads[chip], (((1,), (1,)), ((), ())), preferred_element_type=F32
        )
    weight[...] = total
    for out, who, kind in ((keep, core, F32), (give, 1 - core, BF16)):
        for z in range(8):
            features = pl.ds(pl.multiple_of(who * 256 + z * 32, 32), 32)
            for at in range(16):
                out[z, at * 32 : (at + 1) * 32, :] = acc[at, features, :].astype(kind)
            rows = pl.ds(pl.multiple_of(who * half + (z % 2) * 8, 8), 8)
            mine = weight[rows, (z // 2) * 128 : (z // 2 + 1) * 128]
            out[z, 512:528, :] = jnp.concatenate([mine, jnp.zeros_like(mine)], axis=0).astype(kind)


def slice_kernel(place, table, parts, *refs):
    pieces, (tab, gsum, self_piece, tacc) = refs[:18], refs[18:]
    fact_pos, core = place[0], place[2]
    total = parts[0].astype(F32)
    for z in range(1, parts.shape[0]):
        total = total + parts[z].astype(F32)
    self_piece[...] = total[512:520]
    for at in range(16):
        gsum[at] = total[at * 32 : (at + 1) * 32].astype(BF16)
    tacc[...] = jnp.zeros_like(tacc)
    for side in range(2):
        column = 8 * (core if side == 0 else 1 - core)
        for at, shift in enumerate(ORDER + (4,)):
            h = (fact_pos + shift) & 7
            kind = column_kind(place, table, side, h)
            grad = gsum[column + h]
            if shift == 4:
                low, high = pieces[side * 9 + 7], pieces[side * 9 + 8]
                rows = jnp.concatenate([low[...], high[...]], axis=0)
            else:
                rows = pieces[side * 9 + at][...]
            tacc[kind] += jnp.dot(grad, rows, preferred_element_type=F32)
    for q in range(4):
        for t in range(3):
            at = q * 96 + t * 32
            tab[at : at + 32, :] = tacc[t, :, q * 128 : (q + 1) * 128].astype(BF16)


def pack_kernel(place, parts, gsum, self_piece, out):
    core = place[2]
    total = jnp.sum(parts[...].astype(F32), axis=0)
    piece = jnp.concatenate([total, self_piece[...]], axis=0).astype(BF16)
    for z in range(out.shape[0]):
        out[z, 0:32, :] = gsum[core * 8 + z]
        out[z, 32:64, :] = gsum[(1 - core) * 8 + z]
        out[z, 64:96, :] = piece


def final_kernel(place, table, own, sib, kept, given, w, grad_dims, grad_self, grad_tab):
    even = place[2] == 0
    scale = F32(32768.0**-0.5)
    kind = table[place[0] * 32 + place[1]]
    mine, other = kept[...].astype(F32).reshape(256, 128), given[...].astype(F32).reshape(256, 128)
    turned = jnp.concatenate([jnp.where(even, mine, other), jnp.where(even, other, mine)], axis=0)
    grad_dims[...] = lax.dot_general(
        turned.T.astype(BF16), w[kind], (((1,), (1,)), ((), ())), preferred_element_type=F32
    )
    for q in range(4):
        for group in range(2):
            tables = [[[], [], []], [[], [], []]]
            for z in range(4 * group, 4 * group + 4):
                for chip in range(16):
                    mine, other = own[chip, z].astype(F32) * scale, sib[chip, z].astype(F32) * scale
                    pair = (jnp.where(even, mine, other), jnp.where(even, other, mine))
                    for core in range(2):
                        if z // 2 == q:
                            row = (2 * chip + core) * 16 + (z % 2) * 8
                            grad_self[row : row + 8, q * 128 : (q + 1) * 128] = pair[core][24:32]
                        if chip // 4 == q:
                            first = (chip % 4) * 24
                            for t in range(3):
                                lo, hi = max(first, t * 32), min(first + 24, t * 32 + 32)
                                if lo < hi:
                                    tables[core][t].append(pair[core][lo - first : hi - first])
            for core in range(2):
                for t in range(3):
                    column = core * 256 + group * 128
                    both = jnp.concatenate(tables[core][t], axis=0)
                    grad_tab[t, q * 128 : (q + 1) * 128, column : column + 128] = both.T


def body(facts, dims, tiles, links, link_count, block_table, w_self, w_tables, cot):
    n_fact = lax.axis_size("fact")
    n_dim = lax.axis_size("dim")
    fact_pos = lax.axis_index("fact")
    dim_pos = lax.axis_index("dim")
    chips = n_dim // 2
    same = [[2 * m + core for m in range(chips)] for core in range(2)]
    pair = [(d, d ^ 1) for d in range(n_dim)]
    rows, width = dims.shape
    slots, block, _ = tiles.shape
    place = jnp.stack([fact_pos, dim_pos, dim_pos & 1, dim_pos >> 1]).astype(jnp.int32)

    def swap(x):
        return lax.ppermute(x, "dim", pair)

    def shift(x, by):
        return lax.ppermute(x, "fact", [(i, (i + by) % n_fact) for i in range(n_fact)])

    def by_chip(x):
        return lax.all_to_all(x, "dim", 0, 0, tiled=True, axis_index_groups=same)

    def by_fact(x):
        return lax.all_to_all(x, "fact", 0, 0, tiled=True)

    pieces, up, down = [dims], dims, dims
    for _ in range(3):
        up, down = shift(up, 1), shift(down, -1)
        pieces += [up, down]
    pieces_sib = [swap(x) for x in pieces]
    far = [shift(up[: rows // 2], 1), shift(down[rows // 2 :], -1)]
    tiles_sib = swap(tiles)

    lists, counts, proj, facts_t = call(
        prepare_kernel,
        (
            jax.ShapeDtypeStruct((2 * LIST,), jnp.int32),
            jax.ShapeDtypeStruct((2,), jnp.int32),
            jax.ShapeDtypeStruct((2 * EARLY, rows, width), BF16),
            jax.ShapeDtypeStruct((width, block), BF16),
        ),
        [SMEM] * 6 + [VMEM] * (2 + 2 * EARLY),
        flops=4 * EARLY * rows * width * width,
        moved=6 << 20,
        out_specs=(SMEM, SMEM, VMEM, VMEM),
    )(
        place, block_table, links, swap(links), link_count, swap(link_count), facts, w_tables,
        *pieces[:EARLY], *pieces_sib[:EARLY],
    )
    *far, proj = lax.optimization_barrier((*far, proj))
    pieces, pieces_sib = pieces + far, pieces_sib + [swap(x) for x in far]
    partial = call(
        forward_kernel,
        jax.ShapeDtypeStruct((chips, 544, 128), BF16),
        [SMEM] * 4 + [VMEM] * (5 + 2 * (9 - EARLY)),
        [pltpu.VMEM((2 * n_fact, rows, width), BF16), pltpu.VMEM((chips + 1, block, width), F32)],
        flops=2 * slots * block * block * width,
        moved=8 << 20,
    )(place, block_table, lists, counts, proj, *pieces[EARLY:], *pieces_sib[EARLY:], w_tables, facts_t, tiles, tiles_sib)
    parts = by_chip(partial)

    fact_out, spread, facts_t = call(
        middle_kernel,
        (
            jax.ShapeDtypeStruct((block, width), BF16),
            jax.ShapeDtypeStruct((chips, width, block), BF16),
            jax.ShapeDtypeStruct((chips, width // chips, block), BF16),
        ),
        [VMEM] * 4,
        flops=2 * block * width * width,
        moved=5 << 20,
    )(parts, facts, w_self, cot)
    grads = by_chip(spread)

    keep, give = call(
        backward_kernel,
        (jax.ShapeDtypeStruct((n_fact, 528, 128), F32), jax.ShapeDtypeStruct((n_fact, 528, 128), BF16)),
        [SMEM] * 3 + [VMEM] * 4,
        [pltpu.VMEM((2 * n_fact + 1, width, block), F32), pltpu.VMEM((width // chips, width), F32)],
        flops=2 * slots * block * block * width,
        moved=9 << 20,
    )(place, lists, counts, grads, facts_t, tiles, tiles_sib)
    slices = by_fact((keep + swap(give).astype(F32)).astype(BF16))

    tab, gsum, self_piece = call(
        slice_kernel,
        (
            jax.ShapeDtypeStruct((384, 128), BF16),
            jax.ShapeDtypeStruct((2 * n_fact, 32, 128), BF16),
            jax.ShapeDtypeStruct((8, 128), F32),
        ),
        [SMEM] * 2 + [VMEM] * 19,
        [pltpu.VMEM((3, 32, width), F32)],
        flops=4 * n_fact * 32 * 128 * width,
        moved=3 << 20,
    )(place, block_table, slices, *pieces, *pieces_sib)
    tab = by_chip(tab.reshape(chips, 24, 128))
    packed = call(
        pack_kernel, jax.ShapeDtypeStruct((n_fact, 96, 128), BF16), [SMEM] + [VMEM] * 3, moved=1 << 19
    )(place, tab, gsum, self_piece)
    packed = by_fact(packed)
    pieces_own = by_chip(jnp.broadcast_to(packed[None, :, 64:, :], (chips, n_fact, 32, 128)))
    given = swap(packed[:, 32:64, :])

    grad_dims, grad_self, grad_tab = call(
        final_kernel,
        (
            jax.ShapeDtypeStruct((rows, width), F32),
            jax.ShapeDtypeStruct((width, width), F32),
            jax.ShapeDtypeStruct((3, width, width), F32),
        ),
        [SMEM] * 2 + [VMEM] * 5,
        moved=8 << 20,
    )(place, block_table, pieces_own, swap(pieces_own), packed[:, :32, :], given, w_tables)
    return (fact_out, grad_dims, grad_self, grad_tab)


def solution(mesh):
    split = P(("fact", "dim"), None)
    return jax.shard_map(
        body,
        mesh=mesh,
        in_specs=(split, split, P(("fact", "dim"), None, None), split, P(("fact", "dim")), P(), P(), P(), split),
        out_specs=(split, split, P(), P()),
        check_vma=False,
    )
```

time: 239 us -> 204 us (0.85)
  waiting for transfers between devices: 44.2 us -> 10.9 us
  blocking collectives: 116 us -> 134 us
  between operations: 14.9 us -> 1.47 us
  Pallas kernels: 12.9 us -> 19.8 us
  other arithmetic: 5.02 us -> 0.32 us
  starting transfers between devices: 37.2 us -> 33.1 us
    all_gather x1 -> x0, waiting for transfers between devices: 35.2 us -> none  [body(): dims_all = lax.all_gather(late_dims, 'fact', axis=0)]
    all_to_all x2 -> x4, blocking collectives: 54.4 us -> 89.2 us  [by_chip(): return lax.all_to_all(x, 'dim', 0, 0, tiled=True, axis_index_groups=same)]
    all_to_all x1 -> x0, blocking collectives: 16.1 us -> none  [body(): tab = lax.all_to_all(tab.reshape(n_dim, 24, 128), 'dim', 0, 0, tiled=True)]
    all_to_all x1 -> x0, starting transfers between devices: 3.72 us -> none  [by_chip(): return lax.all_to_all(x, 'dim', 0, 0, tiled=True, axis_index_groups=same)]
    pallas_call x3, Pallas kernels: 1.74 us -> 5.28 us  [the longest x1 3.55 us: body(): call(prepare_kernel, (jax.ShapeDtypeStruct((2 * LIST,), jnp.int32), jax.S...]
    reduce_sum x6 -> x0, other arithmetic: 2.47 us -> none  [the longest x2 2.04 us: compact(): return (listed, jnp.sum(active.astype(jnp.int32)))]
    ppermute x13 -> x15, waiting for transfers between devices: 5.47 us -> 6.92 us  [swap(): return lax.ppermute(x, 'dim', pair)]
    unnamed x26 -> x23, local copies, waits for them, and re-layouts: 5.58 us -> 4.69 us
  transfers between devices with their start and end apart: 23 -> 23, of which waited for: 7 -> 8; matrix products, arithmetic and copies ran while one was open for 2% -> 0% of each run, Pallas kernels for 0% -> 2%
where the time goes in v3:
time: 204 us; the launch traced here: 205 us
  blocking collectives  134 us (66%)
  starting transfers between devices  33.1 us (16%)
  Pallas kernels  19.8 us (10%)
  waiting for transfers between devices  10.9 us (5%)
  local copies, waits for them, and re-layouts  4.91 us (2%)
    all_to_all x4, blocking collectives, by_chip(): return lax.all_to_all(x, 'dim', 0, 0, tiled=True, axis_index_groups=same)  89.2 us
    all_to_all x2, blocking collectives, by_fact(): return lax.all_to_all(x, 'fact', 0, 0, tiled=True)  44.9 us
    ppermute x15, starting transfers between devices, swap(): return lax.ppermute(x, 'dim', pair)  21 us
    ppermute x8, starting transfers between devices, shift(): lax.ppermute(x, 'fact', [(i, (i + by) % n_fact) for i in range(n_fact)])  12.1 us
    ppermute x15, waiting for transfers between devices, swap(): return lax.ppermute(x, 'dim', pair)  6.92 us
    pallas_call x1, Pallas kernels, body(): call(backward_kernel, (jax.ShapeDtypeStruct((n_fact, 528, 128), F32), jax...  5.08 us
    pallas_call x1, Pallas kernels, body(): call(forward_kernel, jax.ShapeDtypeStruct((chips, 544, 128), BF16), [SMEM...  4.73 us
    unnamed x23, local copies, waits for them, and re-layouts  4.69 us
  transfers between devices with their start and end apart: 23, of which 8 were waited for; matrix products, arithmetic and copies ran while one was open for 0% of the time, Pallas kernels for 2%

profile of v3, /device:TPU:1, one launch (start us, length us, event | category | flops | bytes accessed | tf_op | source)
XLA Modules:
  0.0 204.6 jit_solution(15756621463675978473)
XLA Ops:
  0.6 3.3 %collective-permute-start.19 = (bf16[32,128,128]{2,1,0:T(8,128)(2,1)}, bf16[32,128,128]{2,1,0:T(8,128)(2,1)S(1)}, u32[]{:S(2)}, u32[]{:S(2)}) collective-permute-start(bf16[32,128,128]{2,1,0:T(8,128)(2,1)} %tiles_own.1), channel_id=1, source_target_pairs={{0,1},{1,0},{2,3},{3,2},{4,5},{5,4},{6,7},{7,6},{8,9},{9,8},{10,11... | collective-permute-start | bytes 3145736 | tf_op jit(solution)/shard_map/ppermute | solution.py:229
  4.0 3.9 %collective-permute-start.3 = (bf16[128,512]{1,0:T(8,128)(2,1)}, bf16[128,512]{1,0:T(8,128)(2,1)S(1)}, u32[]{:S(2)}, u32[]{:S(2)}) collective-permute-start(bf16[128,512]{1,0:T(8,128)(2,1)} %refs_0_.3), channel_id=1, source_target_pairs={{0,224},{32,0},{64,32},{96,64},{128,96},{160,128},{192,160},{224,1... | collective-permute-start | bytes 393224 | tf_op jit(solution)/shard_map/ppermute | solution.py:232
  7.8 3.2 %collective-permute-done.3.refs_2_ = bf16[128,512]{1,0:T(8,128)(2,1)S(1)} collective-permute-done((bf16[128,512]{1,0:T(8,128)(2,1)}, bf16[128,512]{1,0:T(8,128)(2,1)S(1)}, u32[]{:S(2)}, u32[]{:S(2)}) %collective-permute-start.3) | collective-permute-done | bytes 131104 | tf_op jit(solution)/shard_map/ppermute | solution.py:232
  11.0 3.3 %collective-permute-start.5 = (bf16[128,512]{1,0:T(8,128)(2,1)S(1)}, bf16[128,512]{1,0:T(8,128)(2,1)S(1)}, u32[]{:S(2)}, u32[]{:S(2)}) collective-permute-start(bf16[128,512]{1,0:T(8,128)(2,1)S(1)} %collective-permute-done.3.refs_2_), channel_id=1, source_target_pairs={{0,224},{32,0},{64,32},{96,64},{128,96},{160,128},{192,160},{224,1... | collective-permute-start | bytes 393224 | tf_op jit(solution)/shard_map/ppermute | solution.py:232
  14.3 1.1 collective-permute-start.6
  15.4 0.8 collective-permute-done.5.refs_4_
  16.2 3.4 %collective-permute-start.13 = (bf16[128,512]{1,0:T(8,128)(2,1)S(1)}, bf16[128,512]{1,0:T(8,128)(2,1)S(1)}, u32[]{:S(2)}, u32[]{:S(2)}) collective-permute-start(bf16[128,512]{1,0:T(8,128)(2,1)S(1)} %collective-permute-done.5.refs_4_), channel_id=1, source_target_pairs={{0,224},{32,0},{64,32},{96,64},{128,96},{160,128},{192,160},{224,1... | collective-permute-start | bytes 393224 | tf_op jit(solution)/shard_map/ppermute | solution.py:232
  19.6 2.0 %collective-permute-start.1 = (s32[1]{0:T(128)}, s32[1]{0:T(128)}, u32[]{:S(2)}, u32[]{:S(2)}) collective-permute-start(s32[1]{0:T(128)} %param.13), channel_id=1, source_target_pairs={{0,1},{1,0},{2,3},{3,2},{4,5},{5,4},{6,7},{7,6},{8,9},{9,8},{10,11... | collective-permute-start | bytes 20 | tf_op jit(solution)/shard_map/ppermute | solution.py:229
  21.7 0.8 copy.14.links_own
  22.5 0.3 collective-permute-done.1.count_sib
  22.8 0.3 collective-permute-start
  23.1 0.9 collective-permute-done.links_sib
  24.0 0.3 collective-permute-start.8
  24.3 0.2 collective-permute-start.7
  24.5 0.3 collective-permute-start.10
  24.8 3.1 %collective-permute-start.9 = (bf16[128,512]{1,0:T(8,128)(2,1)S(1)}, bf16[128,512]{1,0:T(8,128)(2,1)S(1)}, u32[]{:S(2)}, u32[]{:S(2)}) collective-permute-start(bf16[128,512]{1,0:T(8,128)(2,1)S(1)} %collective-permute-done.4.refs_3_), channel_id=1, source_target_pairs={{0,1},{1,0},{2,3},{3,2},{4,5},{5,4},{6,7},{7,6},{8,9},{9,8},{10,11... | collective-permute-start | bytes 393224 | tf_op jit(solution)/shard_map/ppermute | solution.py:229
  27.9 0.4 collective-permute-start.14
  28.3 1.2 collective-permute-start.12
  29.4 0.6 collective-permute-start.16
  30.0 0.3 collective-permute-start.15
  30.3 0.1 pad_add_fusion.place
  31.0 1.4 copy-done
  32.4 0.9 copy-done.3
  33.3 0.9 copy-done.5
  34.2 0.7 copy-done.9
  34.9 3.5 %shard_map.120 = (s32[80]{0:T(128)S(1)}, s32[2]{0:T(128)S(1)}, bf16[10,128,512]{2,1,0:T(8,128)(2,1)S(1)}, bf16[512,128]{1,0:T(8,128)(2,1)S(1)}) custom-call(s32[4]{0:T(128)S(1)} %pad_add_fusion.place, s32[256]{0:T(256)S(1)} %copy-done.9, s32[32,2]{1,0:T(8,128)S(1)} %copy.14.links_own, s32[32,2]{1,0:T(8,128)S(1)} %collective-permute-done.links_sib, ...), custom_call_target="tpu_custom_call" | custom-call | flops 671088640 | bytes 6291456 | tf_op jit(solution)/shard_map/pallas_call | solution.py:248
  38.5 0.3 collective-permute-start.17
  38.8 0.3 collective-permute-start.18
  39.1 0.7 collective-permute-done.17.refs_6_.refs_16_
  39.8 0.2 collective-permute-done.18.refs_7_.refs_17_
  40.1 4.7 %shard_map.121 = bf16[16,544,128]{2,1,0:T(8,128)(2,1)S(1)} custom-call(s32[4]{0:T(128)S(1)} %pad_add_fusion.place, s32[256]{0:T(256)S(1)} %copy-done.9, s32[80]{0:T(128)S(1)} %get-tuple-element.22.lists, s32[2]{0:T(128)S(1)} %get-tuple-element.23.counts, bf16[10,128,512]{2,1,0:T(8,128)(2,1)S(1)} %get-tuple-element.25.proj, ...), custom_call_target="tpu_custom_call" | custom-call | flops 536870912 | bytes 8388608 | tf_op jit(solution)/shard_map/pallas_call | solution.py:266
  44.9 34.0 %all_to_all.30.parts = bf16[16,544,128]{2,1,0:T(8,128)(2,1)S(1)} all-to-all(bf16[16,544,128]{2,1,0:T(8,128)(2,1)S(1)} %shard_map.121), channel_id=1, replica_groups={{0,2,4,6,8,10,12,14,16,18,20,22,24,26,28,30},{1,3,5,7,9,11,13,15,17,19,..., dimensions={0} | all-to-all | bytes 4456448 | tf_op jit(solution)/shard_map/all_to_all | solution.py:235
  78.9 1.2 shard_map.122
  80.1 28.0 %all_to_all.31.grads = bf16[16,512,128]{2,1,0:T(8,128)(2,1)S(1)} all-to-all(bf16[16,512,128]{2,1,0:T(8,128)(2,1)S(1)} %get-tuple-element.30), channel_id=1, replica_groups={{0,2,4,6,8,10,12,14,16,18,20,22,24,26,28,30},{1,3,5,7,9,11,13,15,17,19,..., dimensions={0} | all-to-all | bytes 4194304 | tf_op jit(solution)/shard_map/all_to_all | solution.py:235
  108.1 5.1 %shard_map.123 = (f32[8,528,128]{2,1,0:T(8,128)S(1)}, bf16[8,528,128]{2,1,0:T(8,128)(2,1)S(1)}) custom-call(s32[4]{0:T(128)S(1)} %pad_add_fusion.place, s32[80]{0:T(128)S(1)} %get-tuple-element.22.lists, s32[2]{0:T(128)S(1)} %get-tuple-element.23.counts, bf16[16,512,128]{2,1,0:T(8,128)(2,1)S(1)} %all_to_all.31.grads, ...), custom_call_target="tpu_custom_call" | custom-call | flops 536870912 | bytes 9437184 | tf_op jit(solution)/shard_map/pallas_call | solution.py:289
  113.1 4.0 %collective-permute-start.20 = (bf16[8,528,128]{2,1,0:T(8,128)(2,1)S(1)}, bf16[8,528,128]{2,1,0:T(8,128)(2,1)S(1)}, u32[]{:S(2)}, u32[]{:S(2)}) collective-permute-start(bf16[8,528,128]{2,1,0:T(8,128)(2,1)S(1)} %get-tuple-element.33), channel_id=1, source_target_pairs={{0,1},{1,0},{2,3},{3,2},{4,5},{5,4},{6,7},{7,6},{8,9},{9,8},{10,11... | collective-permute-start | bytes 3244040 | tf_op jit(solution)/shard_map/ppermute | solution.py:229
  117.2 2.3 %collective-permute-done.20 = bf16[8,528,128]{2,1,0:T(8,128)(2,1)S(1)} collective-permute-done((bf16[8,528,128]{2,1,0:T(8,128)(2,1)S(1)}, bf16[8,528,128]{2,1,0:T(8,128)(2,1)S(1)}, u32[]{:S(2)}, u32[]{:S(2)}) %collective-permute-start.20) | collective-permute-done | bytes 1081376 | tf_op jit(solution)/shard_map/ppermute | solution.py:229
  119.5 0.2 add_convert_fusion
  119.8 33.9 %all_to_all.32.parts = bf16[8,528,128]{2,1,0:T(8,128)(2,1)S(1)} all-to-all(bf16[8,528,128]{2,1,0:T(8,128)(2,1)S(1)} %add_convert_fusion), channel_id=1, replica_groups=mesh['fact'=8,'dim'=32] {'fact'}, dimensions={0} | all-to-all | bytes 2162688 | tf_op jit(solution)/shard_map/all_to_all | solution.py:238
  153.7 1.2 shard_map.124
  154.8 10.7 %all_to_all.33.parts = bf16[16,24,128]{2,1,0:T(8,128)(2,1)S(1)} all-to-all(bf16[16,24,128]{2,1,0:T(8,128)(2,1)S(1)} %bitcast.5), channel_id=1, replica_groups={{0,2,4,6,8,10,12,14,16,18,20,22,24,26,28,30},{1,3,5,7,9,11,13,15,17,19,..., dimensions={0} | all-to-all | bytes 196608 | tf_op jit(solution)/shard_map/all_to_all | solution.py:235
  165.5 0.6 shard_map.125
  166.1 11.0 %all_to_all.34 = bf16[8,96,128]{2,1,0:T(8,128)(2,1)S(1)} all-to-all(bf16[8,96,128]{2,1,0:T(8,128)(2,1)S(1)} %shard_map.125), channel_id=1, replica_groups=mesh['fact'=8,'dim'=32] {'fact'}, dimensions={0} | all-to-all | bytes 393216 | tf_op jit(solution)/shard_map/all_to_all | solution.py:238
  177.1 0.2 broadcast_in_dim.2
  177.3 16.5 %all_to_all.35.own = bf16[16,8,32,128]{3,2,1,0:T(8,128)(2,1)S(1)} all-to-all(bf16[16,8,32,128]{3,2,1,0:T(8,128)(2,1)S(1)} %broadcast_in_dim.2), channel_id=1, replica_groups={{0,2,4,6,8,10,12,14,16,18,20,22,24,26,28,30},{1,3,5,7,9,11,13,15,17,19,..., dimensions={0} | all-to-all | bytes 2097152 | tf_op jit(solution)/shard_map/all_to_all | solution.py:235
  193.8 4.8 %collective-permute-start.21 = (bf16[16,8,32,128]{3,2,1,0:T(8,128)(2,1)S(1)}, bf16[16,8,32,128]{3,2,1,0:T(8,128)(2,1)S(1)}, u32[]{:S(2)}, u32[]{:S(2)}) collective-permute-start(bf16[16,8,32,128]{3,2,1,0:T(8,128)(2,1)S(1)} %all_to_all.35.own), channel_id=1, source_target_pairs={{0,1},{1,0},{2,3},{3,2},{4,5},{5,4},{6,7},{7,6},{8,9},{9,8},{10,11... | collective-permute-start | bytes 3145736 | tf_op jit(solution)/shard_map/ppermute | solution.py:229
  198.7 2.4 %collective-permute-done.22.given = bf16[8,32,128]{2,1,0:T(8,128)(2,1)S(1)} collective-permute-done((bf16[8,32,128]{2,1,0:T(8,128)(2,1)S(1)}, bf16[8,32,128]{2,1,0:T(8,128)(2,1)S(1)}, u32[]{:S(2)}, u32[]{:S(2)}) %collective-permute-start.22) | collective-permute-done | bytes 65568 | tf_op jit(solution)/shard_map/ppermute | solution.py:229
  201.1 3.6 %shard_map.126 = (f32[128,512]{1,0:T(8,128)}, f32[512,512]{1,0:T(8,128)}, f32[3,512,512]{2,1,0:T(8,128)}) custom-call(s32[4]{0:T(128)S(1)} %pad_add_fusion.place, s32[256]{0:T(256)S(1)} %copy-done.10, bf16[16,8,32,128]{3,2,1,0:T(8,128)(2,1)S(1)} %all_to_all.35.own, bf16[16,8,32,128]{3,2,1,0:T(8,128)(2,1)S(1)} %collective-permute-done.21.sib, ...), custom_call_target="tpu_custom_call" | custom-call | bytes 8388608 | tf_op jit(solution)/shard_map/pallas_call | solution.py:319
  (40 shorter events, 0.1 us)
Async XLA Ops:
  0.6 39.5 %collective-permute-start.19 = (bf16[32,128,128]{2,1,0:T(8,128)(2,1)}, bf16[32,128,128]{2,1,0:T(8,128)(2,1)S(1)}, u32[]{:S(2)}, u32[]{:S(2)}) collective-permute-start(bf16[32,128,128]{2,1,0:T(8,128)(2,1)} %tiles_own.1), channel_id=1, source_target_pairs={{0,1},{1,0},{2,3},{3,2},{4,5},{5,4},{6,7},{7,6},{8,9},{9,8},{10,11... | collective-permute-start | bytes 3145736 | tf_op jit(solution)/shard_map/ppermute | solution.py:229
  4.0 7.0 %collective-permute-start.3 = (bf16[128,512]{1,0:T(8,128)(2,1)}, bf16[128,512]{1,0:T(8,128)(2,1)S(1)}, u32[]{:S(2)}, u32[]{:S(2)}) collective-permute-start(bf16[128,512]{1,0:T(8,128)(2,1)} %refs_0_.3), channel_id=1, source_target_pairs={{0,224},{32,0},{64,32},{96,64},{128,96},{160,128},{192,160},{224,1... | collective-permute-start | bytes 393224 | tf_op jit(solution)/shard_map/ppermute | solution.py:232
  7.8 6.5 %collective-permute-start.2 = (bf16[128,512]{1,0:T(8,128)(2,1)}, bf16[128,512]{1,0:T(8,128)(2,1)S(1)}, u32[]{:S(2)}, u32[]{:S(2)}) collective-permute-start(bf16[128,512]{1,0:T(8,128)(2,1)} %refs_0_.3), channel_id=1, source_target_pairs={{0,32},{32,64},{64,96},{96,128},{128,160},{160,192},{192,224},{224... | collective-permute-start | bytes 393224 | tf_op jit(solution)/shard_map/ppermute | solution.py:232
  11.0 5.3 %collective-permute-start.5 = (bf16[128,512]{1,0:T(8,128)(2,1)S(1)}, bf16[128,512]{1,0:T(8,128)(2,1)S(1)}, u32[]{:S(2)}, u32[]{:S(2)}) collective-permute-start(bf16[128,512]{1,0:T(8,128)(2,1)S(1)} %collective-permute-done.3.refs_2_), channel_id=1, source_target_pairs={{0,224},{32,0},{64,32},{96,64},{128,96},{160,128},{192,160},{224,1... | collective-permute-start | bytes 393224 | tf_op jit(solution)/shard_map/ppermute | solution.py:232
  14.3 5.4 %collective-permute-start.4 = (bf16[128,512]{1,0:T(8,128)(2,1)S(1)}, bf16[128,512]{1,0:T(8,128)(2,1)S(1)}, u32[]{:S(2)}, u32[]{:S(2)}) collective-permute-start(bf16[128,512]{1,0:T(8,128)(2,1)S(1)} %collective-permute-done.2.refs_1_), channel_id=1, source_target_pairs={{0,32},{32,64},{64,96},{96,128},{128,160},{160,192},{192,224},{224... | collective-permute-start | bytes 393224 | tf_op jit(solution)/shard_map/ppermute | solution.py:232
  14.3 10.0 %collective-permute-start.6 = (bf16[128,512]{1,0:T(8,128)(2,1)}, bf16[128,512]{1,0:T(8,128)(2,1)S(1)}, u32[]{:S(2)}, u32[]{:S(2)}) collective-permute-start(bf16[128,512]{1,0:T(8,128)(2,1)} %refs_0_.3), channel_id=1, source_target_pairs={{0,1},{1,0},{2,3},{3,2},{4,5},{5,4},{6,7},{7,6},{8,9},{9,8},{10,11... | collective-permute-start | bytes 393224 | tf_op jit(solution)/shard_map/ppermute | solution.py:229
  16.2 8.2 %collective-permute-start.13 = (bf16[128,512]{1,0:T(8,128)(2,1)S(1)}, bf16[128,512]{1,0:T(8,128)(2,1)S(1)}, u32[]{:S(2)}, u32[]{:S(2)}) collective-permute-start(bf16[128,512]{1,0:T(8,128)(2,1)S(1)} %collective-permute-done.5.refs_4_), channel_id=1, source_target_pairs={{0,224},{32,0},{64,32},{96,64},{128,96},{160,128},{192,160},{224,1... | collective-permute-start | bytes 393224 | tf_op jit(solution)/shard_map/ppermute | solution.py:232
  19.6 5.1 %collective-permute-start.11 = (bf16[128,512]{1,0:T(8,128)(2,1)S(1)}, bf16[128,512]{1,0:T(8,128)(2,1)S(1)}, u32[]{:S(2)}, u32[]{:S(2)}) collective-permute-start(bf16[128,512]{1,0:T(8,128)(2,1)S(1)} %collective-permute-done.4.refs_3_), channel_id=1, source_target_pairs={{0,32},{32,64},{64,96},{96,128},{128,160},{160,192},{192,224},{224... | collective-permute-start | bytes 393224 | tf_op jit(solution)/shard_map/ppermute | solution.py:232
  19.6 3.1 %collective-permute-start.1 = (s32[1]{0:T(128)}, s32[1]{0:T(128)}, u32[]{:S(2)}, u32[]{:S(2)}) collective-permute-start(s32[1]{0:T(128)} %param.13), channel_id=1, source_target_pairs={{0,1},{1,0},{2,3},{3,2},{4,5},{5,4},{6,7},{7,6},{8,9},{9,8},{10,11... | collective-permute-start | bytes 20 | tf_op jit(solution)/shard_map/ppermute | solution.py:229
  22.8 1.2 collective-permute-start
  24.0 3.9 %collective-permute-start.8 = (bf16[128,512]{1,0:T(8,128)(2,1)S(1)}, bf16[128,512]{1,0:T(8,128)(2,1)S(1)}, u32[]{:S(2)}, u32[]{:S(2)}) collective-permute-start(bf16[128,512]{1,0:T(8,128)(2,1)S(1)} %collective-permute-done.3.refs_2_), channel_id=1, source_target_pairs={{0,1},{1,0},{2,3},{3,2},{4,5},{5,4},{6,7},{7,6},{8,9},{9,8},{10,11... | collective-permute-start | bytes 393224 | tf_op jit(solution)/shard_map/ppermute | solution.py:229
  24.3 4.0 %collective-permute-start.7 = (bf16[128,512]{1,0:T(8,128)(2,1)S(1)}, bf16[128,512]{1,0:T(8,128)(2,1)S(1)}, u32[]{:S(2)}, u32[]{:S(2)}) collective-permute-start(bf16[128,512]{1,0:T(8,128)(2,1)S(1)} %collective-permute-done.2.refs_1_), channel_id=1, source_target_pairs={{0,1},{1,0},{2,3},{3,2},{4,5},{5,4},{6,7},{7,6},{8,9},{9,8},{10,11... | collective-permute-start | bytes 393224 | tf_op jit(solution)/shard_map/ppermute | solution.py:229
  24.5 5.0 %collective-permute-start.10 = (bf16[128,512]{1,0:T(8,128)(2,1)S(1)}, bf16[128,512]{1,0:T(8,128)(2,1)S(1)}, u32[]{:S(2)}, u32[]{:S(2)}) collective-permute-start(bf16[128,512]{1,0:T(8,128)(2,1)S(1)} %collective-permute-done.5.refs_4_), channel_id=1, source_target_pairs={{0,1},{1,0},{2,3},{3,2},{4,5},{5,4},{6,7},{7,6},{8,9},{9,8},{10,11... | collective-permute-start | bytes 393224 | tf_op jit(solution)/shard_map/ppermute | solution.py:229
  24.8 5.2 %collective-permute-start.9 = (bf16[128,512]{1,0:T(8,128)(2,1)S(1)}, bf16[128,512]{1,0:T(8,128)(2,1)S(1)}, u32[]{:S(2)}, u32[]{:S(2)}) collective-permute-start(bf16[128,512]{1,0:T(8,128)(2,1)S(1)} %collective-permute-done.4.refs_3_), channel_id=1, source_target_pairs={{0,1},{1,0},{2,3},{3,2},{4,5},{5,4},{6,7},{7,6},{8,9},{9,8},{10,11... | collective-permute-start | bytes 393224 | tf_op jit(solution)/shard_map/ppermute | solution.py:229
  27.9 10.6 %collective-permute-start.14 = (bf16[64,512]{1,0:T(8,128)(2,1)S(1)}, bf16[64,512]{1,0:T(8,128)(2,1)S(1)}, u32[]{:S(2)}, u32[]{:S(2)}) collective-permute-start(bf16[64,512]{1,0:T(8,128)(2,1)S(1)} %slice.21), channel_id=1, source_target_pairs={{0,224},{32,0},{64,32},{96,64},{128,96},{160,128},{192,160},{224,1... | collective-permute-start | bytes 196616 | tf_op jit(solution)/shard_map/ppermute | solution.py:232
  28.3 10.2 %collective-permute-start.12 = (bf16[64,512]{1,0:T(8,128)(2,1)S(1)}, bf16[64,512]{1,0:T(8,128)(2,1)S(1)}, u32[]{:S(2)}, u32[]{:S(2)}) collective-permute-start(bf16[64,512]{1,0:T(8,128)(2,1)S(1)} %slice.20), channel_id=1, source_target_pairs={{0,32},{32,64},{64,96},{96,128},{128,160},{160,192},{192,224},{224... | collective-permute-start | bytes 196616 | tf_op jit(solution)/shard_map/ppermute | solution.py:232
  29.4 10.6 %collective-permute-start.16 = (bf16[128,512]{1,0:T(8,128)(2,1)S(1)}, bf16[128,512]{1,0:T(8,128)(2,1)S(1)}, u32[]{:S(2)}, u32[]{:S(2)}) collective-permute-start(bf16[128,512]{1,0:T(8,128)(2,1)S(1)} %collective-permute-done.13.refs_1_.refs_6_), channel_id=1, source_target_pairs={{0,1},{1,0},{2,3},{3,2},{4,5},{5,4},{6,7},{7,6},{8,9},{9,8},{10,11... | collective-permute-start | bytes 393224 | tf_op jit(solution)/shard_map/ppermute | solution.py:229
  30.0 10.1 %collective-permute-start.15 = (bf16[128,512]{1,0:T(8,128)(2,1)S(1)}, bf16[128,512]{1,0:T(8,128)(2,1)S(1)}, u32[]{:S(2)}, u32[]{:S(2)}) collective-permute-start(bf16[128,512]{1,0:T(8,128)(2,1)S(1)} %collective-permute-done.11.refs_0_.refs_5_), channel_id=1, source_target_pairs={{0,1},{1,0},{2,3},{3,2},{4,5},{5,4},{6,7},{7,6},{8,9},{9,8},{10,11... | collective-permute-start | bytes 393224 | tf_op jit(solution)/shard_map/ppermute | solution.py:229
  31.0 1.4 copy-start
  32.4 0.9 copy-start.3
  33.3 0.9 copy-start.5
  34.2 0.7 copy-start.9
  34.9 5.2 %copy-start.1 = (bf16[3,512,512]{2,1,0:T(8,128)(2,1)S(1)}, bf16[3,512,512]{2,1,0:T(8,128)(2,1)}, u32[]{:S(2)}) copy-start(bf16[3,512,512]{2,1,0:T(8,128)(2,1)} %w.5) | copy-start | bytes 4718596
  34.9 5.2 %copy-start.2 = (bf16[32,128,128]{2,1,0:T(8,128)(2,1)S(1)}, bf16[32,128,128]{2,1,0:T(8,128)(2,1)}, u32[]{:S(2)}) copy-start(bf16[32,128,128]{2,1,0:T(8,128)(2,1)} %tiles_own.1) | copy-start | bytes 3145732
  38.5 1.3 collective-permute-start.17
  38.8 1.3 collective-permute-start.18
  44.9 34.0 %copy-start.4 = (bf16[128,512]{1,0:T(8,128)(2,1)S(1)}, bf16[128,512]{1,0:T(8,128)(2,1)}, u32[]{:S(2)}) copy-start(bf16[128,512]{1,0:T(8,128)(2,1)} %facts.3) | copy-start | bytes 393220
  44.9 34.0 %copy-start.7 = (bf16[512,512]{1,0:T(8,128)(2,1)S(1)}, bf16[512,512]{1,0:T(8,128)(2,1)}, u32[]{:S(2)}) copy-start(bf16[512,512]{1,0:T(8,128)(2,1)} %w.4) | copy-start | bytes 1572868
  44.9 34.0 %copy-start.8 = (bf16[128,512]{1,0:T(8,128)(2,1)S(1)}, bf16[128,512]{1,0:T(8,128)(2,1)}, u32[]{:S(2)}) copy-start(bf16[128,512]{1,0:T(8,128)(2,1)} %cot.1) | copy-start | bytes 393220
  113.1 6.4 %collective-permute-start.20 = (bf16[8,528,128]{2,1,0:T(8,128)(2,1)S(1)}, bf16[8,528,128]{2,1,0:T(8,128)(2,1)S(1)}, u32[]{:S(2)}, u32[]{:S(2)}) collective-permute-start(bf16[8,528,128]{2,1,0:T(8,128)(2,1)S(1)} %get-tuple-element.33), channel_id=1, source_target_pairs={{0,1},{1,0},{2,3},{3,2},{4,5},{5,4},{6,7},{7,6},{8,9},{9,8},{10,11... | collective-permute-start | bytes 3244040 | tf_op jit(solution)/shard_map/ppermute | solution.py:229
  119.7 33.9 %copy-start.6 = (bf16[128,512]{1,0:T(8,128)(2,1)S(1)}, bf16[128,512]{1,0:T(8,128)(2,1)}, u32[]{:S(2)}) copy-start(bf16[128,512]{1,0:T(8,128)(2,1)} %refs_0_.3) | copy-start | bytes 393220
  119.8 33.9 %copy-start.10 = (s32[256]{0:T(256)S(1)}, s32[256]{0:T(256)}, u32[]{:S(2)}) copy-start(s32[256]{0:T(256)} %table.7) | copy-start | bytes 3076
  193.8 7.2 %collective-permute-start.21 = (bf16[16,8,32,128]{3,2,1,0:T(8,128)(2,1)S(1)}, bf16[16,8,32,128]{3,2,1,0:T(8,128)(2,1)S(1)}, u32[]{:S(2)}, u32[]{:S(2)}) collective-permute-start(bf16[16,8,32,128]{3,2,1,0:T(8,128)(2,1)S(1)} %all_to_all.35.own), channel_id=1, source_target_pairs={{0,1},{1,0},{2,3},{3,2},{4,5},{5,4},{6,7},{7,6},{8,9},{9,8},{10,11... | collective-permute-start | bytes 3145736 | tf_op jit(solution)/shard_map/ppermute | solution.py:229
  198.7 2.4 %collective-permute-start.22 = (bf16[8,32,128]{2,1,0:T(8,128)(2,1)S(1)}, bf16[8,32,128]{2,1,0:T(8,128)(2,1)S(1)}, u32[]{:S(2)}, u32[]{:S(2)}) collective-permute-start(bf16[8,32,128]{2,1,0:T(8,128)(2,1)S(1)} %get-tuple-element.40), channel_id=1, source_target_pairs={{0,1},{1,0},{2,3},{3,2},{4,5},{5,4},{6,7},{7,6},{8,9},{9,8},{10,11... | collective-permute-start | bytes 196616 | tf_op jit(solution)/shard_map/ppermute | solution.py:229

commit v4 on v3

--- a/solution.py
+++ b/solution.py
@@ -10,7 +10,7 @@
 VMEM = pl.BlockSpec(memory_space=pltpu.VMEM)
 SMEM = pl.BlockSpec(memory_space=pltpu.SMEM)
 PARAMS = pltpu.CompilerParams(vmem_limit_bytes=24 * 1024 * 1024)
-UNROLL = 2
+UNROLL = 4
 
 
 ORDER = (0, -1, 1, -2, 2, -3, 3)
@@ -39,32 +39,40 @@
     return table[h * 32 + (dim_pos if side == 0 else dim_pos + 1 - 2 * place[2])]
 
 
-def prepare_kernel(place, table, links_own, links_sib, count_own, count_sib, facts, w, *refs):
-    early, (lists, counts, proj, facts_t) = refs[: 2 * EARLY], refs[2 * EARLY :]
+def prepare_kernel(place, table, links_own, links_sib, facts, dims, w, lists, counts, facts_t, proj):
     fact_pos, core = place[0], place[2]
-    for side, (links, count) in enumerate(((links_own, count_own), (links_sib, count_sib))):
+    for side, links in enumerate((links_own, links_sib)):
         n = jnp.int32(0)
         for slot in range(32):
-            target = links[slot, 0] - fact_pos * 32
-            lists[side * LIST + n] = slot + ((links[slot, 1] >> 5) << 5) + ((target >> 1) << 8)
-            n = n + jnp.where((slot < count[0]) & ((target & 1) == core), 1, 0)
-        lists[side * LIST + n] = 16 << 8
+            target = links[0, slot] - fact_pos * 32
+            lists[side * LIST + n] = slot + ((links[1, slot] >> 5) << 5) + ((target >> 1) << 8)
+            n = n + jnp.where((slot < links[0, 32]) & ((target & 1) == core), 1, 0)
+        for spare in range(UNROLL - 1):
+            lists[side * LIST + n + spare] = 16 << 8
         counts[side] = n
+    kind = column_kind(place, table, 0, fact_pos)
+    proj[...] = jnp.dot(dims[...], w[kind], preferred_element_type=F32).astype(BF16)
+    facts_t[...] = facts[...].astype(F32).T.astype(BF16)
+
+
+def project_kernel(place, table, w, *refs):
+    early, proj = refs[:-1], refs[-1]
+    at = 0
     for side in range(2):
-        for at, shift in enumerate(ORDER[:EARLY]):
-            kind = column_kind(place, table, side, (fact_pos + shift) & 7)
-            value = jnp.dot(early[side * EARLY + at][...], w[kind], preferred_element_type=F32)
-            proj[side * EARLY + at] = value.astype(BF16)
-    facts_t[...] = facts[...].astype(F32).T.astype(BF16)
-
-
-def forward_kernel(place, table, lists, counts, proj, *refs):
+        for shift in ORDER[1 - side : EARLY]:
+            kind = column_kind(place, table, side, (place[0] + shift) & 7)
+            proj[at] = jnp.dot(early[at][...], w[kind], preferred_element_type=F32).astype(BF16)
+            at += 1
+
+
+def forward_kernel(place, table, lists, counts, proj_own, proj, *refs):
     late = 9 - EARLY
     sides, (w, facts_t, tiles_own, tiles_sib, out, panel, acc) = (refs[:late], refs[late : 2 * late]), refs[2 * late :]
     fact_pos = place[0]
     for side, pieces in enumerate(sides):
         for at, shift in enumerate(ORDER[:EARLY]):
-            panel[side * 8 + ((fact_pos + shift) & 7)] = proj[side * EARLY + at]
+            value = proj_own[...] if side + at == 0 else proj[side * EARLY + at - 1]
+            panel[side * 8 + ((fact_pos + shift) & 7)] = value
         blocks = [x[...] for x in pieces[:-2]] + [jnp.concatenate([pieces[-2][...], pieces[-1][...]], axis=0)]
         for shift, rows in zip(ORDER[EARLY:] + (4,), blocks):
             h = (fact_pos + shift) & 7
@@ -180,15 +188,19 @@
         out[z, 64:96, :] = piece
 
 
-def final_kernel(place, table, own, sib, kept, given, w, grad_dims, grad_self, grad_tab):
+def rows_kernel(place, table, kept, given, w, grad_dims):
     even = place[2] == 0
-    scale = F32(32768.0**-0.5)
     kind = table[place[0] * 32 + place[1]]
     mine, other = kept[...].astype(F32).reshape(256, 128), given[...].astype(F32).reshape(256, 128)
     turned = jnp.concatenate([jnp.where(even, mine, other), jnp.where(even, other, mine)], axis=0)
     grad_dims[...] = lax.dot_general(
         turned.T.astype(BF16), w[kind], (((1,), (1,)), ((), ())), preferred_element_type=F32
     )
+
+
+def final_kernel(place, own, sib, grad_self, grad_tab):
+    even = place[2] == 0
+    scale = F32(32768.0**-0.5)
     for q in range(4):
         for group in range(2):
             tables = [[[], [], []], [[], [], []]]
@@ -237,40 +249,50 @@
     def by_fact(x):
         return lax.all_to_all(x, "fact", 0, 0, tiled=True)
 
+    count = jnp.broadcast_to(link_count[None, :], (2, 1))
+    links_own = jnp.concatenate([links.T, count], axis=1)
+    links_sib = swap(links_own)
+    lists, counts, facts_t, proj_own = call(
+        prepare_kernel,
+        (
+            jax.ShapeDtypeStruct((2 * LIST,), jnp.int32),
+            jax.ShapeDtypeStruct((2,), jnp.int32),
+            jax.ShapeDtypeStruct((width, block), BF16),
+            jax.ShapeDtypeStruct((rows, width), BF16),
+        ),
+        [SMEM] * 4 + [VMEM] * 3,
+        flops=2 * rows * width * width,
+        moved=3 << 20,
+        out_specs=(SMEM, SMEM, VMEM, VMEM),
+    )(place, block_table, links_own, links_sib, facts, dims, w_tables)
+    tiles_sib = swap(tiles)
+
     pieces, up, down = [dims], dims, dims
-    for _ in range(3):
+    for step in range(3):
+        if step == 2:
+            up, down, proj_own = lax.optimization_barrier((up, down, proj_own))
         up, down = shift(up, 1), shift(down, -1)
         pieces += [up, down]
     pieces_sib = [swap(x) for x in pieces]
     far = [shift(up[: rows // 2], 1), shift(down[rows // 2 :], -1)]
-    tiles_sib = swap(tiles)
-
-    lists, counts, proj, facts_t = call(
-        prepare_kernel,
-        (
-            jax.ShapeDtypeStruct((2 * LIST,), jnp.int32),
-            jax.ShapeDtypeStruct((2,), jnp.int32),
-            jax.ShapeDtypeStruct((2 * EARLY, rows, width), BF16),
-            jax.ShapeDtypeStruct((width, block), BF16),
-        ),
-        [SMEM] * 6 + [VMEM] * (2 + 2 * EARLY),
-        flops=4 * EARLY * rows * width * width,
-        moved=6 << 20,
-        out_specs=(SMEM, SMEM, VMEM, VMEM),
-    )(
-        place, block_table, links, swap(links), link_count, swap(link_count), facts, w_tables,
-        *pieces[:EARLY], *pieces_sib[:EARLY],
-    )
+    early = pieces[1:EARLY] + pieces_sib[:EARLY]
+    proj = call(
+        project_kernel,
+        jax.ShapeDtypeStruct((len(early), rows, width), BF16),
+        [SMEM] * 2 + [VMEM] * (1 + len(early)),
+        flops=2 * len(early) * rows * width * width,
+        moved=4 << 20,
+    )(place, block_table, w_tables, *early)
     *far, proj = lax.optimization_barrier((*far, proj))
     pieces, pieces_sib = pieces + far, pieces_sib + [swap(x) for x in far]
     partial = call(
         forward_kernel,
         jax.ShapeDtypeStruct((chips, 544, 128), BF16),
-        [SMEM] * 4 + [VMEM] * (5 + 2 * (9 - EARLY)),
+        [SMEM] * 4 + [VMEM] * (6 + 2 * (9 - EARLY)),
         [pltpu.VMEM((2 * n_fact, rows, width), BF16), pltpu.VMEM((chips + 1, block, width), F32)],
         flops=2 * slots * block * block * width,
         moved=8 << 20,
-    )(place, block_table, lists, counts, proj, *pieces[EARLY:], *pieces_sib[EARLY:], w_tables, facts_t, tiles, tiles_sib)
+    )(place, block_table, lists, counts, proj_own, proj, *pieces[EARLY:], *pieces_sib[EARLY:], w_tables, facts_t, tiles, tiles_sib)
     parts = by_chip(partial)
 
     fact_out, spread, facts_t = call(
@@ -316,16 +338,19 @@
     pieces_own = by_chip(jnp.broadcast_to(packed[None, :, 64:, :], (chips, n_fact, 32, 128)))
     given = swap(packed[:, 32:64, :])
 
-    grad_dims, grad_self, grad_tab = call(
+    grad_dims = call(
+        rows_kernel,
+        jax.ShapeDtypeStruct((rows, width), F32),
+        [SMEM] * 2 + [VMEM] * 3,
+        flops=2 * rows * width * width,
+        moved=2 << 20,
+    )(place, block_table, packed[:, :32, :], given, w_tables)
+    grad_self, grad_tab = call(
         final_kernel,
-        (
-            jax.ShapeDtypeStruct((rows, width), F32),
-            jax.ShapeDtypeStruct((width, width), F32),
-            jax.ShapeDtypeStruct((3, width, width), F32),
-        ),
-        [SMEM] * 2 + [VMEM] * 5,
+        (jax.ShapeDtypeStruct((width, width), F32), jax.ShapeDtypeStruct((3, width, width), F32)),
+        [SMEM] + [VMEM] * 2,
         moved=8 << 20,
-    )(place, block_table, pieces_own, swap(pieces_own), packed[:, :32, :], given, w_tables)
+    )(place, pieces_own, swap(pieces_own))
     return (fact_out, grad_dims, grad_self, grad_tab)
 
 

time: 204 us -> 203 us (level)
  starting transfers between devices: 33.1 us -> 27.2 us
  blocking collectives: 134 us -> 138 us
  waiting for transfers between devices: 10.9 us -> 13.4 us
    ppermute x15 -> x14, starting transfers between devices: 21 us -> 14.1 us  [swap(): return lax.ppermute(x, 'dim', pair)]
    all_to_all x4, blocking collectives: 89.2 us -> 92.4 us  [by_chip(): return lax.all_to_all(x, 'dim', 0, 0, tiled=True, axis_index_groups=same)]
    pallas_call x1 -> x3, Pallas kernels: 3.58 us -> 6.39 us  [the longest x1 3.49 us: body(): call(final_kernel, (jax.ShapeDtypeStruct((width, width), F32), jax.ShapeD...]
    ppermute x8, waiting for transfers between devices: 3.97 us -> 6.35 us  [shift(): lax.ppermute(x, 'fact', [(i, (i + by) % n_fact) for i in range(n_fact)])]
    unnamed x23 -> x22, local copies, waits for them, and re-layouts: 4.69 us -> 3.94 us
    ppermute x15 -> x14, waiting for transfers between devices: 6.92 us -> 7.04 us  [swap(): return lax.ppermute(x, 'dim', pair)]
  transfers between devices with their start and end apart: 23 -> 22, of which waited for: 8 -> 7; matrix products, arithmetic and copies ran while one was open for 0% -> 0% of each run, Pallas kernels for 2% -> 2%
where the time goes in v4:
time: 203 us
  blocking collectives  138 us (68%)
  starting transfers between devices  27.2 us (13%)
  Pallas kernels  17.9 us (9%)
  waiting for transfers between devices  13.4 us (7%)
  local copies, waits for them, and re-layouts  4.84 us (2%)
    all_to_all x4, blocking collectives, by_chip(): return lax.all_to_all(x, 'dim', 0, 0, tiled=True, axis_index_groups=same)  92.4 us
    all_to_all x2, blocking collectives, by_fact(): return lax.all_to_all(x, 'fact', 0, 0, tiled=True)  45.2 us
    ppermute x14, starting transfers between devices, swap(): return lax.ppermute(x, 'dim', pair)  14.1 us
    ppermute x8, starting transfers between devices, shift(): lax.ppermute(x, 'fact', [(i, (i + by) % n_fact) for i in range(n_fact)])  13.2 us
    ppermute x14, waiting for transfers between devices, swap(): return lax.ppermute(x, 'dim', pair)  7.04 us
    ppermute x8, waiting for transfers between devices, shift(): lax.ppermute(x, 'fact', [(i, (i + by) % n_fact) for i in range(n_fact)])  6.35 us
  transfers between devices with their start and end apart: 22, of which 7 were waited for; matrix products, arithmetic and copies ran while one was open for 0% of the time, Pallas kernels for 2%

profile of v4, /device:TPU:1, one launch (start us, length us, event | category | flops | bytes accessed | tf_op | source)
XLA Modules:
  0.0 202.7 jit_solution(7715824602927428678)
XLA Ops:
  0.6 3.3 %collective-permute-start.18 = (bf16[32,128,128]{2,1,0:T(8,128)(2,1)}, bf16[32,128,128]{2,1,0:T(8,128)(2,1)S(1)}, u32[]{:S(2)}, u32[]{:S(2)}) collective-permute-start(bf16[32,128,128]{2,1,0:T(8,128)(2,1)} %tiles_own.1), channel_id=1, source_target_pairs={{0,1},{1,0},{2,3},{3,2},{4,5},{5,4},{6,7},{7,6},{8,9},{9,8},{10,11... | collective-permute-start | bytes 3145736 | tf_op jit(solution)/shard_map/ppermute | solution.py:241
  4.0 3.9 %collective-permute-start.3 = (bf16[128,512]{1,0:T(8,128)(2,1)}, bf16[128,512]{1,0:T(8,128)(2,1)S(1)}, u32[]{:S(2)}, u32[]{:S(2)}) collective-permute-start(bf16[128,512]{1,0:T(8,128)(2,1)} %refs_0_.1), channel_id=1, source_target_pairs={{0,224},{32,0},{64,32},{96,64},{128,96},{160,128},{192,160},{224,1... | collective-permute-start | bytes 393224 | tf_op jit(solution)/shard_map/ppermute | solution.py:244
  7.8 3.2 %collective-permute-done.3.refs_1_.refs_2_ = bf16[128,512]{1,0:T(8,128)(2,1)S(1)} collective-permute-done((bf16[128,512]{1,0:T(8,128)(2,1)}, bf16[128,512]{1,0:T(8,128)(2,1)S(1)}, u32[]{:S(2)}, u32[]{:S(2)}) %collective-permute-start.3) | collective-permute-done | bytes 131104 | tf_op jit(solution)/shard_map/ppermute | solution.py:244
  11.0 3.3 %collective-permute-start.4 = (bf16[128,512]{1,0:T(8,128)(2,1)S(1)}, bf16[128,512]{1,0:T(8,128)(2,1)S(1)}, u32[]{:S(2)}, u32[]{:S(2)}) collective-permute-start(bf16[128,512]{1,0:T(8,128)(2,1)S(1)} %collective-permute-done.3.refs_1_.refs_2_), channel_id=1, source_target_pairs={{0,224},{32,0},{64,32},{96,64},{128,96},{160,128},{192,160},{224,1... | collective-permute-start | bytes 393224 | tf_op jit(solution)/shard_map/ppermute | solution.py:244
  14.3 1.1 collective-permute-start.9
  16.1 0.7 concatenate.3.links_own
  16.8 0.1 pad_add_fusion.place
  16.9 1.1 collective-permute-done.links_sib
  17.9 1.4 copy-done
  19.3 0.9 copy-done.3
  20.2 0.9 copy-done.5
  21.1 0.7 copy-done.9
  21.8 1.6 shard_map.120
  23.5 0.0 copy-start.2
  23.5 0.1 collective-permute-start.5
  23.6 3.0 %collective-permute-start.7 = (bf16[128,512]{1,0:T(8,128)(2,1)S(1)}, bf16[128,512]{1,0:T(8,128)(2,1)S(1)}, u32[]{:S(2)}, u32[]{:S(2)}) collective-permute-start(bf16[128,512]{1,0:T(8,128)(2,1)S(1)} %collective-permute-done.4.refs_3_.refs_4_), channel_id=1, source_target_pairs={{0,224},{32,0},{64,32},{96,64},{128,96},{160,128},{192,160},{224,1... | collective-permute-start | bytes 393224 | tf_op jit(solution)/shard_map/ppermute | solution.py:244
  26.6 0.5 collective-permute-start.11
  27.1 0.0 collective-permute-start.10
  27.1 3.2 %collective-permute-done.5.refs_0_.refs_5_ = bf16[128,512]{1,0:T(8,128)(2,1)S(1)} collective-permute-done((bf16[128,512]{1,0:T(8,128)(2,1)S(1)}, bf16[128,512]{1,0:T(8,128)(2,1)S(1)}, u32[]{:S(2)}, u32[]{:S(2)}) %collective-permute-start.5) | collective-permute-done | bytes 131104 | tf_op jit(solution)/shard_map/ppermute | solution.py:244
  30.3 0.7 collective-permute-start.13
  31.0 0.1 collective-permute-start.6
  31.1 2.8 %collective-permute-start.8 = (bf16[64,512]{1,0:T(8,128)(2,1)S(1)}, bf16[64,512]{1,0:T(8,128)(2,1)S(1)}, u32[]{:S(2)}, u32[]{:S(2)}) collective-permute-start(bf16[64,512]{1,0:T(8,128)(2,1)S(1)} %slice.21), channel_id=1, source_target_pairs={{0,224},{32,0},{64,32},{96,64},{128,96},{160,128},{192,160},{224,1... | collective-permute-start | bytes 196616 | tf_op jit(solution)/shard_map/ppermute | solution.py:244
  33.9 0.9 collective-permute-start.14
  34.8 0.3 collective-permute-start.15
  35.1 1.3 shard_map.121.proj
  36.5 0.6 collective-permute-start.16
  37.0 0.0 collective-permute-start.17
  37.1 0.9 collective-permute-done.16.refs_6_.refs_16_
  37.9 0.4 collective-permute-done.17.refs_7_.refs_17_
  38.3 3.3 %shard_map.122 = bf16[16,544,128]{2,1,0:T(8,128)(2,1)S(1)} custom-call(s32[4]{0:T(128)S(1)} %pad_add_fusion.place, s32[256]{0:T(256)S(1)} %copy-done.9, s32[80]{0:T(128)S(1)} %get-tuple-element.24.lists, s32[2]{0:T(128)S(1)} %get-tuple-element.25.counts, bf16[128,512]{1,0:T(8,128)(2,1)S(1)} %get-tuple-element.27.proj_own, ...), custom_call_target="tpu_custom_call" | custom-call | flops 536870912 | bytes 8388608 | tf_op jit(solution)/shard_map/pallas_call | solution.py:288
  41.7 36.3 %all_to_all.30.parts = bf16[16,544,128]{2,1,0:T(8,128)(2,1)S(1)} all-to-all(bf16[16,544,128]{2,1,0:T(8,128)(2,1)S(1)} %shard_map.122), channel_id=1, replica_groups={{0,2,4,6,8,10,12,14,16,18,20,22,24,26,28,30},{1,3,5,7,9,11,13,15,17,19,..., dimensions={0} | all-to-all | bytes 4456448 | tf_op jit(solution)/shard_map/all_to_all | solution.py:247
  78.0 1.2 shard_map.123
  79.2 30.0 %all_to_all.31.grads = bf16[16,512,128]{2,1,0:T(8,128)(2,1)S(1)} all-to-all(bf16[16,512,128]{2,1,0:T(8,128)(2,1)S(1)} %get-tuple-element.35), channel_id=1, replica_groups={{0,2,4,6,8,10,12,14,16,18,20,22,24,26,28,30},{1,3,5,7,9,11,13,15,17,19,..., dimensions={0} | all-to-all | bytes 4194304 | tf_op jit(solution)/shard_map/all_to_all | solution.py:247
  109.2 3.6 %shard_map.124 = (f32[8,528,128]{2,1,0:T(8,128)S(1)}, bf16[8,528,128]{2,1,0:T(8,128)(2,1)S(1)}) custom-call(s32[4]{0:T(128)S(1)} %pad_add_fusion.place, s32[80]{0:T(128)S(1)} %get-tuple-element.24.lists, s32[2]{0:T(128)S(1)} %get-tuple-element.25.counts, bf16[16,512,128]{2,1,0:T(8,128)(2,1)S(1)} %all_to_all.31.grads, ...), custom_call_target="tpu_custom_call" | custom-call | flops 536870912 | bytes 9437184 | tf_op jit(solution)/shard_map/pallas_call | solution.py:311
  112.8 1.8 collective-permute-start.19
  114.6 2.3 %collective-permute-done.19 = bf16[8,528,128]{2,1,0:T(8,128)(2,1)S(1)} collective-permute-done((bf16[8,528,128]{2,1,0:T(8,128)(2,1)S(1)}, bf16[8,528,128]{2,1,0:T(8,128)(2,1)S(1)}, u32[]{:S(2)}, u32[]{:S(2)}) %collective-permute-start.19) | collective-permute-done | bytes 1081376 | tf_op jit(solution)/shard_map/ppermute | solution.py:241
  117.0 0.2 add_convert_fusion
  117.2 34.1 %all_to_all.32.parts = bf16[8,528,128]{2,1,0:T(8,128)(2,1)S(1)} all-to-all(bf16[8,528,128]{2,1,0:T(8,128)(2,1)S(1)} %add_convert_fusion), channel_id=1, replica_groups=mesh['fact'=8,'dim'=32] {'fact'}, dimensions={0} | all-to-all | bytes 2162688 | tf_op jit(solution)/shard_map/all_to_all | solution.py:250
  151.3 1.2 shard_map.125
  152.5 9.5 %all_to_all.33.parts = bf16[16,24,128]{2,1,0:T(8,128)(2,1)S(1)} all-to-all(bf16[16,24,128]{2,1,0:T(8,128)(2,1)S(1)} %bitcast.8), channel_id=1, replica_groups={{0,2,4,6,8,10,12,14,16,18,20,22,24,26,28,30},{1,3,5,7,9,11,13,15,17,19,..., dimensions={0} | all-to-all | bytes 196608 | tf_op jit(solution)/shard_map/all_to_all | solution.py:247
  162.0 0.6 shard_map.126
  162.6 11.0 %all_to_all.34 = bf16[8,96,128]{2,1,0:T(8,128)(2,1)S(1)} all-to-all(bf16[8,96,128]{2,1,0:T(8,128)(2,1)S(1)} %shard_map.126), channel_id=1, replica_groups=mesh['fact'=8,'dim'=32] {'fact'}, dimensions={0} | all-to-all | bytes 393216 | tf_op jit(solution)/shard_map/all_to_all | solution.py:250
  173.7 0.2 broadcast_in_dim.5
  173.9 16.5 %all_to_all.35.own = bf16[16,8,32,128]{3,2,1,0:T(8,128)(2,1)S(1)} all-to-all(bf16[16,8,32,128]{3,2,1,0:T(8,128)(2,1)S(1)} %broadcast_in_dim.5), channel_id=1, replica_groups={{0,2,4,6,8,10,12,14,16,18,20,22,24,26,28,30},{1,3,5,7,9,11,13,15,17,19,..., dimensions={0} | all-to-all | bytes 2097152 | tf_op jit(solution)/shard_map/all_to_all | solution.py:247
  190.4 4.8 %collective-permute-start.21 = (bf16[16,8,32,128]{3,2,1,0:T(8,128)(2,1)S(1)}, bf16[16,8,32,128]{3,2,1,0:T(8,128)(2,1)S(1)}, u32[]{:S(2)}, u32[]{:S(2)}) collective-permute-start(bf16[16,8,32,128]{3,2,1,0:T(8,128)(2,1)S(1)} %all_to_all.35.own), channel_id=1, source_target_pairs={{0,1},{1,0},{2,3},{3,2},{4,5},{5,4},{6,7},{7,6},{8,9},{9,8},{10,11... | collective-permute-start | bytes 3145736 | tf_op jit(solution)/shard_map/ppermute | solution.py:241
  195.2 2.4 %collective-permute-done.20.given = bf16[8,32,128]{2,1,0:T(8,128)(2,1)S(1)} collective-permute-done((bf16[8,32,128]{2,1,0:T(8,128)(2,1)S(1)}, bf16[8,32,128]{2,1,0:T(8,128)(2,1)S(1)}, u32[]{:S(2)}, u32[]{:S(2)}) %collective-permute-start.20) | collective-permute-done | bytes 65568 | tf_op jit(solution)/shard_map/ppermute | solution.py:241
  197.6 1.6 shard_map.127
  199.2 3.5 %shard_map.128 = (f32[512,512]{1,0:T(8,128)}, f32[3,512,512]{2,1,0:T(8,128)}) custom-call(s32[4]{0:T(128)S(1)} %pad_add_fusion.place, bf16[16,8,32,128]{3,2,1,0:T(8,128)(2,1)S(1)} %all_to_all.35.own, bf16[16,8,32,128]{3,2,1,0:T(8,128)(2,1)S(1)} %collective-permute-done.21.sib), custom_call_target="tpu_custom_call" | custom-call | bytes 8388608 | tf_op jit(solution)/shard_map/pallas_call | solution.py:348
  (40 shorter events, 0.1 us)
Async XLA Ops:
  0.6 37.7 %collective-permute-start.18 = (bf16[32,128,128]{2,1,0:T(8,128)(2,1)}, bf16[32,128,128]{2,1,0:T(8,128)(2,1)S(1)}, u32[]{:S(2)}, u32[]{:S(2)}) collective-permute-start(bf16[32,128,128]{2,1,0:T(8,128)(2,1)} %tiles_own.1), channel_id=1, source_target_pairs={{0,1},{1,0},{2,3},{3,2},{4,5},{5,4},{6,7},{7,6},{8,9},{9,8},{10,11... | collective-permute-start | bytes 3145736 | tf_op jit(solution)/shard_map/ppermute | solution.py:241
  4.0 7.0 %collective-permute-start.3 = (bf16[128,512]{1,0:T(8,128)(2,1)}, bf16[128,512]{1,0:T(8,128)(2,1)S(1)}, u32[]{:S(2)}, u32[]{:S(2)}) collective-permute-start(bf16[128,512]{1,0:T(8,128)(2,1)} %refs_0_.1), channel_id=1, source_target_pairs={{0,224},{32,0},{64,32},{96,64},{128,96},{160,128},{192,160},{224,1... | collective-permute-start | bytes 393224 | tf_op jit(solution)/shard_map/ppermute | solution.py:244
  7.8 6.5 %collective-permute-start.1 = (bf16[128,512]{1,0:T(8,128)(2,1)}, bf16[128,512]{1,0:T(8,128)(2,1)S(1)}, u32[]{:S(2)}, u32[]{:S(2)}) collective-permute-start(bf16[128,512]{1,0:T(8,128)(2,1)} %refs_0_.1), channel_id=1, source_target_pairs={{0,32},{32,64},{64,96},{96,128},{128,160},{160,192},{192,224},{224... | collective-permute-start | bytes 393224 | tf_op jit(solution)/shard_map/ppermute | solution.py:244
  11.0 12.5 %collective-permute-start.4 = (bf16[128,512]{1,0:T(8,128)(2,1)S(1)}, bf16[128,512]{1,0:T(8,128)(2,1)S(1)}, u32[]{:S(2)}, u32[]{:S(2)}) collective-permute-start(bf16[128,512]{1,0:T(8,128)(2,1)S(1)} %collective-permute-done.3.refs_1_.refs_2_), channel_id=1, source_target_pairs={{0,224},{32,0},{64,32},{96,64},{128,96},{160,128},{192,160},{224,1... | collective-permute-start | bytes 393224 | tf_op jit(solution)/shard_map/ppermute | solution.py:244
  14.3 9.2 %collective-permute-start.2 = (bf16[128,512]{1,0:T(8,128)(2,1)S(1)}, bf16[128,512]{1,0:T(8,128)(2,1)S(1)}, u32[]{:S(2)}, u32[]{:S(2)}) collective-permute-start(bf16[128,512]{1,0:T(8,128)(2,1)S(1)} %collective-permute-done.1.refs_0_.refs_1_), channel_id=1, source_target_pairs={{0,32},{32,64},{64,96},{96,128},{128,160},{160,192},{192,224},{224... | collective-permute-start | bytes 393224 | tf_op jit(solution)/shard_map/ppermute | solution.py:244
  14.3 12.8 %collective-permute-start.9 = (bf16[128,512]{1,0:T(8,128)(2,1)}, bf16[128,512]{1,0:T(8,128)(2,1)S(1)}, u32[]{:S(2)}, u32[]{:S(2)}) collective-permute-start(bf16[128,512]{1,0:T(8,128)(2,1)} %refs_0_.1), channel_id=1, source_target_pairs={{0,1},{1,0},{2,3},{3,2},{4,5},{5,4},{6,7},{7,6},{8,9},{9,8},{10,11... | collective-permute-start | bytes 393224 | tf_op jit(solution)/shard_map/ppermute | solution.py:241
  16.8 1.1 collective-permute-start
  17.9 1.4 copy-start
  19.3 0.9 copy-start.3
  20.2 0.9 copy-start.5
  21.1 0.7 copy-start.9
  21.8 13.3 %copy-start.1 = (bf16[3,512,512]{2,1,0:T(8,128)(2,1)S(1)}, bf16[3,512,512]{2,1,0:T(8,128)(2,1)}, u32[]{:S(2)}) copy-start(bf16[3,512,512]{2,1,0:T(8,128)(2,1)} %w.7) | copy-start | bytes 4718596
  23.5 14.9 %copy-start.2 = (bf16[32,128,128]{2,1,0:T(8,128)(2,1)S(1)}, bf16[32,128,128]{2,1,0:T(8,128)(2,1)}, u32[]{:S(2)}) copy-start(bf16[32,128,128]{2,1,0:T(8,128)(2,1)} %tiles_own.1) | copy-start | bytes 3145732
  23.5 6.8 %collective-permute-start.5 = (bf16[128,512]{1,0:T(8,128)(2,1)S(1)}, bf16[128,512]{1,0:T(8,128)(2,1)S(1)}, u32[]{:S(2)}, u32[]{:S(2)}) collective-permute-start(bf16[128,512]{1,0:T(8,128)(2,1)S(1)} %collective-permute-done.2.refs_2_.refs_3_), channel_id=1, source_target_pairs={{0,32},{32,64},{64,96},{96,128},{128,160},{160,192},{192,224},{224... | collective-permute-start | bytes 393224 | tf_op jit(solution)/shard_map/ppermute | solution.py:244
  23.6 7.4 %collective-permute-start.7 = (bf16[128,512]{1,0:T(8,128)(2,1)S(1)}, bf16[128,512]{1,0:T(8,128)(2,1)S(1)}, u32[]{:S(2)}, u32[]{:S(2)}) collective-permute-start(bf16[128,512]{1,0:T(8,128)(2,1)S(1)} %collective-permute-done.4.refs_3_.refs_4_), channel_id=1, source_target_pairs={{0,224},{32,0},{64,32},{96,64},{128,96},{160,128},{192,160},{224,1... | collective-permute-start | bytes 393224 | tf_op jit(solution)/shard_map/ppermute | solution.py:244
  26.6 4.4 %collective-permute-start.11 = (bf16[128,512]{1,0:T(8,128)(2,1)S(1)}, bf16[128,512]{1,0:T(8,128)(2,1)S(1)}, u32[]{:S(2)}, u32[]{:S(2)}) collective-permute-start(bf16[128,512]{1,0:T(8,128)(2,1)S(1)} %collective-permute-done.3.refs_1_.refs_2_), channel_id=1, source_target_pairs={{0,1},{1,0},{2,3},{3,2},{4,5},{5,4},{6,7},{7,6},{8,9},{9,8},{10,11... | collective-permute-start | bytes 393224 | tf_op jit(solution)/shard_map/ppermute | solution.py:241
  27.1 4.0 %collective-permute-start.10 = (bf16[128,512]{1,0:T(8,128)(2,1)S(1)}, bf16[128,512]{1,0:T(8,128)(2,1)S(1)}, u32[]{:S(2)}, u32[]{:S(2)}) collective-permute-start(bf16[128,512]{1,0:T(8,128)(2,1)S(1)} %collective-permute-done.1.refs_0_.refs_1_), channel_id=1, source_target_pairs={{0,1},{1,0},{2,3},{3,2},{4,5},{5,4},{6,7},{7,6},{8,9},{9,8},{10,11... | collective-permute-start | bytes 393224 | tf_op jit(solution)/shard_map/ppermute | solution.py:241
  30.3 3.6 %collective-permute-start.13 = (bf16[128,512]{1,0:T(8,128)(2,1)S(1)}, bf16[128,512]{1,0:T(8,128)(2,1)S(1)}, u32[]{:S(2)}, u32[]{:S(2)}) collective-permute-start(bf16[128,512]{1,0:T(8,128)(2,1)S(1)} %collective-permute-done.4.refs_3_.refs_4_), channel_id=1, source_target_pairs={{0,1},{1,0},{2,3},{3,2},{4,5},{5,4},{6,7},{7,6},{8,9},{9,8},{10,11... | collective-permute-start | bytes 393224 | tf_op jit(solution)/shard_map/ppermute | solution.py:241
  31.0 3.9 %collective-permute-start.12 = (bf16[128,512]{1,0:T(8,128)(2,1)S(1)}, bf16[128,512]{1,0:T(8,128)(2,1)S(1)}, u32[]{:S(2)}, u32[]{:S(2)}) collective-permute-start(bf16[128,512]{1,0:T(8,128)(2,1)S(1)} %collective-permute-done.2.refs_2_.refs_3_), channel_id=1, source_target_pairs={{0,1},{1,0},{2,3},{3,2},{4,5},{5,4},{6,7},{7,6},{8,9},{9,8},{10,11... | collective-permute-start | bytes 393224 | tf_op jit(solution)/shard_map/ppermute | solution.py:241
  31.0 5.4 %collective-permute-start.6 = (bf16[64,512]{1,0:T(8,128)(2,1)S(1)}, bf16[64,512]{1,0:T(8,128)(2,1)S(1)}, u32[]{:S(2)}, u32[]{:S(2)}) collective-permute-start(bf16[64,512]{1,0:T(8,128)(2,1)S(1)} %slice.20), channel_id=1, source_target_pairs={{0,32},{32,64},{64,96},{96,128},{128,160},{160,192},{192,224},{224... | collective-permute-start | bytes 196616 | tf_op jit(solution)/shard_map/ppermute | solution.py:244
  31.1 5.4 %collective-permute-start.8 = (bf16[64,512]{1,0:T(8,128)(2,1)S(1)}, bf16[64,512]{1,0:T(8,128)(2,1)S(1)}, u32[]{:S(2)}, u32[]{:S(2)}) collective-permute-start(bf16[64,512]{1,0:T(8,128)(2,1)S(1)} %slice.21), channel_id=1, source_target_pairs={{0,224},{32,0},{64,32},{96,64},{128,96},{160,128},{192,160},{224,1... | collective-permute-start | bytes 196616 | tf_op jit(solution)/shard_map/ppermute | solution.py:244
  33.9 4.4 %collective-permute-start.14 = (bf16[128,512]{1,0:T(8,128)(2,1)S(1)}, bf16[128,512]{1,0:T(8,128)(2,1)S(1)}, u32[]{:S(2)}, u32[]{:S(2)}) collective-permute-start(bf16[128,512]{1,0:T(8,128)(2,1)S(1)} %collective-permute-done.5.refs_0_.refs_5_), channel_id=1, source_target_pairs={{0,1},{1,0},{2,3},{3,2},{4,5},{5,4},{6,7},{7,6},{8,9},{9,8},{10,11... | collective-permute-start | bytes 393224 | tf_op jit(solution)/shard_map/ppermute | solution.py:241
  34.8 3.5 %collective-permute-start.15 = (bf16[128,512]{1,0:T(8,128)(2,1)S(1)}, bf16[128,512]{1,0:T(8,128)(2,1)S(1)}, u32[]{:S(2)}, u32[]{:S(2)}) collective-permute-start(bf16[128,512]{1,0:T(8,128)(2,1)S(1)} %collective-permute-done.7.refs_1_.refs_6_), channel_id=1, source_target_pairs={{0,1},{1,0},{2,3},{3,2},{4,5},{5,4},{6,7},{7,6},{8,9},{9,8},{10,11... | collective-permute-start | bytes 393224 | tf_op jit(solution)/shard_map/ppermute | solution.py:241
  36.5 1.5 collective-permute-start.16
  37.0 1.3 collective-permute-start.17
  41.7 36.4 %copy-start.4 = (bf16[128,512]{1,0:T(8,128)(2,1)S(1)}, bf16[128,512]{1,0:T(8,128)(2,1)}, u32[]{:S(2)}) copy-start(bf16[128,512]{1,0:T(8,128)(2,1)} %facts.3) | copy-start | bytes 393220
  41.7 36.3 %copy-start.7 = (bf16[512,512]{1,0:T(8,128)(2,1)S(1)}, bf16[512,512]{1,0:T(8,128)(2,1)}, u32[]{:S(2)}) copy-start(bf16[512,512]{1,0:T(8,128)(2,1)} %w.6) | copy-start | bytes 1572868
  41.7 36.3 %copy-start.8 = (bf16[128,512]{1,0:T(8,128)(2,1)S(1)}, bf16[128,512]{1,0:T(8,128)(2,1)}, u32[]{:S(2)}) copy-start(bf16[128,512]{1,0:T(8,128)(2,1)} %cot.1) | copy-start | bytes 393220
  112.8 4.1 %collective-permute-start.19 = (bf16[8,528,128]{2,1,0:T(8,128)(2,1)S(1)}, bf16[8,528,128]{2,1,0:T(8,128)(2,1)S(1)}, u32[]{:S(2)}, u32[]{:S(2)}) collective-permute-start(bf16[8,528,128]{2,1,0:T(8,128)(2,1)S(1)} %get-tuple-element.38), channel_id=1, source_target_pairs={{0,1},{1,0},{2,3},{3,2},{4,5},{5,4},{6,7},{7,6},{8,9},{9,8},{10,11... | collective-permute-start | bytes 3244040 | tf_op jit(solution)/shard_map/ppermute | solution.py:241
  117.2 34.2 %copy-start.6 = (bf16[128,512]{1,0:T(8,128)(2,1)S(1)}, bf16[128,512]{1,0:T(8,128)(2,1)}, u32[]{:S(2)}) copy-start(bf16[128,512]{1,0:T(8,128)(2,1)} %refs_0_.1) | copy-start | bytes 393220
  117.2 34.1 %copy-start.10 = (s32[256]{0:T(256)S(1)}, s32[256]{0:T(256)}, u32[]{:S(2)}) copy-start(s32[256]{0:T(256)} %table.9) | copy-start | bytes 3076
  190.4 8.8 %collective-permute-start.21 = (bf16[16,8,32,128]{3,2,1,0:T(8,128)(2,1)S(1)}, bf16[16,8,32,128]{3,2,1,0:T(8,128)(2,1)S(1)}, u32[]{:S(2)}, u32[]{:S(2)}) collective-permute-start(bf16[16,8,32,128]{3,2,1,0:T(8,128)(2,1)S(1)} %all_to_all.35.own), channel_id=1, source_target_pairs={{0,1},{1,0},{2,3},{3,2},{4,5},{5,4},{6,7},{7,6},{8,9},{9,8},{10,11... | collective-permute-start | bytes 3145736 | tf_op jit(solution)/shard_map/ppermute | solution.py:241
  195.2 2.4 %collective-permute-start.20 = (bf16[8,32,128]{2,1,0:T(8,128)(2,1)S(1)}, bf16[8,32,128]{2,1,0:T(8,128)(2,1)S(1)}, u32[]{:S(2)}, u32[]{:S(2)}) collective-permute-start(bf16[8,32,128]{2,1,0:T(8,128)(2,1)S(1)} %get-tuple-element.45), channel_id=1, source_target_pairs={{0,1},{1,0},{2,3},{3,2},{4,5},{5,4},{6,7},{7,6},{8,9},{9,8},{10,11... | collective-permute-start | bytes 196616 | tf_op jit(solution)/shard_map/ppermute | solution.py:241

commit v5 on v4

--- a/solution.py
+++ b/solution.py
@@ -16,6 +16,7 @@
 ORDER = (0, -1, 1, -2, 2, -3, 3)
 EARLY = 5
 LIST = 40
+COUNT, KIND, PLACE, INFO = 80, 96, 112, 128
 
 
 def call(kernel, out_shape, in_specs, scratch=(), flops=0, moved=0, out_specs=None):
@@ -34,49 +35,46 @@
     return code & 31, (code >> 5) & 7, code >> 8
 
 
-def column_kind(place, table, side, h):
-    dim_pos = place[1]
-    return table[h * 32 + (dim_pos if side == 0 else dim_pos + 1 - 2 * place[2])]
-
-
-def prepare_kernel(place, table, links_own, links_sib, facts, dims, w, lists, counts, facts_t, proj):
-    fact_pos, core = place[0], place[2]
+def prepare_kernel(place, links_own, links_sib, table, info):
+    fact_pos, dim_pos, core = place[0], place[1], place[2]
     for side, links in enumerate((links_own, links_sib)):
         n = jnp.int32(0)
         for slot in range(32):
             target = links[0, slot] - fact_pos * 32
-            lists[side * LIST + n] = slot + ((links[1, slot] >> 5) << 5) + ((target >> 1) << 8)
+            info[side * LIST + n] = slot + ((links[1, slot] >> 5) << 5) + ((target >> 1) << 8)
             n = n + jnp.where((slot < links[0, 32]) & ((target & 1) == core), 1, 0)
         for spare in range(UNROLL - 1):
-            lists[side * LIST + n + spare] = 16 << 8
-        counts[side] = n
-    kind = column_kind(place, table, 0, fact_pos)
-    proj[...] = jnp.dot(dims[...], w[kind], preferred_element_type=F32).astype(BF16)
-    facts_t[...] = facts[...].astype(F32).T.astype(BF16)
-
-
-def project_kernel(place, table, w, *refs):
-    early, proj = refs[:-1], refs[-1]
+            info[side * LIST + n + spare] = 16 << 8
+        info[COUNT + side] = n
+    for i in range(4):
+        info[PLACE + i] = place[i]
+    for h in range(8):
+        info[KIND + h] = table[h * 32 + dim_pos]
+        info[KIND + 8 + h] = table[h * 32 + dim_pos + 1 - 2 * core]
+
+
+def project_kernel(info, w, facts, *refs):
+    early, (proj, facts_t) = refs[:-2], refs[-2:]
     at = 0
     for side in range(2):
-        for shift in ORDER[1 - side : EARLY]:
-            kind = column_kind(place, table, side, (place[0] + shift) & 7)
+        for shift in ORDER[:EARLY]:
+            kind = info[KIND + side * 8 + ((info[PLACE] + shift) & 7)]
             proj[at] = jnp.dot(early[at][...], w[kind], preferred_element_type=F32).astype(BF16)
             at += 1
-
-
-def forward_kernel(place, table, lists, counts, proj_own, proj, *refs):
+    facts_t[...] = facts[...].astype(F32).T.astype(BF16)
+
+
+def forward_kernel(info, proj, *refs):
     late = 9 - EARLY
     sides, (w, facts_t, tiles_own, tiles_sib, out, panel, acc) = (refs[:late], refs[late : 2 * late]), refs[2 * late :]
-    fact_pos = place[0]
+    fact_pos = info[PLACE]
     for side, pieces in enumerate(sides):
         for at, shift in enumerate(ORDER[:EARLY]):
-            value = proj_own[...] if side + at == 0 else proj[side * EARLY + at - 1]
-            panel[side * 8 + ((fact_pos + shift) & 7)] = value
+            panel[side * 8 + ((fact_pos + shift) & 7)] = proj[side * EARLY + at]
         blocks = [x[...] for x in pieces[:-2]] + [jnp.concatenate([pieces[-2][...], pieces[-1][...]], axis=0)]
         for shift, rows in zip(ORDER[EARLY:] + (4,), blocks):
             h = (fact_pos + shift) & 7
-            value = jnp.dot(rows, w[column_kind(place, table, side, h)], preferred_element_type=F32)
+            value = jnp.dot(rows, w[info[KIND + side * 8 + h]], preferred_element_type=F32)
             panel[side * 8 + h] = value.astype(BF16)
     acc[...] = jnp.zeros_like(acc)
     for side, tiles in enumerate((tiles_own, tiles_sib)):
@@ -84,13 +82,13 @@
         def step(i, carry, side=side, tiles=tiles):
             found = []
             for u in range(UNROLL):
-                slot, holder, chip = decode(lists[side * LIST + i * UNROLL + u])
+                slot, holder, chip = decode(info[side * LIST + i * UNROLL + u])
                 found.append((chip, jnp.dot(tiles[slot], panel[side * 8 + holder], preferred_element_type=F32)))
             for chip, value in found:
                 acc[chip] += value
             return carry
 
-        lax.fori_loop(0, (counts[side] + UNROLL - 1) // UNROLL, step, 0)
+        lax.fori_loop(0, (info[COUNT + side] + UNROLL - 1) // UNROLL, step, 0)
     for chip in range(out.shape[0]):
         for q in range(4):
             out[chip, q * 128 : (q + 1) * 128, :] = acc[chip, :, q * 128 : (q + 1) * 128].astype(BF16)
@@ -115,8 +113,8 @@
         facts_t[chip] = parts[chip, 512:544, :]
 
 
-def backward_kernel(place, lists, counts, grads, facts_t, tiles_own, tiles_sib, keep, give, acc, weight):
-    core = place[2]
+def backward_kernel(info, grads, facts_t, tiles_own, tiles_sib, keep, give, acc, weight):
+    fact_pos, core = info[PLACE], info[PLACE + 2]
     acc[...] = jnp.zeros_like(acc)
     for side, tiles in enumerate((tiles_own, tiles_sib)):
         base = 8 * (core if side == 0 else 1 - core)
@@ -124,7 +122,7 @@
         def step(i, carry, side=side, tiles=tiles, base=base):
             found = []
             for u in range(UNROLL):
-                slot, holder, chip = decode(lists[side * LIST + i * UNROLL + u])
+                slot, holder, chip = decode(info[side * LIST + i * UNROLL + u])
                 at = jnp.where(chip == 16, 16, base + holder)
                 value = jnp.dot(grads[jnp.minimum(chip, 15)], tiles[slot], preferred_element_type=F32)
                 found.append((at, value))
@@ -132,30 +130,31 @@
                 acc[at] += value
             return carry
 
-        lax.fori_loop(0, (counts[side] + UNROLL - 1) // UNROLL, step, 0)
-    half = weight.shape[0] // 2
-    total = jnp.zeros(weight.shape, F32)
+        lax.fori_loop(0, (info[COUNT + side] + UNROLL - 1) // UNROLL, step, 0)
+    piece, width = facts_t.shape[1], grads.shape[1]
+    half = piece // 2
+    total = jnp.zeros((piece, width), F32)
     for chip in range(grads.shape[0]):
         total = total + lax.dot_general(
             facts_t[chip], grads[chip], (((1,), (1,)), ((), ())), preferred_element_type=F32
         )
-    weight[...] = total
+    for q in range(4):
+        weight[q] = total[:, q * 128 : (q + 1) * 128]
     for out, who, kind in ((keep, core, F32), (give, 1 - core, BF16)):
-        for z in range(8):
+        for k in range(8):
+            z = (fact_pos + k) & 7
             features = pl.ds(pl.multiple_of(who * 256 + z * 32, 32), 32)
             for at in range(16):
-                out[z, at * 32 : (at + 1) * 32, :] = acc[at, features, :].astype(kind)
-            rows = pl.ds(pl.multiple_of(who * half + (z % 2) * 8, 8), 8)
-            mine = weight[rows, (z // 2) * 128 : (z // 2 + 1) * 128]
-            out[z, 512:528, :] = jnp.concatenate([mine, jnp.zeros_like(mine)], axis=0).astype(kind)
-
-
-def slice_kernel(place, table, parts, *refs):
+                out[k, at * 32 : (at + 1) * 32, :] = acc[at, features, :].astype(kind)
+            rows = pl.ds(pl.multiple_of(who * half + (z & 1) * 8, 8), 8)
+            mine = weight[z >> 1, rows, :]
+            out[k, 512:528, :] = jnp.concatenate([mine, jnp.zeros_like(mine)], axis=0).astype(kind)
+
+
+def slice_kernel(info, kept, given, from_below, from_above, *refs):
     pieces, (tab, gsum, self_piece, tacc) = refs[:18], refs[18:]
-    fact_pos, core = place[0], place[2]
-    total = parts[0].astype(F32)
-    for z in range(1, parts.shape[0]):
-        total = total + parts[z].astype(F32)
+    fact_pos, core = info[PLACE], info[PLACE + 2]
+    total = kept[...] + given[...].astype(F32) + from_below[...].astype(F32) + from_above[...].astype(F32)
     self_piece[...] = total[512:520]
     for at in range(16):
         gsum[at] = total[at * 32 : (at + 1) * 32].astype(BF16)
@@ -164,7 +163,7 @@
         column = 8 * (core if side == 0 else 1 - core)
         for at, shift in enumerate(ORDER + (4,)):
             h = (fact_pos + shift) & 7
-            kind = column_kind(place, table, side, h)
+            kind = info[KIND + side * 8 + h]
             grad = gsum[column + h]
             if shift == 4:
                 low, high = pieces[side * 9 + 7], pieces[side * 9 + 8]
@@ -178,8 +177,8 @@
             tab[at : at + 32, :] = tacc[t, :, q * 128 : (q + 1) * 128].astype(BF16)
 
 
-def pack_kernel(place, parts, gsum, self_piece, out):
-    core = place[2]
+def pack_kernel(info, parts, gsum, self_piece, out):
+    core = info[PLACE + 2]
     total = jnp.sum(parts[...].astype(F32), axis=0)
     piece = jnp.concatenate([total, self_piece[...]], axis=0).astype(BF16)
     for z in range(out.shape[0]):
@@ -188,9 +187,9 @@
         out[z, 64:96, :] = piece
 
 
-def rows_kernel(place, table, kept, given, w, grad_dims):
-    even = place[2] == 0
-    kind = table[place[0] * 32 + place[1]]
+def rows_kernel(info, kept, given, w, grad_dims):
+    even = info[PLACE + 2] == 0
+    kind = info[KIND + info[PLACE]]
     mine, other = kept[...].astype(F32).reshape(256, 128), given[...].astype(F32).reshape(256, 128)
     turned = jnp.concatenate([jnp.where(even, mine, other), jnp.where(even, other, mine)], axis=0)
     grad_dims[...] = lax.dot_general(
@@ -198,8 +197,8 @@
     )
 
 
-def final_kernel(place, own, sib, grad_self, grad_tab):
-    even = place[2] == 0
+def final_kernel(info, own, sib, grad_self, grad_tab):
+    even = info[PLACE + 2] == 0
     scale = F32(32768.0**-0.5)
     for q in range(4):
         for group in range(2):
@@ -252,47 +251,42 @@
     count = jnp.broadcast_to(link_count[None, :], (2, 1))
     links_own = jnp.concatenate([links.T, count], axis=1)
     links_sib = swap(links_own)
-    lists, counts, facts_t, proj_own = call(
+    info = call(
         prepare_kernel,
-        (
-            jax.ShapeDtypeStruct((2 * LIST,), jnp.int32),
-            jax.ShapeDtypeStruct((2,), jnp.int32),
-            jax.ShapeDtypeStruct((width, block), BF16),
-            jax.ShapeDtypeStruct((rows, width), BF16),
-        ),
-        [SMEM] * 4 + [VMEM] * 3,
-        flops=2 * rows * width * width,
-        moved=3 << 20,
-        out_specs=(SMEM, SMEM, VMEM, VMEM),
-    )(place, block_table, links_own, links_sib, facts, dims, w_tables)
+        jax.ShapeDtypeStruct((INFO,), jnp.int32),
+        [SMEM] * 4,
+        flops=1 << 31,
+        moved=4096,
+        out_specs=SMEM,
+    )(place, links_own, links_sib, block_table)
     tiles_sib = swap(tiles)
 
     pieces, up, down = [dims], dims, dims
     for step in range(3):
         if step == 2:
-            up, down, proj_own = lax.optimization_barrier((up, down, proj_own))
+            up, down, info = lax.optimization_barrier((up, down, info))
         up, down = shift(up, 1), shift(down, -1)
         pieces += [up, down]
     pieces_sib = [swap(x) for x in pieces]
     far = [shift(up[: rows // 2], 1), shift(down[rows // 2 :], -1)]
-    early = pieces[1:EARLY] + pieces_sib[:EARLY]
-    proj = call(
+    early = pieces[:EARLY] + pieces_sib[:EARLY]
+    proj, facts_t = call(
         project_kernel,
-        jax.ShapeDtypeStruct((len(early), rows, width), BF16),
-        [SMEM] * 2 + [VMEM] * (1 + len(early)),
+        (jax.ShapeDtypeStruct((len(early), rows, width), BF16), jax.ShapeDtypeStruct((width, block), BF16)),
+        [SMEM] + [VMEM] * (2 + len(early)),
         flops=2 * len(early) * rows * width * width,
         moved=4 << 20,
-    )(place, block_table, w_tables, *early)
+    )(info, w_tables, facts, *early)
     *far, proj = lax.optimization_barrier((*far, proj))
     pieces, pieces_sib = pieces + far, pieces_sib + [swap(x) for x in far]
     partial = call(
         forward_kernel,
         jax.ShapeDtypeStruct((chips, 544, 128), BF16),
-        [SMEM] * 4 + [VMEM] * (6 + 2 * (9 - EARLY)),
+        [SMEM] + [VMEM] * (5 + 2 * (9 - EARLY)),
         [pltpu.VMEM((2 * n_fact, rows, width), BF16), pltpu.VMEM((chips + 1, block, width), F32)],
         flops=2 * slots * block * block * width,
         moved=8 << 20,
-    )(place, block_table, lists, counts, proj_own, proj, *pieces[EARLY:], *pieces_sib[EARLY:], w_tables, facts_t, tiles, tiles_sib)
+    )(info, proj, *pieces[EARLY:], *pieces_sib[EARLY:], w_tables, facts_t, tiles, tiles_sib)
     parts = by_chip(partial)
 
     fact_out, spread, facts_t = call(
@@ -311,12 +305,21 @@
     keep, give = call(
         backward_kernel,
         (jax.ShapeDtypeStruct((n_fact, 528, 128), F32), jax.ShapeDtypeStruct((n_fact, 528, 128), BF16)),
-        [SMEM] * 3 + [VMEM] * 4,
-        [pltpu.VMEM((2 * n_fact + 1, width, block), F32), pltpu.VMEM((width // chips, width), F32)],
+        [SMEM] + [VMEM] * 4,
+        [pltpu.VMEM((2 * n_fact + 1, width, block), F32), pltpu.VMEM((4, width // chips, 128), F32)],
         flops=2 * slots * block * block * width,
         moved=9 << 20,
-    )(place, lists, counts, grads, facts_t, tiles, tiles_sib)
-    slices = by_fact((keep + swap(give).astype(F32)).astype(BF16))
+    )(info, grads, facts_t, tiles, tiles_sib)
+    give = swap(give)
+
+    def partial_sum(k, arrived):
+        return (keep[k] + give[k].astype(F32) + arrived.astype(F32)).astype(BF16)
+
+    up = shift((keep[4] + give[4].astype(F32)).astype(BF16), 1)
+    down = shift((keep[5] + give[5].astype(F32)).astype(BF16), -1)
+    for k in (3, 2):
+        up, down = shift(partial_sum(k, up), 1), shift(partial_sum(9 - k, down), -1)
+    up = shift(partial_sum(1, up), 1)
 
     tab, gsum, self_piece = call(
         slice_kernel,
@@ -325,15 +328,15 @@
             jax.ShapeDtypeStruct((2 * n_fact, 32, 128), BF16),
             jax.ShapeDtypeStruct((8, 128), F32),
         ),
-        [SMEM] * 2 + [VMEM] * 19,
+        [SMEM] + [VMEM] * 22,
         [pltpu.VMEM((3, 32, width), F32)],
         flops=4 * n_fact * 32 * 128 * width,
         moved=3 << 20,
-    )(place, block_table, slices, *pieces, *pieces_sib)
+    )(info, keep[0], give[0], up, down, *pieces, *pieces_sib)
     tab = by_chip(tab.reshape(chips, 24, 128))
     packed = call(
         pack_kernel, jax.ShapeDtypeStruct((n_fact, 96, 128), BF16), [SMEM] + [VMEM] * 3, moved=1 << 19
-    )(place, tab, gsum, self_piece)
+    )(info, tab, gsum, self_piece)
     packed = by_fact(packed)
     pieces_own = by_chip(jnp.broadcast_to(packed[None, :, 64:, :], (chips, n_fact, 32, 128)))
     given = swap(packed[:, 32:64, :])
@@ -341,16 +344,16 @@
     grad_dims = call(
         rows_kernel,
         jax.ShapeDtypeStruct((rows, width), F32),
-        [SMEM] * 2 + [VMEM] * 3,
+        [SMEM] + [VMEM] * 3,
         flops=2 * rows * width * width,
         moved=2 << 20,
-    )(place, block_table, packed[:, :32, :], given, w_tables)
+    )(info, packed[:, :32, :], given, w_tables)
     grad_self, grad_tab = call(
         final_kernel,
         (jax.ShapeDtypeStruct((width, width), F32), jax.ShapeDtypeStruct((3, width, width), F32)),
         [SMEM] + [VMEM] * 2,
         moved=8 << 20,
-    )(place, pieces_own, swap(pieces_own))
+    )(info, pieces_own, swap(pieces_own))
     return (fact_out, grad_dims, grad_self, grad_tab)
 
 

time: 203 us -> 197 us (0.970)
  blocking collectives: 138 us -> 102 us
  starting transfers between devices: 27.2 us -> 45.3 us
  waiting for transfers between devices: 13.4 us -> 27.2 us
  local copies, waits for them, and re-layouts: 4.84 us -> 1.62 us
    all_to_all x2 -> x1, blocking collectives: 45.2 us -> 11.4 us  [by_fact(): return lax.all_to_all(x, 'fact', 0, 0, tiled=True)]
    ppermute x8 -> x15, waiting for transfers between devices: 6.35 us -> 21.2 us  [shift(): lax.ppermute(x, 'fact', [(i, (i + by) % n_fact) for i in range(n_fact)])]
    ppermute x14, starting transfers between devices: 14.1 us -> 23.2 us  [swap(): return lax.ppermute(x, 'dim', pair)]
    ppermute x8 -> x15, starting transfers between devices: 13.2 us -> 22.1 us  [shift(): lax.ppermute(x, 'fact', [(i, (i + by) % n_fact) for i in range(n_fact)])]
    unnamed x22 -> x14, local copies, waits for them, and re-layouts: 3.94 us -> 0.7 us
  transfers between devices with their start and end apart: 22 -> 29, of which waited for: 7 -> 11; matrix products, arithmetic and copies ran while one was open for 0% -> 0% of each run, Pallas kernels for 2% -> 2%
where the time goes in v5:
time: 197 us; the launch traced here: 196 us
  blocking collectives  102 us (52%)
  starting transfers between devices  45.3 us (23%)
  waiting for transfers between devices  27.2 us (14%)
  Pallas kernels  18.3 us (9%)
    all_to_all x4, blocking collectives, by_chip(): return lax.all_to_all(x, 'dim', 0, 0, tiled=True, axis_index_groups=same)  90.6 us
    ppermute x14, starting transfers between devices, swap(): return lax.ppermute(x, 'dim', pair)  23.2 us
    ppermute x15, starting transfers between devices, shift(): lax.ppermute(x, 'fact', [(i, (i + by) % n_fact) for i in range(n_fact)])  22.1 us
    ppermute x15, waiting for transfers between devices, shift(): lax.ppermute(x, 'fact', [(i, (i + by) % n_fact) for i in range(n_fact)])  21.2 us
    all_to_all x1, blocking collectives, by_fact(): return lax.all_to_all(x, 'fact', 0, 0, tiled=True)  11.4 us
    ppermute x14, waiting for transfers between devices, swap(): return lax.ppermute(x, 'dim', pair)  5.92 us
  transfers between devices with their start and end apart: 29, of which 11 were waited for; matrix products, arithmetic and copies ran while one was open for 0% of the time, Pallas kernels for 2%

profile of v5, /device:TPU:1, one launch (start us, length us, event | category | flops | bytes accessed | tf_op | source)
XLA Modules:
  0.0 196.3 jit_solution(14004256356212060955)
XLA Ops:
  0.6 3.3 %collective-permute-start.18 = (bf16[32,128,128]{2,1,0:T(8,128)(2,1)}, bf16[32,128,128]{2,1,0:T(8,128)(2,1)S(1)}, u32[]{:S(2)}, u32[]{:S(2)}) collective-permute-start(bf16[32,128,128]{2,1,0:T(8,128)(2,1)} %tiles_own.1), channel_id=1, source_target_pairs={{0,1},{1,0},{2,3},{3,2},{4,5},{5,4},{6,7},{7,6},{8,9},{9,8},{10,11... | collective-permute-start | bytes 3145736 | tf_op jit(solution)/shard_map/ppermute | solution.py:240
  4.0 3.9 %collective-permute-start.2 = (bf16[128,512]{1,0:T(8,128)(2,1)}, bf16[128,512]{1,0:T(8,128)(2,1)S(1)}, u32[]{:S(2)}, u32[]{:S(2)}) collective-permute-start(bf16[128,512]{1,0:T(8,128)(2,1)} %refs_0_.3), channel_id=1, source_target_pairs={{0,224},{32,0},{64,32},{96,64},{128,96},{160,128},{192,160},{224,1... | collective-permute-start | bytes 393224 | tf_op jit(solution)/shard_map/ppermute | solution.py:243
  7.8 0.4 collective-permute-start.9
  8.8 0.7 concatenate.3.links_own
  9.5 0.2 collective-permute-start.4
  9.7 1.2 collective-permute-done.2.refs_2_
  11.0 3.3 %collective-permute-start.3 = (bf16[128,512]{1,0:T(8,128)(2,1)S(1)}, bf16[128,512]{1,0:T(8,128)(2,1)S(1)}, u32[]{:S(2)}, u32[]{:S(2)}) collective-permute-start(bf16[128,512]{1,0:T(8,128)(2,1)S(1)} %collective-permute-done.2.refs_2_), channel_id=1, source_target_pairs={{0,224},{32,0},{64,32},{96,64},{128,96},{160,128},{192,160},{224,1... | collective-permute-start | bytes 393224 | tf_op jit(solution)/shard_map/ppermute | solution.py:243
  14.3 0.7 copy-done.6
  15.0 1.5 shard_map.120.info
  16.5 2.8 %collective-permute-done.1.refs_3_ = bf16[128,512]{1,0:T(8,128)(2,1)S(1)} collective-permute-done((bf16[128,512]{1,0:T(8,128)(2,1)S(1)}, bf16[128,512]{1,0:T(8,128)(2,1)S(1)}, u32[]{:S(2)}, u32[]{:S(2)}) %collective-permute-start.1) | collective-permute-done | bytes 131104 | tf_op jit(solution)/shard_map/ppermute | solution.py:243
  19.3 2.7 %collective-permute-start.7 = (bf16[128,512]{1,0:T(8,128)(2,1)S(1)}, bf16[128,512]{1,0:T(8,128)(2,1)S(1)}, u32[]{:S(2)}, u32[]{:S(2)}) collective-permute-start(bf16[128,512]{1,0:T(8,128)(2,1)S(1)} %collective-permute-done.3.refs_4_), channel_id=1, source_target_pairs={{0,224},{32,0},{64,32},{96,64},{128,96},{160,128},{192,160},{224,1... | collective-permute-start | bytes 393224 | tf_op jit(solution)/shard_map/ppermute | solution.py:243
  22.0 2.9 %collective-permute-start.11 = (bf16[128,512]{1,0:T(8,128)(2,1)S(1)}, bf16[128,512]{1,0:T(8,128)(2,1)S(1)}, u32[]{:S(2)}, u32[]{:S(2)}) collective-permute-start(bf16[128,512]{1,0:T(8,128)(2,1)S(1)} %collective-permute-done.2.refs_2_), channel_id=1, source_target_pairs={{0,1},{1,0},{2,3},{3,2},{4,5},{5,4},{6,7},{7,6},{8,9},{9,8},{10,11... | collective-permute-start | bytes 393224 | tf_op jit(solution)/shard_map/ppermute | solution.py:240
  24.9 2.9 %collective-permute-start.13 = (bf16[128,512]{1,0:T(8,128)(2,1)S(1)}, bf16[128,512]{1,0:T(8,128)(2,1)S(1)}, u32[]{:S(2)}, u32[]{:S(2)}) collective-permute-start(bf16[128,512]{1,0:T(8,128)(2,1)S(1)} %collective-permute-done.3.refs_4_), channel_id=1, source_target_pairs={{0,1},{1,0},{2,3},{3,2},{4,5},{5,4},{6,7},{7,6},{8,9},{9,8},{10,11... | collective-permute-start | bytes 393224 | tf_op jit(solution)/shard_map/ppermute | solution.py:240
  27.9 3.0 %collective-permute-start.8 = (bf16[64,512]{1,0:T(8,128)(2,1)S(1)}, bf16[64,512]{1,0:T(8,128)(2,1)S(1)}, u32[]{:S(2)}, u32[]{:S(2)}) collective-permute-start(bf16[64,512]{1,0:T(8,128)(2,1)S(1)} %slice.85), channel_id=1, source_target_pairs={{0,224},{32,0},{64,32},{96,64},{128,96},{160,128},{192,160},{224,1... | collective-permute-start | bytes 196616 | tf_op jit(solution)/shard_map/ppermute | solution.py:243
  31.0 0.7 collective-permute-start.14
  31.7 0.3 collective-permute-start.15
  31.9 1.4 shard_map.121
  33.4 0.5 collective-permute-start.16
  34.0 0.8 collective-permute-done.16.refs_6_.refs_16_
  34.8 0.4 collective-permute-done.17.refs_7_.refs_17_
  35.2 3.6 %shard_map.122 = bf16[16,544,128]{2,1,0:T(8,128)(2,1)S(1)} custom-call(s32[128]{0:T(128)S(1)} %shard_map.120.info, bf16[10,128,512]{2,1,0:T(8,128)(2,1)S(1)} %get-tuple-element.26.proj, bf16[128,512]{1,0:T(8,128)(2,1)S(1)} %collective-permute-done.5.refs_0_.refs_5_, bf16[128,512]{1,0:T(8,128)(2,1)S(1)} %collective-permute-done.7.refs_1_.refs_6_, ...), custom_call_target="tpu_custom_call" | custom-call | flops 536870912 | bytes 8388608 | tf_op jit(solution)/shard_map/pallas_call | solution.py:282
  38.8 36.6 %all_to_all.25.parts = bf16[16,544,128]{2,1,0:T(8,128)(2,1)S(1)} all-to-all(bf16[16,544,128]{2,1,0:T(8,128)(2,1)S(1)} %shard_map.122), channel_id=1, replica_groups={{0,2,4,6,8,10,12,14,16,18,20,22,24,26,28,30},{1,3,5,7,9,11,13,15,17,19,..., dimensions={0} | all-to-all | bytes 4456448 | tf_op jit(solution)/shard_map/all_to_all | solution.py:246
  75.5 1.2 shard_map.123
  76.6 30.1 %all_to_all.26.grads = bf16[16,512,128]{2,1,0:T(8,128)(2,1)S(1)} all-to-all(bf16[16,512,128]{2,1,0:T(8,128)(2,1)S(1)} %get-tuple-element.31), channel_id=1, replica_groups={{0,2,4,6,8,10,12,14,16,18,20,22,24,26,28,30},{1,3,5,7,9,11,13,15,17,19,..., dimensions={0} | all-to-all | bytes 4194304 | tf_op jit(solution)/shard_map/all_to_all | solution.py:246
  106.7 3.9 %shard_map.124 = (f32[8,528,128]{2,1,0:T(8,128)S(1)}, bf16[8,528,128]{2,1,0:T(8,128)(2,1)S(1)}) custom-call(s32[128]{0:T(128)S(1)} %shard_map.120.info, bf16[16,512,128]{2,1,0:T(8,128)(2,1)S(1)} %all_to_all.26.grads, bf16[16,32,128]{2,1,0:T(8,128)(2,1)S(1)} %get-tuple-element.32.facts_t, bf16[32,128,128]{2,1,0:T(8,128)(2,1)S(1)} %copy-done.1, ...), custom_call_target="tpu_custom_call" | custom-call | flops 536870912 | bytes 9437184 | tf_op jit(solution)/shard_map/pallas_call | solution.py:305
  110.6 2.2 %collective-permute-start.19 = (bf16[8,528,128]{2,1,0:T(8,128)(2,1)S(1)}, bf16[8,528,128]{2,1,0:T(8,128)(2,1)S(1)}, u32[]{:S(2)}, u32[]{:S(2)}) collective-permute-start(bf16[8,528,128]{2,1,0:T(8,128)(2,1)S(1)} %get-tuple-element.34), channel_id=1, source_target_pairs={{0,1},{1,0},{2,3},{3,2},{4,5},{5,4},{6,7},{7,6},{8,9},{9,8},{10,11... | collective-permute-start | bytes 3244040 | tf_op jit(solution)/shard_map/ppermute | solution.py:240
  112.8 2.3 %collective-permute-done.19 = bf16[8,528,128]{2,1,0:T(8,128)(2,1)S(1)} collective-permute-done((bf16[8,528,128]{2,1,0:T(8,128)(2,1)S(1)}, bf16[8,528,128]{2,1,0:T(8,128)(2,1)S(1)}, u32[]{:S(2)}, u32[]{:S(2)}) %collective-permute-start.19) | collective-permute-done | bytes 1081376 | tf_op jit(solution)/shard_map/ppermute | solution.py:240
  115.2 2.2 %collective-permute-start.24 = (bf16[528,128]{1,0:T(8,128)(2,1)S(1)}, bf16[528,128]{1,0:T(8,128)(2,1)S(1)}, u32[]{:S(2)}, u32[]{:S(2)}) collective-permute-start(bf16[528,128]{1,0:T(8,128)(2,1)S(1)} %get-tuple-element.42), channel_id=1, source_target_pairs={{0,224},{32,0},{64,32},{96,64},{128,96},{160,128},{192,160},{224,1... | collective-permute-start | bytes 405512 | tf_op jit(solution)/shard_map/ppermute | solution.py:243
  117.5 2.6 %collective-permute-done.24 = bf16[528,128]{1,0:T(8,128)(2,1)S(1)} collective-permute-done((bf16[528,128]{1,0:T(8,128)(2,1)S(1)}, bf16[528,128]{1,0:T(8,128)(2,1)S(1)}, u32[]{:S(2)}, u32[]{:S(2)}) %collective-permute-start.24) | collective-permute-done | bytes 135200 | tf_op jit(solution)/shard_map/ppermute | solution.py:243
  120.1 3.5 %collective-permute-start.25 = (bf16[528,128]{1,0:T(8,128)(2,1)S(1)}, bf16[528,128]{1,0:T(8,128)(2,1)S(1)}, u32[]{:S(2)}, u32[]{:S(2)}) collective-permute-start(bf16[528,128]{1,0:T(8,128)(2,1)S(1)} %fusion), channel_id=1, source_target_pairs={{0,224},{32,0},{64,32},{96,64},{128,96},{160,128},{192,160},{224,1... | collective-permute-start | bytes 405512 | tf_op jit(solution)/shard_map/ppermute | solution.py:243
  123.6 2.0 %collective-permute-done.25 = bf16[528,128]{1,0:T(8,128)(2,1)S(1)} collective-permute-done((bf16[528,128]{1,0:T(8,128)(2,1)S(1)}, bf16[528,128]{1,0:T(8,128)(2,1)S(1)}, u32[]{:S(2)}, u32[]{:S(2)}) %collective-permute-start.25) | collective-permute-done | bytes 135200 | tf_op jit(solution)/shard_map/ppermute | solution.py:243
  125.6 0.1 fusion.1
  125.7 0.4 collective-permute-start.21
  126.1 5.2 %collective-permute-done.21 = bf16[528,128]{1,0:T(8,128)(2,1)S(1)} collective-permute-done((bf16[528,128]{1,0:T(8,128)(2,1)S(1)}, bf16[528,128]{1,0:T(8,128)(2,1)S(1)}, u32[]{:S(2)}, u32[]{:S(2)}) %collective-permute-start.21) | collective-permute-done | bytes 135200 | tf_op jit(solution)/shard_map/ppermute | solution.py:243
  131.4 2.7 %collective-permute-start.26 = (bf16[528,128]{1,0:T(8,128)(2,1)S(1)}, bf16[528,128]{1,0:T(8,128)(2,1)S(1)}, u32[]{:S(2)}, u32[]{:S(2)}) collective-permute-start(bf16[528,128]{1,0:T(8,128)(2,1)S(1)} %get-tuple-element.40), channel_id=1, source_target_pairs={{0,224},{32,0},{64,32},{96,64},{128,96},{160,128},{192,160},{224,1... | collective-permute-start | bytes 405512 | tf_op jit(solution)/shard_map/ppermute | solution.py:243
  134.1 2.4 %collective-permute-done.22 = bf16[528,128]{1,0:T(8,128)(2,1)S(1)} collective-permute-done((bf16[528,128]{1,0:T(8,128)(2,1)S(1)}, bf16[528,128]{1,0:T(8,128)(2,1)S(1)}, u32[]{:S(2)}, u32[]{:S(2)}) %collective-permute-start.22) | collective-permute-done | bytes 135200 | tf_op jit(solution)/shard_map/ppermute | solution.py:243
  136.5 0.3 collective-permute-start.23
  136.9 5.0 %collective-permute-done.23.from_below = bf16[528,128]{1,0:T(8,128)(2,1)S(1)} collective-permute-done((bf16[528,128]{1,0:T(8,128)(2,1)S(1)}, bf16[528,128]{1,0:T(8,128)(2,1)S(1)}, u32[]{:S(2)}, u32[]{:S(2)}) %collective-permute-start.23) | collective-permute-done | bytes 135200 | tf_op jit(solution)/shard_map/ppermute | solution.py:243
  141.9 1.0 shard_map.125
  143.0 9.2 %all_to_all.27.parts = bf16[16,24,128]{2,1,0:T(8,128)(2,1)S(1)} all-to-all(bf16[16,24,128]{2,1,0:T(8,128)(2,1)S(1)} %bitcast.36), channel_id=1, replica_groups={{0,2,4,6,8,10,12,14,16,18,20,22,24,26,28,30},{1,3,5,7,9,11,13,15,17,19,..., dimensions={0} | all-to-all | bytes 196608 | tf_op jit(solution)/shard_map/all_to_all | solution.py:246
  152.2 0.6 shard_map.126
  152.8 11.4 %all_to_all.28 = bf16[8,96,128]{2,1,0:T(8,128)(2,1)S(1)} all-to-all(bf16[8,96,128]{2,1,0:T(8,128)(2,1)S(1)} %shard_map.126), channel_id=1, replica_groups=mesh['fact'=8,'dim'=32] {'fact'}, dimensions={0} | all-to-all | bytes 393216 | tf_op jit(solution)/shard_map/all_to_all | solution.py:249
  164.2 0.2 broadcast_in_dim.5
  164.4 14.7 %all_to_all.29.own = bf16[16,8,32,128]{3,2,1,0:T(8,128)(2,1)S(1)} all-to-all(bf16[16,8,32,128]{3,2,1,0:T(8,128)(2,1)S(1)} %broadcast_in_dim.5), channel_id=1, replica_groups={{0,2,4,6,8,10,12,14,16,18,20,22,24,26,28,30},{1,3,5,7,9,11,13,15,17,19,..., dimensions={0} | all-to-all | bytes 2097152 | tf_op jit(solution)/shard_map/all_to_all | solution.py:246
  179.1 9.8 %collective-permute-start.28 = (bf16[16,8,32,128]{3,2,1,0:T(8,128)(2,1)S(1)}, bf16[16,8,32,128]{3,2,1,0:T(8,128)(2,1)S(1)}, u32[]{:S(2)}, u32[]{:S(2)}) collective-permute-start(bf16[16,8,32,128]{3,2,1,0:T(8,128)(2,1)S(1)} %all_to_all.29.own), channel_id=1, source_target_pairs={{0,1},{1,0},{2,3},{3,2},{4,5},{5,4},{6,7},{7,6},{8,9},{9,8},{10,11... | collective-permute-start | bytes 3145736 | tf_op jit(solution)/shard_map/ppermute | solution.py:240
  188.9 2.4 %collective-permute-done.27.given = bf16[8,32,128]{2,1,0:T(8,128)(2,1)S(1)} collective-permute-done((bf16[8,32,128]{2,1,0:T(8,128)(2,1)S(1)}, bf16[8,32,128]{2,1,0:T(8,128)(2,1)S(1)}, u32[]{:S(2)}, u32[]{:S(2)}) %collective-permute-start.27) | collective-permute-done | bytes 65568 | tf_op jit(solution)/shard_map/ppermute | solution.py:240
  191.2 1.6 shard_map.127
  192.8 3.5 %shard_map.128 = (f32[512,512]{1,0:T(8,128)}, f32[3,512,512]{2,1,0:T(8,128)}) custom-call(s32[128]{0:T(128)S(1)} %shard_map.120.info, bf16[16,8,32,128]{3,2,1,0:T(8,128)(2,1)S(1)} %all_to_all.29.own, bf16[16,8,32,128]{3,2,1,0:T(8,128)(2,1)S(1)} %collective-permute-done.28.sib), custom_call_target="tpu_custom_call" | custom-call | bytes 8388608 | tf_op jit(solution)/shard_map/pallas_call | solution.py:351
  (50 shorter events, 0.7 us)
Async XLA Ops:
  0.6 34.5 %collective-permute-start.18 = (bf16[32,128,128]{2,1,0:T(8,128)(2,1)}, bf16[32,128,128]{2,1,0:T(8,128)(2,1)S(1)}, u32[]{:S(2)}, u32[]{:S(2)}) collective-permute-start(bf16[32,128,128]{2,1,0:T(8,128)(2,1)} %tiles_own.1), channel_id=1, source_target_pairs={{0,1},{1,0},{2,3},{3,2},{4,5},{5,4},{6,7},{7,6},{8,9},{9,8},{10,11... | collective-permute-start | bytes 3145736 | tf_op jit(solution)/shard_map/ppermute | solution.py:240
  4.0 7.0 %collective-permute-start.2 = (bf16[128,512]{1,0:T(8,128)(2,1)}, bf16[128,512]{1,0:T(8,128)(2,1)S(1)}, u32[]{:S(2)}, u32[]{:S(2)}) collective-permute-start(bf16[128,512]{1,0:T(8,128)(2,1)} %refs_0_.3), channel_id=1, source_target_pairs={{0,224},{32,0},{64,32},{96,64},{128,96},{160,128},{192,160},{224,1... | collective-permute-start | bytes 393224 | tf_op jit(solution)/shard_map/ppermute | solution.py:243
  7.8 6.5 %collective-permute-start = (bf16[128,512]{1,0:T(8,128)(2,1)}, bf16[128,512]{1,0:T(8,128)(2,1)S(1)}, u32[]{:S(2)}, u32[]{:S(2)}) collective-permute-start(bf16[128,512]{1,0:T(8,128)(2,1)} %refs_0_.3), channel_id=1, source_target_pairs={{0,32},{32,64},{64,96},{96,128},{128,160},{160,192},{192,224},{224... | collective-permute-start | bytes 393224 | tf_op jit(solution)/shard_map/ppermute | solution.py:243
  7.8 17.0 %collective-permute-start.9 = (bf16[128,512]{1,0:T(8,128)(2,1)}, bf16[128,512]{1,0:T(8,128)(2,1)S(1)}, u32[]{:S(2)}, u32[]{:S(2)}) collective-permute-start(bf16[128,512]{1,0:T(8,128)(2,1)} %refs_0_.3), channel_id=1, source_target_pairs={{0,1},{1,0},{2,3},{3,2},{4,5},{5,4},{6,7},{7,6},{8,9},{9,8},{10,11... | collective-permute-start | bytes 393224 | tf_op jit(solution)/shard_map/ppermute | solution.py:240
  9.5 4.8 %collective-permute-start.4 = (s32[2,33]{1,0:T(2,128)S(1)}, s32[2,33]{1,0:T(2,128)S(1)}, u32[]{:S(2)}, u32[]{:S(2)}) collective-permute-start(s32[2,33]{1,0:T(2,128)S(1)} %concatenate.3.links_own), channel_id=1, source_target_pairs={{0,1},{1,0},{2,3},{3,2},{4,5},{5,4},{6,7},{7,6},{8,9},{9,8},{10,11... | collective-permute-start | bytes 800 | tf_op jit(solution)/shard_map/ppermute | solution.py:240
  9.7 22.2 %copy-start = (bf16[3,512,512]{2,1,0:T(8,128)(2,1)S(1)}, bf16[3,512,512]{2,1,0:T(8,128)(2,1)}, u32[]{:S(2)}) copy-start(bf16[3,512,512]{2,1,0:T(8,128)(2,1)} %w.5) | copy-start | bytes 4718596
  9.7 22.2 %copy-start.2 = (bf16[128,512]{1,0:T(8,128)(2,1)S(1)}, bf16[128,512]{1,0:T(8,128)(2,1)}, u32[]{:S(2)}) copy-start(bf16[128,512]{1,0:T(8,128)(2,1)} %facts.3) | copy-start | bytes 393220
  9.7 22.2 %copy-start.3 = (bf16[128,512]{1,0:T(8,128)(2,1)S(1)}, bf16[128,512]{1,0:T(8,128)(2,1)}, u32[]{:S(2)}) copy-start(bf16[128,512]{1,0:T(8,128)(2,1)} %refs_0_.3) | copy-start | bytes 393220
  11.0 5.5 %collective-permute-start.3 = (bf16[128,512]{1,0:T(8,128)(2,1)S(1)}, bf16[128,512]{1,0:T(8,128)(2,1)S(1)}, u32[]{:S(2)}, u32[]{:S(2)}) collective-permute-start(bf16[128,512]{1,0:T(8,128)(2,1)S(1)} %collective-permute-done.2.refs_2_), channel_id=1, source_target_pairs={{0,224},{32,0},{64,32},{96,64},{128,96},{160,128},{192,160},{224,1... | collective-permute-start | bytes 393224 | tf_op jit(solution)/shard_map/ppermute | solution.py:243
  14.3 5.0 %collective-permute-start.1 = (bf16[128,512]{1,0:T(8,128)(2,1)S(1)}, bf16[128,512]{1,0:T(8,128)(2,1)S(1)}, u32[]{:S(2)}, u32[]{:S(2)}) collective-permute-start(bf16[128,512]{1,0:T(8,128)(2,1)S(1)} %collective-permute-done.refs_1_), channel_id=1, source_target_pairs={{0,32},{32,64},{64,96},{96,128},{128,160},{160,192},{192,224},{224... | collective-permute-start | bytes 393224 | tf_op jit(solution)/shard_map/ppermute | solution.py:243
  14.3 0.7 copy-start.6
  16.5 18.7 %copy-start.1 = (bf16[32,128,128]{2,1,0:T(8,128)(2,1)S(1)}, bf16[32,128,128]{2,1,0:T(8,128)(2,1)}, u32[]{:S(2)}) copy-start(bf16[32,128,128]{2,1,0:T(8,128)(2,1)} %tiles_own.1) | copy-start | bytes 3145732
  19.3 5.5 %collective-permute-start.5 = (bf16[128,512]{1,0:T(8,128)(2,1)S(1)}, bf16[128,512]{1,0:T(8,128)(2,1)S(1)}, u32[]{:S(2)}, u32[]{:S(2)}) collective-permute-start(bf16[128,512]{1,0:T(8,128)(2,1)S(1)} %collective-permute-done.1.refs_3_), channel_id=1, source_target_pairs={{0,32},{32,64},{64,96},{96,128},{128,160},{160,192},{192,224},{224... | collective-permute-start | bytes 393224 | tf_op jit(solution)/shard_map/ppermute | solution.py:243
  19.3 8.5 %collective-permute-start.7 = (bf16[128,512]{1,0:T(8,128)(2,1)S(1)}, bf16[128,512]{1,0:T(8,128)(2,1)S(1)}, u32[]{:S(2)}, u32[]{:S(2)}) collective-permute-start(bf16[128,512]{1,0:T(8,128)(2,1)S(1)} %collective-permute-done.3.refs_4_), channel_id=1, source_target_pairs={{0,224},{32,0},{64,32},{96,64},{128,96},{160,128},{192,160},{224,1... | collective-permute-start | bytes 393224 | tf_op jit(solution)/shard_map/ppermute | solution.py:243
  22.0 5.8 %collective-permute-start.11 = (bf16[128,512]{1,0:T(8,128)(2,1)S(1)}, bf16[128,512]{1,0:T(8,128)(2,1)S(1)}, u32[]{:S(2)}, u32[]{:S(2)}) collective-permute-start(bf16[128,512]{1,0:T(8,128)(2,1)S(1)} %collective-permute-done.2.refs_2_), channel_id=1, source_target_pairs={{0,1},{1,0},{2,3},{3,2},{4,5},{5,4},{6,7},{7,6},{8,9},{9,8},{10,11... | collective-permute-start | bytes 393224 | tf_op jit(solution)/shard_map/ppermute | solution.py:240
  24.9 3.1 %collective-permute-start.10 = (bf16[128,512]{1,0:T(8,128)(2,1)S(1)}, bf16[128,512]{1,0:T(8,128)(2,1)S(1)}, u32[]{:S(2)}, u32[]{:S(2)}) collective-permute-start(bf16[128,512]{1,0:T(8,128)(2,1)S(1)} %collective-permute-done.refs_1_), channel_id=1, source_target_pairs={{0,1},{1,0},{2,3},{3,2},{4,5},{5,4},{6,7},{7,6},{8,9},{9,8},{10,11... | collective-permute-start | bytes 393224 | tf_op jit(solution)/shard_map/ppermute | solution.py:240
  24.9 6.1 %collective-permute-start.13 = (bf16[128,512]{1,0:T(8,128)(2,1)S(1)}, bf16[128,512]{1,0:T(8,128)(2,1)S(1)}, u32[]{:S(2)}, u32[]{:S(2)}) collective-permute-start(bf16[128,512]{1,0:T(8,128)(2,1)S(1)} %collective-permute-done.3.refs_4_), channel_id=1, source_target_pairs={{0,1},{1,0},{2,3},{3,2},{4,5},{5,4},{6,7},{7,6},{8,9},{9,8},{10,11... | collective-permute-start | bytes 393224 | tf_op jit(solution)/shard_map/ppermute | solution.py:240
  27.8 3.9 %collective-permute-start.12 = (bf16[128,512]{1,0:T(8,128)(2,1)S(1)}, bf16[128,512]{1,0:T(8,128)(2,1)S(1)}, u32[]{:S(2)}, u32[]{:S(2)}) collective-permute-start(bf16[128,512]{1,0:T(8,128)(2,1)S(1)} %collective-permute-done.1.refs_3_), channel_id=1, source_target_pairs={{0,1},{1,0},{2,3},{3,2},{4,5},{5,4},{6,7},{7,6},{8,9},{9,8},{10,11... | collective-permute-start | bytes 393224 | tf_op jit(solution)/shard_map/ppermute | solution.py:240
  27.8 5.5 %collective-permute-start.6 = (bf16[64,512]{1,0:T(8,128)(2,1)S(1)}, bf16[64,512]{1,0:T(8,128)(2,1)S(1)}, u32[]{:S(2)}, u32[]{:S(2)}) collective-permute-start(bf16[64,512]{1,0:T(8,128)(2,1)S(1)} %slice.84), channel_id=1, source_target_pairs={{0,32},{32,64},{64,96},{96,128},{128,160},{160,192},{192,224},{224... | collective-permute-start | bytes 196616 | tf_op jit(solution)/shard_map/ppermute | solution.py:243
  27.9 5.4 %collective-permute-start.8 = (bf16[64,512]{1,0:T(8,128)(2,1)S(1)}, bf16[64,512]{1,0:T(8,128)(2,1)S(1)}, u32[]{:S(2)}, u32[]{:S(2)}) collective-permute-start(bf16[64,512]{1,0:T(8,128)(2,1)S(1)} %slice.85), channel_id=1, source_target_pairs={{0,224},{32,0},{64,32},{96,64},{128,96},{160,128},{192,160},{224,1... | collective-permute-start | bytes 196616 | tf_op jit(solution)/shard_map/ppermute | solution.py:243
  31.0 4.2 %collective-permute-start.14 = (bf16[128,512]{1,0:T(8,128)(2,1)S(1)}, bf16[128,512]{1,0:T(8,128)(2,1)S(1)}, u32[]{:S(2)}, u32[]{:S(2)}) collective-permute-start(bf16[128,512]{1,0:T(8,128)(2,1)S(1)} %collective-permute-done.5.refs_0_.refs_5_), channel_id=1, source_target_pairs={{0,1},{1,0},{2,3},{3,2},{4,5},{5,4},{6,7},{7,6},{8,9},{9,8},{10,11... | collective-permute-start | bytes 393224 | tf_op jit(solution)/shard_map/ppermute | solution.py:240
  31.7 3.5 %collective-permute-start.15 = (bf16[128,512]{1,0:T(8,128)(2,1)S(1)}, bf16[128,512]{1,0:T(8,128)(2,1)S(1)}, u32[]{:S(2)}, u32[]{:S(2)}) collective-permute-start(bf16[128,512]{1,0:T(8,128)(2,1)S(1)} %collective-permute-done.7.refs_1_.refs_6_), channel_id=1, source_target_pairs={{0,1},{1,0},{2,3},{3,2},{4,5},{5,4},{6,7},{7,6},{8,9},{9,8},{10,11... | collective-permute-start | bytes 393224 | tf_op jit(solution)/shard_map/ppermute | solution.py:240
  33.4 1.4 collective-permute-start.16
  33.9 1.3 collective-permute-start.17
  38.8 36.6 %copy-start.4 = (bf16[512,512]{1,0:T(8,128)(2,1)S(1)}, bf16[512,512]{1,0:T(8,128)(2,1)}, u32[]{:S(2)}) copy-start(bf16[512,512]{1,0:T(8,128)(2,1)} %w.4) | copy-start | bytes 1572868
  38.8 36.6 %copy-start.5 = (bf16[128,512]{1,0:T(8,128)(2,1)S(1)}, bf16[128,512]{1,0:T(8,128)(2,1)}, u32[]{:S(2)}) copy-start(bf16[128,512]{1,0:T(8,128)(2,1)} %cot.1) | copy-start | bytes 393220
  110.6 4.5 %collective-permute-start.19 = (bf16[8,528,128]{2,1,0:T(8,128)(2,1)S(1)}, bf16[8,528,128]{2,1,0:T(8,128)(2,1)S(1)}, u32[]{:S(2)}, u32[]{:S(2)}) collective-permute-start(bf16[8,528,128]{2,1,0:T(8,128)(2,1)S(1)} %get-tuple-element.34), channel_id=1, source_target_pairs={{0,1},{1,0},{2,3},{3,2},{4,5},{5,4},{6,7},{7,6},{8,9},{9,8},{10,11... | collective-permute-start | bytes 3244040 | tf_op jit(solution)/shard_map/ppermute | solution.py:240
  115.2 4.9 %collective-permute-start.24 = (bf16[528,128]{1,0:T(8,128)(2,1)S(1)}, bf16[528,128]{1,0:T(8,128)(2,1)S(1)}, u32[]{:S(2)}, u32[]{:S(2)}) collective-permute-start(bf16[528,128]{1,0:T(8,128)(2,1)S(1)} %get-tuple-element.42), channel_id=1, source_target_pairs={{0,224},{32,0},{64,32},{96,64},{128,96},{160,128},{192,160},{224,1... | collective-permute-start | bytes 405512 | tf_op jit(solution)/shard_map/ppermute | solution.py:243
  117.5 6.1 %collective-permute-start.20 = (bf16[528,128]{1,0:T(8,128)(2,1)S(1)}, bf16[528,128]{1,0:T(8,128)(2,1)S(1)}, u32[]{:S(2)}, u32[]{:S(2)}) collective-permute-start(bf16[528,128]{1,0:T(8,128)(2,1)S(1)} %get-tuple-element.43), channel_id=1, source_target_pairs={{0,32},{32,64},{64,96},{96,128},{128,160},{160,192},{192,224},{224... | collective-permute-start | bytes 405512 | tf_op jit(solution)/shard_map/ppermute | solution.py:243
  120.1 5.4 %collective-permute-start.25 = (bf16[528,128]{1,0:T(8,128)(2,1)S(1)}, bf16[528,128]{1,0:T(8,128)(2,1)S(1)}, u32[]{:S(2)}, u32[]{:S(2)}) collective-permute-start(bf16[528,128]{1,0:T(8,128)(2,1)S(1)} %fusion), channel_id=1, source_target_pairs={{0,224},{32,0},{64,32},{96,64},{128,96},{160,128},{192,160},{224,1... | collective-permute-start | bytes 405512 | tf_op jit(solution)/shard_map/ppermute | solution.py:243
  125.7 5.6 %collective-permute-start.21 = (bf16[528,128]{1,0:T(8,128)(2,1)S(1)}, bf16[528,128]{1,0:T(8,128)(2,1)S(1)}, u32[]{:S(2)}, u32[]{:S(2)}) collective-permute-start(bf16[528,128]{1,0:T(8,128)(2,1)S(1)} %get-tuple-element.41), channel_id=1, source_target_pairs={{0,32},{32,64},{64,96},{96,128},{128,160},{160,192},{192,224},{224... | collective-permute-start | bytes 405512 | tf_op jit(solution)/shard_map/ppermute | solution.py:243
  131.3 5.2 %collective-permute-start.22 = (bf16[528,128]{1,0:T(8,128)(2,1)S(1)}, bf16[528,128]{1,0:T(8,128)(2,1)S(1)}, u32[]{:S(2)}, u32[]{:S(2)}) collective-permute-start(bf16[528,128]{1,0:T(8,128)(2,1)S(1)} %fusion.3), channel_id=1, source_target_pairs={{0,32},{32,64},{64,96},{96,128},{128,160},{160,192},{192,224},{224... | collective-permute-start | bytes 405512 | tf_op jit(solution)/shard_map/ppermute | solution.py:243
  131.4 5.5 %collective-permute-start.26 = (bf16[528,128]{1,0:T(8,128)(2,1)S(1)}, bf16[528,128]{1,0:T(8,128)(2,1)S(1)}, u32[]{:S(2)}, u32[]{:S(2)}) collective-permute-start(bf16[528,128]{1,0:T(8,128)(2,1)S(1)} %get-tuple-element.40), channel_id=1, source_target_pairs={{0,224},{32,0},{64,32},{96,64},{128,96},{160,128},{192,160},{224,1... | collective-permute-start | bytes 405512 | tf_op jit(solution)/shard_map/ppermute | solution.py:243
  136.5 5.4 %collective-permute-start.23 = (bf16[528,128]{1,0:T(8,128)(2,1)S(1)}, bf16[528,128]{1,0:T(8,128)(2,1)S(1)}, u32[]{:S(2)}, u32[]{:S(2)}) collective-permute-start(bf16[528,128]{1,0:T(8,128)(2,1)S(1)} %fusion.4), channel_id=1, source_target_pairs={{0,32},{32,64},{64,96},{96,128},{128,160},{160,192},{192,224},{224... | collective-permute-start | bytes 405512 | tf_op jit(solution)/shard_map/ppermute | solution.py:243
  179.1 13.8 %collective-permute-start.28 = (bf16[16,8,32,128]{3,2,1,0:T(8,128)(2,1)S(1)}, bf16[16,8,32,128]{3,2,1,0:T(8,128)(2,1)S(1)}, u32[]{:S(2)}, u32[]{:S(2)}) collective-permute-start(bf16[16,8,32,128]{3,2,1,0:T(8,128)(2,1)S(1)} %all_to_all.29.own), channel_id=1, source_target_pairs={{0,1},{1,0},{2,3},{3,2},{4,5},{5,4},{6,7},{7,6},{8,9},{9,8},{10,11... | collective-permute-start | bytes 3145736 | tf_op jit(solution)/shard_map/ppermute | solution.py:240
  188.9 2.4 %collective-permute-start.27 = (bf16[8,32,128]{2,1,0:T(8,128)(2,1)S(1)}, bf16[8,32,128]{2,1,0:T(8,128)(2,1)S(1)}, u32[]{:S(2)}, u32[]{:S(2)}) collective-permute-start(bf16[8,32,128]{2,1,0:T(8,128)(2,1)S(1)} %get-tuple-element.46), channel_id=1, source_target_pairs={{0,1},{1,0},{2,3},{3,2},{4,5},{5,4},{6,7},{7,6},{8,9},{9,8},{10,11... | collective-permute-start | bytes 196616 | tf_op jit(solution)/shard_map/ppermute | solution.py:240

commit v6 on v5

--- a/solution.py
+++ b/solution.py
@@ -13,8 +13,8 @@
 UNROLL = 4
 
 
-ORDER = (0, -1, 1, -2, 2, -3, 3)
-EARLY = 5
+ORDER = (0, -1, 1, -2, 2, 4, -3, 3)
+EARLY = 6
 LIST = 40
 COUNT, KIND, PLACE, INFO = 80, 96, 112, 128
 
@@ -65,16 +65,15 @@
 
 
 def forward_kernel(info, proj, *refs):
-    late = 9 - EARLY
+    late = len(ORDER) - EARLY
     sides, (w, facts_t, tiles_own, tiles_sib, out, panel, acc) = (refs[:late], refs[late : 2 * late]), refs[2 * late :]
     fact_pos = info[PLACE]
     for side, pieces in enumerate(sides):
         for at, shift in enumerate(ORDER[:EARLY]):
             panel[side * 8 + ((fact_pos + shift) & 7)] = proj[side * EARLY + at]
-        blocks = [x[...] for x in pieces[:-2]] + [jnp.concatenate([pieces[-2][...], pieces[-1][...]], axis=0)]
-        for shift, rows in zip(ORDER[EARLY:] + (4,), blocks):
+        for shift, rows in zip(ORDER[EARLY:], pieces):
             h = (fact_pos + shift) & 7
-            value = jnp.dot(rows, w[info[KIND + side * 8 + h]], preferred_element_type=F32)
+            value = jnp.dot(rows[...], w[info[KIND + side * 8 + h]], preferred_element_type=F32)
             panel[side * 8 + h] = value.astype(BF16)
     acc[...] = jnp.zeros_like(acc)
     for side, tiles in enumerate((tiles_own, tiles_sib)):
@@ -151,26 +150,23 @@
             out[k, 512:528, :] = jnp.concatenate([mine, jnp.zeros_like(mine)], axis=0).astype(kind)
 
 
-def slice_kernel(info, kept, given, from_below, from_above, *refs):
-    pieces, (tab, gsum, self_piece, tacc) = refs[:18], refs[18:]
+def slice_kernel(info, kept, given, from_below, from_above, from_far, *refs):
+    pieces, (tab, gsum, self_piece, tacc) = refs[:16], refs[16:]
     fact_pos, core = info[PLACE], info[PLACE + 2]
-    total = kept[...] + given[...].astype(F32) + from_below[...].astype(F32) + from_above[...].astype(F32)
+    total = kept[...]
+    for arrived in (given, from_below, from_above, from_far):
+        total = total + arrived[...].astype(F32)
     self_piece[...] = total[512:520]
     for at in range(16):
         gsum[at] = total[at * 32 : (at + 1) * 32].astype(BF16)
     tacc[...] = jnp.zeros_like(tacc)
     for side in range(2):
         column = 8 * (core if side == 0 else 1 - core)
-        for at, shift in enumerate(ORDER + (4,)):
+        for at, shift in enumerate(ORDER):
             h = (fact_pos + shift) & 7
             kind = info[KIND + side * 8 + h]
-            grad = gsum[column + h]
-            if shift == 4:
-                low, high = pieces[side * 9 + 7], pieces[side * 9 + 8]
-                rows = jnp.concatenate([low[...], high[...]], axis=0)
-            else:
-                rows = pieces[side * 9 + at][...]
-            tacc[kind] += jnp.dot(grad, rows, preferred_element_type=F32)
+            rows = pieces[side * 8 + at][...]
+            tacc[kind] += jnp.dot(gsum[column + h], rows, preferred_element_type=F32)
     for q in range(4):
         for t in range(3):
             at = q * 96 + t * 32
@@ -261,15 +257,17 @@
     )(place, links_own, links_sib, block_table)
     tiles_sib = swap(tiles)
 
+    far = shift(dims, 4)
     pieces, up, down = [dims], dims, dims
     for step in range(3):
         if step == 2:
-            up, down, info = lax.optimization_barrier((up, down, info))
+            up, down, far, info = lax.optimization_barrier((up, down, far, info))
+            pieces.append(far)
         up, down = shift(up, 1), shift(down, -1)
         pieces += [up, down]
+    pieces, late = pieces[:EARLY], pieces[EARLY:]
     pieces_sib = [swap(x) for x in pieces]
-    far = [shift(up[: rows // 2], 1), shift(down[rows // 2 :], -1)]
-    early = pieces[:EARLY] + pieces_sib[:EARLY]
+    early = pieces + pieces_sib
     proj, facts_t = call(
         project_kernel,
         (jax.ShapeDtypeStruct((len(early), rows, width), BF16), jax.ShapeDtypeStruct((width, block), BF16)),
@@ -277,12 +275,12 @@
         flops=2 * len(early) * rows * width * width,
         moved=4 << 20,
     )(info, w_tables, facts, *early)
-    *far, proj = lax.optimization_barrier((*far, proj))
-    pieces, pieces_sib = pieces + far, pieces_sib + [swap(x) for x in far]
+    *late, proj = lax.optimization_barrier((*late, proj))
+    pieces, pieces_sib = pieces + late, pieces_sib + [swap(x) for x in late]
     partial = call(
         forward_kernel,
         jax.ShapeDtypeStruct((chips, 544, 128), BF16),
-        [SMEM] + [VMEM] * (5 + 2 * (9 - EARLY)),
+        [SMEM] + [VMEM] * (5 + 2 * len(late)),
         [pltpu.VMEM((2 * n_fact, rows, width), BF16), pltpu.VMEM((chips + 1, block, width), F32)],
         flops=2 * slots * block * block * width,
         moved=8 << 20,
@@ -315,11 +313,13 @@
     def partial_sum(k, arrived):
         return (keep[k] + give[k].astype(F32) + arrived.astype(F32)).astype(BF16)
 
-    up = shift((keep[4] + give[4].astype(F32)).astype(BF16), 1)
+    far = shift((keep[4] + give[4].astype(F32)).astype(BF16), 4)
+    up = shift((keep[3] + give[3].astype(F32)).astype(BF16), 1)
     down = shift((keep[5] + give[5].astype(F32)).astype(BF16), -1)
-    for k in (3, 2):
-        up, down = shift(partial_sum(k, up), 1), shift(partial_sum(9 - k, down), -1)
-    up = shift(partial_sum(1, up), 1)
+    for k in (2, 1):
+        if k == 1:
+            up, down, far = lax.optimization_barrier((up, down, far))
+        up, down = shift(partial_sum(k, up), 1), shift(partial_sum(8 - k, down), -1)
 
     tab, gsum, self_piece = call(
         slice_kernel,
@@ -328,11 +328,11 @@
             jax.ShapeDtypeStruct((2 * n_fact, 32, 128), BF16),
             jax.ShapeDtypeStruct((8, 128), F32),
         ),
-        [SMEM] + [VMEM] * 22,
+        [SMEM] + [VMEM] * 21,
         [pltpu.VMEM((3, 32, width), F32)],
         flops=4 * n_fact * 32 * 128 * width,
         moved=3 << 20,
-    )(info, keep[0], give[0], up, down, *pieces, *pieces_sib)
+    )(info, keep[0], give[0], up, down, far, *pieces, *pieces_sib)
     tab = by_chip(tab.reshape(chips, 24, 128))
     packed = call(
         pack_kernel, jax.ShapeDtypeStruct((n_fact, 96, 128), BF16), [SMEM] + [VMEM] * 3, moved=1 << 19

time: 197 us -> 196 us (level)
  blocking collectives: 102 us -> 104 us
    ppermute x15 -> x14, starting transfers between devices: 22.1 us -> 18 us  [shift(): lax.ppermute(x, 'fact', [(i, (i + by) % n_fact) for i in range(n_fact)])]
    all_to_all x4, blocking collectives: 90.6 us -> 93.2 us  [by_chip(): return lax.all_to_all(x, 'dim', 0, 0, tiled=True, axis_index_groups=same)]
    ppermute x14 -> x13, starting transfers between devices: 23.2 us -> 25.6 us  [swap(): return lax.ppermute(x, 'dim', pair)]
    ppermute x14 -> x13, waiting for transfers between devices: 5.92 us -> 6.81 us  [swap(): return lax.ppermute(x, 'dim', pair)]
    ppermute x15 -> x14, waiting for transfers between devices: 21.2 us -> 20.7 us  [shift(): lax.ppermute(x, 'fact', [(i, (i + by) % n_fact) for i in range(n_fact)])]
  transfers between devices with their start and end apart: 29 -> 27, of which waited for: 11 -> 14; matrix products, arithmetic and copies ran while one was open for 0% -> 0% of each run, Pallas kernels for 2% -> 2%
where the time goes in v6:
time: 196 us; the launch traced here: 195 us
  blocking collectives  104 us (53%)
  starting transfers between devices  43.6 us (22%)
  waiting for transfers between devices  27.5 us (14%)
  Pallas kernels  16.6 us (8%)
    all_to_all x4, blocking collectives, by_chip(): return lax.all_to_all(x, 'dim', 0, 0, tiled=True, axis_index_groups=same)  93.2 us
    ppermute x13, starting transfers between devices, swap(): return lax.ppermute(x, 'dim', pair)  25.6 us
    ppermute x14, waiting for transfers between devices, shift(): lax.ppermute(x, 'fact', [(i, (i + by) % n_fact) for i in range(n_fact)])  20.7 us
    ppermute x14, starting transfers between devices, shift(): lax.ppermute(x, 'fact', [(i, (i + by) % n_fact) for i in range(n_fact)])  18 us
    all_to_all x1, blocking collectives, by_fact(): return lax.all_to_all(x, 'fact', 0, 0, tiled=True)  11 us
    ppermute x13, waiting for transfers between devices, swap(): return lax.ppermute(x, 'dim', pair)  6.81 us
  transfers between devices with their start and end apart: 27, of which 14 were waited for; matrix products, arithmetic and copies ran while one was open for 0% of the time, Pallas kernels for 2%

profile of v6, /device:TPU:1, one launch (start us, length us, event | category | flops | bytes accessed | tf_op | source)
XLA Modules:
  0.0 195.4 jit_solution(14239960148576948165)
XLA Ops:
  0.6 3.3 %collective-permute-start.16 = (bf16[32,128,128]{2,1,0:T(8,128)(2,1)}, bf16[32,128,128]{2,1,0:T(8,128)(2,1)S(1)}, u32[]{:S(2)}, u32[]{:S(2)}) collective-permute-start(bf16[32,128,128]{2,1,0:T(8,128)(2,1)} %tiles_own.1), channel_id=1, source_target_pairs={{0,1},{1,0},{2,3},{3,2},{4,5},{5,4},{6,7},{7,6},{8,9},{9,8},{10,11... | collective-permute-start | bytes 3145736 | tf_op jit(solution)/shard_map/ppermute | solution.py:236
  4.0 3.9 %collective-permute-start.2 = (bf16[128,512]{1,0:T(8,128)(2,1)}, bf16[128,512]{1,0:T(8,128)(2,1)S(1)}, u32[]{:S(2)}, u32[]{:S(2)}) collective-permute-start(bf16[128,512]{1,0:T(8,128)(2,1)} %refs_0_.3), channel_id=1, source_target_pairs={{0,224},{32,0},{64,32},{96,64},{128,96},{160,128},{192,160},{224,1... | collective-permute-start | bytes 393224 | tf_op jit(solution)/shard_map/ppermute | solution.py:239
  7.8 2.8 %collective-permute-start.4 = (bf16[128,512]{1,0:T(8,128)(2,1)}, bf16[128,512]{1,0:T(8,128)(2,1)S(1)}, u32[]{:S(2)}, u32[]{:S(2)}) collective-permute-start(bf16[128,512]{1,0:T(8,128)(2,1)} %refs_0_.3), channel_id=1, source_target_pairs={{0,128},{32,160},{64,192},{96,224},{128,0},{160,32},{192,64},{224,... | collective-permute-start | bytes 393224 | tf_op jit(solution)/shard_map/ppermute | solution.py:239
  10.6 0.4 collective-permute-done.2.refs_2_
  11.0 3.3 %collective-permute-start.3 = (bf16[128,512]{1,0:T(8,128)(2,1)S(1)}, bf16[128,512]{1,0:T(8,128)(2,1)S(1)}, u32[]{:S(2)}, u32[]{:S(2)}) collective-permute-start(bf16[128,512]{1,0:T(8,128)(2,1)S(1)} %collective-permute-done.2.refs_2_), channel_id=1, source_target_pairs={{0,224},{32,0},{64,32},{96,64},{128,96},{160,128},{192,160},{224,1... | collective-permute-start | bytes 393224 | tf_op jit(solution)/shard_map/ppermute | solution.py:239
  14.3 0.4 collective-permute-done.refs_1_
  15.4 0.7 concatenate.3.links_own
  16.1 6.6 %collective-permute-start.5 = (s32[2,33]{1,0:T(2,128)S(1)}, s32[2,33]{1,0:T(2,128)S(1)}, u32[]{:S(2)}, u32[]{:S(2)}) collective-permute-start(s32[2,33]{1,0:T(2,128)S(1)} %concatenate.3.links_own), channel_id=1, source_target_pairs={{0,1},{1,0},{2,3},{3,2},{4,5},{5,4},{6,7},{7,6},{8,9},{9,8},{10,11... | collective-permute-start | bytes 800 | tf_op jit(solution)/shard_map/ppermute | solution.py:236
  22.7 0.7 collective-permute-done.5.links_sib
  23.5 0.3 collective-permute-start.8
  23.8 0.2 collective-permute-start.10
  24.0 0.3 collective-permute-start.9
  24.3 3.2 %collective-permute-start.12 = (bf16[128,512]{1,0:T(8,128)(2,1)S(1)}, bf16[128,512]{1,0:T(8,128)(2,1)S(1)}, u32[]{:S(2)}, u32[]{:S(2)}) collective-permute-start(bf16[128,512]{1,0:T(8,128)(2,1)S(1)} %collective-permute-done.3.refs_4_), channel_id=1, source_target_pairs={{0,1},{1,0},{2,3},{3,2},{4,5},{5,4},{6,7},{7,6},{8,9},{9,8},{10,11... | collective-permute-start | bytes 393224 | tf_op jit(solution)/shard_map/ppermute | solution.py:236
  27.5 0.7 copy-done.6
  28.2 1.5 shard_map.120.info
  29.8 0.5 collective-permute-start.11
  30.3 2.7 %collective-permute-start.7 = (bf16[128,512]{1,0:T(8,128)(2,1)S(1)}, bf16[128,512]{1,0:T(8,128)(2,1)S(1)}, u32[]{:S(2)}, u32[]{:S(2)}) collective-permute-start(bf16[128,512]{1,0:T(8,128)(2,1)S(1)} %collective-permute-done.3.refs_4_), channel_id=1, source_target_pairs={{0,224},{32,0},{64,32},{96,64},{128,96},{160,128},{192,160},{224,1... | collective-permute-start | bytes 393224 | tf_op jit(solution)/shard_map/ppermute | solution.py:239
  33.1 1.6 shard_map.121
  34.6 2.0 %collective-permute-done.6.refs_0_.refs_6_ = bf16[128,512]{1,0:T(8,128)(2,1)S(1)} collective-permute-done((bf16[128,512]{1,0:T(8,128)(2,1)S(1)}, bf16[128,512]{1,0:T(8,128)(2,1)S(1)}, u32[]{:S(2)}, u32[]{:S(2)}) %collective-permute-start.6) | collective-permute-done | bytes 131104 | tf_op jit(solution)/shard_map/ppermute | solution.py:239
  36.6 0.9 collective-permute-start.14
  37.5 1.0 collective-permute-done.14.refs_2_.refs_14_
  38.5 0.4 collective-permute-done.15.refs_3_.refs_15_
  38.8 2.7 %shard_map.122 = bf16[16,544,128]{2,1,0:T(8,128)(2,1)S(1)} custom-call(s32[128]{0:T(128)S(1)} %shard_map.120.info, bf16[12,128,512]{2,1,0:T(8,128)(2,1)S(1)} %get-tuple-element.31.proj, bf16[128,512]{1,0:T(8,128)(2,1)S(1)} %collective-permute-done.6.refs_0_.refs_6_, bf16[128,512]{1,0:T(8,128)(2,1)S(1)} %collective-permute-done.7.refs_1_.refs_7_, ...), custom_call_target="tpu_custom_call" | custom-call | flops 536870912 | bytes 8388608 | tf_op jit(solution)/shard_map/pallas_call | solution.py:280
  41.5 37.8 %all_to_all.25.parts = bf16[16,544,128]{2,1,0:T(8,128)(2,1)S(1)} all-to-all(bf16[16,544,128]{2,1,0:T(8,128)(2,1)S(1)} %shard_map.122), channel_id=1, replica_groups={{0,2,4,6,8,10,12,14,16,18,20,22,24,26,28,30},{1,3,5,7,9,11,13,15,17,19,..., dimensions={0} | all-to-all | bytes 4456448 | tf_op jit(solution)/shard_map/all_to_all | solution.py:242
  79.3 1.2 shard_map.123
  80.5 30.1 %all_to_all.26.grads = bf16[16,512,128]{2,1,0:T(8,128)(2,1)S(1)} all-to-all(bf16[16,512,128]{2,1,0:T(8,128)(2,1)S(1)} %get-tuple-element.36), channel_id=1, replica_groups={{0,2,4,6,8,10,12,14,16,18,20,22,24,26,28,30},{1,3,5,7,9,11,13,15,17,19,..., dimensions={0} | all-to-all | bytes 4194304 | tf_op jit(solution)/shard_map/all_to_all | solution.py:242
  110.6 3.0 %shard_map.124 = (f32[8,528,128]{2,1,0:T(8,128)S(1)}, bf16[8,528,128]{2,1,0:T(8,128)(2,1)S(1)}) custom-call(s32[128]{0:T(128)S(1)} %shard_map.120.info, bf16[16,512,128]{2,1,0:T(8,128)(2,1)S(1)} %all_to_all.26.grads, bf16[16,32,128]{2,1,0:T(8,128)(2,1)S(1)} %get-tuple-element.37.facts_t, bf16[32,128,128]{2,1,0:T(8,128)(2,1)S(1)} %copy-done.1, ...), custom_call_target="tpu_custom_call" | custom-call | flops 536870912 | bytes 9437184 | tf_op jit(solution)/shard_map/pallas_call | solution.py:303
  113.6 2.1 %collective-permute-start.17 = (bf16[8,528,128]{2,1,0:T(8,128)(2,1)S(1)}, bf16[8,528,128]{2,1,0:T(8,128)(2,1)S(1)}, u32[]{:S(2)}, u32[]{:S(2)}) collective-permute-start(bf16[8,528,128]{2,1,0:T(8,128)(2,1)S(1)} %get-tuple-element.39), channel_id=1, source_target_pairs={{0,1},{1,0},{2,3},{3,2},{4,5},{5,4},{6,7},{7,6},{8,9},{9,8},{10,11... | collective-permute-start | bytes 3244040 | tf_op jit(solution)/shard_map/ppermute | solution.py:236
  115.7 2.3 %collective-permute-done.17 = bf16[8,528,128]{2,1,0:T(8,128)(2,1)S(1)} collective-permute-done((bf16[8,528,128]{2,1,0:T(8,128)(2,1)S(1)}, bf16[8,528,128]{2,1,0:T(8,128)(2,1)S(1)}, u32[]{:S(2)}, u32[]{:S(2)}) %collective-permute-start.17) | collective-permute-done | bytes 1081376 | tf_op jit(solution)/shard_map/ppermute | solution.py:236
  118.1 2.2 %collective-permute-start.20 = (bf16[528,128]{1,0:T(8,128)(2,1)S(1)}, bf16[528,128]{1,0:T(8,128)(2,1)S(1)}, u32[]{:S(2)}, u32[]{:S(2)}) collective-permute-start(bf16[528,128]{1,0:T(8,128)(2,1)S(1)} %get-tuple-element.51), channel_id=1, source_target_pairs={{0,224},{32,0},{64,32},{96,64},{128,96},{160,128},{192,160},{224,1... | collective-permute-start | bytes 405512 | tf_op jit(solution)/shard_map/ppermute | solution.py:239
  120.4 3.1 %collective-permute-done.20 = bf16[528,128]{1,0:T(8,128)(2,1)S(1)} collective-permute-done((bf16[528,128]{1,0:T(8,128)(2,1)S(1)}, bf16[528,128]{1,0:T(8,128)(2,1)S(1)}, u32[]{:S(2)}, u32[]{:S(2)}) %collective-permute-start.20) | collective-permute-done | bytes 135200 | tf_op jit(solution)/shard_map/ppermute | solution.py:239
  123.4 7.4 %collective-permute-done.18 = bf16[528,128]{1,0:T(8,128)(2,1)S(1)} collective-permute-done((bf16[528,128]{1,0:T(8,128)(2,1)S(1)}, bf16[528,128]{1,0:T(8,128)(2,1)S(1)}, u32[]{:S(2)}, u32[]{:S(2)}) %collective-permute-start.18) | collective-permute-done | bytes 135200 | tf_op jit(solution)/shard_map/ppermute | solution.py:239
  131.1 1.5 collective-permute-start.19
  132.6 2.4 %collective-permute-done.21 = bf16[528,128]{1,0:T(8,128)(2,1)S(1)} collective-permute-done((bf16[528,128]{1,0:T(8,128)(2,1)S(1)}, bf16[528,128]{1,0:T(8,128)(2,1)S(1)}, u32[]{:S(2)}, u32[]{:S(2)}) %collective-permute-start.21) | collective-permute-done | bytes 135200 | tf_op jit(solution)/shard_map/ppermute | solution.py:239
  135.0 1.3 collective-permute-done.19
  136.5 1.4 collective-permute-start.23
  137.9 2.4 %collective-permute-done.24.from_above = bf16[528,128]{1,0:T(8,128)(2,1)S(1)} collective-permute-done((bf16[528,128]{1,0:T(8,128)(2,1)S(1)}, bf16[528,128]{1,0:T(8,128)(2,1)S(1)}, u32[]{:S(2)}, u32[]{:S(2)}) %collective-permute-start.24) | collective-permute-done | bytes 135200 | tf_op jit(solution)/shard_map/ppermute | solution.py:239
  140.3 1.3 collective-permute-done.23.from_below
  141.6 1.1 shard_map.125
  142.7 10.6 %all_to_all.27.parts = bf16[16,24,128]{2,1,0:T(8,128)(2,1)S(1)} all-to-all(bf16[16,24,128]{2,1,0:T(8,128)(2,1)S(1)} %bitcast.34), channel_id=1, replica_groups={{0,2,4,6,8,10,12,14,16,18,20,22,24,26,28,30},{1,3,5,7,9,11,13,15,17,19,..., dimensions={0} | all-to-all | bytes 196608 | tf_op jit(solution)/shard_map/all_to_all | solution.py:242
  153.3 0.6 shard_map.126
  153.8 11.0 %all_to_all.28 = bf16[8,96,128]{2,1,0:T(8,128)(2,1)S(1)} all-to-all(bf16[8,96,128]{2,1,0:T(8,128)(2,1)S(1)} %shard_map.126), channel_id=1, replica_groups=mesh['fact'=8,'dim'=32] {'fact'}, dimensions={0} | all-to-all | bytes 393216 | tf_op jit(solution)/shard_map/all_to_all | solution.py:245
  164.9 0.2 broadcast_in_dim.5
  165.1 14.7 %all_to_all.29.own = bf16[16,8,32,128]{3,2,1,0:T(8,128)(2,1)S(1)} all-to-all(bf16[16,8,32,128]{3,2,1,0:T(8,128)(2,1)S(1)} %broadcast_in_dim.5), channel_id=1, replica_groups={{0,2,4,6,8,10,12,14,16,18,20,22,24,26,28,30},{1,3,5,7,9,11,13,15,17,19,..., dimensions={0} | all-to-all | bytes 2097152 | tf_op jit(solution)/shard_map/all_to_all | solution.py:242
  179.8 8.2 %collective-permute-start.26 = (bf16[16,8,32,128]{3,2,1,0:T(8,128)(2,1)S(1)}, bf16[16,8,32,128]{3,2,1,0:T(8,128)(2,1)S(1)}, u32[]{:S(2)}, u32[]{:S(2)}) collective-permute-start(bf16[16,8,32,128]{3,2,1,0:T(8,128)(2,1)S(1)} %all_to_all.29.own), channel_id=1, source_target_pairs={{0,1},{1,0},{2,3},{3,2},{4,5},{5,4},{6,7},{7,6},{8,9},{9,8},{10,11... | collective-permute-start | bytes 3145736 | tf_op jit(solution)/shard_map/ppermute | solution.py:236
  188.0 2.4 %collective-permute-done.25.given = bf16[8,32,128]{2,1,0:T(8,128)(2,1)S(1)} collective-permute-done((bf16[8,32,128]{2,1,0:T(8,128)(2,1)S(1)}, bf16[8,32,128]{2,1,0:T(8,128)(2,1)S(1)}, u32[]{:S(2)}, u32[]{:S(2)}) %collective-permute-start.25) | collective-permute-done | bytes 65568 | tf_op jit(solution)/shard_map/ppermute | solution.py:236
  190.4 1.6 shard_map.127
  191.9 3.5 %shard_map.128 = (f32[512,512]{1,0:T(8,128)}, f32[3,512,512]{2,1,0:T(8,128)}) custom-call(s32[128]{0:T(128)S(1)} %shard_map.120.info, bf16[16,8,32,128]{3,2,1,0:T(8,128)(2,1)S(1)} %all_to_all.29.own, bf16[16,8,32,128]{3,2,1,0:T(8,128)(2,1)S(1)} %collective-permute-done.26.sib), custom_call_target="tpu_custom_call" | custom-call | bytes 8388608 | tf_op jit(solution)/shard_map/pallas_call | solution.py:351
  (42 shorter events, 0.8 us)
Async XLA Ops:
  0.6 38.2 %collective-permute-start.16 = (bf16[32,128,128]{2,1,0:T(8,128)(2,1)}, bf16[32,128,128]{2,1,0:T(8,128)(2,1)S(1)}, u32[]{:S(2)}, u32[]{:S(2)}) collective-permute-start(bf16[32,128,128]{2,1,0:T(8,128)(2,1)} %tiles_own.1), channel_id=1, source_target_pairs={{0,1},{1,0},{2,3},{3,2},{4,5},{5,4},{6,7},{7,6},{8,9},{9,8},{10,11... | collective-permute-start | bytes 3145736 | tf_op jit(solution)/shard_map/ppermute | solution.py:236
  4.0 7.0 %collective-permute-start.2 = (bf16[128,512]{1,0:T(8,128)(2,1)}, bf16[128,512]{1,0:T(8,128)(2,1)S(1)}, u32[]{:S(2)}, u32[]{:S(2)}) collective-permute-start(bf16[128,512]{1,0:T(8,128)(2,1)} %refs_0_.3), channel_id=1, source_target_pairs={{0,224},{32,0},{64,32},{96,64},{128,96},{160,128},{192,160},{224,1... | collective-permute-start | bytes 393224 | tf_op jit(solution)/shard_map/ppermute | solution.py:239
  7.8 6.9 %collective-permute-start = (bf16[128,512]{1,0:T(8,128)(2,1)}, bf16[128,512]{1,0:T(8,128)(2,1)S(1)}, u32[]{:S(2)}, u32[]{:S(2)}) collective-permute-start(bf16[128,512]{1,0:T(8,128)(2,1)} %refs_0_.3), channel_id=1, source_target_pairs={{0,32},{32,64},{64,96},{96,128},{128,160},{160,192},{192,224},{224... | collective-permute-start | bytes 393224 | tf_op jit(solution)/shard_map/ppermute | solution.py:239
  7.8 16.0 %collective-permute-start.4 = (bf16[128,512]{1,0:T(8,128)(2,1)}, bf16[128,512]{1,0:T(8,128)(2,1)S(1)}, u32[]{:S(2)}, u32[]{:S(2)}) collective-permute-start(bf16[128,512]{1,0:T(8,128)(2,1)} %refs_0_.3), channel_id=1, source_target_pairs={{0,128},{32,160},{64,192},{96,224},{128,0},{160,32},{192,64},{224,... | collective-permute-start | bytes 393224 | tf_op jit(solution)/shard_map/ppermute | solution.py:239
  11.0 13.0 %collective-permute-start.3 = (bf16[128,512]{1,0:T(8,128)(2,1)S(1)}, bf16[128,512]{1,0:T(8,128)(2,1)S(1)}, u32[]{:S(2)}, u32[]{:S(2)}) collective-permute-start(bf16[128,512]{1,0:T(8,128)(2,1)S(1)} %collective-permute-done.2.refs_2_), channel_id=1, source_target_pairs={{0,224},{32,0},{64,32},{96,64},{128,96},{160,128},{192,160},{224,1... | collective-permute-start | bytes 393224 | tf_op jit(solution)/shard_map/ppermute | solution.py:239
  14.7 9.6 %collective-permute-start.1 = (bf16[128,512]{1,0:T(8,128)(2,1)S(1)}, bf16[128,512]{1,0:T(8,128)(2,1)S(1)}, u32[]{:S(2)}, u32[]{:S(2)}) collective-permute-start(bf16[128,512]{1,0:T(8,128)(2,1)S(1)} %collective-permute-done.refs_1_), channel_id=1, source_target_pairs={{0,32},{32,64},{64,96},{96,128},{128,160},{160,192},{192,224},{224... | collective-permute-start | bytes 393224 | tf_op jit(solution)/shard_map/ppermute | solution.py:239
  16.1 7.4 %collective-permute-start.5 = (s32[2,33]{1,0:T(2,128)S(1)}, s32[2,33]{1,0:T(2,128)S(1)}, u32[]{:S(2)}, u32[]{:S(2)}) collective-permute-start(s32[2,33]{1,0:T(2,128)S(1)} %concatenate.3.links_own), channel_id=1, source_target_pairs={{0,1},{1,0},{2,3},{3,2},{4,5},{5,4},{6,7},{7,6},{8,9},{9,8},{10,11... | collective-permute-start | bytes 800 | tf_op jit(solution)/shard_map/ppermute | solution.py:236
  22.7 10.3 %copy-start = (bf16[3,512,512]{2,1,0:T(8,128)(2,1)S(1)}, bf16[3,512,512]{2,1,0:T(8,128)(2,1)}, u32[]{:S(2)}) copy-start(bf16[3,512,512]{2,1,0:T(8,128)(2,1)} %w.5) | copy-start | bytes 4718596
  22.7 10.3 %copy-start.2 = (bf16[128,512]{1,0:T(8,128)(2,1)S(1)}, bf16[128,512]{1,0:T(8,128)(2,1)}, u32[]{:S(2)}) copy-start(bf16[128,512]{1,0:T(8,128)(2,1)} %facts.3) | copy-start | bytes 393220
  22.7 10.3 %copy-start.3 = (bf16[128,512]{1,0:T(8,128)(2,1)S(1)}, bf16[128,512]{1,0:T(8,128)(2,1)}, u32[]{:S(2)}) copy-start(bf16[128,512]{1,0:T(8,128)(2,1)} %refs_0_.3) | copy-start | bytes 393220
  23.5 6.2 %collective-permute-start.8 = (bf16[128,512]{1,0:T(8,128)(2,1)}, bf16[128,512]{1,0:T(8,128)(2,1)S(1)}, u32[]{:S(2)}, u32[]{:S(2)}) collective-permute-start(bf16[128,512]{1,0:T(8,128)(2,1)} %refs_0_.3), channel_id=1, source_target_pairs={{0,1},{1,0},{2,3},{3,2},{4,5},{5,4},{6,7},{7,6},{8,9},{9,8},{10,11... | collective-permute-start | bytes 393224 | tf_op jit(solution)/shard_map/ppermute | solution.py:236
  23.8 6.0 %collective-permute-start.10 = (bf16[128,512]{1,0:T(8,128)(2,1)S(1)}, bf16[128,512]{1,0:T(8,128)(2,1)S(1)}, u32[]{:S(2)}, u32[]{:S(2)}) collective-permute-start(bf16[128,512]{1,0:T(8,128)(2,1)S(1)} %collective-permute-done.2.refs_2_), channel_id=1, source_target_pairs={{0,1},{1,0},{2,3},{3,2},{4,5},{5,4},{6,7},{7,6},{8,9},{9,8},{10,11... | collective-permute-start | bytes 393224 | tf_op jit(solution)/shard_map/ppermute | solution.py:236
  24.0 6.3 %collective-permute-start.9 = (bf16[128,512]{1,0:T(8,128)(2,1)S(1)}, bf16[128,512]{1,0:T(8,128)(2,1)S(1)}, u32[]{:S(2)}, u32[]{:S(2)}) collective-permute-start(bf16[128,512]{1,0:T(8,128)(2,1)S(1)} %collective-permute-done.refs_1_), channel_id=1, source_target_pairs={{0,1},{1,0},{2,3},{3,2},{4,5},{5,4},{6,7},{7,6},{8,9},{9,8},{10,11... | collective-permute-start | bytes 393224 | tf_op jit(solution)/shard_map/ppermute | solution.py:236
  24.3 6.0 %collective-permute-start.12 = (bf16[128,512]{1,0:T(8,128)(2,1)S(1)}, bf16[128,512]{1,0:T(8,128)(2,1)S(1)}, u32[]{:S(2)}, u32[]{:S(2)}) collective-permute-start(bf16[128,512]{1,0:T(8,128)(2,1)S(1)} %collective-permute-done.3.refs_4_), channel_id=1, source_target_pairs={{0,1},{1,0},{2,3},{3,2},{4,5},{5,4},{6,7},{7,6},{8,9},{9,8},{10,11... | collective-permute-start | bytes 393224 | tf_op jit(solution)/shard_map/ppermute | solution.py:236
  27.5 0.7 copy-start.6
  29.7 9.1 %copy-start.1 = (bf16[32,128,128]{2,1,0:T(8,128)(2,1)S(1)}, bf16[32,128,128]{2,1,0:T(8,128)(2,1)}, u32[]{:S(2)}) copy-start(bf16[32,128,128]{2,1,0:T(8,128)(2,1)} %tiles_own.1) | copy-start | bytes 3145732
  29.7 3.3 %collective-permute-start.13 = (bf16[128,512]{1,0:T(8,128)(2,1)S(1)}, bf16[128,512]{1,0:T(8,128)(2,1)S(1)}, u32[]{:S(2)}, u32[]{:S(2)}) collective-permute-start(bf16[128,512]{1,0:T(8,128)(2,1)S(1)} %collective-permute-done.4.refs_5_), channel_id=1, source_target_pairs={{0,1},{1,0},{2,3},{3,2},{4,5},{5,4},{6,7},{7,6},{8,9},{9,8},{10,11... | collective-permute-start | bytes 393224 | tf_op jit(solution)/shard_map/ppermute | solution.py:236
  29.8 3.2 %collective-permute-start.11 = (bf16[128,512]{1,0:T(8,128)(2,1)S(1)}, bf16[128,512]{1,0:T(8,128)(2,1)S(1)}, u32[]{:S(2)}, u32[]{:S(2)}) collective-permute-start(bf16[128,512]{1,0:T(8,128)(2,1)S(1)} %collective-permute-done.1.refs_3_), channel_id=1, source_target_pairs={{0,1},{1,0},{2,3},{3,2},{4,5},{5,4},{6,7},{7,6},{8,9},{9,8},{10,11... | collective-permute-start | bytes 393224 | tf_op jit(solution)/shard_map/ppermute | solution.py:236
  30.3 6.3 %collective-permute-start.6 = (bf16[128,512]{1,0:T(8,128)(2,1)S(1)}, bf16[128,512]{1,0:T(8,128)(2,1)S(1)}, u32[]{:S(2)}, u32[]{:S(2)}) collective-permute-start(bf16[128,512]{1,0:T(8,128)(2,1)S(1)} %collective-permute-done.1.refs_3_), channel_id=1, source_target_pairs={{0,32},{32,64},{64,96},{96,128},{128,160},{160,192},{192,224},{224... | collective-permute-start | bytes 393224 | tf_op jit(solution)/shard_map/ppermute | solution.py:239
  30.3 6.3 %collective-permute-start.7 = (bf16[128,512]{1,0:T(8,128)(2,1)S(1)}, bf16[128,512]{1,0:T(8,128)(2,1)S(1)}, u32[]{:S(2)}, u32[]{:S(2)}) collective-permute-start(bf16[128,512]{1,0:T(8,128)(2,1)S(1)} %collective-permute-done.3.refs_4_), channel_id=1, source_target_pairs={{0,224},{32,0},{64,32},{96,64},{128,96},{160,128},{192,160},{224,1... | collective-permute-start | bytes 393224 | tf_op jit(solution)/shard_map/ppermute | solution.py:239
  36.6 1.9 collective-permute-start.14
  37.5 1.3 collective-permute-start.15
  41.5 37.8 %copy-start.4 = (bf16[512,512]{1,0:T(8,128)(2,1)S(1)}, bf16[512,512]{1,0:T(8,128)(2,1)}, u32[]{:S(2)}) copy-start(bf16[512,512]{1,0:T(8,128)(2,1)} %w.4) | copy-start | bytes 1572868
  41.5 37.8 %copy-start.5 = (bf16[128,512]{1,0:T(8,128)(2,1)S(1)}, bf16[128,512]{1,0:T(8,128)(2,1)}, u32[]{:S(2)}) copy-start(bf16[128,512]{1,0:T(8,128)(2,1)} %cot.1) | copy-start | bytes 393220
  113.6 4.4 %collective-permute-start.17 = (bf16[8,528,128]{2,1,0:T(8,128)(2,1)S(1)}, bf16[8,528,128]{2,1,0:T(8,128)(2,1)S(1)}, u32[]{:S(2)}, u32[]{:S(2)}) collective-permute-start(bf16[8,528,128]{2,1,0:T(8,128)(2,1)S(1)} %get-tuple-element.39), channel_id=1, source_target_pairs={{0,1},{1,0},{2,3},{3,2},{4,5},{5,4},{6,7},{7,6},{8,9},{9,8},{10,11... | collective-permute-start | bytes 3244040 | tf_op jit(solution)/shard_map/ppermute | solution.py:236
  118.1 5.3 %collective-permute-start.20 = (bf16[528,128]{1,0:T(8,128)(2,1)S(1)}, bf16[528,128]{1,0:T(8,128)(2,1)S(1)}, u32[]{:S(2)}, u32[]{:S(2)}) collective-permute-start(bf16[528,128]{1,0:T(8,128)(2,1)S(1)} %get-tuple-element.51), channel_id=1, source_target_pairs={{0,224},{32,0},{64,32},{96,64},{128,96},{160,128},{192,160},{224,1... | collective-permute-start | bytes 405512 | tf_op jit(solution)/shard_map/ppermute | solution.py:239
  120.4 10.5 %collective-permute-start.18 = (bf16[528,128]{1,0:T(8,128)(2,1)S(1)}, bf16[528,128]{1,0:T(8,128)(2,1)S(1)}, u32[]{:S(2)}, u32[]{:S(2)}) collective-permute-start(bf16[528,128]{1,0:T(8,128)(2,1)S(1)} %get-tuple-element.52), channel_id=1, source_target_pairs={{0,32},{32,64},{64,96},{96,128},{128,160},{160,192},{192,224},{224... | collective-permute-start | bytes 405512 | tf_op jit(solution)/shard_map/ppermute | solution.py:239
  120.4 12.2 %collective-permute-start.22 = (bf16[528,128]{1,0:T(8,128)(2,1)S(1)}, bf16[528,128]{1,0:T(8,128)(2,1)S(1)}, u32[]{:S(2)}, u32[]{:S(2)}) collective-permute-start(bf16[528,128]{1,0:T(8,128)(2,1)S(1)} %get-tuple-element.50), channel_id=1, source_target_pairs={{0,128},{32,160},{64,192},{96,224},{128,0},{160,32},{192,64},{224,... | collective-permute-start | bytes 405512 | tf_op jit(solution)/shard_map/ppermute | solution.py:239
  131.0 3.9 %collective-permute-start.21 = (bf16[528,128]{1,0:T(8,128)(2,1)S(1)}, bf16[528,128]{1,0:T(8,128)(2,1)S(1)}, u32[]{:S(2)}, u32[]{:S(2)}) collective-permute-start(bf16[528,128]{1,0:T(8,128)(2,1)S(1)} %get-tuple-element.53), channel_id=1, source_target_pairs={{0,224},{32,0},{64,32},{96,64},{128,96},{160,128},{192,160},{224,1... | collective-permute-start | bytes 405512 | tf_op jit(solution)/shard_map/ppermute | solution.py:239
  131.1 5.2 %collective-permute-start.19 = (bf16[528,128]{1,0:T(8,128)(2,1)S(1)}, bf16[528,128]{1,0:T(8,128)(2,1)S(1)}, u32[]{:S(2)}, u32[]{:S(2)}) collective-permute-start(bf16[528,128]{1,0:T(8,128)(2,1)S(1)} %get-tuple-element.54), channel_id=1, source_target_pairs={{0,32},{32,64},{64,96},{96,128},{128,160},{160,192},{192,224},{224... | collective-permute-start | bytes 405512 | tf_op jit(solution)/shard_map/ppermute | solution.py:239
  136.4 3.9 %collective-permute-start.24 = (bf16[528,128]{1,0:T(8,128)(2,1)S(1)}, bf16[528,128]{1,0:T(8,128)(2,1)S(1)}, u32[]{:S(2)}, u32[]{:S(2)}) collective-permute-start(bf16[528,128]{1,0:T(8,128)(2,1)S(1)} %get-tuple-element.48), channel_id=1, source_target_pairs={{0,224},{32,0},{64,32},{96,64},{128,96},{160,128},{192,160},{224,1... | collective-permute-start | bytes 405512 | tf_op jit(solution)/shard_map/ppermute | solution.py:239
  136.5 5.1 %collective-permute-start.23 = (bf16[528,128]{1,0:T(8,128)(2,1)S(1)}, bf16[528,128]{1,0:T(8,128)(2,1)S(1)}, u32[]{:S(2)}, u32[]{:S(2)}) collective-permute-start(bf16[528,128]{1,0:T(8,128)(2,1)S(1)} %get-tuple-element.49), channel_id=1, source_target_pairs={{0,32},{32,64},{64,96},{96,128},{128,160},{160,192},{192,224},{224... | collective-permute-start | bytes 405512 | tf_op jit(solution)/shard_map/ppermute | solution.py:239
  179.8 12.1 %collective-permute-start.26 = (bf16[16,8,32,128]{3,2,1,0:T(8,128)(2,1)S(1)}, bf16[16,8,32,128]{3,2,1,0:T(8,128)(2,1)S(1)}, u32[]{:S(2)}, u32[]{:S(2)}) collective-permute-start(bf16[16,8,32,128]{3,2,1,0:T(8,128)(2,1)S(1)} %all_to_all.29.own), channel_id=1, source_target_pairs={{0,1},{1,0},{2,3},{3,2},{4,5},{5,4},{6,7},{7,6},{8,9},{9,8},{10,11... | collective-permute-start | bytes 3145736 | tf_op jit(solution)/shard_map/ppermute | solution.py:236
  188.0 2.4 %collective-permute-start.25 = (bf16[8,32,128]{2,1,0:T(8,128)(2,1)S(1)}, bf16[8,32,128]{2,1,0:T(8,128)(2,1)S(1)}, u32[]{:S(2)}, u32[]{:S(2)}) collective-permute-start(bf16[8,32,128]{2,1,0:T(8,128)(2,1)S(1)} %get-tuple-element.57), channel_id=1, source_target_pairs={{0,1},{1,0},{2,3},{3,2},{4,5},{5,4},{6,7},{7,6},{8,9},{9,8},{10,11... | collective-permute-start | bytes 196616 | tf_op jit(solution)/shard_map/ppermute | solution.py:236

commit v7 on v6

--- a/solution.py
+++ b/solution.py
@@ -13,8 +13,12 @@
 UNROLL = 4
 
 
-ORDER = (0, -1, 1, -2, 2, 4, -3, 3)
-EARLY = 6
+PIECES = [(0, 0, 0, 0), (0, 1, 1, 0)]
+for _step in (1, 2, 3):
+    PIECES += [(2 * _step - 1, 0, 0, -_step), (2 * _step - 1, 1, 1, -_step)]
+    PIECES += [(2 * _step, 0, 1, _step), (2 * _step, 1, 0, _step)]
+PIECES += [(7, 0, 0, 4), (8, 0, 1, 4)]
+EARLY = 10
 LIST = 40
 COUNT, KIND, PLACE, INFO = 80, 96, 112, 128
 
@@ -53,27 +57,27 @@
         info[KIND + 8 + h] = table[h * 32 + dim_pos + 1 - 2 * core]
 
 
+def holder_of(info, shift):
+    return (info[PLACE] + shift * (1 - 2 * info[PLACE + 2])) & 7
+
+
 def project_kernel(info, w, facts, *refs):
     early, (proj, facts_t) = refs[:-2], refs[-2:]
-    at = 0
-    for side in range(2):
-        for shift in ORDER[:EARLY]:
-            kind = info[KIND + side * 8 + ((info[PLACE] + shift) & 7)]
-            proj[at] = jnp.dot(early[at][...], w[kind], preferred_element_type=F32).astype(BF16)
-            at += 1
+    for at, (array, row, side, shift) in enumerate(PIECES[:EARLY]):
+        kind = info[KIND + side * 8 + holder_of(info, shift)]
+        proj[at] = jnp.dot(early[array][row], w[kind], preferred_element_type=F32).astype(BF16)
     facts_t[...] = facts[...].astype(F32).T.astype(BF16)
 
 
 def forward_kernel(info, proj, *refs):
-    late = len(ORDER) - EARLY
-    sides, (w, facts_t, tiles_own, tiles_sib, out, panel, acc) = (refs[:late], refs[late : 2 * late]), refs[2 * late :]
-    fact_pos = info[PLACE]
-    for side, pieces in enumerate(sides):
-        for at, shift in enumerate(ORDER[:EARLY]):
-            panel[side * 8 + ((fact_pos + shift) & 7)] = proj[side * EARLY + at]
-        for shift, rows in zip(ORDER[EARLY:], pieces):
-            h = (fact_pos + shift) & 7
-            value = jnp.dot(rows[...], w[info[KIND + side * 8 + h]], preferred_element_type=F32)
+    late, (w, facts_t, tiles_own, tiles_sib, out, panel, acc) = refs[:4], refs[4:]
+    for at, (array, row, side, shift) in enumerate(PIECES):
+        h = holder_of(info, shift)
+        if at < EARLY:
+            panel[side * 8 + h] = proj[at]
+        else:
+            kind = info[KIND + side * 8 + h]
+            value = jnp.dot(late[array - 5][row], w[kind], preferred_element_type=F32)
             panel[side * 8 + h] = value.astype(BF16)
     acc[...] = jnp.zeros_like(acc)
     for side, tiles in enumerate((tiles_own, tiles_sib)):
@@ -151,8 +155,8 @@
 
 
 def slice_kernel(info, kept, given, from_below, from_above, from_far, *refs):
-    pieces, (tab, gsum, self_piece, tacc) = refs[:16], refs[16:]
-    fact_pos, core = info[PLACE], info[PLACE + 2]
+    pieces, (tab, gsum, self_piece, tacc) = refs[:9], refs[9:]
+    core = info[PLACE + 2]
     total = kept[...]
     for arrived in (given, from_below, from_above, from_far):
         total = total + arrived[...].astype(F32)
@@ -160,13 +164,11 @@
     for at in range(16):
         gsum[at] = total[at * 32 : (at + 1) * 32].astype(BF16)
     tacc[...] = jnp.zeros_like(tacc)
-    for side in range(2):
-        column = 8 * (core if side == 0 else 1 - core)
-        for at, shift in enumerate(ORDER):
-            h = (fact_pos + shift) & 7
-            kind = info[KIND + side * 8 + h]
-            rows = pieces[side * 8 + at][...]
-            tacc[kind] += jnp.dot(gsum[column + h], rows, preferred_element_type=F32)
+    for array, row, side, shift in PIECES:
+        h = holder_of(info, shift)
+        kind = info[KIND + side * 8 + h]
+        grad = gsum[8 * (core if side == 0 else 1 - core) + h]
+        tacc[kind] += jnp.dot(grad, pieces[array][row], preferred_element_type=F32)
     for q in range(4):
         for t in range(3):
             at = q * 96 + t * 32
@@ -257,34 +259,39 @@
     )(place, links_own, links_sib, block_table)
     tiles_sib = swap(tiles)
 
-    far = shift(dims, 4)
-    pieces, up, down = [dims], dims, dims
-    for step in range(3):
-        if step == 2:
-            up, down, far, info = lax.optimization_barrier((up, down, far, info))
-            pieces.append(far)
-        up, down = shift(up, 1), shift(down, -1)
-        pieces += [up, down]
-    pieces, late = pieces[:EARLY], pieces[EARLY:]
-    pieces_sib = [swap(x) for x in pieces]
-    early = pieces + pieces_sib
+    around = [
+        (f * n_dim + d, (f + 1 - 2 * (d % 2)) % n_fact * n_dim + d) for f in range(n_fact) for d in range(n_dim)
+    ]
+
+    def along(x):
+        return lax.ppermute(x, ("fact", "dim"), around)
+
+    moving = jnp.stack([dims, swap(dims)])
+    early = [moving]
+    for step in range(2):
+        moving = along(moving)
+        early += [moving, swap(moving)]
+    moving, info = lax.optimization_barrier((moving, info))
+    moving = along(moving)
+    late = [moving, swap(moving)]
+    far = along(moving[:1])
     proj, facts_t = call(
         project_kernel,
-        (jax.ShapeDtypeStruct((len(early), rows, width), BF16), jax.ShapeDtypeStruct((width, block), BF16)),
+        (jax.ShapeDtypeStruct((EARLY, rows, width), BF16), jax.ShapeDtypeStruct((width, block), BF16)),
         [SMEM] + [VMEM] * (2 + len(early)),
-        flops=2 * len(early) * rows * width * width,
+        flops=2 * EARLY * rows * width * width,
         moved=4 << 20,
     )(info, w_tables, facts, *early)
-    *late, proj = lax.optimization_barrier((*late, proj))
-    pieces, pieces_sib = pieces + late, pieces_sib + [swap(x) for x in late]
+    far, proj = lax.optimization_barrier((far, proj))
+    late += [far, swap(far)]
     partial = call(
         forward_kernel,
         jax.ShapeDtypeStruct((chips, 544, 128), BF16),
-        [SMEM] + [VMEM] * (5 + 2 * len(late)),
+        [SMEM] + [VMEM] * (5 + len(late)),
         [pltpu.VMEM((2 * n_fact, rows, width), BF16), pltpu.VMEM((chips + 1, block, width), F32)],
         flops=2 * slots * block * block * width,
         moved=8 << 20,
-    )(info, proj, *pieces[EARLY:], *pieces_sib[EARLY:], w_tables, facts_t, tiles, tiles_sib)
+    )(info, proj, *late, w_tables, facts_t, tiles, tiles_sib)
     parts = by_chip(partial)
 
     fact_out, spread, facts_t = call(
@@ -328,11 +335,11 @@
             jax.ShapeDtypeStruct((2 * n_fact, 32, 128), BF16),
             jax.ShapeDtypeStruct((8, 128), F32),
         ),
-        [SMEM] + [VMEM] * 21,
+        [SMEM] + [VMEM] * 14,
         [pltpu.VMEM((3, 32, width), F32)],
         flops=4 * n_fact * 32 * 128 * width,
         moved=3 << 20,
-    )(info, keep[0], give[0], up, down, far, *pieces, *pieces_sib)
+    )(info, keep[0], give[0], up, down, far, *early, *late)
     tab = by_chip(tab.reshape(chips, 24, 128))
     packed = call(
         pack_kernel, jax.ShapeDtypeStruct((n_fact, 96, 128), BF16), [SMEM] + [VMEM] * 3, moved=1 << 19

time: 196 us -> 193 us (0.985)
  waiting for transfers between devices: 27.5 us -> 24.3 us
  blocking collectives: 104 us -> 102 us
    ppermute x0 -> x4, starting transfers between devices: none -> 13.3 us  [along(): return lax.ppermute(x, ('fact', 'dim'), around)]
    ppermute x14 -> x7, waiting for transfers between devices: 20.7 us -> 12.2 us  [shift(): lax.ppermute(x, 'fact', [(i, (i + by) % n_fact) for i in range(n_fact)])]
    ppermute x14 -> x7, starting transfers between devices: 18 us -> 10.9 us  [shift(): lax.ppermute(x, 'fact', [(i, (i + by) % n_fact) for i in range(n_fact)])]
    ppermute x13 -> x10, starting transfers between devices: 25.6 us -> 19.2 us  [swap(): return lax.ppermute(x, 'dim', pair)]
    ppermute x0 -> x4, waiting for transfers between devices: none -> 5.16 us  [along(): return lax.ppermute(x, ('fact', 'dim'), around)]
    all_to_all x4, blocking collectives: 93.2 us -> 89.2 us  [by_chip(): return lax.all_to_all(x, 'dim', 0, 0, tiled=True, axis_index_groups=same)]
    all_to_all x1, blocking collectives: 11 us -> 13.3 us  [by_fact(): return lax.all_to_all(x, 'fact', 0, 0, tiled=True)]
    ppermute x13 -> x10, waiting for transfers between devices: 6.81 us -> 6.91 us  [swap(): return lax.ppermute(x, 'dim', pair)]
  transfers between devices with their start and end apart: 27 -> 21, of which waited for: 14 -> 11; matrix products, arithmetic and copies ran while one was open for 0% -> 0% of each run, Pallas kernels for 2% -> 2%
where the time goes in v7:
time: 193 us
  blocking collectives  102 us (53%)
  starting transfers between devices  43.4 us (22%)
  waiting for transfers between devices  24.3 us (13%)
  Pallas kernels  18.3 us (9%)
    all_to_all x4, blocking collectives, by_chip(): return lax.all_to_all(x, 'dim', 0, 0, tiled=True, axis_index_groups=same)  89.2 us
    ppermute x10, starting transfers between devices, swap(): return lax.ppermute(x, 'dim', pair)  19.2 us
    ppermute x4, starting transfers between devices, along(): return lax.ppermute(x, ('fact', 'dim'), around)  13.3 us
    all_to_all x1, blocking collectives, by_fact(): return lax.all_to_all(x, 'fact', 0, 0, tiled=True)  13.3 us
    ppermute x7, waiting for transfers between devices, shift(): lax.ppermute(x, 'fact', [(i, (i + by) % n_fact) for i in range(n_fact)])  12.2 us
    ppermute x7, starting transfers between devices, shift(): lax.ppermute(x, 'fact', [(i, (i + by) % n_fact) for i in range(n_fact)])  10.9 us
    ppermute x10, waiting for transfers between devices, swap(): return lax.ppermute(x, 'dim', pair)  6.91 us
    ppermute x4, waiting for transfers between devices, along(): return lax.ppermute(x, ('fact', 'dim'), around)  5.16 us
  transfers between devices with their start and end apart: 21, of which 11 were waited for; matrix products, arithmetic and copies ran while one was open for 0% of the time, Pallas kernels for 2%

profile of v7, /device:TPU:1, one launch (start us, length us, event | category | flops | bytes accessed | tf_op | source)
XLA Modules:
  0.0 193.0 jit_solution(11944066594797370229)
XLA Ops:
  0.6 3.3 %collective-permute-start = (bf16[128,512]{1,0:T(8,128)(2,1)}, bf16[128,512]{1,0:T(8,128)(2,1)S(1)}, u32[]{:S(2)}, u32[]{:S(2)}) collective-permute-start(bf16[128,512]{1,0:T(8,128)(2,1)} %param.10), channel_id=1, source_target_pairs={{0,1},{1,0},{2,3},{3,2},{4,5},{5,4},{6,7},{7,6},{8,9},{9,8},{10,11... | collective-permute-start | bytes 393224 | tf_op jit(solution)/shard_map/ppermute | solution.py:238
  4.0 1.2 collective-permute-done
  5.2 0.9 pad_maximum_fusion.refs_0_
  6.1 3.9 %collective-permute-start.1 = (bf16[2,128,512]{2,1,0:T(8,128)(2,1)S(1)}, bf16[2,128,512]{2,1,0:T(8,128)(2,1)S(1)}, u32[]{:S(2)}, u32[]{:S(2)}) collective-permute-start(bf16[2,128,512]{2,1,0:T(8,128)(2,1)S(1)} %pad_maximum_fusion.refs_0_), channel_id=1, source_target_pairs={{0,32},{1,225},{2,34},{3,227},{4,36},{5,229},{6,38},{7,231},{8,40}... | collective-permute-start | bytes 786440 | tf_op jit(solution)/shard_map/ppermute | solution.py:267
  10.7 0.7 concatenate.3.links_own
  11.3 0.5 collective-permute-start.3
  11.9 1.5 collective-permute-done.1.refs_1_
  13.3 3.1 %collective-permute-start.2 = (bf16[2,128,512]{2,1,0:T(8,128)(2,1)S(1)}, bf16[2,128,512]{2,1,0:T(8,128)(2,1)S(1)}, u32[]{:S(2)}, u32[]{:S(2)}) collective-permute-start(bf16[2,128,512]{2,1,0:T(8,128)(2,1)S(1)} %collective-permute-done.1.refs_1_), channel_id=1, source_target_pairs={{0,32},{1,225},{2,34},{3,227},{4,36},{5,229},{6,38},{7,231},{8,40}... | collective-permute-start | bytes 786440 | tf_op jit(solution)/shard_map/ppermute | solution.py:267
  16.5 0.8 copy-done.5
  17.3 1.5 shard_map.120.info
  18.9 0.9 collective-permute-done.2.refs_3_
  19.8 3.1 %collective-permute-start.4 = (bf16[2,128,512]{2,1,0:T(8,128)(2,1)S(1)}, bf16[2,128,512]{2,1,0:T(8,128)(2,1)S(1)}, u32[]{:S(2)}, u32[]{:S(2)}) collective-permute-start(bf16[2,128,512]{2,1,0:T(8,128)(2,1)S(1)} %collective-permute-done.2.refs_3_), channel_id=1, source_target_pairs={{0,32},{1,225},{2,34},{3,227},{4,36},{5,229},{6,38},{7,231},{8,40}... | collective-permute-start | bytes 786440 | tf_op jit(solution)/shard_map/ppermute | solution.py:267
  22.9 0.5 collective-permute-start.7
  23.4 2.8 %collective-permute-done.4.refs_0_.refs_5_ = bf16[2,128,512]{2,1,0:T(8,128)(2,1)S(1)} collective-permute-done((bf16[2,128,512]{2,1,0:T(8,128)(2,1)S(1)}, bf16[2,128,512]{2,1,0:T(8,128)(2,1)S(1)}, u32[]{:S(2)}, u32[]{:S(2)}) %collective-permute-start.4) | collective-permute-done | bytes 262176 | tf_op jit(solution)/shard_map/ppermute | solution.py:267
  26.2 3.2 %collective-permute-start.5 = (bf16[1,128,512]{2,1,0:T(8,128)(2,1)S(1)}, bf16[1,128,512]{2,1,0:T(8,128)(2,1)S(1)}, u32[]{:S(2)}, u32[]{:S(2)}) collective-permute-start(bf16[1,128,512]{2,1,0:T(8,128)(2,1)S(1)} %slice.80), channel_id=1, source_target_pairs={{0,32},{1,225},{2,34},{3,227},{4,36},{5,229},{6,38},{7,231},{8,40}... | collective-permute-start | bytes 393224 | tf_op jit(solution)/shard_map/ppermute | solution.py:267
  29.4 1.0 collective-permute-start.8
  30.4 1.4 shard_map.121
  31.8 4.6 %collective-permute-start.9 = (bf16[1,128,512]{2,1,0:T(8,128)(2,1)S(1)}, bf16[1,128,512]{2,1,0:T(8,128)(2,1)S(1)}, u32[]{:S(2)}, u32[]{:S(2)}) collective-permute-start(bf16[1,128,512]{2,1,0:T(8,128)(2,1)S(1)} %collective-permute-done.5.refs_2_.refs_7_), channel_id=1, source_target_pairs={{0,1},{1,0},{2,3},{3,2},{4,5},{5,4},{6,7},{7,6},{8,9},{9,8},{10,11... | collective-permute-start | bytes 393224 | tf_op jit(solution)/shard_map/ppermute | solution.py:238
  36.4 1.0 collective-permute-done.9.refs_3_.refs_8_
  37.4 3.6 %shard_map.122 = bf16[16,544,128]{2,1,0:T(8,128)(2,1)S(1)} custom-call(s32[128]{0:T(128)S(1)} %shard_map.120.info, bf16[10,128,512]{2,1,0:T(8,128)(2,1)S(1)} %get-tuple-element.26.proj, bf16[2,128,512]{2,1,0:T(8,128)(2,1)S(1)} %collective-permute-done.4.refs_0_.refs_5_, bf16[2,128,512]{2,1,0:T(8,128)(2,1)S(1)} %collective-permute-done.8.refs_1_.refs_6_, ...), custom_call_target="tpu_custom_call" | custom-call | flops 536870912 | bytes 8388608 | tf_op jit(solution)/shard_map/pallas_call | solution.py:287
  41.1 34.9 %all_to_all.25.parts = bf16[16,544,128]{2,1,0:T(8,128)(2,1)S(1)} all-to-all(bf16[16,544,128]{2,1,0:T(8,128)(2,1)S(1)} %shard_map.122), channel_id=1, replica_groups={{0,2,4,6,8,10,12,14,16,18,20,22,24,26,28,30},{1,3,5,7,9,11,13,15,17,19,..., dimensions={0} | all-to-all | bytes 4456448 | tf_op jit(solution)/shard_map/all_to_all | solution.py:244
  76.0 1.2 shard_map.123
  77.2 30.1 %all_to_all.26.grads = bf16[16,512,128]{2,1,0:T(8,128)(2,1)S(1)} all-to-all(bf16[16,512,128]{2,1,0:T(8,128)(2,1)S(1)} %get-tuple-element.30), channel_id=1, replica_groups={{0,2,4,6,8,10,12,14,16,18,20,22,24,26,28,30},{1,3,5,7,9,11,13,15,17,19,..., dimensions={0} | all-to-all | bytes 4194304 | tf_op jit(solution)/shard_map/all_to_all | solution.py:244
  107.3 3.9 %shard_map.124 = (f32[8,528,128]{2,1,0:T(8,128)S(1)}, bf16[8,528,128]{2,1,0:T(8,128)(2,1)S(1)}) custom-call(s32[128]{0:T(128)S(1)} %shard_map.120.info, bf16[16,512,128]{2,1,0:T(8,128)(2,1)S(1)} %all_to_all.26.grads, bf16[16,32,128]{2,1,0:T(8,128)(2,1)S(1)} %get-tuple-element.31.facts_t, bf16[32,128,128]{2,1,0:T(8,128)(2,1)S(1)} %copy-done.1, ...), custom_call_target="tpu_custom_call" | custom-call | flops 536870912 | bytes 9437184 | tf_op jit(solution)/shard_map/pallas_call | solution.py:310
  111.2 2.8 %collective-permute-start.11 = (bf16[8,528,128]{2,1,0:T(8,128)(2,1)S(1)}, bf16[8,528,128]{2,1,0:T(8,128)(2,1)S(1)}, u32[]{:S(2)}, u32[]{:S(2)}) collective-permute-start(bf16[8,528,128]{2,1,0:T(8,128)(2,1)S(1)} %get-tuple-element.33), channel_id=1, source_target_pairs={{0,1},{1,0},{2,3},{3,2},{4,5},{5,4},{6,7},{7,6},{8,9},{9,8},{10,11... | collective-permute-start | bytes 3244040 | tf_op jit(solution)/shard_map/ppermute | solution.py:238
  114.0 2.3 %collective-permute-done.11 = bf16[8,528,128]{2,1,0:T(8,128)(2,1)S(1)} collective-permute-done((bf16[8,528,128]{2,1,0:T(8,128)(2,1)S(1)}, bf16[8,528,128]{2,1,0:T(8,128)(2,1)S(1)}, u32[]{:S(2)}, u32[]{:S(2)}) %collective-permute-start.11) | collective-permute-done | bytes 1081376 | tf_op jit(solution)/shard_map/ppermute | solution.py:238
  116.3 0.1 fusion.6
  116.5 1.5 collective-permute-start.12
  118.0 4.8 %collective-permute-start.16 = (bf16[528,128]{1,0:T(8,128)(2,1)S(1)}, bf16[528,128]{1,0:T(8,128)(2,1)S(1)}, u32[]{:S(2)}, u32[]{:S(2)}) collective-permute-start(bf16[528,128]{1,0:T(8,128)(2,1)S(1)} %get-tuple-element.44), channel_id=1, source_target_pairs={{0,128},{32,160},{64,192},{96,224},{128,0},{160,32},{192,64},{224,... | collective-permute-start | bytes 405512 | tf_op jit(solution)/shard_map/ppermute | solution.py:241
  122.8 0.2 collective-permute-done.12
  123.0 0.1 fusion.1
  123.1 1.1 collective-permute-start.15
  124.3 0.4 collective-permute-start.13
  124.7 6.9 %collective-permute-done.16.from_far = bf16[528,128]{1,0:T(8,128)(2,1)S(1)} collective-permute-done((bf16[528,128]{1,0:T(8,128)(2,1)S(1)}, bf16[528,128]{1,0:T(8,128)(2,1)S(1)}, u32[]{:S(2)}, u32[]{:S(2)}) %collective-permute-start.16) | collective-permute-done | bytes 135200 | tf_op jit(solution)/shard_map/ppermute | solution.py:241
  131.6 0.1 fusion
  131.7 3.0 %collective-permute-start.18 = (bf16[528,128]{1,0:T(8,128)(2,1)S(1)}, bf16[528,128]{1,0:T(8,128)(2,1)S(1)}, u32[]{:S(2)}, u32[]{:S(2)}) collective-permute-start(bf16[528,128]{1,0:T(8,128)(2,1)S(1)} %get-tuple-element.42), channel_id=1, source_target_pairs={{0,224},{32,0},{64,32},{96,64},{128,96},{160,128},{192,160},{224,1... | collective-permute-start | bytes 405512 | tf_op jit(solution)/shard_map/ppermute | solution.py:241
  134.7 2.0 %collective-permute-done.18.from_above = bf16[528,128]{1,0:T(8,128)(2,1)S(1)} collective-permute-done((bf16[528,128]{1,0:T(8,128)(2,1)S(1)}, bf16[528,128]{1,0:T(8,128)(2,1)S(1)}, u32[]{:S(2)}, u32[]{:S(2)}) %collective-permute-start.18) | collective-permute-done | bytes 135200 | tf_op jit(solution)/shard_map/ppermute | solution.py:241
  136.7 3.1 %collective-permute-done.17.from_below = bf16[528,128]{1,0:T(8,128)(2,1)S(1)} collective-permute-done((bf16[528,128]{1,0:T(8,128)(2,1)S(1)}, bf16[528,128]{1,0:T(8,128)(2,1)S(1)}, u32[]{:S(2)}, u32[]{:S(2)}) %collective-permute-start.17) | collective-permute-done | bytes 135200 | tf_op jit(solution)/shard_map/ppermute | solution.py:241
  139.7 1.1 shard_map.125
  140.8 9.2 %all_to_all.27.parts = bf16[16,24,128]{2,1,0:T(8,128)(2,1)S(1)} all-to-all(bf16[16,24,128]{2,1,0:T(8,128)(2,1)S(1)} %bitcast.36), channel_id=1, replica_groups={{0,2,4,6,8,10,12,14,16,18,20,22,24,26,28,30},{1,3,5,7,9,11,13,15,17,19,..., dimensions={0} | all-to-all | bytes 196608 | tf_op jit(solution)/shard_map/all_to_all | solution.py:244
  150.1 0.6 shard_map.126
  150.6 13.3 %all_to_all.28 = bf16[8,96,128]{2,1,0:T(8,128)(2,1)S(1)} all-to-all(bf16[8,96,128]{2,1,0:T(8,128)(2,1)S(1)} %shard_map.126), channel_id=1, replica_groups=mesh['fact'=8,'dim'=32] {'fact'}, dimensions={0} | all-to-all | bytes 393216 | tf_op jit(solution)/shard_map/all_to_all | solution.py:247
  164.0 0.2 broadcast_in_dim.5
  164.2 14.9 %all_to_all.29.own = bf16[16,8,32,128]{3,2,1,0:T(8,128)(2,1)S(1)} all-to-all(bf16[16,8,32,128]{3,2,1,0:T(8,128)(2,1)S(1)} %broadcast_in_dim.5), channel_id=1, replica_groups={{0,2,4,6,8,10,12,14,16,18,20,22,24,26,28,30},{1,3,5,7,9,11,13,15,17,19,..., dimensions={0} | all-to-all | bytes 2097152 | tf_op jit(solution)/shard_map/all_to_all | solution.py:244
  179.1 6.5 %collective-permute-start.20 = (bf16[16,8,32,128]{3,2,1,0:T(8,128)(2,1)S(1)}, bf16[16,8,32,128]{3,2,1,0:T(8,128)(2,1)S(1)}, u32[]{:S(2)}, u32[]{:S(2)}) collective-permute-start(bf16[16,8,32,128]{3,2,1,0:T(8,128)(2,1)S(1)} %all_to_all.29.own), channel_id=1, source_target_pairs={{0,1},{1,0},{2,3},{3,2},{4,5},{5,4},{6,7},{7,6},{8,9},{9,8},{10,11... | collective-permute-start | bytes 3145736 | tf_op jit(solution)/shard_map/ppermute | solution.py:238
  185.6 2.4 %collective-permute-done.19.given = bf16[8,32,128]{2,1,0:T(8,128)(2,1)S(1)} collective-permute-done((bf16[8,32,128]{2,1,0:T(8,128)(2,1)S(1)}, bf16[8,32,128]{2,1,0:T(8,128)(2,1)S(1)}, u32[]{:S(2)}, u32[]{:S(2)}) %collective-permute-start.19) | collective-permute-done | bytes 65568 | tf_op jit(solution)/shard_map/ppermute | solution.py:238
  188.0 1.6 shard_map.127
  189.5 3.5 %shard_map.128 = (f32[512,512]{1,0:T(8,128)}, f32[3,512,512]{2,1,0:T(8,128)}) custom-call(s32[128]{0:T(128)S(1)} %shard_map.120.info, bf16[16,8,32,128]{3,2,1,0:T(8,128)(2,1)S(1)} %all_to_all.29.own, bf16[16,8,32,128]{3,2,1,0:T(8,128)(2,1)S(1)} %collective-permute-done.20.sib), custom_call_target="tpu_custom_call" | custom-call | bytes 8388608 | tf_op jit(solution)/shard_map/pallas_call | solution.py:358
  (30 shorter events, 0.3 us)
Async XLA Ops:
  0.6 4.5 %collective-permute-start = (bf16[128,512]{1,0:T(8,128)(2,1)}, bf16[128,512]{1,0:T(8,128)(2,1)S(1)}, u32[]{:S(2)}, u32[]{:S(2)}) collective-permute-start(bf16[128,512]{1,0:T(8,128)(2,1)} %param.10), channel_id=1, source_target_pairs={{0,1},{1,0},{2,3},{3,2},{4,5},{5,4},{6,7},{7,6},{8,9},{9,8},{10,11... | collective-permute-start | bytes 393224 | tf_op jit(solution)/shard_map/ppermute | solution.py:238
  6.1 7.2 %collective-permute-start.1 = (bf16[2,128,512]{2,1,0:T(8,128)(2,1)S(1)}, bf16[2,128,512]{2,1,0:T(8,128)(2,1)S(1)}, u32[]{:S(2)}, u32[]{:S(2)}) collective-permute-start(bf16[2,128,512]{2,1,0:T(8,128)(2,1)S(1)} %pad_maximum_fusion.refs_0_), channel_id=1, source_target_pairs={{0,32},{1,225},{2,34},{3,227},{4,36},{5,229},{6,38},{7,231},{8,40}... | collective-permute-start | bytes 786440 | tf_op jit(solution)/shard_map/ppermute | solution.py:267
  10.0 26.4 %collective-permute-start.10 = (bf16[32,128,128]{2,1,0:T(8,128)(2,1)}, bf16[32,128,128]{2,1,0:T(8,128)(2,1)S(1)}, u32[]{:S(2)}, u32[]{:S(2)}) collective-permute-start(bf16[32,128,128]{2,1,0:T(8,128)(2,1)} %tiles_own.1), channel_id=1, source_target_pairs={{0,1},{1,0},{2,3},{3,2},{4,5},{5,4},{6,7},{7,6},{8,9},{9,8},{10,11... | collective-permute-start | bytes 3145736 | tf_op jit(solution)/shard_map/ppermute | solution.py:238
  11.3 5.2 %collective-permute-start.3 = (s32[2,33]{1,0:T(2,128)S(1)}, s32[2,33]{1,0:T(2,128)S(1)}, u32[]{:S(2)}, u32[]{:S(2)}) collective-permute-start(s32[2,33]{1,0:T(2,128)S(1)} %concatenate.3.links_own), channel_id=1, source_target_pairs={{0,1},{1,0},{2,3},{3,2},{4,5},{5,4},{6,7},{7,6},{8,9},{9,8},{10,11... | collective-permute-start | bytes 800 | tf_op jit(solution)/shard_map/ppermute | solution.py:238
  13.3 6.4 %collective-permute-start.2 = (bf16[2,128,512]{2,1,0:T(8,128)(2,1)S(1)}, bf16[2,128,512]{2,1,0:T(8,128)(2,1)S(1)}, u32[]{:S(2)}, u32[]{:S(2)}) collective-permute-start(bf16[2,128,512]{2,1,0:T(8,128)(2,1)S(1)} %collective-permute-done.1.refs_1_), channel_id=1, source_target_pairs={{0,32},{1,225},{2,34},{3,227},{4,36},{5,229},{6,38},{7,231},{8,40}... | collective-permute-start | bytes 786440 | tf_op jit(solution)/shard_map/ppermute | solution.py:267
  16.5 13.9 %copy-start = (bf16[3,512,512]{2,1,0:T(8,128)(2,1)S(1)}, bf16[3,512,512]{2,1,0:T(8,128)(2,1)}, u32[]{:S(2)}) copy-start(bf16[3,512,512]{2,1,0:T(8,128)(2,1)} %w.5) | copy-start | bytes 4718596
  16.5 13.9 %copy-start.2 = (bf16[128,512]{1,0:T(8,128)(2,1)S(1)}, bf16[128,512]{1,0:T(8,128)(2,1)}, u32[]{:S(2)}) copy-start(bf16[128,512]{1,0:T(8,128)(2,1)} %facts.3) | copy-start | bytes 393220
  16.5 0.8 copy-start.5
  18.9 18.6 %copy-start.1 = (bf16[32,128,128]{2,1,0:T(8,128)(2,1)S(1)}, bf16[32,128,128]{2,1,0:T(8,128)(2,1)}, u32[]{:S(2)}) copy-start(bf16[32,128,128]{2,1,0:T(8,128)(2,1)} %tiles_own.1) | copy-start | bytes 3145732
  19.8 6.4 %collective-permute-start.4 = (bf16[2,128,512]{2,1,0:T(8,128)(2,1)S(1)}, bf16[2,128,512]{2,1,0:T(8,128)(2,1)S(1)}, u32[]{:S(2)}, u32[]{:S(2)}) collective-permute-start(bf16[2,128,512]{2,1,0:T(8,128)(2,1)S(1)} %collective-permute-done.2.refs_3_), channel_id=1, source_target_pairs={{0,32},{1,225},{2,34},{3,227},{4,36},{5,229},{6,38},{7,231},{8,40}... | collective-permute-start | bytes 786440 | tf_op jit(solution)/shard_map/ppermute | solution.py:267
  22.9 7.5 %collective-permute-start.6 = (bf16[2,128,512]{2,1,0:T(8,128)(2,1)S(1)}, bf16[2,128,512]{2,1,0:T(8,128)(2,1)S(1)}, u32[]{:S(2)}, u32[]{:S(2)}) collective-permute-start(bf16[2,128,512]{2,1,0:T(8,128)(2,1)S(1)} %collective-permute-done.1.refs_1_), channel_id=1, source_target_pairs={{0,1},{1,0},{2,3},{3,2},{4,5},{5,4},{6,7},{7,6},{8,9},{9,8},{10,11... | collective-permute-start | bytes 786440 | tf_op jit(solution)/shard_map/ppermute | solution.py:238
  22.9 7.5 %collective-permute-start.7 = (bf16[2,128,512]{2,1,0:T(8,128)(2,1)S(1)}, bf16[2,128,512]{2,1,0:T(8,128)(2,1)S(1)}, u32[]{:S(2)}, u32[]{:S(2)}) collective-permute-start(bf16[2,128,512]{2,1,0:T(8,128)(2,1)S(1)} %collective-permute-done.2.refs_3_), channel_id=1, source_target_pairs={{0,1},{1,0},{2,3},{3,2},{4,5},{5,4},{6,7},{7,6},{8,9},{9,8},{10,11... | collective-permute-start | bytes 786440 | tf_op jit(solution)/shard_map/ppermute | solution.py:238
  26.2 5.6 %collective-permute-start.5 = (bf16[1,128,512]{2,1,0:T(8,128)(2,1)S(1)}, bf16[1,128,512]{2,1,0:T(8,128)(2,1)S(1)}, u32[]{:S(2)}, u32[]{:S(2)}) collective-permute-start(bf16[1,128,512]{2,1,0:T(8,128)(2,1)S(1)} %slice.80), channel_id=1, source_target_pairs={{0,32},{1,225},{2,34},{3,227},{4,36},{5,229},{6,38},{7,231},{8,40}... | collective-permute-start | bytes 393224 | tf_op jit(solution)/shard_map/ppermute | solution.py:267
  29.4 8.0 %collective-permute-start.8 = (bf16[2,128,512]{2,1,0:T(8,128)(2,1)S(1)}, bf16[2,128,512]{2,1,0:T(8,128)(2,1)S(1)}, u32[]{:S(2)}, u32[]{:S(2)}) collective-permute-start(bf16[2,128,512]{2,1,0:T(8,128)(2,1)S(1)} %collective-permute-done.4.refs_0_.refs_5_), channel_id=1, source_target_pairs={{0,1},{1,0},{2,3},{3,2},{4,5},{5,4},{6,7},{7,6},{8,9},{9,8},{10,11... | collective-permute-start | bytes 786440 | tf_op jit(solution)/shard_map/ppermute | solution.py:238
  31.8 5.6 %collective-permute-start.9 = (bf16[1,128,512]{2,1,0:T(8,128)(2,1)S(1)}, bf16[1,128,512]{2,1,0:T(8,128)(2,1)S(1)}, u32[]{:S(2)}, u32[]{:S(2)}) collective-permute-start(bf16[1,128,512]{2,1,0:T(8,128)(2,1)S(1)} %collective-permute-done.5.refs_2_.refs_7_), channel_id=1, source_target_pairs={{0,1},{1,0},{2,3},{3,2},{4,5},{5,4},{6,7},{7,6},{8,9},{9,8},{10,11... | collective-permute-start | bytes 393224 | tf_op jit(solution)/shard_map/ppermute | solution.py:238
  41.1 34.9 %copy-start.3 = (bf16[512,512]{1,0:T(8,128)(2,1)S(1)}, bf16[512,512]{1,0:T(8,128)(2,1)}, u32[]{:S(2)}) copy-start(bf16[512,512]{1,0:T(8,128)(2,1)} %w.4) | copy-start | bytes 1572868
  41.1 34.9 %copy-start.4 = (bf16[128,512]{1,0:T(8,128)(2,1)S(1)}, bf16[128,512]{1,0:T(8,128)(2,1)}, u32[]{:S(2)}) copy-start(bf16[128,512]{1,0:T(8,128)(2,1)} %cot.1) | copy-start | bytes 393220
  111.2 5.1 %collective-permute-start.11 = (bf16[8,528,128]{2,1,0:T(8,128)(2,1)S(1)}, bf16[8,528,128]{2,1,0:T(8,128)(2,1)S(1)}, u32[]{:S(2)}, u32[]{:S(2)}) collective-permute-start(bf16[8,528,128]{2,1,0:T(8,128)(2,1)S(1)} %get-tuple-element.33), channel_id=1, source_target_pairs={{0,1},{1,0},{2,3},{3,2},{4,5},{5,4},{6,7},{7,6},{8,9},{9,8},{10,11... | collective-permute-start | bytes 3244040 | tf_op jit(solution)/shard_map/ppermute | solution.py:238
  116.4 6.3 %collective-permute-start.14 = (bf16[528,128]{1,0:T(8,128)(2,1)S(1)}, bf16[528,128]{1,0:T(8,128)(2,1)S(1)}, u32[]{:S(2)}, u32[]{:S(2)}) collective-permute-start(bf16[528,128]{1,0:T(8,128)(2,1)S(1)} %get-tuple-element.45), channel_id=1, source_target_pairs={{0,224},{32,0},{64,32},{96,64},{128,96},{160,128},{192,160},{224,1... | collective-permute-start | bytes 405512 | tf_op jit(solution)/shard_map/ppermute | solution.py:241
  116.5 6.5 %collective-permute-start.12 = (bf16[528,128]{1,0:T(8,128)(2,1)S(1)}, bf16[528,128]{1,0:T(8,128)(2,1)S(1)}, u32[]{:S(2)}, u32[]{:S(2)}) collective-permute-start(bf16[528,128]{1,0:T(8,128)(2,1)S(1)} %get-tuple-element.46), channel_id=1, source_target_pairs={{0,32},{32,64},{64,96},{96,128},{128,160},{160,192},{192,224},{224... | collective-permute-start | bytes 405512 | tf_op jit(solution)/shard_map/ppermute | solution.py:241
  118.0 13.6 %collective-permute-start.16 = (bf16[528,128]{1,0:T(8,128)(2,1)S(1)}, bf16[528,128]{1,0:T(8,128)(2,1)S(1)}, u32[]{:S(2)}, u32[]{:S(2)}) collective-permute-start(bf16[528,128]{1,0:T(8,128)(2,1)S(1)} %get-tuple-element.44), channel_id=1, source_target_pairs={{0,128},{32,160},{64,192},{96,224},{128,0},{160,32},{192,64},{224,... | collective-permute-start | bytes 405512 | tf_op jit(solution)/shard_map/ppermute | solution.py:241
  123.1 8.4 %collective-permute-start.15 = (bf16[528,128]{1,0:T(8,128)(2,1)S(1)}, bf16[528,128]{1,0:T(8,128)(2,1)S(1)}, u32[]{:S(2)}, u32[]{:S(2)}) collective-permute-start(bf16[528,128]{1,0:T(8,128)(2,1)S(1)} %get-tuple-element.47), channel_id=1, source_target_pairs={{0,224},{32,0},{64,32},{96,64},{128,96},{160,128},{192,160},{224,1... | collective-permute-start | bytes 405512 | tf_op jit(solution)/shard_map/ppermute | solution.py:241
  124.3 7.3 %collective-permute-start.13 = (bf16[528,128]{1,0:T(8,128)(2,1)S(1)}, bf16[528,128]{1,0:T(8,128)(2,1)S(1)}, u32[]{:S(2)}, u32[]{:S(2)}) collective-permute-start(bf16[528,128]{1,0:T(8,128)(2,1)S(1)} %get-tuple-element.48), channel_id=1, source_target_pairs={{0,32},{32,64},{64,96},{96,128},{128,160},{160,192},{192,224},{224... | collective-permute-start | bytes 405512 | tf_op jit(solution)/shard_map/ppermute | solution.py:241
  131.7 5.0 %collective-permute-start.18 = (bf16[528,128]{1,0:T(8,128)(2,1)S(1)}, bf16[528,128]{1,0:T(8,128)(2,1)S(1)}, u32[]{:S(2)}, u32[]{:S(2)}) collective-permute-start(bf16[528,128]{1,0:T(8,128)(2,1)S(1)} %get-tuple-element.42), channel_id=1, source_target_pairs={{0,224},{32,0},{64,32},{96,64},{128,96},{160,128},{192,160},{224,1... | collective-permute-start | bytes 405512 | tf_op jit(solution)/shard_map/ppermute | solution.py:241
  134.7 5.1 %collective-permute-start.17 = (bf16[528,128]{1,0:T(8,128)(2,1)S(1)}, bf16[528,128]{1,0:T(8,128)(2,1)S(1)}, u32[]{:S(2)}, u32[]{:S(2)}) collective-permute-start(bf16[528,128]{1,0:T(8,128)(2,1)S(1)} %get-tuple-element.43), channel_id=1, source_target_pairs={{0,32},{32,64},{64,96},{96,128},{128,160},{160,192},{192,224},{224... | collective-permute-start | bytes 405512 | tf_op jit(solution)/shard_map/ppermute | solution.py:241
  179.1 10.4 %collective-permute-start.20 = (bf16[16,8,32,128]{3,2,1,0:T(8,128)(2,1)S(1)}, bf16[16,8,32,128]{3,2,1,0:T(8,128)(2,1)S(1)}, u32[]{:S(2)}, u32[]{:S(2)}) collective-permute-start(bf16[16,8,32,128]{3,2,1,0:T(8,128)(2,1)S(1)} %all_to_all.29.own), channel_id=1, source_target_pairs={{0,1},{1,0},{2,3},{3,2},{4,5},{5,4},{6,7},{7,6},{8,9},{9,8},{10,11... | collective-permute-start | bytes 3145736 | tf_op jit(solution)/shard_map/ppermute | solution.py:238
  185.6 2.4 %collective-permute-start.19 = (bf16[8,32,128]{2,1,0:T(8,128)(2,1)S(1)}, bf16[8,32,128]{2,1,0:T(8,128)(2,1)S(1)}, u32[]{:S(2)}, u32[]{:S(2)}) collective-permute-start(bf16[8,32,128]{2,1,0:T(8,128)(2,1)S(1)} %get-tuple-element.51), channel_id=1, source_target_pairs={{0,1},{1,0},{2,3},{3,2},{4,5},{5,4},{6,7},{7,6},{8,9},{9,8},{10,11... | collective-permute-start | bytes 196616 | tf_op jit(solution)/shard_map/ppermute | solution.py:238

commit v8 on v5

--- a/solution.py
+++ b/solution.py
@@ -151,10 +151,12 @@
             out[k, 512:528, :] = jnp.concatenate([mine, jnp.zeros_like(mine)], axis=0).astype(kind)
 
 
-def slice_kernel(info, kept, given, from_below, from_above, *refs):
+def slice_kernel(info, kept, given, from_below, from_above, from_far, *refs):
     pieces, (tab, gsum, self_piece, tacc) = refs[:18], refs[18:]
     fact_pos, core = info[PLACE], info[PLACE + 2]
-    total = kept[...] + given[...].astype(F32) + from_below[...].astype(F32) + from_above[...].astype(F32)
+    total = kept[...]
+    for arrived in (given, from_below, from_above, from_far):
+        total = total + arrived[...].astype(F32)
     self_piece[...] = total[512:520]
     for at in range(16):
         gsum[at] = total[at * 32 : (at + 1) * 32].astype(BF16)
@@ -200,28 +202,31 @@
 def final_kernel(info, own, sib, grad_self, grad_tab):
     even = info[PLACE + 2] == 0
     scale = F32(32768.0**-0.5)
-    for q in range(4):
-        for group in range(2):
-            tables = [[[], [], []], [[], [], []]]
-            for z in range(4 * group, 4 * group + 4):
-                for chip in range(16):
-                    mine, other = own[chip, z].astype(F32) * scale, sib[chip, z].astype(F32) * scale
-                    pair = (jnp.where(even, mine, other), jnp.where(even, other, mine))
-                    for core in range(2):
-                        if z // 2 == q:
-                            row = (2 * chip + core) * 16 + (z % 2) * 8
-                            grad_self[row : row + 8, q * 128 : (q + 1) * 128] = pair[core][24:32]
-                        if chip // 4 == q:
-                            first = (chip % 4) * 24
-                            for t in range(3):
-                                lo, hi = max(first, t * 32), min(first + 24, t * 32 + 32)
-                                if lo < hi:
-                                    tables[core][t].append(pair[core][lo - first : hi - first])
-            for core in range(2):
-                for t in range(3):
-                    column = core * 256 + group * 128
-                    both = jnp.concatenate(tables[core][t], axis=0)
-                    grad_tab[t, q * 128 : (q + 1) * 128, column : column + 128] = both.T
+    q = pl.program_id(0)
+
+    def both_cores(chip, z):
+        mine, other = own[chip, z].astype(F32) * scale, sib[chip, z].astype(F32) * scale
+        return jnp.where(even, mine, other), jnp.where(even, other, mine)
+
+    for chip in range(16):
+        for half in range(2):
+            for core, piece in enumerate(both_cores(chip, 2 * q + half)):
+                row = (2 * chip + core) * 16 + half * 8
+                grad_self[row : row + 8, :] = piece[24:32]
+    for group in range(2):
+        tables = [[[], [], []], [[], [], []]]
+        for z in range(4 * group, 4 * group + 4):
+            for i in range(4):
+                first = i * 24
+                for core, piece in enumerate(both_cores(4 * q + i, z)):
+                    for t in range(3):
+                        lo, hi = max(first, t * 32), min(first + 24, t * 32 + 32)
+                        if lo < hi:
+                            tables[core][t].append(piece[lo - first : hi - first])
+        for core in range(2):
+            for t in range(3):
+                column = core * 256 + group * 128
+                grad_tab[t, :, column : column + 128] = jnp.concatenate(tables[core][t], axis=0).T
 
 
 def body(facts, dims, tiles, links, link_count, block_table, w_self, w_tables, cot):
@@ -315,11 +320,13 @@
     def partial_sum(k, arrived):
         return (keep[k] + give[k].astype(F32) + arrived.astype(F32)).astype(BF16)
 
-    up = shift((keep[4] + give[4].astype(F32)).astype(BF16), 1)
+    up = shift((keep[3] + give[3].astype(F32)).astype(BF16), 1)
     down = shift((keep[5] + give[5].astype(F32)).astype(BF16), -1)
-    for k in (3, 2):
-        up, down = shift(partial_sum(k, up), 1), shift(partial_sum(9 - k, down), -1)
-    up = shift(partial_sum(1, up), 1)
+    far, up, down = lax.optimization_barrier(((keep[4] + give[4].astype(F32)).astype(BF16), up, down))
+    far = shift(far, 4)
+    for k in (2, 1):
+        up, down = lax.optimization_barrier((partial_sum(k, up), partial_sum(8 - k, down)))
+        up, down = shift(up, 1), shift(down, -1)
 
     tab, gsum, self_piece = call(
         slice_kernel,
@@ -328,11 +335,11 @@
             jax.ShapeDtypeStruct((2 * n_fact, 32, 128), BF16),
             jax.ShapeDtypeStruct((8, 128), F32),
         ),
-        [SMEM] + [VMEM] * 22,
+        [SMEM] + [VMEM] * 23,
         [pltpu.VMEM((3, 32, width), F32)],
         flops=4 * n_fact * 32 * 128 * width,
         moved=3 << 20,
-    )(info, keep[0], give[0], up, down, *pieces, *pieces_sib)
+    )(info, keep[0], give[0], up, down, far, *pieces, *pieces_sib)
     tab = by_chip(tab.reshape(chips, 24, 128))
     packed = call(
         pack_kernel, jax.ShapeDtypeStruct((n_fact, 96, 128), BF16), [SMEM] + [VMEM] * 3, moved=1 << 19
@@ -348,11 +355,17 @@
         flops=2 * rows * width * width,
         moved=2 << 20,
     )(info, packed[:, :32, :], given, w_tables)
-    grad_self, grad_tab = call(
+    grad_self, grad_tab = pl.pallas_call(
         final_kernel,
-        (jax.ShapeDtypeStruct((width, width), F32), jax.ShapeDtypeStruct((3, width, width), F32)),
-        [SMEM] + [VMEM] * 2,
-        moved=8 << 20,
+        out_shape=(jax.ShapeDtypeStruct((width, width), F32), jax.ShapeDtypeStruct((3, width, width), F32)),
+        grid=(4,),
+        in_specs=[SMEM, VMEM, VMEM],
+        out_specs=(
+            pl.BlockSpec((width, 128), lambda q: (0, q)),
+            pl.BlockSpec((3, 128, width), lambda q: (0, q, 0)),
+        ),
+        compiler_params=PARAMS,
+        cost_estimate=pl.CostEstimate(flops=0, bytes_accessed=8 << 20, transcendentals=0),
     )(info, pieces_own, swap(pieces_own))
     return (fact_out, grad_dims, grad_self, grad_tab)
 

time: 197 us -> 194 us (0.985)
  waiting for transfers between devices: 27.2 us -> 20.8 us
  blocking collectives: 102 us -> 105 us
    ppermute x15, waiting for transfers between devices: 21.2 us -> 14.9 us  [shift(): lax.ppermute(x, 'fact', [(i, (i + by) % n_fact) for i in range(n_fact)])]
    ppermute x15, starting transfers between devices: 22.1 us -> 24.7 us  [shift(): lax.ppermute(x, 'fact', [(i, (i + by) % n_fact) for i in range(n_fact)])]
    all_to_all x4, blocking collectives: 90.6 us -> 93 us  [by_chip(): return lax.all_to_all(x, 'dim', 0, 0, tiled=True, axis_index_groups=same)]
  transfers between devices with their start and end apart: 29 -> 29, of which waited for: 11 -> 12; matrix products, arithmetic and copies ran while one was open for 0% -> 0% of each run, Pallas kernels for 2% -> 2%
where the time goes in v8:
time: 194 us
  blocking collectives  105 us (54%)
  starting transfers between devices  46.7 us (24%)
  waiting for transfers between devices  20.8 us (11%)
  Pallas kernels  17.5 us (9%)
    all_to_all x4, blocking collectives, by_chip(): return lax.all_to_all(x, 'dim', 0, 0, tiled=True, axis_index_groups=same)  93 us
    ppermute x15, starting transfers between devices, shift(): lax.ppermute(x, 'fact', [(i, (i + by) % n_fact) for i in range(n_fact)])  24.7 us
    ppermute x14, starting transfers between devices, swap(): return lax.ppermute(x, 'dim', pair)  22 us
    ppermute x15, waiting for transfers between devices, shift(): lax.ppermute(x, 'fact', [(i, (i + by) % n_fact) for i in range(n_fact)])  14.9 us
    all_to_all x1, blocking collectives, by_fact(): return lax.all_to_all(x, 'fact', 0, 0, tiled=True)  12.4 us
    ppermute x14, waiting for transfers between devices, swap(): return lax.ppermute(x, 'dim', pair)  5.92 us
  transfers between devices with their start and end apart: 29, of which 12 were waited for; matrix products, arithmetic and copies ran while one was open for 0% of the time, Pallas kernels for 2%

profile of v8, /device:TPU:1, one launch (start us, length us, event | category | flops | bytes accessed | tf_op | source)
XLA Modules:
  0.0 194.0 jit_solution(9574863826660712906)
XLA Ops:
  0.6 3.3 %collective-permute-start.18 = (bf16[32,128,128]{2,1,0:T(8,128)(2,1)}, bf16[32,128,128]{2,1,0:T(8,128)(2,1)S(1)}, u32[]{:S(2)}, u32[]{:S(2)}) collective-permute-start(bf16[32,128,128]{2,1,0:T(8,128)(2,1)} %tiles_own.1), channel_id=1, source_target_pairs={{0,1},{1,0},{2,3},{3,2},{4,5},{5,4},{6,7},{7,6},{8,9},{9,8},{10,11... | collective-permute-start | bytes 3145736 | tf_op jit(solution)/shard_map/ppermute | solution.py:245
  4.0 3.9 %collective-permute-start.2 = (bf16[128,512]{1,0:T(8,128)(2,1)}, bf16[128,512]{1,0:T(8,128)(2,1)S(1)}, u32[]{:S(2)}, u32[]{:S(2)}) collective-permute-start(bf16[128,512]{1,0:T(8,128)(2,1)} %refs_0_.3), channel_id=1, source_target_pairs={{0,224},{32,0},{64,32},{96,64},{128,96},{160,128},{192,160},{224,1... | collective-permute-start | bytes 393224 | tf_op jit(solution)/shard_map/ppermute | solution.py:248
  7.8 0.4 collective-permute-start.9
  8.8 0.7 concatenate.3.links_own
  9.5 0.2 collective-permute-start.4
  9.7 1.2 collective-permute-done.2.refs_2_
  11.0 3.3 %collective-permute-start.3 = (bf16[128,512]{1,0:T(8,128)(2,1)S(1)}, bf16[128,512]{1,0:T(8,128)(2,1)S(1)}, u32[]{:S(2)}, u32[]{:S(2)}) collective-permute-start(bf16[128,512]{1,0:T(8,128)(2,1)S(1)} %collective-permute-done.2.refs_2_), channel_id=1, source_target_pairs={{0,224},{32,0},{64,32},{96,64},{128,96},{160,128},{192,160},{224,1... | collective-permute-start | bytes 393224 | tf_op jit(solution)/shard_map/ppermute | solution.py:248
  14.3 0.7 copy-done.6
  15.0 1.5 shard_map.120.info
  16.5 2.8 %collective-permute-done.1.refs_3_ = bf16[128,512]{1,0:T(8,128)(2,1)S(1)} collective-permute-done((bf16[128,512]{1,0:T(8,128)(2,1)S(1)}, bf16[128,512]{1,0:T(8,128)(2,1)S(1)}, u32[]{:S(2)}, u32[]{:S(2)}) %collective-permute-start.1) | collective-permute-done | bytes 131104 | tf_op jit(solution)/shard_map/ppermute | solution.py:248
  19.3 2.7 %collective-permute-start.7 = (bf16[128,512]{1,0:T(8,128)(2,1)S(1)}, bf16[128,512]{1,0:T(8,128)(2,1)S(1)}, u32[]{:S(2)}, u32[]{:S(2)}) collective-permute-start(bf16[128,512]{1,0:T(8,128)(2,1)S(1)} %collective-permute-done.3.refs_4_), channel_id=1, source_target_pairs={{0,224},{32,0},{64,32},{96,64},{128,96},{160,128},{192,160},{224,1... | collective-permute-start | bytes 393224 | tf_op jit(solution)/shard_map/ppermute | solution.py:248
  22.0 2.9 %collective-permute-start.11 = (bf16[128,512]{1,0:T(8,128)(2,1)S(1)}, bf16[128,512]{1,0:T(8,128)(2,1)S(1)}, u32[]{:S(2)}, u32[]{:S(2)}) collective-permute-start(bf16[128,512]{1,0:T(8,128)(2,1)S(1)} %collective-permute-done.2.refs_2_), channel_id=1, source_target_pairs={{0,1},{1,0},{2,3},{3,2},{4,5},{5,4},{6,7},{7,6},{8,9},{9,8},{10,11... | collective-permute-start | bytes 393224 | tf_op jit(solution)/shard_map/ppermute | solution.py:245
  24.9 2.9 %collective-permute-start.13 = (bf16[128,512]{1,0:T(8,128)(2,1)S(1)}, bf16[128,512]{1,0:T(8,128)(2,1)S(1)}, u32[]{:S(2)}, u32[]{:S(2)}) collective-permute-start(bf16[128,512]{1,0:T(8,128)(2,1)S(1)} %collective-permute-done.3.refs_4_), channel_id=1, source_target_pairs={{0,1},{1,0},{2,3},{3,2},{4,5},{5,4},{6,7},{7,6},{8,9},{9,8},{10,11... | collective-permute-start | bytes 393224 | tf_op jit(solution)/shard_map/ppermute | solution.py:245
  27.9 3.0 %collective-permute-start.8 = (bf16[64,512]{1,0:T(8,128)(2,1)S(1)}, bf16[64,512]{1,0:T(8,128)(2,1)S(1)}, u32[]{:S(2)}, u32[]{:S(2)}) collective-permute-start(bf16[64,512]{1,0:T(8,128)(2,1)S(1)} %slice.85), channel_id=1, source_target_pairs={{0,224},{32,0},{64,32},{96,64},{128,96},{160,128},{192,160},{224,1... | collective-permute-start | bytes 196616 | tf_op jit(solution)/shard_map/ppermute | solution.py:248
  31.0 0.7 collective-permute-start.14
  31.7 0.3 collective-permute-start.15
  31.9 1.4 shard_map.121
  33.4 0.5 collective-permute-start.16
  34.0 0.8 collective-permute-done.16.refs_6_.refs_16_
  34.8 0.4 collective-permute-done.17.refs_7_.refs_17_
  35.2 3.4 %shard_map.122 = bf16[16,544,128]{2,1,0:T(8,128)(2,1)S(1)} custom-call(s32[128]{0:T(128)S(1)} %shard_map.120.info, bf16[10,128,512]{2,1,0:T(8,128)(2,1)S(1)} %get-tuple-element.33.proj, bf16[128,512]{1,0:T(8,128)(2,1)S(1)} %collective-permute-done.5.refs_0_.refs_5_, bf16[128,512]{1,0:T(8,128)(2,1)S(1)} %collective-permute-done.7.refs_1_.refs_6_, ...), custom_call_target="tpu_custom_call" | custom-call | flops 536870912 | bytes 8388608 | tf_op jit(solution)/shard_map/pallas_call | solution.py:287
  38.6 36.1 %all_to_all.25.parts = bf16[16,544,128]{2,1,0:T(8,128)(2,1)S(1)} all-to-all(bf16[16,544,128]{2,1,0:T(8,128)(2,1)S(1)} %shard_map.122), channel_id=1, replica_groups={{0,2,4,6,8,10,12,14,16,18,20,22,24,26,28,30},{1,3,5,7,9,11,13,15,17,19,..., dimensions={0} | all-to-all | bytes 4456448 | tf_op jit(solution)/shard_map/all_to_all | solution.py:251
  74.7 1.2 shard_map.123
  75.8 30.2 %all_to_all.26.grads = bf16[16,512,128]{2,1,0:T(8,128)(2,1)S(1)} all-to-all(bf16[16,512,128]{2,1,0:T(8,128)(2,1)S(1)} %get-tuple-element.38), channel_id=1, replica_groups={{0,2,4,6,8,10,12,14,16,18,20,22,24,26,28,30},{1,3,5,7,9,11,13,15,17,19,..., dimensions={0} | all-to-all | bytes 4194304 | tf_op jit(solution)/shard_map/all_to_all | solution.py:251
  106.0 3.6 %shard_map.124 = (f32[8,528,128]{2,1,0:T(8,128)S(1)}, bf16[8,528,128]{2,1,0:T(8,128)(2,1)S(1)}) custom-call(s32[128]{0:T(128)S(1)} %shard_map.120.info, bf16[16,512,128]{2,1,0:T(8,128)(2,1)S(1)} %all_to_all.26.grads, bf16[16,32,128]{2,1,0:T(8,128)(2,1)S(1)} %get-tuple-element.39.facts_t, bf16[32,128,128]{2,1,0:T(8,128)(2,1)S(1)} %copy-done.1, ...), custom_call_target="tpu_custom_call" | custom-call | flops 536870912 | bytes 9437184 | tf_op jit(solution)/shard_map/pallas_call | solution.py:310
  109.7 1.7 collective-permute-start.19
  111.4 2.3 %collective-permute-done.19 = bf16[8,528,128]{2,1,0:T(8,128)(2,1)S(1)} collective-permute-done((bf16[8,528,128]{2,1,0:T(8,128)(2,1)S(1)}, bf16[8,528,128]{2,1,0:T(8,128)(2,1)S(1)}, u32[]{:S(2)}, u32[]{:S(2)}) %collective-permute-start.19) | collective-permute-done | bytes 1081376 | tf_op jit(solution)/shard_map/ppermute | solution.py:245
  113.8 3.6 %collective-permute-start.21 = (bf16[528,128]{1,0:T(8,128)(2,1)S(1)}, bf16[528,128]{1,0:T(8,128)(2,1)S(1)}, u32[]{:S(2)}, u32[]{:S(2)}) collective-permute-start(bf16[528,128]{1,0:T(8,128)(2,1)S(1)} %get-tuple-element.58), channel_id=1, source_target_pairs={{0,224},{32,0},{64,32},{96,64},{128,96},{160,128},{192,160},{224,1... | collective-permute-start | bytes 405512 | tf_op jit(solution)/shard_map/ppermute | solution.py:248
  117.5 2.6 %collective-permute-done.21 = bf16[528,128]{1,0:T(8,128)(2,1)S(1)} collective-permute-done((bf16[528,128]{1,0:T(8,128)(2,1)S(1)}, bf16[528,128]{1,0:T(8,128)(2,1)S(1)}, u32[]{:S(2)}, u32[]{:S(2)}) %collective-permute-start.21) | collective-permute-done | bytes 135200 | tf_op jit(solution)/shard_map/ppermute | solution.py:248
  120.1 3.1 %collective-permute-done.20 = bf16[528,128]{1,0:T(8,128)(2,1)S(1)} collective-permute-done((bf16[528,128]{1,0:T(8,128)(2,1)S(1)}, bf16[528,128]{1,0:T(8,128)(2,1)S(1)}, u32[]{:S(2)}, u32[]{:S(2)}) %collective-permute-start.20) | collective-permute-done | bytes 135200 | tf_op jit(solution)/shard_map/ppermute | solution.py:248
  123.2 0.1 fusion.1
  123.4 2.7 %collective-permute-start.23 = (bf16[528,128]{1,0:T(8,128)(2,1)S(1)}, bf16[528,128]{1,0:T(8,128)(2,1)S(1)}, u32[]{:S(2)}, u32[]{:S(2)}) collective-permute-start(bf16[528,128]{1,0:T(8,128)(2,1)S(1)} %get-tuple-element.45), channel_id=1, source_target_pairs={{0,224},{32,0},{64,32},{96,64},{128,96},{160,128},{192,160},{224,1... | collective-permute-start | bytes 405512 | tf_op jit(solution)/shard_map/ppermute | solution.py:248
  126.0 2.2 %collective-permute-start.26 = (bf16[528,128]{1,0:T(8,128)(2,1)S(1)}, bf16[528,128]{1,0:T(8,128)(2,1)S(1)}, u32[]{:S(2)}, u32[]{:S(2)}) collective-permute-start(bf16[528,128]{1,0:T(8,128)(2,1)S(1)} %get-tuple-element.48), channel_id=1, source_target_pairs={{0,128},{32,160},{64,192},{96,224},{128,0},{160,32},{192,64},{224,... | collective-permute-start | bytes 405512 | tf_op jit(solution)/shard_map/ppermute | solution.py:248
  128.2 0.7 collective-permute-done.22
  128.9 0.1 fusion
  129.1 3.1 %collective-permute-start.25 = (bf16[528,128]{1,0:T(8,128)(2,1)S(1)}, bf16[528,128]{1,0:T(8,128)(2,1)S(1)}, u32[]{:S(2)}, u32[]{:S(2)}) collective-permute-start(bf16[528,128]{1,0:T(8,128)(2,1)S(1)} %get-tuple-element.47), channel_id=1, source_target_pairs={{0,224},{32,0},{64,32},{96,64},{128,96},{160,128},{192,160},{224,1... | collective-permute-start | bytes 405512 | tf_op jit(solution)/shard_map/ppermute | solution.py:248
  132.3 3.8 %collective-permute-done.26.from_far = bf16[528,128]{1,0:T(8,128)(2,1)S(1)} collective-permute-done((bf16[528,128]{1,0:T(8,128)(2,1)S(1)}, bf16[528,128]{1,0:T(8,128)(2,1)S(1)}, u32[]{:S(2)}, u32[]{:S(2)}) %collective-permute-start.26) | collective-permute-done | bytes 135200 | tf_op jit(solution)/shard_map/ppermute | solution.py:248
  136.1 0.6 collective-permute-done.24.from_below
  136.7 1.1 shard_map.125
  137.8 12.0 %all_to_all.27.parts = bf16[16,24,128]{2,1,0:T(8,128)(2,1)S(1)} all-to-all(bf16[16,24,128]{2,1,0:T(8,128)(2,1)S(1)} %bitcast.34), channel_id=1, replica_groups={{0,2,4,6,8,10,12,14,16,18,20,22,24,26,28,30},{1,3,5,7,9,11,13,15,17,19,..., dimensions={0} | all-to-all | bytes 196608 | tf_op jit(solution)/shard_map/all_to_all | solution.py:251
  149.8 0.6 shard_map.126
  150.4 12.4 %all_to_all.28 = bf16[8,96,128]{2,1,0:T(8,128)(2,1)S(1)} all-to-all(bf16[8,96,128]{2,1,0:T(8,128)(2,1)S(1)} %shard_map.126), channel_id=1, replica_groups=mesh['fact'=8,'dim'=32] {'fact'}, dimensions={0} | all-to-all | bytes 393216 | tf_op jit(solution)/shard_map/all_to_all | solution.py:254
  162.8 0.2 broadcast_in_dim.5
  163.1 14.7 %all_to_all.29.own = bf16[16,8,32,128]{3,2,1,0:T(8,128)(2,1)S(1)} all-to-all(bf16[16,8,32,128]{3,2,1,0:T(8,128)(2,1)S(1)} %broadcast_in_dim.5), channel_id=1, replica_groups={{0,2,4,6,8,10,12,14,16,18,20,22,24,26,28,30},{1,3,5,7,9,11,13,15,17,19,..., dimensions={0} | all-to-all | bytes 2097152 | tf_op jit(solution)/shard_map/all_to_all | solution.py:251
  177.7 9.0 %collective-permute-start.28 = (bf16[16,8,32,128]{3,2,1,0:T(8,128)(2,1)S(1)}, bf16[16,8,32,128]{3,2,1,0:T(8,128)(2,1)S(1)}, u32[]{:S(2)}, u32[]{:S(2)}) collective-permute-start(bf16[16,8,32,128]{3,2,1,0:T(8,128)(2,1)S(1)} %all_to_all.29.own), channel_id=1, source_target_pairs={{0,1},{1,0},{2,3},{3,2},{4,5},{5,4},{6,7},{7,6},{8,9},{9,8},{10,11... | collective-permute-start | bytes 3145736 | tf_op jit(solution)/shard_map/ppermute | solution.py:245
  186.8 2.4 %collective-permute-done.27.given = bf16[8,32,128]{2,1,0:T(8,128)(2,1)S(1)} collective-permute-done((bf16[8,32,128]{2,1,0:T(8,128)(2,1)S(1)}, bf16[8,32,128]{2,1,0:T(8,128)(2,1)S(1)}, u32[]{:S(2)}, u32[]{:S(2)}) %collective-permute-start.27) | collective-permute-done | bytes 65568 | tf_op jit(solution)/shard_map/ppermute | solution.py:245
  189.2 1.6 shard_map.127
  190.7 3.3 %shard_map.128 = (f32[512,512]{1,0:T(8,128)}, f32[3,512,512]{2,1,0:T(8,128)}) custom-call(s32[128]{0:T(128)S(1)} %shard_map.120.info, bf16[16,8,32,128]{3,2,1,0:T(8,128)(2,1)S(1)} %all_to_all.29.own, bf16[16,8,32,128]{3,2,1,0:T(8,128)(2,1)S(1)} %collective-permute-done.28.sib), custom_call_target="tpu_custom_call" | custom-call | bytes 8388608 | tf_op jit(solution)/shard_map/pallas_call | solution.py:358
  (48 shorter events, 0.7 us)
Async XLA Ops:
  0.6 34.5 %collective-permute-start.18 = (bf16[32,128,128]{2,1,0:T(8,128)(2,1)}, bf16[32,128,128]{2,1,0:T(8,128)(2,1)S(1)}, u32[]{:S(2)}, u32[]{:S(2)}) collective-permute-start(bf16[32,128,128]{2,1,0:T(8,128)(2,1)} %tiles_own.1), channel_id=1, source_target_pairs={{0,1},{1,0},{2,3},{3,2},{4,5},{5,4},{6,7},{7,6},{8,9},{9,8},{10,11... | collective-permute-start | bytes 3145736 | tf_op jit(solution)/shard_map/ppermute | solution.py:245
  4.0 7.0 %collective-permute-start.2 = (bf16[128,512]{1,0:T(8,128)(2,1)}, bf16[128,512]{1,0:T(8,128)(2,1)S(1)}, u32[]{:S(2)}, u32[]{:S(2)}) collective-permute-start(bf16[128,512]{1,0:T(8,128)(2,1)} %refs_0_.3), channel_id=1, source_target_pairs={{0,224},{32,0},{64,32},{96,64},{128,96},{160,128},{192,160},{224,1... | collective-permute-start | bytes 393224 | tf_op jit(solution)/shard_map/ppermute | solution.py:248
  7.8 6.5 %collective-permute-start = (bf16[128,512]{1,0:T(8,128)(2,1)}, bf16[128,512]{1,0:T(8,128)(2,1)S(1)}, u32[]{:S(2)}, u32[]{:S(2)}) collective-permute-start(bf16[128,512]{1,0:T(8,128)(2,1)} %refs_0_.3), channel_id=1, source_target_pairs={{0,32},{32,64},{64,96},{96,128},{128,160},{160,192},{192,224},{224... | collective-permute-start | bytes 393224 | tf_op jit(solution)/shard_map/ppermute | solution.py:248
  7.8 17.0 %collective-permute-start.9 = (bf16[128,512]{1,0:T(8,128)(2,1)}, bf16[128,512]{1,0:T(8,128)(2,1)S(1)}, u32[]{:S(2)}, u32[]{:S(2)}) collective-permute-start(bf16[128,512]{1,0:T(8,128)(2,1)} %refs_0_.3), channel_id=1, source_target_pairs={{0,1},{1,0},{2,3},{3,2},{4,5},{5,4},{6,7},{7,6},{8,9},{9,8},{10,11... | collective-permute-start | bytes 393224 | tf_op jit(solution)/shard_map/ppermute | solution.py:245
  9.5 4.8 %collective-permute-start.4 = (s32[2,33]{1,0:T(2,128)S(1)}, s32[2,33]{1,0:T(2,128)S(1)}, u32[]{:S(2)}, u32[]{:S(2)}) collective-permute-start(s32[2,33]{1,0:T(2,128)S(1)} %concatenate.3.links_own), channel_id=1, source_target_pairs={{0,1},{1,0},{2,3},{3,2},{4,5},{5,4},{6,7},{7,6},{8,9},{9,8},{10,11... | collective-permute-start | bytes 800 | tf_op jit(solution)/shard_map/ppermute | solution.py:245
  9.7 22.2 %copy-start = (bf16[3,512,512]{2,1,0:T(8,128)(2,1)S(1)}, bf16[3,512,512]{2,1,0:T(8,128)(2,1)}, u32[]{:S(2)}) copy-start(bf16[3,512,512]{2,1,0:T(8,128)(2,1)} %w.5) | copy-start | bytes 4718596
  9.7 22.2 %copy-start.2 = (bf16[128,512]{1,0:T(8,128)(2,1)S(1)}, bf16[128,512]{1,0:T(8,128)(2,1)}, u32[]{:S(2)}) copy-start(bf16[128,512]{1,0:T(8,128)(2,1)} %facts.3) | copy-start | bytes 393220
  9.7 22.2 %copy-start.3 = (bf16[128,512]{1,0:T(8,128)(2,1)S(1)}, bf16[128,512]{1,0:T(8,128)(2,1)}, u32[]{:S(2)}) copy-start(bf16[128,512]{1,0:T(8,128)(2,1)} %refs_0_.3) | copy-start | bytes 393220
  11.0 5.5 %collective-permute-start.3 = (bf16[128,512]{1,0:T(8,128)(2,1)S(1)}, bf16[128,512]{1,0:T(8,128)(2,1)S(1)}, u32[]{:S(2)}, u32[]{:S(2)}) collective-permute-start(bf16[128,512]{1,0:T(8,128)(2,1)S(1)} %collective-permute-done.2.refs_2_), channel_id=1, source_target_pairs={{0,224},{32,0},{64,32},{96,64},{128,96},{160,128},{192,160},{224,1... | collective-permute-start | bytes 393224 | tf_op jit(solution)/shard_map/ppermute | solution.py:248
  14.3 5.0 %collective-permute-start.1 = (bf16[128,512]{1,0:T(8,128)(2,1)S(1)}, bf16[128,512]{1,0:T(8,128)(2,1)S(1)}, u32[]{:S(2)}, u32[]{:S(2)}) collective-permute-start(bf16[128,512]{1,0:T(8,128)(2,1)S(1)} %collective-permute-done.refs_1_), channel_id=1, source_target_pairs={{0,32},{32,64},{64,96},{96,128},{128,160},{160,192},{192,224},{224... | collective-permute-start | bytes 393224 | tf_op jit(solution)/shard_map/ppermute | solution.py:248
  14.3 0.7 copy-start.6
  16.5 18.7 %copy-start.1 = (bf16[32,128,128]{2,1,0:T(8,128)(2,1)S(1)}, bf16[32,128,128]{2,1,0:T(8,128)(2,1)}, u32[]{:S(2)}) copy-start(bf16[32,128,128]{2,1,0:T(8,128)(2,1)} %tiles_own.1) | copy-start | bytes 3145732
  19.3 5.5 %collective-permute-start.5 = (bf16[128,512]{1,0:T(8,128)(2,1)S(1)}, bf16[128,512]{1,0:T(8,128)(2,1)S(1)}, u32[]{:S(2)}, u32[]{:S(2)}) collective-permute-start(bf16[128,512]{1,0:T(8,128)(2,1)S(1)} %collective-permute-done.1.refs_3_), channel_id=1, source_target_pairs={{0,32},{32,64},{64,96},{96,128},{128,160},{160,192},{192,224},{224... | collective-permute-start | bytes 393224 | tf_op jit(solution)/shard_map/ppermute | solution.py:248
  19.3 8.5 %collective-permute-start.7 = (bf16[128,512]{1,0:T(8,128)(2,1)S(1)}, bf16[128,512]{1,0:T(8,128)(2,1)S(1)}, u32[]{:S(2)}, u32[]{:S(2)}) collective-permute-start(bf16[128,512]{1,0:T(8,128)(2,1)S(1)} %collective-permute-done.3.refs_4_), channel_id=1, source_target_pairs={{0,224},{32,0},{64,32},{96,64},{128,96},{160,128},{192,160},{224,1... | collective-permute-start | bytes 393224 | tf_op jit(solution)/shard_map/ppermute | solution.py:248
  22.0 5.8 %collective-permute-start.11 = (bf16[128,512]{1,0:T(8,128)(2,1)S(1)}, bf16[128,512]{1,0:T(8,128)(2,1)S(1)}, u32[]{:S(2)}, u32[]{:S(2)}) collective-permute-start(bf16[128,512]{1,0:T(8,128)(2,1)S(1)} %collective-permute-done.2.refs_2_), channel_id=1, source_target_pairs={{0,1},{1,0},{2,3},{3,2},{4,5},{5,4},{6,7},{7,6},{8,9},{9,8},{10,11... | collective-permute-start | bytes 393224 | tf_op jit(solution)/shard_map/ppermute | solution.py:245
  24.9 3.1 %collective-permute-start.10 = (bf16[128,512]{1,0:T(8,128)(2,1)S(1)}, bf16[128,512]{1,0:T(8,128)(2,1)S(1)}, u32[]{:S(2)}, u32[]{:S(2)}) collective-permute-start(bf16[128,512]{1,0:T(8,128)(2,1)S(1)} %collective-permute-done.refs_1_), channel_id=1, source_target_pairs={{0,1},{1,0},{2,3},{3,2},{4,5},{5,4},{6,7},{7,6},{8,9},{9,8},{10,11... | collective-permute-start | bytes 393224 | tf_op jit(solution)/shard_map/ppermute | solution.py:245
  24.9 6.1 %collective-permute-start.13 = (bf16[128,512]{1,0:T(8,128)(2,1)S(1)}, bf16[128,512]{1,0:T(8,128)(2,1)S(1)}, u32[]{:S(2)}, u32[]{:S(2)}) collective-permute-start(bf16[128,512]{1,0:T(8,128)(2,1)S(1)} %collective-permute-done.3.refs_4_), channel_id=1, source_target_pairs={{0,1},{1,0},{2,3},{3,2},{4,5},{5,4},{6,7},{7,6},{8,9},{9,8},{10,11... | collective-permute-start | bytes 393224 | tf_op jit(solution)/shard_map/ppermute | solution.py:245
  27.8 3.9 %collective-permute-start.12 = (bf16[128,512]{1,0:T(8,128)(2,1)S(1)}, bf16[128,512]{1,0:T(8,128)(2,1)S(1)}, u32[]{:S(2)}, u32[]{:S(2)}) collective-permute-start(bf16[128,512]{1,0:T(8,128)(2,1)S(1)} %collective-permute-done.1.refs_3_), channel_id=1, source_target_pairs={{0,1},{1,0},{2,3},{3,2},{4,5},{5,4},{6,7},{7,6},{8,9},{9,8},{10,11... | collective-permute-start | bytes 393224 | tf_op jit(solution)/shard_map/ppermute | solution.py:245
  27.8 5.5 %collective-permute-start.6 = (bf16[64,512]{1,0:T(8,128)(2,1)S(1)}, bf16[64,512]{1,0:T(8,128)(2,1)S(1)}, u32[]{:S(2)}, u32[]{:S(2)}) collective-permute-start(bf16[64,512]{1,0:T(8,128)(2,1)S(1)} %slice.84), channel_id=1, source_target_pairs={{0,32},{32,64},{64,96},{96,128},{128,160},{160,192},{192,224},{224... | collective-permute-start | bytes 196616 | tf_op jit(solution)/shard_map/ppermute | solution.py:248
  27.9 5.4 %collective-permute-start.8 = (bf16[64,512]{1,0:T(8,128)(2,1)S(1)}, bf16[64,512]{1,0:T(8,128)(2,1)S(1)}, u32[]{:S(2)}, u32[]{:S(2)}) collective-permute-start(bf16[64,512]{1,0:T(8,128)(2,1)S(1)} %slice.85), channel_id=1, source_target_pairs={{0,224},{32,0},{64,32},{96,64},{128,96},{160,128},{192,160},{224,1... | collective-permute-start | bytes 196616 | tf_op jit(solution)/shard_map/ppermute | solution.py:248
  31.0 4.2 %collective-permute-start.14 = (bf16[128,512]{1,0:T(8,128)(2,1)S(1)}, bf16[128,512]{1,0:T(8,128)(2,1)S(1)}, u32[]{:S(2)}, u32[]{:S(2)}) collective-permute-start(bf16[128,512]{1,0:T(8,128)(2,1)S(1)} %collective-permute-done.5.refs_0_.refs_5_), channel_id=1, source_target_pairs={{0,1},{1,0},{2,3},{3,2},{4,5},{5,4},{6,7},{7,6},{8,9},{9,8},{10,11... | collective-permute-start | bytes 393224 | tf_op jit(solution)/shard_map/ppermute | solution.py:245
  31.7 3.5 %collective-permute-start.15 = (bf16[128,512]{1,0:T(8,128)(2,1)S(1)}, bf16[128,512]{1,0:T(8,128)(2,1)S(1)}, u32[]{:S(2)}, u32[]{:S(2)}) collective-permute-start(bf16[128,512]{1,0:T(8,128)(2,1)S(1)} %collective-permute-done.7.refs_1_.refs_6_), channel_id=1, source_target_pairs={{0,1},{1,0},{2,3},{3,2},{4,5},{5,4},{6,7},{7,6},{8,9},{9,8},{10,11... | collective-permute-start | bytes 393224 | tf_op jit(solution)/shard_map/ppermute | solution.py:245
  33.4 1.4 collective-permute-start.16
  33.9 1.3 collective-permute-start.17
  38.5 36.1 %copy-start.4 = (bf16[512,512]{1,0:T(8,128)(2,1)S(1)}, bf16[512,512]{1,0:T(8,128)(2,1)}, u32[]{:S(2)}) copy-start(bf16[512,512]{1,0:T(8,128)(2,1)} %w.4) | copy-start | bytes 1572868
  38.6 36.1 %copy-start.5 = (bf16[128,512]{1,0:T(8,128)(2,1)S(1)}, bf16[128,512]{1,0:T(8,128)(2,1)}, u32[]{:S(2)}) copy-start(bf16[128,512]{1,0:T(8,128)(2,1)} %cot.1) | copy-start | bytes 393220
  109.7 4.0 %collective-permute-start.19 = (bf16[8,528,128]{2,1,0:T(8,128)(2,1)S(1)}, bf16[8,528,128]{2,1,0:T(8,128)(2,1)S(1)}, u32[]{:S(2)}, u32[]{:S(2)}) collective-permute-start(bf16[8,528,128]{2,1,0:T(8,128)(2,1)S(1)} %get-tuple-element.41), channel_id=1, source_target_pairs={{0,1},{1,0},{2,3},{3,2},{4,5},{5,4},{6,7},{7,6},{8,9},{9,8},{10,11... | collective-permute-start | bytes 3244040 | tf_op jit(solution)/shard_map/ppermute | solution.py:245
  113.8 6.2 %collective-permute-start.21 = (bf16[528,128]{1,0:T(8,128)(2,1)S(1)}, bf16[528,128]{1,0:T(8,128)(2,1)S(1)}, u32[]{:S(2)}, u32[]{:S(2)}) collective-permute-start(bf16[528,128]{1,0:T(8,128)(2,1)S(1)} %get-tuple-element.58), channel_id=1, source_target_pairs={{0,224},{32,0},{64,32},{96,64},{128,96},{160,128},{192,160},{224,1... | collective-permute-start | bytes 405512 | tf_op jit(solution)/shard_map/ppermute | solution.py:248
  117.5 5.7 %collective-permute-start.20 = (bf16[528,128]{1,0:T(8,128)(2,1)S(1)}, bf16[528,128]{1,0:T(8,128)(2,1)S(1)}, u32[]{:S(2)}, u32[]{:S(2)}) collective-permute-start(bf16[528,128]{1,0:T(8,128)(2,1)S(1)} %get-tuple-element.59), channel_id=1, source_target_pairs={{0,32},{32,64},{64,96},{96,128},{128,160},{160,192},{192,224},{224... | collective-permute-start | bytes 405512 | tf_op jit(solution)/shard_map/ppermute | solution.py:248
  123.3 5.7 %collective-permute-start.22 = (bf16[528,128]{1,0:T(8,128)(2,1)S(1)}, bf16[528,128]{1,0:T(8,128)(2,1)S(1)}, u32[]{:S(2)}, u32[]{:S(2)}) collective-permute-start(bf16[528,128]{1,0:T(8,128)(2,1)S(1)} %get-tuple-element.44), channel_id=1, source_target_pairs={{0,32},{32,64},{64,96},{96,128},{128,160},{160,192},{192,224},{224... | collective-permute-start | bytes 405512 | tf_op jit(solution)/shard_map/ppermute | solution.py:248
  123.4 5.6 %collective-permute-start.23 = (bf16[528,128]{1,0:T(8,128)(2,1)S(1)}, bf16[528,128]{1,0:T(8,128)(2,1)S(1)}, u32[]{:S(2)}, u32[]{:S(2)}) collective-permute-start(bf16[528,128]{1,0:T(8,128)(2,1)S(1)} %get-tuple-element.45), channel_id=1, source_target_pairs={{0,224},{32,0},{64,32},{96,64},{128,96},{160,128},{192,160},{224,1... | collective-permute-start | bytes 405512 | tf_op jit(solution)/shard_map/ppermute | solution.py:248
  126.0 10.0 %collective-permute-start.26 = (bf16[528,128]{1,0:T(8,128)(2,1)S(1)}, bf16[528,128]{1,0:T(8,128)(2,1)S(1)}, u32[]{:S(2)}, u32[]{:S(2)}) collective-permute-start(bf16[528,128]{1,0:T(8,128)(2,1)S(1)} %get-tuple-element.48), channel_id=1, source_target_pairs={{0,128},{32,160},{64,192},{96,224},{128,0},{160,32},{192,64},{224,... | collective-permute-start | bytes 405512 | tf_op jit(solution)/shard_map/ppermute | solution.py:248
  129.0 7.6 %collective-permute-start.24 = (bf16[528,128]{1,0:T(8,128)(2,1)S(1)}, bf16[528,128]{1,0:T(8,128)(2,1)S(1)}, u32[]{:S(2)}, u32[]{:S(2)}) collective-permute-start(bf16[528,128]{1,0:T(8,128)(2,1)S(1)} %get-tuple-element.46), channel_id=1, source_target_pairs={{0,32},{32,64},{64,96},{96,128},{128,160},{160,192},{192,224},{224... | collective-permute-start | bytes 405512 | tf_op jit(solution)/shard_map/ppermute | solution.py:248
  129.1 7.6 %collective-permute-start.25 = (bf16[528,128]{1,0:T(8,128)(2,1)S(1)}, bf16[528,128]{1,0:T(8,128)(2,1)S(1)}, u32[]{:S(2)}, u32[]{:S(2)}) collective-permute-start(bf16[528,128]{1,0:T(8,128)(2,1)S(1)} %get-tuple-element.47), channel_id=1, source_target_pairs={{0,224},{32,0},{64,32},{96,64},{128,96},{160,128},{192,160},{224,1... | collective-permute-start | bytes 405512 | tf_op jit(solution)/shard_map/ppermute | solution.py:248
  177.7 13.0 %collective-permute-start.28 = (bf16[16,8,32,128]{3,2,1,0:T(8,128)(2,1)S(1)}, bf16[16,8,32,128]{3,2,1,0:T(8,128)(2,1)S(1)}, u32[]{:S(2)}, u32[]{:S(2)}) collective-permute-start(bf16[16,8,32,128]{3,2,1,0:T(8,128)(2,1)S(1)} %all_to_all.29.own), channel_id=1, source_target_pairs={{0,1},{1,0},{2,3},{3,2},{4,5},{5,4},{6,7},{7,6},{8,9},{9,8},{10,11... | collective-permute-start | bytes 3145736 | tf_op jit(solution)/shard_map/ppermute | solution.py:245
  186.8 2.4 %collective-permute-start.27 = (bf16[8,32,128]{2,1,0:T(8,128)(2,1)S(1)}, bf16[8,32,128]{2,1,0:T(8,128)(2,1)S(1)}, u32[]{:S(2)}, u32[]{:S(2)}) collective-permute-start(bf16[8,32,128]{2,1,0:T(8,128)(2,1)S(1)} %get-tuple-element.63), channel_id=1, source_target_pairs={{0,1},{1,0},{2,3},{3,2},{4,5},{5,4},{6,7},{7,6},{8,9},{9,8},{10,11... | collective-permute-start | bytes 196616 | tf_op jit(solution)/shard_map/ppermute | solution.py:245

commit v9 on v8

--- a/solution.py
+++ b/solution.py
@@ -13,8 +13,8 @@
 UNROLL = 4
 
 
-ORDER = (0, -1, 1, -2, 2, -3, 3)
-EARLY = 5
+ORDER = (0, -1, 1, -2, 2, 4, -3, 3)
+EARLY = 6
 LIST = 40
 COUNT, KIND, PLACE, INFO = 80, 96, 112, 128
 
@@ -65,16 +65,15 @@
 
 
 def forward_kernel(info, proj, *refs):
-    late = 9 - EARLY
+    late = len(ORDER) - EARLY
     sides, (w, facts_t, tiles_own, tiles_sib, out, panel, acc) = (refs[:late], refs[late : 2 * late]), refs[2 * late :]
     fact_pos = info[PLACE]
     for side, pieces in enumerate(sides):
         for at, shift in enumerate(ORDER[:EARLY]):
             panel[side * 8 + ((fact_pos + shift) & 7)] = proj[side * EARLY + at]
-        blocks = [x[...] for x in pieces[:-2]] + [jnp.concatenate([pieces[-2][...], pieces[-1][...]], axis=0)]
-        for shift, rows in zip(ORDER[EARLY:] + (4,), blocks):
+        for shift, rows in zip(ORDER[EARLY:], pieces):
             h = (fact_pos + shift) & 7
-            value = jnp.dot(rows, w[info[KIND + side * 8 + h]], preferred_element_type=F32)
+            value = jnp.dot(rows[...], w[info[KIND + side * 8 + h]], preferred_element_type=F32)
             panel[side * 8 + h] = value.astype(BF16)
     acc[...] = jnp.zeros_like(acc)
     for side, tiles in enumerate((tiles_own, tiles_sib)):
@@ -152,7 +151,7 @@
 
 
 def slice_kernel(info, kept, given, from_below, from_above, from_far, *refs):
-    pieces, (tab, gsum, self_piece, tacc) = refs[:18], refs[18:]
+    pieces, (tab, gsum_own, gsum_sib, self_piece, tacc, gsum) = refs[:16], refs[16:]
     fact_pos, core = info[PLACE], info[PLACE + 2]
     total = kept[...]
     for arrived in (given, from_below, from_above, from_far):
@@ -163,36 +162,34 @@
     tacc[...] = jnp.zeros_like(tacc)
     for side in range(2):
         column = 8 * (core if side == 0 else 1 - core)
-        for at, shift in enumerate(ORDER + (4,)):
+        for at, shift in enumerate(ORDER):
             h = (fact_pos + shift) & 7
             kind = info[KIND + side * 8 + h]
-            grad = gsum[column + h]
-            if shift == 4:
-                low, high = pieces[side * 9 + 7], pieces[side * 9 + 8]
-                rows = jnp.concatenate([low[...], high[...]], axis=0)
-            else:
-                rows = pieces[side * 9 + at][...]
-            tacc[kind] += jnp.dot(grad, rows, preferred_element_type=F32)
+            rows = pieces[side * 8 + at][...]
+            tacc[kind] += jnp.dot(gsum[column + h], rows, preferred_element_type=F32)
+    for h in range(8):
+        gsum_own[h] = gsum[core * 8 + h]
+        gsum_sib[h] = gsum[(1 - core) * 8 + h]
     for q in range(4):
         for t in range(3):
             at = q * 96 + t * 32
             tab[at : at + 32, :] = tacc[t, :, q * 128 : (q + 1) * 128].astype(BF16)
 
 
-def pack_kernel(info, parts, gsum, self_piece, out):
-    core = info[PLACE + 2]
+def pack_kernel(parts, gsum, gsum_arrived, self_piece, out):
     total = jnp.sum(parts[...].astype(F32), axis=0)
     piece = jnp.concatenate([total, self_piece[...]], axis=0).astype(BF16)
     for z in range(out.shape[0]):
-        out[z, 0:32, :] = gsum[core * 8 + z]
-        out[z, 32:64, :] = gsum[(1 - core) * 8 + z]
+        out[z, 0:32, :] = gsum[z]
+        out[z, 32:64, :] = gsum_arrived[z]
         out[z, 64:96, :] = piece
 
 
-def rows_kernel(info, kept, given, w, grad_dims):
+def rows_kernel(info, packed, w, grad_dims):
     even = info[PLACE + 2] == 0
     kind = info[KIND + info[PLACE]]
-    mine, other = kept[...].astype(F32).reshape(256, 128), given[...].astype(F32).reshape(256, 128)
+    mine = packed[:, 0:32, :].astype(F32).reshape(256, 128)
+    other = packed[:, 32:64, :].astype(F32).reshape(256, 128)
     turned = jnp.concatenate([jnp.where(even, mine, other), jnp.where(even, other, mine)], axis=0)
     grad_dims[...] = lax.dot_general(
         turned.T.astype(BF16), w[kind], (((1,), (1,)), ((), ())), preferred_element_type=F32
@@ -266,15 +263,16 @@
     )(place, links_own, links_sib, block_table)
     tiles_sib = swap(tiles)
 
-    pieces, up, down = [dims], dims, dims
-    for step in range(3):
-        if step == 2:
-            up, down, info = lax.optimization_barrier((up, down, info))
-        up, down = shift(up, 1), shift(down, -1)
-        pieces += [up, down]
+    up, down = shift(dims, 1), shift(dims, -1)
+    far, up, down = lax.optimization_barrier((dims, up, down))
+    far = shift(far, 4)
+    pieces = [dims, up, down]
+    up, down = shift(up, 1), shift(down, -1)
+    up, down, far, info = lax.optimization_barrier((up, down, far, info))
+    pieces += [up, down, far]
+    late = [shift(up, 1), shift(down, -1)]
     pieces_sib = [swap(x) for x in pieces]
-    far = [shift(up[: rows // 2], 1), shift(down[rows // 2 :], -1)]
-    early = pieces[:EARLY] + pieces_sib[:EARLY]
+    early = pieces + pieces_sib
     proj, facts_t = call(
         project_kernel,
         (jax.ShapeDtypeStruct((len(early), rows, width), BF16), jax.ShapeDtypeStruct((width, block), BF16)),
@@ -282,16 +280,16 @@
         flops=2 * len(early) * rows * width * width,
         moved=4 << 20,
     )(info, w_tables, facts, *early)
-    *far, proj = lax.optimization_barrier((*far, proj))
-    pieces, pieces_sib = pieces + far, pieces_sib + [swap(x) for x in far]
+    *late, proj = lax.optimization_barrier((*late, proj))
+    late_sib = [swap(x) for x in late]
     partial = call(
         forward_kernel,
         jax.ShapeDtypeStruct((chips, 544, 128), BF16),
-        [SMEM] + [VMEM] * (5 + 2 * (9 - EARLY)),
+        [SMEM] + [VMEM] * (5 + 2 * len(late)),
         [pltpu.VMEM((2 * n_fact, rows, width), BF16), pltpu.VMEM((chips + 1, block, width), F32)],
         flops=2 * slots * block * block * width,
         moved=8 << 20,
-    )(info, proj, *pieces[EARLY:], *pieces_sib[EARLY:], w_tables, facts_t, tiles, tiles_sib)
+    )(info, proj, *late, *late_sib, w_tables, facts_t, tiles, tiles_sib)
     parts = by_chip(partial)
 
     fact_out, spread, facts_t = call(
@@ -322,39 +320,40 @@
 
     up = shift((keep[3] + give[3].astype(F32)).astype(BF16), 1)
     down = shift((keep[5] + give[5].astype(F32)).astype(BF16), -1)
-    far, up, down = lax.optimization_barrier(((keep[4] + give[4].astype(F32)).astype(BF16), up, down))
-    far = shift(far, 4)
+    far_sum, up, down = lax.optimization_barrier(((keep[4] + give[4].astype(F32)).astype(BF16), up, down))
+    far_sum = shift(far_sum, 4)
     for k in (2, 1):
         up, down = lax.optimization_barrier((partial_sum(k, up), partial_sum(8 - k, down)))
         up, down = shift(up, 1), shift(down, -1)
 
-    tab, gsum, self_piece = call(
+    tab, gsum_own, gsum_sib, self_piece = call(
         slice_kernel,
         (
             jax.ShapeDtypeStruct((384, 128), BF16),
-            jax.ShapeDtypeStruct((2 * n_fact, 32, 128), BF16),
+            jax.ShapeDtypeStruct((n_fact, 32, 128), BF16),
+            jax.ShapeDtypeStruct((n_fact, 32, 128), BF16),
             jax.ShapeDtypeStruct((8, 128), F32),
         ),
-        [SMEM] + [VMEM] * 23,
-        [pltpu.VMEM((3, 32, width), F32)],
+        [SMEM] + [VMEM] * 21,
+        [pltpu.VMEM((3, 32, width), F32), pltpu.VMEM((2 * n_fact, 32, 128), BF16)],
         flops=4 * n_fact * 32 * 128 * width,
         moved=3 << 20,
-    )(info, keep[0], give[0], up, down, far, *pieces, *pieces_sib)
+    )(info, keep[0], give[0], up, down, far_sum, *pieces, *late, *pieces_sib, *late_sib)
+    gsum_arrived = swap(gsum_sib)
     tab = by_chip(tab.reshape(chips, 24, 128))
     packed = call(
-        pack_kernel, jax.ShapeDtypeStruct((n_fact, 96, 128), BF16), [SMEM] + [VMEM] * 3, moved=1 << 19
-    )(info, tab, gsum, self_piece)
+        pack_kernel, jax.ShapeDtypeStruct((n_fact, 96, 128), BF16), [VMEM] * 4, moved=1 << 19
+    )(tab, gsum_own, gsum_arrived, self_piece)
     packed = by_fact(packed)
     pieces_own = by_chip(jnp.broadcast_to(packed[None, :, 64:, :], (chips, n_fact, 32, 128)))
-    given = swap(packed[:, 32:64, :])
 
     grad_dims = call(
         rows_kernel,
         jax.ShapeDtypeStruct((rows, width), F32),
-        [SMEM] + [VMEM] * 3,
+        [SMEM] + [VMEM] * 2,
         flops=2 * rows * width * width,
         moved=2 << 20,
-    )(info, packed[:, :32, :], given, w_tables)
+    )(info, packed, w_tables)
     grad_self, grad_tab = pl.pallas_call(
         final_kernel,
         out_shape=(jax.ShapeDtypeStruct((width, width), F32), jax.ShapeDtypeStruct((3, width, width), F32)),

time: 194 us -> 198 us (1.021)
  waiting for transfers between devices: 20.8 us -> 40 us
  blocking collectives: 105 us -> 96 us
  starting transfers between devices: 46.7 us -> 40.6 us
    ppermute x15 -> x14, waiting for transfers between devices: 14.9 us -> 30.2 us  [shift(): lax.ppermute(x, 'fact', [(i, (i + by) % n_fact) for i in range(n_fact)])]
    all_to_all x4 -> x3, blocking collectives: 93 us -> 84 us  [by_chip(): return lax.all_to_all(x, 'dim', 0, 0, tiled=True, axis_index_groups=same)]
    ppermute x15 -> x14, starting transfers between devices: 24.7 us -> 16.9 us  [shift(): lax.ppermute(x, 'fact', [(i, (i + by) % n_fact) for i in range(n_fact)])]
    all_to_all x0 -> x1, starting transfers between devices: none -> 3.51 us  [by_chip(): return lax.all_to_all(x, 'dim', 0, 0, tiled=True, axis_index_groups=same)]
    all_to_all x0 -> x1, waiting for transfers between devices: none -> 3.48 us  [by_chip(): return lax.all_to_all(x, 'dim', 0, 0, tiled=True, axis_index_groups=same)]
    ppermute x14 -> x13, starting transfers between devices: 22 us -> 20.2 us  [swap(): return lax.ppermute(x, 'dim', pair)]
    ppermute x14 -> x13, waiting for transfers between devices: 5.92 us -> 6.24 us  [swap(): return lax.ppermute(x, 'dim', pair)]
  transfers between devices with their start and end apart: 29 -> 28, of which waited for: 12 -> 19; matrix products, arithmetic and copies ran while one was open for 0% -> 0% of each run, Pallas kernels for 2% -> 2%
where the time goes in v9:
time: 198 us; the launch traced here: 197 us
  blocking collectives  96 us (48%)
  starting transfers between devices  40.6 us (21%)
  waiting for transfers between devices  40 us (20%)
  Pallas kernels  17.1 us (9%)
    all_to_all x3, blocking collectives, by_chip(): return lax.all_to_all(x, 'dim', 0, 0, tiled=True, axis_index_groups=same)  84 us
    ppermute x14, waiting for transfers between devices, shift(): lax.ppermute(x, 'fact', [(i, (i + by) % n_fact) for i in range(n_fact)])  30.2 us
    ppermute x13, starting transfers between devices, swap(): return lax.ppermute(x, 'dim', pair)  20.2 us
    ppermute x14, starting transfers between devices, shift(): lax.ppermute(x, 'fact', [(i, (i + by) % n_fact) for i in range(n_fact)])  16.9 us
    all_to_all x1, blocking collectives, by_fact(): return lax.all_to_all(x, 'fact', 0, 0, tiled=True)  12 us
    ppermute x13, waiting for transfers between devices, swap(): return lax.ppermute(x, 'dim', pair)  6.24 us
  transfers between devices with their start and end apart: 28, of which 19 were waited for; matrix products, arithmetic and copies ran while one was open for 0% of the time, Pallas kernels for 2%

profile of v9, /device:TPU:1, one launch (start us, length us, event | category | flops | bytes accessed | tf_op | source)
XLA Modules:
  0.0 197.2 jit_solution(17628462326511053119)
XLA Ops:
  0.6 3.3 %collective-permute-start.16 = (bf16[32,128,128]{2,1,0:T(8,128)(2,1)}, bf16[32,128,128]{2,1,0:T(8,128)(2,1)S(1)}, u32[]{:S(2)}, u32[]{:S(2)}) collective-permute-start(bf16[32,128,128]{2,1,0:T(8,128)(2,1)} %tiles_own.1), channel_id=1, source_target_pairs={{0,1},{1,0},{2,3},{3,2},{4,5},{5,4},{6,7},{7,6},{8,9},{9,8},{10,11... | collective-permute-start | bytes 3145736 | tf_op jit(solution)/shard_map/ppermute | solution.py:242
  4.0 3.9 %collective-permute-start.1 = (bf16[128,512]{1,0:T(8,128)(2,1)}, bf16[128,512]{1,0:T(8,128)(2,1)S(1)}, u32[]{:S(2)}, u32[]{:S(2)}) collective-permute-start(bf16[128,512]{1,0:T(8,128)(2,1)} %refs_0_.3), channel_id=1, source_target_pairs={{0,224},{32,0},{64,32},{96,64},{128,96},{160,128},{192,160},{224,1... | collective-permute-start | bytes 393224 | tf_op jit(solution)/shard_map/ppermute | solution.py:245
  7.8 3.2 %collective-permute-done.1.refs_2_ = bf16[128,512]{1,0:T(8,128)(2,1)S(1)} collective-permute-done((bf16[128,512]{1,0:T(8,128)(2,1)}, bf16[128,512]{1,0:T(8,128)(2,1)S(1)}, u32[]{:S(2)}, u32[]{:S(2)}) %collective-permute-start.1) | collective-permute-done | bytes 131104 | tf_op jit(solution)/shard_map/ppermute | solution.py:245
  11.0 3.0 %collective-permute-done.refs_1_ = bf16[128,512]{1,0:T(8,128)(2,1)S(1)} collective-permute-done((bf16[128,512]{1,0:T(8,128)(2,1)}, bf16[128,512]{1,0:T(8,128)(2,1)S(1)}, u32[]{:S(2)}, u32[]{:S(2)}) %collective-permute-start) | collective-permute-done | bytes 131104 | tf_op jit(solution)/shard_map/ppermute | solution.py:245
  14.0 1.5 collective-permute-start.4
  15.5 1.3 collective-permute-start.8
  17.4 0.7 concatenate.3.links_own
  18.2 0.6 collective-permute-start.9
  18.8 0.5 collective-permute-done.5.links_sib
  19.5 6.1 %collective-permute-done.4.refs_5_ = bf16[128,512]{1,0:T(8,128)(2,1)S(1)} collective-permute-done((bf16[128,512]{1,0:T(8,128)(2,1)}, bf16[128,512]{1,0:T(8,128)(2,1)S(1)}, u32[]{:S(2)}, u32[]{:S(2)}) %collective-permute-start.4) | collective-permute-done | bytes 131104 | tf_op jit(solution)/shard_map/ppermute | solution.py:245
  25.6 0.7 copy-done.6
  26.3 1.5 shard_map.120.info
  28.1 0.8 collective-permute-start.10
  28.9 0.5 collective-permute-done.3.refs_4_
  29.4 2.1 %collective-permute-start.13 = (bf16[128,512]{1,0:T(8,128)(2,1)S(1)}, bf16[128,512]{1,0:T(8,128)(2,1)S(1)}, u32[]{:S(2)}, u32[]{:S(2)}) collective-permute-start(bf16[128,512]{1,0:T(8,128)(2,1)S(1)} %collective-permute-done.4.refs_5_), channel_id=1, source_target_pairs={{0,1},{1,0},{2,3},{3,2},{4,5},{5,4},{6,7},{7,6},{8,9},{9,8},{10,11... | collective-permute-start | bytes 393224 | tf_op jit(solution)/shard_map/ppermute | solution.py:242
  31.6 0.5 collective-permute-start.12
  32.1 0.5 collective-permute-done.13.refs_11_.refs_13_
  32.6 2.2 %collective-permute-start.7 = (bf16[128,512]{1,0:T(8,128)(2,1)S(1)}, bf16[128,512]{1,0:T(8,128)(2,1)S(1)}, u32[]{:S(2)}, u32[]{:S(2)}) collective-permute-start(bf16[128,512]{1,0:T(8,128)(2,1)S(1)} %collective-permute-done.3.refs_4_), channel_id=1, source_target_pairs={{0,224},{32,0},{64,32},{96,64},{128,96},{160,128},{192,160},{224,1... | collective-permute-start | bytes 393224 | tf_op jit(solution)/shard_map/ppermute | solution.py:245
  34.8 1.6 shard_map.121
  36.4 2.0 collective-permute-done.6.refs_0_.refs_6_
  38.4 0.9 collective-permute-start.14
  39.2 1.0 collective-permute-done.14.refs_2_.refs_14_
  40.6 3.0 %shard_map.122 = bf16[16,544,128]{2,1,0:T(8,128)(2,1)S(1)} custom-call(s32[128]{0:T(128)S(1)} %shard_map.120.info, bf16[12,128,512]{2,1,0:T(8,128)(2,1)S(1)} %get-tuple-element.42.proj, bf16[128,512]{1,0:T(8,128)(2,1)S(1)} %collective-permute-done.6.refs_0_.refs_6_, bf16[128,512]{1,0:T(8,128)(2,1)S(1)} %collective-permute-done.7.refs_1_.refs_7_, ...), custom_call_target="tpu_custom_call" | custom-call | flops 536870912 | bytes 8388608 | tf_op jit(solution)/shard_map/pallas_call | solution.py:285
  43.6 37.5 %all_to_all.25.parts = bf16[16,544,128]{2,1,0:T(8,128)(2,1)S(1)} all-to-all(bf16[16,544,128]{2,1,0:T(8,128)(2,1)S(1)} %shard_map.122), channel_id=1, replica_groups={{0,2,4,6,8,10,12,14,16,18,20,22,24,26,28,30},{1,3,5,7,9,11,13,15,17,19,..., dimensions={0} | all-to-all | bytes 4456448 | tf_op jit(solution)/shard_map/all_to_all | solution.py:248
  81.1 1.2 shard_map.123
  82.3 29.7 %all_to_all.26.grads = bf16[16,512,128]{2,1,0:T(8,128)(2,1)S(1)} all-to-all(bf16[16,512,128]{2,1,0:T(8,128)(2,1)S(1)} %get-tuple-element.47), channel_id=1, replica_groups={{0,2,4,6,8,10,12,14,16,18,20,22,24,26,28,30},{1,3,5,7,9,11,13,15,17,19,..., dimensions={0} | all-to-all | bytes 4194304 | tf_op jit(solution)/shard_map/all_to_all | solution.py:248
  111.9 3.3 %shard_map.124 = (f32[8,528,128]{2,1,0:T(8,128)S(1)}, bf16[8,528,128]{2,1,0:T(8,128)(2,1)S(1)}) custom-call(s32[128]{0:T(128)S(1)} %shard_map.120.info, bf16[16,512,128]{2,1,0:T(8,128)(2,1)S(1)} %all_to_all.26.grads, bf16[16,32,128]{2,1,0:T(8,128)(2,1)S(1)} %get-tuple-element.48.facts_t, bf16[32,128,128]{2,1,0:T(8,128)(2,1)S(1)} %copy-done.1, ...), custom_call_target="tpu_custom_call" | custom-call | flops 536870912 | bytes 9437184 | tf_op jit(solution)/shard_map/pallas_call | solution.py:308
  115.2 3.0 %collective-permute-start.17 = (bf16[8,528,128]{2,1,0:T(8,128)(2,1)S(1)}, bf16[8,528,128]{2,1,0:T(8,128)(2,1)S(1)}, u32[]{:S(2)}, u32[]{:S(2)}) collective-permute-start(bf16[8,528,128]{2,1,0:T(8,128)(2,1)S(1)} %get-tuple-element.50), channel_id=1, source_target_pairs={{0,1},{1,0},{2,3},{3,2},{4,5},{5,4},{6,7},{7,6},{8,9},{9,8},{10,11... | collective-permute-start | bytes 3244040 | tf_op jit(solution)/shard_map/ppermute | solution.py:242
  118.2 2.3 %collective-permute-done.17 = bf16[8,528,128]{2,1,0:T(8,128)(2,1)S(1)} collective-permute-done((bf16[8,528,128]{2,1,0:T(8,128)(2,1)S(1)}, bf16[8,528,128]{2,1,0:T(8,128)(2,1)S(1)}, u32[]{:S(2)}, u32[]{:S(2)}) %collective-permute-start.17) | collective-permute-done | bytes 1081376 | tf_op jit(solution)/shard_map/ppermute | solution.py:242
  120.7 2.5 %collective-permute-start.19 = (bf16[528,128]{1,0:T(8,128)(2,1)S(1)}, bf16[528,128]{1,0:T(8,128)(2,1)S(1)}, u32[]{:S(2)}, u32[]{:S(2)}) collective-permute-start(bf16[528,128]{1,0:T(8,128)(2,1)S(1)} %get-tuple-element.68), channel_id=1, source_target_pairs={{0,224},{32,0},{64,32},{96,64},{128,96},{160,128},{192,160},{224,1... | collective-permute-start | bytes 405512 | tf_op jit(solution)/shard_map/ppermute | solution.py:245
  123.2 2.6 %collective-permute-done.19 = bf16[528,128]{1,0:T(8,128)(2,1)S(1)} collective-permute-done((bf16[528,128]{1,0:T(8,128)(2,1)S(1)}, bf16[528,128]{1,0:T(8,128)(2,1)S(1)}, u32[]{:S(2)}, u32[]{:S(2)}) %collective-permute-start.19) | collective-permute-done | bytes 135200 | tf_op jit(solution)/shard_map/ppermute | solution.py:245
  125.8 3.1 %collective-permute-done.18 = bf16[528,128]{1,0:T(8,128)(2,1)S(1)} collective-permute-done((bf16[528,128]{1,0:T(8,128)(2,1)S(1)}, bf16[528,128]{1,0:T(8,128)(2,1)S(1)}, u32[]{:S(2)}, u32[]{:S(2)}) %collective-permute-start.18) | collective-permute-done | bytes 135200 | tf_op jit(solution)/shard_map/ppermute | solution.py:245
  129.1 2.7 %collective-permute-start.21 = (bf16[528,128]{1,0:T(8,128)(2,1)S(1)}, bf16[528,128]{1,0:T(8,128)(2,1)S(1)}, u32[]{:S(2)}, u32[]{:S(2)}) collective-permute-start(bf16[528,128]{1,0:T(8,128)(2,1)S(1)} %get-tuple-element.54), channel_id=1, source_target_pairs={{0,224},{32,0},{64,32},{96,64},{128,96},{160,128},{192,160},{224,1... | collective-permute-start | bytes 405512 | tf_op jit(solution)/shard_map/ppermute | solution.py:245
  131.7 2.9 %collective-permute-done.20 = bf16[528,128]{1,0:T(8,128)(2,1)S(1)} collective-permute-done((bf16[528,128]{1,0:T(8,128)(2,1)S(1)}, bf16[528,128]{1,0:T(8,128)(2,1)S(1)}, u32[]{:S(2)}, u32[]{:S(2)}) %collective-permute-start.20) | collective-permute-done | bytes 135200 | tf_op jit(solution)/shard_map/ppermute | solution.py:245
  134.6 3.9 %collective-permute-done.21 = bf16[528,128]{1,0:T(8,128)(2,1)S(1)} collective-permute-done((bf16[528,128]{1,0:T(8,128)(2,1)S(1)}, bf16[528,128]{1,0:T(8,128)(2,1)S(1)}, u32[]{:S(2)}, u32[]{:S(2)}) %collective-permute-start.21) | collective-permute-done | bytes 135200 | tf_op jit(solution)/shard_map/ppermute | solution.py:245
  138.7 3.7 %collective-permute-start.23 = (bf16[528,128]{1,0:T(8,128)(2,1)S(1)}, bf16[528,128]{1,0:T(8,128)(2,1)S(1)}, u32[]{:S(2)}, u32[]{:S(2)}) collective-permute-start(bf16[528,128]{1,0:T(8,128)(2,1)S(1)} %get-tuple-element.56), channel_id=1, source_target_pairs={{0,224},{32,0},{64,32},{96,64},{128,96},{160,128},{192,160},{224,1... | collective-permute-start | bytes 405512 | tf_op jit(solution)/shard_map/ppermute | solution.py:245
  142.4 2.8 %collective-permute-done.22.from_below = bf16[528,128]{1,0:T(8,128)(2,1)S(1)} collective-permute-done((bf16[528,128]{1,0:T(8,128)(2,1)S(1)}, bf16[528,128]{1,0:T(8,128)(2,1)S(1)}, u32[]{:S(2)}, u32[]{:S(2)}) %collective-permute-start.22) | collective-permute-done | bytes 135200 | tf_op jit(solution)/shard_map/ppermute | solution.py:245
  145.2 1.7 shard_map.125
  146.9 3.5 %all-to-all-start.2 = ((bf16[16,24,128]{2,1,0:T(8,128)(2,1)}), bf16[16,24,128]{2,1,0:T(8,128)(2,1)S(1)}, u32[]{:S(2)}, u32[]{:S(2)}) async-start(bf16[16,24,128]{2,1,0:T(8,128)(2,1)} %bitcast.15), calls=%async_computation.2 | async-start | bytes 196608 | tf_op jit(solution)/shard_map/all_to_all | solution.py:248
  150.4 2.2 %collective-permute-start.25 = (bf16[8,32,128]{2,1,0:T(8,128)(2,1)S(1)}, bf16[8,32,128]{2,1,0:T(8,128)(2,1)S(1)}, u32[]{:S(2)}, u32[]{:S(2)}) collective-permute-start(bf16[8,32,128]{2,1,0:T(8,128)(2,1)S(1)} %get-tuple-element.60), channel_id=1, source_target_pairs={{0,1},{1,0},{2,3},{3,2},{4,5},{5,4},{6,7},{7,6},{8,9},{9,8},{10,11... | collective-permute-start | bytes 196616 | tf_op jit(solution)/shard_map/ppermute | solution.py:242
  152.7 0.9 collective-permute-done.25.gsum_arrived
  153.6 3.5 %all-to-all-done.2.parts = bf16[16,24,128]{2,1,0:T(8,128)(2,1)S(1)} async-done(((bf16[16,24,128]{2,1,0:T(8,128)(2,1)}), bf16[16,24,128]{2,1,0:T(8,128)(2,1)S(1)}, u32[]{:S(2)}, u32[]{:S(2)}) %all-to-all-start.2) | async-done | bytes 98336 | tf_op jit(solution)/shard_map/all_to_all | solution.py:248
  157.1 12.0 %all_to_all.27.packed = bf16[8,96,128]{2,1,0:T(8,128)(2,1)S(1)} all-to-all(bf16[8,96,128]{2,1,0:T(8,128)(2,1)S(1)} %shard_map.126), channel_id=1, replica_groups=mesh['fact'=8,'dim'=32] {'fact'}, dimensions={0} | all-to-all | bytes 393216 | tf_op jit(solution)/shard_map/all_to_all | solution.py:251
  169.3 16.9 %all_to_all.28.own = bf16[16,8,32,128]{3,2,1,0:T(8,128)(2,1)S(1)} all-to-all(bf16[16,8,32,128]{3,2,1,0:T(8,128)(2,1)S(1)} %broadcast_in_dim.5), channel_id=1, replica_groups={{0,2,4,6,8,10,12,14,16,18,20,22,24,26,28,30},{1,3,5,7,9,11,13,15,17,19,..., dimensions={0} | all-to-all | bytes 2097152 | tf_op jit(solution)/shard_map/all_to_all | solution.py:248
  186.2 5.4 %collective-permute-start.26 = (bf16[16,8,32,128]{3,2,1,0:T(8,128)(2,1)S(1)}, bf16[16,8,32,128]{3,2,1,0:T(8,128)(2,1)S(1)}, u32[]{:S(2)}, u32[]{:S(2)}) collective-permute-start(bf16[16,8,32,128]{3,2,1,0:T(8,128)(2,1)S(1)} %all_to_all.28.own), channel_id=1, source_target_pairs={{0,1},{1,0},{2,3},{3,2},{4,5},{5,4},{6,7},{7,6},{8,9},{9,8},{10,11... | collective-permute-start | bytes 3145736 | tf_op jit(solution)/shard_map/ppermute | solution.py:242
  191.6 1.6 shard_map.127
  193.2 0.7 collective-permute-done.26.sib
  193.9 3.3 %shard_map.128 = (f32[512,512]{1,0:T(8,128)}, f32[3,512,512]{2,1,0:T(8,128)}) custom-call(s32[128]{0:T(128)S(1)} %shard_map.120.info, bf16[16,8,32,128]{3,2,1,0:T(8,128)(2,1)S(1)} %all_to_all.28.own, bf16[16,8,32,128]{3,2,1,0:T(8,128)(2,1)S(1)} %collective-permute-done.26.sib), custom_call_target="tpu_custom_call" | custom-call | bytes 8388608 | tf_op jit(solution)/shard_map/pallas_call | solution.py:357
  (43 shorter events, 1.8 us)
Async XLA Ops:
  0.6 40.0 %collective-permute-start.16 = (bf16[32,128,128]{2,1,0:T(8,128)(2,1)}, bf16[32,128,128]{2,1,0:T(8,128)(2,1)S(1)}, u32[]{:S(2)}, u32[]{:S(2)}) collective-permute-start(bf16[32,128,128]{2,1,0:T(8,128)(2,1)} %tiles_own.1), channel_id=1, source_target_pairs={{0,1},{1,0},{2,3},{3,2},{4,5},{5,4},{6,7},{7,6},{8,9},{9,8},{10,11... | collective-permute-start | bytes 3145736 | tf_op jit(solution)/shard_map/ppermute | solution.py:242
  4.0 7.0 %collective-permute-start.1 = (bf16[128,512]{1,0:T(8,128)(2,1)}, bf16[128,512]{1,0:T(8,128)(2,1)S(1)}, u32[]{:S(2)}, u32[]{:S(2)}) collective-permute-start(bf16[128,512]{1,0:T(8,128)(2,1)} %refs_0_.3), channel_id=1, source_target_pairs={{0,224},{32,0},{64,32},{96,64},{128,96},{160,128},{192,160},{224,1... | collective-permute-start | bytes 393224 | tf_op jit(solution)/shard_map/ppermute | solution.py:245
  7.8 6.1 %collective-permute-start = (bf16[128,512]{1,0:T(8,128)(2,1)}, bf16[128,512]{1,0:T(8,128)(2,1)S(1)}, u32[]{:S(2)}, u32[]{:S(2)}) collective-permute-start(bf16[128,512]{1,0:T(8,128)(2,1)} %refs_0_.3), channel_id=1, source_target_pairs={{0,32},{32,64},{64,96},{96,128},{128,160},{160,192},{192,224},{224... | collective-permute-start | bytes 393224 | tf_op jit(solution)/shard_map/ppermute | solution.py:245
  14.0 11.7 %collective-permute-start.4 = (bf16[128,512]{1,0:T(8,128)(2,1)}, bf16[128,512]{1,0:T(8,128)(2,1)S(1)}, u32[]{:S(2)}, u32[]{:S(2)}) collective-permute-start(bf16[128,512]{1,0:T(8,128)(2,1)} %refs_0_.3), channel_id=1, source_target_pairs={{0,128},{32,160},{64,192},{96,224},{128,0},{160,32},{192,64},{224,... | collective-permute-start | bytes 393224 | tf_op jit(solution)/shard_map/ppermute | solution.py:245
  15.5 16.1 %collective-permute-start.8 = (bf16[128,512]{1,0:T(8,128)(2,1)}, bf16[128,512]{1,0:T(8,128)(2,1)S(1)}, u32[]{:S(2)}, u32[]{:S(2)}) collective-permute-start(bf16[128,512]{1,0:T(8,128)(2,1)} %refs_0_.3), channel_id=1, source_target_pairs={{0,1},{1,0},{2,3},{3,2},{4,5},{5,4},{6,7},{7,6},{8,9},{9,8},{10,11... | collective-permute-start | bytes 393224 | tf_op jit(solution)/shard_map/ppermute | solution.py:242
  18.1 1.1 collective-permute-start.5
  18.2 16.6 %copy-start = (bf16[3,512,512]{2,1,0:T(8,128)(2,1)S(1)}, bf16[3,512,512]{2,1,0:T(8,128)(2,1)}, u32[]{:S(2)}) copy-start(bf16[3,512,512]{2,1,0:T(8,128)(2,1)} %w.5) | copy-start | bytes 4718596
  18.2 16.6 %copy-start.2 = (bf16[128,512]{1,0:T(8,128)(2,1)S(1)}, bf16[128,512]{1,0:T(8,128)(2,1)}, u32[]{:S(2)}) copy-start(bf16[128,512]{1,0:T(8,128)(2,1)} %facts.3) | copy-start | bytes 393220
  18.2 16.6 %copy-start.3 = (bf16[128,512]{1,0:T(8,128)(2,1)S(1)}, bf16[128,512]{1,0:T(8,128)(2,1)}, u32[]{:S(2)}) copy-start(bf16[128,512]{1,0:T(8,128)(2,1)} %refs_0_.3) | copy-start | bytes 393220
  18.2 13.4 %collective-permute-start.9 = (bf16[128,512]{1,0:T(8,128)(2,1)S(1)}, bf16[128,512]{1,0:T(8,128)(2,1)S(1)}, u32[]{:S(2)}, u32[]{:S(2)}) collective-permute-start(bf16[128,512]{1,0:T(8,128)(2,1)S(1)} %collective-permute-done.refs_1_), channel_id=1, source_target_pairs={{0,1},{1,0},{2,3},{3,2},{4,5},{5,4},{6,7},{7,6},{8,9},{9,8},{10,11... | collective-permute-start | bytes 393224 | tf_op jit(solution)/shard_map/ppermute | solution.py:242
  19.2 8.9 %collective-permute-start.2 = (bf16[128,512]{1,0:T(8,128)(2,1)S(1)}, bf16[128,512]{1,0:T(8,128)(2,1)S(1)}, u32[]{:S(2)}, u32[]{:S(2)}) collective-permute-start(bf16[128,512]{1,0:T(8,128)(2,1)S(1)} %collective-permute-done.refs_1_), channel_id=1, source_target_pairs={{0,32},{32,64},{64,96},{96,128},{128,160},{160,192},{192,224},{224... | collective-permute-start | bytes 393224 | tf_op jit(solution)/shard_map/ppermute | solution.py:245
  25.6 3.8 %collective-permute-start.3 = (bf16[128,512]{1,0:T(8,128)(2,1)S(1)}, bf16[128,512]{1,0:T(8,128)(2,1)S(1)}, u32[]{:S(2)}, u32[]{:S(2)}) collective-permute-start(bf16[128,512]{1,0:T(8,128)(2,1)S(1)} %collective-permute-done.1.refs_2_), channel_id=1, source_target_pairs={{0,224},{32,0},{64,32},{96,64},{128,96},{160,128},{192,160},{224,1... | collective-permute-start | bytes 393224 | tf_op jit(solution)/shard_map/ppermute | solution.py:245
  25.6 0.7 copy-start.6
  27.8 12.8 %copy-start.1 = (bf16[32,128,128]{2,1,0:T(8,128)(2,1)S(1)}, bf16[32,128,128]{2,1,0:T(8,128)(2,1)}, u32[]{:S(2)}) copy-start(bf16[32,128,128]{2,1,0:T(8,128)(2,1)} %tiles_own.1) | copy-start | bytes 3145732
  28.1 4.0 %collective-permute-start.10 = (bf16[128,512]{1,0:T(8,128)(2,1)S(1)}, bf16[128,512]{1,0:T(8,128)(2,1)S(1)}, u32[]{:S(2)}, u32[]{:S(2)}) collective-permute-start(bf16[128,512]{1,0:T(8,128)(2,1)S(1)} %collective-permute-done.1.refs_2_), channel_id=1, source_target_pairs={{0,1},{1,0},{2,3},{3,2},{4,5},{5,4},{6,7},{7,6},{8,9},{9,8},{10,11... | collective-permute-start | bytes 393224 | tf_op jit(solution)/shard_map/ppermute | solution.py:242
  29.4 3.1 %collective-permute-start.13 = (bf16[128,512]{1,0:T(8,128)(2,1)S(1)}, bf16[128,512]{1,0:T(8,128)(2,1)S(1)}, u32[]{:S(2)}, u32[]{:S(2)}) collective-permute-start(bf16[128,512]{1,0:T(8,128)(2,1)S(1)} %collective-permute-done.4.refs_5_), channel_id=1, source_target_pairs={{0,1},{1,0},{2,3},{3,2},{4,5},{5,4},{6,7},{7,6},{8,9},{9,8},{10,11... | collective-permute-start | bytes 393224 | tf_op jit(solution)/shard_map/ppermute | solution.py:242
  31.6 3.2 %collective-permute-start.11 = (bf16[128,512]{1,0:T(8,128)(2,1)S(1)}, bf16[128,512]{1,0:T(8,128)(2,1)S(1)}, u32[]{:S(2)}, u32[]{:S(2)}) collective-permute-start(bf16[128,512]{1,0:T(8,128)(2,1)S(1)} %collective-permute-done.2.refs_3_), channel_id=1, source_target_pairs={{0,1},{1,0},{2,3},{3,2},{4,5},{5,4},{6,7},{7,6},{8,9},{9,8},{10,11... | collective-permute-start | bytes 393224 | tf_op jit(solution)/shard_map/ppermute | solution.py:242
  31.6 3.2 %collective-permute-start.12 = (bf16[128,512]{1,0:T(8,128)(2,1)S(1)}, bf16[128,512]{1,0:T(8,128)(2,1)S(1)}, u32[]{:S(2)}, u32[]{:S(2)}) collective-permute-start(bf16[128,512]{1,0:T(8,128)(2,1)S(1)} %collective-permute-done.3.refs_4_), channel_id=1, source_target_pairs={{0,1},{1,0},{2,3},{3,2},{4,5},{5,4},{6,7},{7,6},{8,9},{9,8},{10,11... | collective-permute-start | bytes 393224 | tf_op jit(solution)/shard_map/ppermute | solution.py:242
  32.1 6.3 %collective-permute-start.6 = (bf16[128,512]{1,0:T(8,128)(2,1)S(1)}, bf16[128,512]{1,0:T(8,128)(2,1)S(1)}, u32[]{:S(2)}, u32[]{:S(2)}) collective-permute-start(bf16[128,512]{1,0:T(8,128)(2,1)S(1)} %collective-permute-done.2.refs_3_), channel_id=1, source_target_pairs={{0,32},{32,64},{64,96},{96,128},{128,160},{160,192},{192,224},{224... | collective-permute-start | bytes 393224 | tf_op jit(solution)/shard_map/ppermute | solution.py:245
  32.6 5.8 %collective-permute-start.7 = (bf16[128,512]{1,0:T(8,128)(2,1)S(1)}, bf16[128,512]{1,0:T(8,128)(2,1)S(1)}, u32[]{:S(2)}, u32[]{:S(2)}) collective-permute-start(bf16[128,512]{1,0:T(8,128)(2,1)S(1)} %collective-permute-done.3.refs_4_), channel_id=1, source_target_pairs={{0,224},{32,0},{64,32},{96,64},{128,96},{160,128},{192,160},{224,1... | collective-permute-start | bytes 393224 | tf_op jit(solution)/shard_map/ppermute | solution.py:245
  38.4 1.9 collective-permute-start.14
  39.2 1.3 collective-permute-start.15
  43.6 37.5 %copy-start.4 = (bf16[512,512]{1,0:T(8,128)(2,1)S(1)}, bf16[512,512]{1,0:T(8,128)(2,1)}, u32[]{:S(2)}) copy-start(bf16[512,512]{1,0:T(8,128)(2,1)} %w.4) | copy-start | bytes 1572868
  43.6 37.5 %copy-start.5 = (bf16[128,512]{1,0:T(8,128)(2,1)S(1)}, bf16[128,512]{1,0:T(8,128)(2,1)}, u32[]{:S(2)}) copy-start(bf16[128,512]{1,0:T(8,128)(2,1)} %cot.1) | copy-start | bytes 393220
  115.2 5.4 %collective-permute-start.17 = (bf16[8,528,128]{2,1,0:T(8,128)(2,1)S(1)}, bf16[8,528,128]{2,1,0:T(8,128)(2,1)S(1)}, u32[]{:S(2)}, u32[]{:S(2)}) collective-permute-start(bf16[8,528,128]{2,1,0:T(8,128)(2,1)S(1)} %get-tuple-element.50), channel_id=1, source_target_pairs={{0,1},{1,0},{2,3},{3,2},{4,5},{5,4},{6,7},{7,6},{8,9},{9,8},{10,11... | collective-permute-start | bytes 3244040 | tf_op jit(solution)/shard_map/ppermute | solution.py:242
  120.7 5.1 %collective-permute-start.19 = (bf16[528,128]{1,0:T(8,128)(2,1)S(1)}, bf16[528,128]{1,0:T(8,128)(2,1)S(1)}, u32[]{:S(2)}, u32[]{:S(2)}) collective-permute-start(bf16[528,128]{1,0:T(8,128)(2,1)S(1)} %get-tuple-element.68), channel_id=1, source_target_pairs={{0,224},{32,0},{64,32},{96,64},{128,96},{160,128},{192,160},{224,1... | collective-permute-start | bytes 405512 | tf_op jit(solution)/shard_map/ppermute | solution.py:245
  123.2 5.7 %collective-permute-start.18 = (bf16[528,128]{1,0:T(8,128)(2,1)S(1)}, bf16[528,128]{1,0:T(8,128)(2,1)S(1)}, u32[]{:S(2)}, u32[]{:S(2)}) collective-permute-start(bf16[528,128]{1,0:T(8,128)(2,1)S(1)} %get-tuple-element.69), channel_id=1, source_target_pairs={{0,32},{32,64},{64,96},{96,128},{128,160},{160,192},{192,224},{224... | collective-permute-start | bytes 405512 | tf_op jit(solution)/shard_map/ppermute | solution.py:245
  129.0 5.7 %collective-permute-start.20 = (bf16[528,128]{1,0:T(8,128)(2,1)S(1)}, bf16[528,128]{1,0:T(8,128)(2,1)S(1)}, u32[]{:S(2)}, u32[]{:S(2)}) collective-permute-start(bf16[528,128]{1,0:T(8,128)(2,1)S(1)} %get-tuple-element.53), channel_id=1, source_target_pairs={{0,32},{32,64},{64,96},{96,128},{128,160},{160,192},{192,224},{224... | collective-permute-start | bytes 405512 | tf_op jit(solution)/shard_map/ppermute | solution.py:245
  129.1 9.5 %collective-permute-start.21 = (bf16[528,128]{1,0:T(8,128)(2,1)S(1)}, bf16[528,128]{1,0:T(8,128)(2,1)S(1)}, u32[]{:S(2)}, u32[]{:S(2)}) collective-permute-start(bf16[528,128]{1,0:T(8,128)(2,1)S(1)} %get-tuple-element.54), channel_id=1, source_target_pairs={{0,224},{32,0},{64,32},{96,64},{128,96},{160,128},{192,160},{224,1... | collective-permute-start | bytes 405512 | tf_op jit(solution)/shard_map/ppermute | solution.py:245
  131.7 10.7 %collective-permute-start.24 = (bf16[528,128]{1,0:T(8,128)(2,1)S(1)}, bf16[528,128]{1,0:T(8,128)(2,1)S(1)}, u32[]{:S(2)}, u32[]{:S(2)}) collective-permute-start(bf16[528,128]{1,0:T(8,128)(2,1)S(1)} %get-tuple-element.57), channel_id=1, source_target_pairs={{0,128},{32,160},{64,192},{96,224},{128,0},{160,32},{192,64},{224,... | collective-permute-start | bytes 405512 | tf_op jit(solution)/shard_map/ppermute | solution.py:245
  138.6 6.5 %collective-permute-start.22 = (bf16[528,128]{1,0:T(8,128)(2,1)S(1)}, bf16[528,128]{1,0:T(8,128)(2,1)S(1)}, u32[]{:S(2)}, u32[]{:S(2)}) collective-permute-start(bf16[528,128]{1,0:T(8,128)(2,1)S(1)} %get-tuple-element.55), channel_id=1, source_target_pairs={{0,32},{32,64},{64,96},{96,128},{128,160},{160,192},{192,224},{224... | collective-permute-start | bytes 405512 | tf_op jit(solution)/shard_map/ppermute | solution.py:245
  138.7 6.5 %collective-permute-start.23 = (bf16[528,128]{1,0:T(8,128)(2,1)S(1)}, bf16[528,128]{1,0:T(8,128)(2,1)S(1)}, u32[]{:S(2)}, u32[]{:S(2)}) collective-permute-start(bf16[528,128]{1,0:T(8,128)(2,1)S(1)} %get-tuple-element.56), channel_id=1, source_target_pairs={{0,224},{32,0},{64,32},{96,64},{128,96},{160,128},{192,160},{224,1... | collective-permute-start | bytes 405512 | tf_op jit(solution)/shard_map/ppermute | solution.py:245
  146.9 10.1 %all-to-all-start.2 = ((bf16[16,24,128]{2,1,0:T(8,128)(2,1)}), bf16[16,24,128]{2,1,0:T(8,128)(2,1)S(1)}, u32[]{:S(2)}, u32[]{:S(2)}) async-start(bf16[16,24,128]{2,1,0:T(8,128)(2,1)} %bitcast.15), calls=%async_computation.2 | async-start | bytes 196608 | tf_op jit(solution)/shard_map/all_to_all | solution.py:248
  150.4 3.1 %collective-permute-start.25 = (bf16[8,32,128]{2,1,0:T(8,128)(2,1)S(1)}, bf16[8,32,128]{2,1,0:T(8,128)(2,1)S(1)}, u32[]{:S(2)}, u32[]{:S(2)}) collective-permute-start(bf16[8,32,128]{2,1,0:T(8,128)(2,1)S(1)} %get-tuple-element.60), channel_id=1, source_target_pairs={{0,1},{1,0},{2,3},{3,2},{4,5},{5,4},{6,7},{7,6},{8,9},{9,8},{10,11... | collective-permute-start | bytes 196616 | tf_op jit(solution)/shard_map/ppermute | solution.py:242
  186.2 7.7 %collective-permute-start.26 = (bf16[16,8,32,128]{3,2,1,0:T(8,128)(2,1)S(1)}, bf16[16,8,32,128]{3,2,1,0:T(8,128)(2,1)S(1)}, u32[]{:S(2)}, u32[]{:S(2)}) collective-permute-start(bf16[16,8,32,128]{3,2,1,0:T(8,128)(2,1)S(1)} %all_to_all.28.own), channel_id=1, source_target_pairs={{0,1},{1,0},{2,3},{3,2},{4,5},{5,4},{6,7},{7,6},{8,9},{9,8},{10,11... | collective-permute-start | bytes 3145736 | tf_op jit(solution)/shard_map/ppermute | solution.py:242

commit v10 on v8

--- a/solution.py
+++ b/solution.py
@@ -15,6 +15,7 @@
 
 ORDER = (0, -1, 1, -2, 2, -3, 3)
 EARLY = 5
+FIRST, REST = (3, 5), (0, 1, 2, 4, 6, 7)
 LIST = 40
 COUNT, KIND, PLACE, INFO = 80, 96, 112, 128
 
@@ -113,7 +114,7 @@
         facts_t[chip] = parts[chip, 512:544, :]
 
 
-def backward_kernel(info, grads, facts_t, tiles_own, tiles_sib, keep, give, acc, weight):
+def backward_kernel(info, grads, facts_t, tiles_own, tiles_sib, keep, give_first, give_rest, acc, weight):
     fact_pos, core = info[PLACE], info[PLACE + 2]
     acc[...] = jnp.zeros_like(acc)
     for side, tiles in enumerate((tiles_own, tiles_sib)):
@@ -140,15 +141,16 @@
         )
     for q in range(4):
         weight[q] = total[:, q * 128 : (q + 1) * 128]
-    for out, who, kind in ((keep, core, F32), (give, 1 - core, BF16)):
-        for k in range(8):
+    given = [(give_first, at, k) for at, k in enumerate(FIRST)] + [(give_rest, at, k) for at, k in enumerate(REST)]
+    for who, kind, slices in ((core, F32, [(keep, k, k) for k in range(8)]), (1 - core, BF16, given)):
+        for out, at, k in slices:
             z = (fact_pos + k) & 7
             features = pl.ds(pl.multiple_of(who * 256 + z * 32, 32), 32)
-            for at in range(16):
-                out[k, at * 32 : (at + 1) * 32, :] = acc[at, features, :].astype(kind)
+            for block in range(16):
+                out[at, block * 32 : (block + 1) * 32, :] = acc[block, features, :].astype(kind)
             rows = pl.ds(pl.multiple_of(who * half + (z & 1) * 8, 8), 8)
             mine = weight[z >> 1, rows, :]
-            out[k, 512:528, :] = jnp.concatenate([mine, jnp.zeros_like(mine)], axis=0).astype(kind)
+            out[at, 512:528, :] = jnp.concatenate([mine, jnp.zeros_like(mine)], axis=0).astype(kind)
 
 
 def slice_kernel(info, kept, given, from_below, from_above, from_far, *refs):
@@ -268,7 +270,7 @@
 
     pieces, up, down = [dims], dims, dims
     for step in range(3):
-        if step == 2:
+        if step == 1:
             up, down, info = lax.optimization_barrier((up, down, info))
         up, down = shift(up, 1), shift(down, -1)
         pieces += [up, down]
@@ -307,23 +309,30 @@
     )(parts, facts, w_self, cot)
     grads = by_chip(spread)
 
-    keep, give = call(
+    keep, give_first, give_rest = call(
         backward_kernel,
-        (jax.ShapeDtypeStruct((n_fact, 528, 128), F32), jax.ShapeDtypeStruct((n_fact, 528, 128), BF16)),
+        (
+            jax.ShapeDtypeStruct((n_fact, 528, 128), F32),
+            jax.ShapeDtypeStruct((len(FIRST), 528, 128), BF16),
+            jax.ShapeDtypeStruct((len(REST), 528, 128), BF16),
+        ),
         [SMEM] + [VMEM] * 4,
         [pltpu.VMEM((2 * n_fact + 1, width, block), F32), pltpu.VMEM((4, width // chips, 128), F32)],
         flops=2 * slots * block * block * width,
         moved=9 << 20,
     )(info, grads, facts_t, tiles, tiles_sib)
-    give = swap(give)
+    give_first, give_rest = lax.optimization_barrier((swap(give_first), give_rest))
+    give_rest = swap(give_rest)
+    give = {k: give_first[at] for at, k in enumerate(FIRST)}
 
     def partial_sum(k, arrived):
         return (keep[k] + give[k].astype(F32) + arrived.astype(F32)).astype(BF16)
 
     up = shift((keep[3] + give[3].astype(F32)).astype(BF16), 1)
     down = shift((keep[5] + give[5].astype(F32)).astype(BF16), -1)
-    far, up, down = lax.optimization_barrier(((keep[4] + give[4].astype(F32)).astype(BF16), up, down))
-    far = shift(far, 4)
+    give_rest, up, down = lax.optimization_barrier((give_rest, up, down))
+    give |= {k: give_rest[at] for at, k in enumerate(REST)}
+    far = shift((keep[4] + give[4].astype(F32)).astype(BF16), 4)
     for k in (2, 1):
         up, down = lax.optimization_barrier((partial_sum(k, up), partial_sum(8 - k, down)))
         up, down = shift(up, 1), shift(down, -1)

time: 194 us -> 193 us (level)
  waiting for transfers between devices: 20.8 us -> 18.7 us
  blocking collectives: 105 us -> 107 us
    ppermute x14 -> x15, starting transfers between devices: 22 us -> 24.9 us  [swap(): return lax.ppermute(x, 'dim', pair)]
    ppermute x14 -> x15, waiting for transfers between devices: 5.92 us -> 5.5 us  [swap(): return lax.ppermute(x, 'dim', pair)]
  transfers between devices with their start and end apart: 29 -> 30, of which waited for: 12 -> 12; matrix products, arithmetic and copies ran while one was open for 0% -> 1% of each run, Pallas kernels for 2% -> 2%
where the time goes in v10:
time: 193 us
  blocking collectives  107 us (55%)
  starting transfers between devices  47.8 us (25%)
  waiting for transfers between devices  18.7 us (10%)
  Pallas kernels  15.7 us (8%)
    all_to_all x4, blocking collectives, by_chip(): return lax.all_to_all(x, 'dim', 0, 0, tiled=True, axis_index_groups=same)  94.7 us
    ppermute x15, starting transfers between devices, swap(): return lax.ppermute(x, 'dim', pair)  24.9 us
    ppermute x15, starting transfers between devices, shift(): lax.ppermute(x, 'fact', [(i, (i + by) % n_fact) for i in range(n_fact)])  23 us
    ppermute x15, waiting for transfers between devices, shift(): lax.ppermute(x, 'fact', [(i, (i + by) % n_fact) for i in range(n_fact)])  13.2 us
    all_to_all x1, blocking collectives, by_fact(): return lax.all_to_all(x, 'fact', 0, 0, tiled=True)  12.5 us
    ppermute x15, waiting for transfers between devices, swap(): return lax.ppermute(x, 'dim', pair)  5.5 us
  transfers between devices with their start and end apart: 30, of which 12 were waited for; matrix products, arithmetic and copies ran while one was open for 1% of the time, Pallas kernels for 2%

profile of v10, /device:TPU:1, one launch (start us, length us, event | category | flops | bytes accessed | tf_op | source)
XLA Modules:
  0.0 193.0 jit_solution(11652912100217311056)
XLA Ops:
  0.6 3.3 %collective-permute-start.18 = (bf16[32,128,128]{2,1,0:T(8,128)(2,1)}, bf16[32,128,128]{2,1,0:T(8,128)(2,1)S(1)}, u32[]{:S(2)}, u32[]{:S(2)}) collective-permute-start(bf16[32,128,128]{2,1,0:T(8,128)(2,1)} %tiles_own.1), channel_id=1, source_target_pairs={{0,1},{1,0},{2,3},{3,2},{4,5},{5,4},{6,7},{7,6},{8,9},{9,8},{10,11... | collective-permute-start | bytes 3145736 | tf_op jit(solution)/shard_map/ppermute | solution.py:247
  4.0 3.9 %collective-permute-start.1 = (bf16[128,512]{1,0:T(8,128)(2,1)}, bf16[128,512]{1,0:T(8,128)(2,1)S(1)}, u32[]{:S(2)}, u32[]{:S(2)}) collective-permute-start(bf16[128,512]{1,0:T(8,128)(2,1)} %refs_0_.3), channel_id=1, source_target_pairs={{0,224},{32,0},{64,32},{96,64},{128,96},{160,128},{192,160},{224,1... | collective-permute-start | bytes 393224 | tf_op jit(solution)/shard_map/ppermute | solution.py:250
  8.5 0.7 concatenate.3.links_own
  9.2 0.4 collective-permute-start.2
  9.6 0.7 collective-permute-done.2.links_sib
  10.3 0.7 copy-done.6
  11.0 1.5 shard_map.120.info
  12.6 1.4 collective-permute-done.refs_1_
  14.0 2.7 %collective-permute-start.6 = (bf16[128,512]{1,0:T(8,128)(2,1)S(1)}, bf16[128,512]{1,0:T(8,128)(2,1)S(1)}, u32[]{:S(2)}, u32[]{:S(2)}) collective-permute-start(bf16[128,512]{1,0:T(8,128)(2,1)S(1)} %collective-permute-done.1.refs_2_), channel_id=1, source_target_pairs={{0,224},{32,0},{64,32},{96,64},{128,96},{160,128},{192,160},{224,1... | collective-permute-start | bytes 393224 | tf_op jit(solution)/shard_map/ppermute | solution.py:250
  16.6 1.7 collective-permute-start.9
  18.4 0.6 collective-permute-done.3.refs_3_
  19.0 2.7 %collective-permute-start.7 = (bf16[128,512]{1,0:T(8,128)(2,1)S(1)}, bf16[128,512]{1,0:T(8,128)(2,1)S(1)}, u32[]{:S(2)}, u32[]{:S(2)}) collective-permute-start(bf16[128,512]{1,0:T(8,128)(2,1)S(1)} %collective-permute-done.6.refs_4_), channel_id=1, source_target_pairs={{0,224},{32,0},{64,32},{96,64},{128,96},{160,128},{192,160},{224,1... | collective-permute-start | bytes 393224 | tf_op jit(solution)/shard_map/ppermute | solution.py:250
  21.7 2.9 %collective-permute-start.11 = (bf16[128,512]{1,0:T(8,128)(2,1)S(1)}, bf16[128,512]{1,0:T(8,128)(2,1)S(1)}, u32[]{:S(2)}, u32[]{:S(2)}) collective-permute-start(bf16[128,512]{1,0:T(8,128)(2,1)S(1)} %collective-permute-done.1.refs_2_), channel_id=1, source_target_pairs={{0,1},{1,0},{2,3},{3,2},{4,5},{5,4},{6,7},{7,6},{8,9},{9,8},{10,11... | collective-permute-start | bytes 393224 | tf_op jit(solution)/shard_map/ppermute | solution.py:247
  24.6 2.9 %collective-permute-start.12 = (bf16[128,512]{1,0:T(8,128)(2,1)S(1)}, bf16[128,512]{1,0:T(8,128)(2,1)S(1)}, u32[]{:S(2)}, u32[]{:S(2)}) collective-permute-start(bf16[128,512]{1,0:T(8,128)(2,1)S(1)} %collective-permute-done.3.refs_3_), channel_id=1, source_target_pairs={{0,1},{1,0},{2,3},{3,2},{4,5},{5,4},{6,7},{7,6},{8,9},{9,8},{10,11... | collective-permute-start | bytes 393224 | tf_op jit(solution)/shard_map/ppermute | solution.py:247
  27.6 3.0 %collective-permute-start.8 = (bf16[64,512]{1,0:T(8,128)(2,1)S(1)}, bf16[64,512]{1,0:T(8,128)(2,1)S(1)}, u32[]{:S(2)}, u32[]{:S(2)}) collective-permute-start(bf16[64,512]{1,0:T(8,128)(2,1)S(1)} %slice.85), channel_id=1, source_target_pairs={{0,224},{32,0},{64,32},{96,64},{128,96},{160,128},{192,160},{224,1... | collective-permute-start | bytes 196616 | tf_op jit(solution)/shard_map/ppermute | solution.py:250
  30.7 0.7 collective-permute-start.14
  31.4 0.3 collective-permute-start.15
  31.6 1.4 shard_map.121
  33.1 0.5 collective-permute-start.16
  33.7 0.8 collective-permute-done.16.refs_6_.refs_16_
  34.5 0.4 collective-permute-done.17.refs_7_.refs_17_
  34.9 2.5 %shard_map.122 = bf16[16,544,128]{2,1,0:T(8,128)(2,1)S(1)} custom-call(s32[128]{0:T(128)S(1)} %shard_map.120.info, bf16[10,128,512]{2,1,0:T(8,128)(2,1)S(1)} %get-tuple-element.36.proj, bf16[128,512]{1,0:T(8,128)(2,1)S(1)} %collective-permute-done.4.refs_0_.refs_5_, bf16[128,512]{1,0:T(8,128)(2,1)S(1)} %collective-permute-done.7.refs_1_.refs_6_, ...), custom_call_target="tpu_custom_call" | custom-call | flops 536870912 | bytes 8388608 | tf_op jit(solution)/shard_map/pallas_call | solution.py:289
  37.4 38.1 %all_to_all.25.parts = bf16[16,544,128]{2,1,0:T(8,128)(2,1)S(1)} all-to-all(bf16[16,544,128]{2,1,0:T(8,128)(2,1)S(1)} %shard_map.122), channel_id=1, replica_groups={{0,2,4,6,8,10,12,14,16,18,20,22,24,26,28,30},{1,3,5,7,9,11,13,15,17,19,..., dimensions={0} | all-to-all | bytes 4456448 | tf_op jit(solution)/shard_map/all_to_all | solution.py:253
  75.5 1.2 shard_map.123
  76.7 30.2 %all_to_all.26.grads = bf16[16,512,128]{2,1,0:T(8,128)(2,1)S(1)} all-to-all(bf16[16,512,128]{2,1,0:T(8,128)(2,1)S(1)} %get-tuple-element.41), channel_id=1, replica_groups={{0,2,4,6,8,10,12,14,16,18,20,22,24,26,28,30},{1,3,5,7,9,11,13,15,17,19,..., dimensions={0} | all-to-all | bytes 4194304 | tf_op jit(solution)/shard_map/all_to_all | solution.py:253
  106.8 2.7 %shard_map.124 = (f32[8,528,128]{2,1,0:T(8,128)S(1)}, bf16[2,528,128]{2,1,0:T(8,128)(2,1)S(1)}, bf16[6,528,128]{2,1,0:T(8,128)(2,1)S(1)}) custom-call(s32[128]{0:T(128)S(1)} %shard_map.120.info, bf16[16,512,128]{2,1,0:T(8,128)(2,1)S(1)} %all_to_all.26.grads, bf16[16,32,128]{2,1,0:T(8,128)(2,1)S(1)} %get-tuple-element.42.facts_t, ...), custom_call_target="tpu_custom_call" | custom-call | flops 536870912 | bytes 9437184 | tf_op jit(solution)/shard_map/pallas_call | solution.py:312
  109.5 2.7 %collective-permute-start.19 = (bf16[2,528,128]{2,1,0:T(8,128)(2,1)S(1)}, bf16[2,528,128]{2,1,0:T(8,128)(2,1)S(1)}, u32[]{:S(2)}, u32[]{:S(2)}) collective-permute-start(bf16[2,528,128]{2,1,0:T(8,128)(2,1)S(1)} %get-tuple-element.44), channel_id=1, source_target_pairs={{0,1},{1,0},{2,3},{3,2},{4,5},{5,4},{6,7},{7,6},{8,9},{9,8},{10,11... | collective-permute-start | bytes 811016 | tf_op jit(solution)/shard_map/ppermute | solution.py:247
  112.2 1.2 collective-permute-done.19
  113.4 0.4 collective-permute-start.20
  113.8 1.9 collective-permute-start.22
  115.7 3.2 %collective-permute-done.22 = bf16[528,128]{1,0:T(8,128)(2,1)S(1)} collective-permute-done((bf16[528,128]{1,0:T(8,128)(2,1)S(1)}, bf16[528,128]{1,0:T(8,128)(2,1)S(1)}, u32[]{:S(2)}, u32[]{:S(2)}) %collective-permute-start.22) | collective-permute-done | bytes 135200 | tf_op jit(solution)/shard_map/ppermute | solution.py:250
  118.9 2.7 %collective-permute-done.21 = bf16[528,128]{1,0:T(8,128)(2,1)S(1)} collective-permute-done((bf16[528,128]{1,0:T(8,128)(2,1)S(1)}, bf16[528,128]{1,0:T(8,128)(2,1)S(1)}, u32[]{:S(2)}, u32[]{:S(2)}) %collective-permute-start.21) | collective-permute-done | bytes 135200 | tf_op jit(solution)/shard_map/ppermute | solution.py:250
  121.9 2.7 %collective-permute-start.24 = (bf16[528,128]{1,0:T(8,128)(2,1)S(1)}, bf16[528,128]{1,0:T(8,128)(2,1)S(1)}, u32[]{:S(2)}, u32[]{:S(2)}) collective-permute-start(bf16[528,128]{1,0:T(8,128)(2,1)S(1)} %get-tuple-element.52), channel_id=1, source_target_pairs={{0,224},{32,0},{64,32},{96,64},{128,96},{160,128},{192,160},{224,1... | collective-permute-start | bytes 405512 | tf_op jit(solution)/shard_map/ppermute | solution.py:250
  124.6 1.9 collective-permute-start.27
  126.5 0.8 collective-permute-done.23
  127.4 4.0 %collective-permute-start.26 = (bf16[528,128]{1,0:T(8,128)(2,1)S(1)}, bf16[528,128]{1,0:T(8,128)(2,1)S(1)}, u32[]{:S(2)}, u32[]{:S(2)}) collective-permute-start(bf16[528,128]{1,0:T(8,128)(2,1)S(1)} %get-tuple-element.54), channel_id=1, source_target_pairs={{0,224},{32,0},{64,32},{96,64},{128,96},{160,128},{192,160},{224,1... | collective-permute-start | bytes 405512 | tf_op jit(solution)/shard_map/ppermute | solution.py:250
  131.5 3.7 %collective-permute-done.27.from_far = bf16[528,128]{1,0:T(8,128)(2,1)S(1)} collective-permute-done((bf16[528,128]{1,0:T(8,128)(2,1)S(1)}, bf16[528,128]{1,0:T(8,128)(2,1)S(1)}, u32[]{:S(2)}, u32[]{:S(2)}) %collective-permute-start.27) | collective-permute-done | bytes 135200 | tf_op jit(solution)/shard_map/ppermute | solution.py:250
  135.1 0.8 collective-permute-done.25.from_below
  136.0 1.1 shard_map.125
  137.0 11.8 %all_to_all.27.parts = bf16[16,24,128]{2,1,0:T(8,128)(2,1)S(1)} all-to-all(bf16[16,24,128]{2,1,0:T(8,128)(2,1)S(1)} %bitcast.34), channel_id=1, replica_groups={{0,2,4,6,8,10,12,14,16,18,20,22,24,26,28,30},{1,3,5,7,9,11,13,15,17,19,..., dimensions={0} | all-to-all | bytes 196608 | tf_op jit(solution)/shard_map/all_to_all | solution.py:253
  148.8 0.6 shard_map.126
  149.4 12.5 %all_to_all.28 = bf16[8,96,128]{2,1,0:T(8,128)(2,1)S(1)} all-to-all(bf16[8,96,128]{2,1,0:T(8,128)(2,1)S(1)} %shard_map.126), channel_id=1, replica_groups=mesh['fact'=8,'dim'=32] {'fact'}, dimensions={0} | all-to-all | bytes 393216 | tf_op jit(solution)/shard_map/all_to_all | solution.py:256
  161.9 0.2 broadcast_in_dim.5
  162.1 14.7 %all_to_all.29.own = bf16[16,8,32,128]{3,2,1,0:T(8,128)(2,1)S(1)} all-to-all(bf16[16,8,32,128]{3,2,1,0:T(8,128)(2,1)S(1)} %broadcast_in_dim.5), channel_id=1, replica_groups={{0,2,4,6,8,10,12,14,16,18,20,22,24,26,28,30},{1,3,5,7,9,11,13,15,17,19,..., dimensions={0} | all-to-all | bytes 2097152 | tf_op jit(solution)/shard_map/all_to_all | solution.py:253
  176.8 9.0 %collective-permute-start.29 = (bf16[16,8,32,128]{3,2,1,0:T(8,128)(2,1)S(1)}, bf16[16,8,32,128]{3,2,1,0:T(8,128)(2,1)S(1)}, u32[]{:S(2)}, u32[]{:S(2)}) collective-permute-start(bf16[16,8,32,128]{3,2,1,0:T(8,128)(2,1)S(1)} %all_to_all.29.own), channel_id=1, source_target_pairs={{0,1},{1,0},{2,3},{3,2},{4,5},{5,4},{6,7},{7,6},{8,9},{9,8},{10,11... | collective-permute-start | bytes 3145736 | tf_op jit(solution)/shard_map/ppermute | solution.py:247
  185.8 2.4 %collective-permute-done.28.given = bf16[8,32,128]{2,1,0:T(8,128)(2,1)S(1)} collective-permute-done((bf16[8,32,128]{2,1,0:T(8,128)(2,1)S(1)}, bf16[8,32,128]{2,1,0:T(8,128)(2,1)S(1)}, u32[]{:S(2)}, u32[]{:S(2)}) %collective-permute-start.28) | collective-permute-done | bytes 65568 | tf_op jit(solution)/shard_map/ppermute | solution.py:247
  188.1 1.6 shard_map.127
  189.7 3.3 %shard_map.128 = (f32[512,512]{1,0:T(8,128)}, f32[3,512,512]{2,1,0:T(8,128)}) custom-call(s32[128]{0:T(128)S(1)} %shard_map.120.info, bf16[16,8,32,128]{3,2,1,0:T(8,128)(2,1)S(1)} %all_to_all.29.own, bf16[16,8,32,128]{3,2,1,0:T(8,128)(2,1)S(1)} %collective-permute-done.29.sib), custom_call_target="tpu_custom_call" | custom-call | bytes 8388608 | tf_op jit(solution)/shard_map/pallas_call | solution.py:367
  (51 shorter events, 0.8 us)
Async XLA Ops:
  0.6 34.3 %collective-permute-start.18 = (bf16[32,128,128]{2,1,0:T(8,128)(2,1)}, bf16[32,128,128]{2,1,0:T(8,128)(2,1)S(1)}, u32[]{:S(2)}, u32[]{:S(2)}) collective-permute-start(bf16[32,128,128]{2,1,0:T(8,128)(2,1)} %tiles_own.1), channel_id=1, source_target_pairs={{0,1},{1,0},{2,3},{3,2},{4,5},{5,4},{6,7},{7,6},{8,9},{9,8},{10,11... | collective-permute-start | bytes 3145736 | tf_op jit(solution)/shard_map/ppermute | solution.py:247
  4.0 8.6 %collective-permute-start.1 = (bf16[128,512]{1,0:T(8,128)(2,1)}, bf16[128,512]{1,0:T(8,128)(2,1)S(1)}, u32[]{:S(2)}, u32[]{:S(2)}) collective-permute-start(bf16[128,512]{1,0:T(8,128)(2,1)} %refs_0_.3), channel_id=1, source_target_pairs={{0,224},{32,0},{64,32},{96,64},{128,96},{160,128},{192,160},{224,1... | collective-permute-start | bytes 393224 | tf_op jit(solution)/shard_map/ppermute | solution.py:250
  7.8 6.1 %collective-permute-start = (bf16[128,512]{1,0:T(8,128)(2,1)}, bf16[128,512]{1,0:T(8,128)(2,1)S(1)}, u32[]{:S(2)}, u32[]{:S(2)}) collective-permute-start(bf16[128,512]{1,0:T(8,128)(2,1)} %refs_0_.3), channel_id=1, source_target_pairs={{0,32},{32,64},{64,96},{96,128},{128,160},{160,192},{192,224},{224... | collective-permute-start | bytes 393224 | tf_op jit(solution)/shard_map/ppermute | solution.py:250
  9.2 1.2 collective-permute-start.2
  9.6 7.1 %copy-start.3 = (bf16[128,512]{1,0:T(8,128)(2,1)S(1)}, bf16[128,512]{1,0:T(8,128)(2,1)}, u32[]{:S(2)}) copy-start(bf16[128,512]{1,0:T(8,128)(2,1)} %refs_0_.3) | copy-start | bytes 393220
  9.6 22.1 %copy-start = (bf16[3,512,512]{2,1,0:T(8,128)(2,1)S(1)}, bf16[3,512,512]{2,1,0:T(8,128)(2,1)}, u32[]{:S(2)}) copy-start(bf16[3,512,512]{2,1,0:T(8,128)(2,1)} %w.5) | copy-start | bytes 4718596
  9.6 22.1 %copy-start.2 = (bf16[128,512]{1,0:T(8,128)(2,1)S(1)}, bf16[128,512]{1,0:T(8,128)(2,1)}, u32[]{:S(2)}) copy-start(bf16[128,512]{1,0:T(8,128)(2,1)} %facts.3) | copy-start | bytes 393220
  10.3 0.7 copy-start.6
  12.5 22.4 %copy-start.1 = (bf16[32,128,128]{2,1,0:T(8,128)(2,1)S(1)}, bf16[32,128,128]{2,1,0:T(8,128)(2,1)}, u32[]{:S(2)}) copy-start(bf16[32,128,128]{2,1,0:T(8,128)(2,1)} %tiles_own.1) | copy-start | bytes 3145732
  14.0 5.0 %collective-permute-start.3 = (bf16[128,512]{1,0:T(8,128)(2,1)S(1)}, bf16[128,512]{1,0:T(8,128)(2,1)S(1)}, u32[]{:S(2)}, u32[]{:S(2)}) collective-permute-start(bf16[128,512]{1,0:T(8,128)(2,1)S(1)} %collective-permute-done.refs_1_), channel_id=1, source_target_pairs={{0,32},{32,64},{64,96},{96,128},{128,160},{160,192},{192,224},{224... | collective-permute-start | bytes 393224 | tf_op jit(solution)/shard_map/ppermute | solution.py:250
  14.0 5.0 %collective-permute-start.6 = (bf16[128,512]{1,0:T(8,128)(2,1)S(1)}, bf16[128,512]{1,0:T(8,128)(2,1)S(1)}, u32[]{:S(2)}, u32[]{:S(2)}) collective-permute-start(bf16[128,512]{1,0:T(8,128)(2,1)S(1)} %collective-permute-done.1.refs_2_), channel_id=1, source_target_pairs={{0,224},{32,0},{64,32},{96,64},{128,96},{160,128},{192,160},{224,1... | collective-permute-start | bytes 393224 | tf_op jit(solution)/shard_map/ppermute | solution.py:250
  16.6 7.9 %collective-permute-start.9 = (bf16[128,512]{1,0:T(8,128)(2,1)S(1)}, bf16[128,512]{1,0:T(8,128)(2,1)S(1)}, u32[]{:S(2)}, u32[]{:S(2)}) collective-permute-start(bf16[128,512]{1,0:T(8,128)(2,1)S(1)} %copy-done.3), channel_id=1, source_target_pairs={{0,1},{1,0},{2,3},{3,2},{4,5},{5,4},{6,7},{7,6},{8,9},{9,8},{10,11... | collective-permute-start | bytes 393224 | tf_op jit(solution)/shard_map/ppermute | solution.py:247
  19.0 5.6 %collective-permute-start.4 = (bf16[128,512]{1,0:T(8,128)(2,1)S(1)}, bf16[128,512]{1,0:T(8,128)(2,1)S(1)}, u32[]{:S(2)}, u32[]{:S(2)}) collective-permute-start(bf16[128,512]{1,0:T(8,128)(2,1)S(1)} %collective-permute-done.3.refs_3_), channel_id=1, source_target_pairs={{0,32},{32,64},{64,96},{96,128},{128,160},{160,192},{192,224},{224... | collective-permute-start | bytes 393224 | tf_op jit(solution)/shard_map/ppermute | solution.py:250
  19.0 8.5 %collective-permute-start.7 = (bf16[128,512]{1,0:T(8,128)(2,1)S(1)}, bf16[128,512]{1,0:T(8,128)(2,1)S(1)}, u32[]{:S(2)}, u32[]{:S(2)}) collective-permute-start(bf16[128,512]{1,0:T(8,128)(2,1)S(1)} %collective-permute-done.6.refs_4_), channel_id=1, source_target_pairs={{0,224},{32,0},{64,32},{96,64},{128,96},{160,128},{192,160},{224,1... | collective-permute-start | bytes 393224 | tf_op jit(solution)/shard_map/ppermute | solution.py:250
  21.7 5.9 %collective-permute-start.11 = (bf16[128,512]{1,0:T(8,128)(2,1)S(1)}, bf16[128,512]{1,0:T(8,128)(2,1)S(1)}, u32[]{:S(2)}, u32[]{:S(2)}) collective-permute-start(bf16[128,512]{1,0:T(8,128)(2,1)S(1)} %collective-permute-done.1.refs_2_), channel_id=1, source_target_pairs={{0,1},{1,0},{2,3},{3,2},{4,5},{5,4},{6,7},{7,6},{8,9},{9,8},{10,11... | collective-permute-start | bytes 393224 | tf_op jit(solution)/shard_map/ppermute | solution.py:247
  24.6 3.1 %collective-permute-start.10 = (bf16[128,512]{1,0:T(8,128)(2,1)S(1)}, bf16[128,512]{1,0:T(8,128)(2,1)S(1)}, u32[]{:S(2)}, u32[]{:S(2)}) collective-permute-start(bf16[128,512]{1,0:T(8,128)(2,1)S(1)} %collective-permute-done.refs_1_), channel_id=1, source_target_pairs={{0,1},{1,0},{2,3},{3,2},{4,5},{5,4},{6,7},{7,6},{8,9},{9,8},{10,11... | collective-permute-start | bytes 393224 | tf_op jit(solution)/shard_map/ppermute | solution.py:247
  24.6 6.1 %collective-permute-start.12 = (bf16[128,512]{1,0:T(8,128)(2,1)S(1)}, bf16[128,512]{1,0:T(8,128)(2,1)S(1)}, u32[]{:S(2)}, u32[]{:S(2)}) collective-permute-start(bf16[128,512]{1,0:T(8,128)(2,1)S(1)} %collective-permute-done.3.refs_3_), channel_id=1, source_target_pairs={{0,1},{1,0},{2,3},{3,2},{4,5},{5,4},{6,7},{7,6},{8,9},{9,8},{10,11... | collective-permute-start | bytes 393224 | tf_op jit(solution)/shard_map/ppermute | solution.py:247
  27.5 3.9 %collective-permute-start.13 = (bf16[128,512]{1,0:T(8,128)(2,1)S(1)}, bf16[128,512]{1,0:T(8,128)(2,1)S(1)}, u32[]{:S(2)}, u32[]{:S(2)}) collective-permute-start(bf16[128,512]{1,0:T(8,128)(2,1)S(1)} %collective-permute-done.6.refs_4_), channel_id=1, source_target_pairs={{0,1},{1,0},{2,3},{3,2},{4,5},{5,4},{6,7},{7,6},{8,9},{9,8},{10,11... | collective-permute-start | bytes 393224 | tf_op jit(solution)/shard_map/ppermute | solution.py:247
  27.5 5.5 %collective-permute-start.5 = (bf16[64,512]{1,0:T(8,128)(2,1)S(1)}, bf16[64,512]{1,0:T(8,128)(2,1)S(1)}, u32[]{:S(2)}, u32[]{:S(2)}) collective-permute-start(bf16[64,512]{1,0:T(8,128)(2,1)S(1)} %slice.84), channel_id=1, source_target_pairs={{0,32},{32,64},{64,96},{96,128},{128,160},{160,192},{192,224},{224... | collective-permute-start | bytes 196616 | tf_op jit(solution)/shard_map/ppermute | solution.py:250
  27.6 5.4 %collective-permute-start.8 = (bf16[64,512]{1,0:T(8,128)(2,1)S(1)}, bf16[64,512]{1,0:T(8,128)(2,1)S(1)}, u32[]{:S(2)}, u32[]{:S(2)}) collective-permute-start(bf16[64,512]{1,0:T(8,128)(2,1)S(1)} %slice.85), channel_id=1, source_target_pairs={{0,224},{32,0},{64,32},{96,64},{128,96},{160,128},{192,160},{224,1... | collective-permute-start | bytes 196616 | tf_op jit(solution)/shard_map/ppermute | solution.py:250
  30.7 4.2 %collective-permute-start.14 = (bf16[128,512]{1,0:T(8,128)(2,1)S(1)}, bf16[128,512]{1,0:T(8,128)(2,1)S(1)}, u32[]{:S(2)}, u32[]{:S(2)}) collective-permute-start(bf16[128,512]{1,0:T(8,128)(2,1)S(1)} %collective-permute-done.4.refs_0_.refs_5_), channel_id=1, source_target_pairs={{0,1},{1,0},{2,3},{3,2},{4,5},{5,4},{6,7},{7,6},{8,9},{9,8},{10,11... | collective-permute-start | bytes 393224 | tf_op jit(solution)/shard_map/ppermute | solution.py:247
  31.4 3.5 %collective-permute-start.15 = (bf16[128,512]{1,0:T(8,128)(2,1)S(1)}, bf16[128,512]{1,0:T(8,128)(2,1)S(1)}, u32[]{:S(2)}, u32[]{:S(2)}) collective-permute-start(bf16[128,512]{1,0:T(8,128)(2,1)S(1)} %collective-permute-done.7.refs_1_.refs_6_), channel_id=1, source_target_pairs={{0,1},{1,0},{2,3},{3,2},{4,5},{5,4},{6,7},{7,6},{8,9},{9,8},{10,11... | collective-permute-start | bytes 393224 | tf_op jit(solution)/shard_map/ppermute | solution.py:247
  33.1 1.4 collective-permute-start.16
  33.6 1.3 collective-permute-start.17
  37.4 38.1 %copy-start.4 = (bf16[512,512]{1,0:T(8,128)(2,1)S(1)}, bf16[512,512]{1,0:T(8,128)(2,1)}, u32[]{:S(2)}) copy-start(bf16[512,512]{1,0:T(8,128)(2,1)} %w.4) | copy-start | bytes 1572868
  37.4 38.1 %copy-start.5 = (bf16[128,512]{1,0:T(8,128)(2,1)S(1)}, bf16[128,512]{1,0:T(8,128)(2,1)}, u32[]{:S(2)}) copy-start(bf16[128,512]{1,0:T(8,128)(2,1)} %cot.1) | copy-start | bytes 393220
  109.5 3.9 %collective-permute-start.19 = (bf16[2,528,128]{2,1,0:T(8,128)(2,1)S(1)}, bf16[2,528,128]{2,1,0:T(8,128)(2,1)S(1)}, u32[]{:S(2)}, u32[]{:S(2)}) collective-permute-start(bf16[2,528,128]{2,1,0:T(8,128)(2,1)S(1)} %get-tuple-element.44), channel_id=1, source_target_pairs={{0,1},{1,0},{2,3},{3,2},{4,5},{5,4},{6,7},{7,6},{8,9},{9,8},{10,11... | collective-permute-start | bytes 811016 | tf_op jit(solution)/shard_map/ppermute | solution.py:247
  113.4 8.3 %collective-permute-start.20 = (bf16[6,528,128]{2,1,0:T(8,128)(2,1)S(1)}, bf16[6,528,128]{2,1,0:T(8,128)(2,1)S(1)}, u32[]{:S(2)}, u32[]{:S(2)}) collective-permute-start(bf16[6,528,128]{2,1,0:T(8,128)(2,1)S(1)} %get-tuple-element.46), channel_id=1, source_target_pairs={{0,1},{1,0},{2,3},{3,2},{4,5},{5,4},{6,7},{7,6},{8,9},{9,8},{10,11... | collective-permute-start | bytes 2433032 | tf_op jit(solution)/shard_map/ppermute | solution.py:247
  113.8 5.1 %collective-permute-start.22 = (bf16[528,128]{1,0:T(8,128)(2,1)S(1)}, bf16[528,128]{1,0:T(8,128)(2,1)S(1)}, u32[]{:S(2)}, u32[]{:S(2)}) collective-permute-start(bf16[528,128]{1,0:T(8,128)(2,1)S(1)} %get-tuple-element.64), channel_id=1, source_target_pairs={{0,224},{32,0},{64,32},{96,64},{128,96},{160,128},{192,160},{224,1... | collective-permute-start | bytes 405512 | tf_op jit(solution)/shard_map/ppermute | solution.py:250
  115.7 5.9 %collective-permute-start.21 = (bf16[528,128]{1,0:T(8,128)(2,1)S(1)}, bf16[528,128]{1,0:T(8,128)(2,1)S(1)}, u32[]{:S(2)}, u32[]{:S(2)}) collective-permute-start(bf16[528,128]{1,0:T(8,128)(2,1)S(1)} %get-tuple-element.65), channel_id=1, source_target_pairs={{0,32},{32,64},{64,96},{96,128},{128,160},{160,192},{192,224},{224... | collective-permute-start | bytes 405512 | tf_op jit(solution)/shard_map/ppermute | solution.py:250
  121.8 5.5 %collective-permute-start.23 = (bf16[528,128]{1,0:T(8,128)(2,1)S(1)}, bf16[528,128]{1,0:T(8,128)(2,1)S(1)}, u32[]{:S(2)}, u32[]{:S(2)}) collective-permute-start(bf16[528,128]{1,0:T(8,128)(2,1)S(1)} %get-tuple-element.51), channel_id=1, source_target_pairs={{0,32},{32,64},{64,96},{96,128},{128,160},{160,192},{192,224},{224... | collective-permute-start | bytes 405512 | tf_op jit(solution)/shard_map/ppermute | solution.py:250
  121.9 5.4 %collective-permute-start.24 = (bf16[528,128]{1,0:T(8,128)(2,1)S(1)}, bf16[528,128]{1,0:T(8,128)(2,1)S(1)}, u32[]{:S(2)}, u32[]{:S(2)}) collective-permute-start(bf16[528,128]{1,0:T(8,128)(2,1)S(1)} %get-tuple-element.52), channel_id=1, source_target_pairs={{0,224},{32,0},{64,32},{96,64},{128,96},{160,128},{192,160},{224,1... | collective-permute-start | bytes 405512 | tf_op jit(solution)/shard_map/ppermute | solution.py:250
  124.6 10.6 %collective-permute-start.27 = (bf16[528,128]{1,0:T(8,128)(2,1)S(1)}, bf16[528,128]{1,0:T(8,128)(2,1)S(1)}, u32[]{:S(2)}, u32[]{:S(2)}) collective-permute-start(bf16[528,128]{1,0:T(8,128)(2,1)S(1)} %get-tuple-element.66), channel_id=1, source_target_pairs={{0,128},{32,160},{64,192},{96,224},{128,0},{160,32},{192,64},{224,... | collective-permute-start | bytes 405512 | tf_op jit(solution)/shard_map/ppermute | solution.py:250
  127.4 8.6 %collective-permute-start.25 = (bf16[528,128]{1,0:T(8,128)(2,1)S(1)}, bf16[528,128]{1,0:T(8,128)(2,1)S(1)}, u32[]{:S(2)}, u32[]{:S(2)}) collective-permute-start(bf16[528,128]{1,0:T(8,128)(2,1)S(1)} %get-tuple-element.53), channel_id=1, source_target_pairs={{0,32},{32,64},{64,96},{96,128},{128,160},{160,192},{192,224},{224... | collective-permute-start | bytes 405512 | tf_op jit(solution)/shard_map/ppermute | solution.py:250
  127.4 8.5 %collective-permute-start.26 = (bf16[528,128]{1,0:T(8,128)(2,1)S(1)}, bf16[528,128]{1,0:T(8,128)(2,1)S(1)}, u32[]{:S(2)}, u32[]{:S(2)}) collective-permute-start(bf16[528,128]{1,0:T(8,128)(2,1)S(1)} %get-tuple-element.54), channel_id=1, source_target_pairs={{0,224},{32,0},{64,32},{96,64},{128,96},{160,128},{192,160},{224,1... | collective-permute-start | bytes 405512 | tf_op jit(solution)/shard_map/ppermute | solution.py:250
  176.8 12.9 %collective-permute-start.29 = (bf16[16,8,32,128]{3,2,1,0:T(8,128)(2,1)S(1)}, bf16[16,8,32,128]{3,2,1,0:T(8,128)(2,1)S(1)}, u32[]{:S(2)}, u32[]{:S(2)}) collective-permute-start(bf16[16,8,32,128]{3,2,1,0:T(8,128)(2,1)S(1)} %all_to_all.29.own), channel_id=1, source_target_pairs={{0,1},{1,0},{2,3},{3,2},{4,5},{5,4},{6,7},{7,6},{8,9},{9,8},{10,11... | collective-permute-start | bytes 3145736 | tf_op jit(solution)/shard_map/ppermute | solution.py:247
  185.8 2.4 %collective-permute-start.28 = (bf16[8,32,128]{2,1,0:T(8,128)(2,1)S(1)}, bf16[8,32,128]{2,1,0:T(8,128)(2,1)S(1)}, u32[]{:S(2)}, u32[]{:S(2)}) collective-permute-start(bf16[8,32,128]{2,1,0:T(8,128)(2,1)S(1)} %get-tuple-element.69), channel_id=1, source_target_pairs={{0,1},{1,0},{2,3},{3,2},{4,5},{5,4},{6,7},{7,6},{8,9},{9,8},{10,11... | collective-permute-start | bytes 196616 | tf_op jit(solution)/shard_map/ppermute | solution.py:247

commit v11 on v10

--- a/solution.py
+++ b/solution.py
@@ -13,7 +13,7 @@
 UNROLL = 4
 
 
-ORDER = (0, -1, 1, -2, 2, -3, 3)
+ORDER = (0, -1, 1, -2, 2, 4, -3, 3)
 EARLY = 5
 FIRST, REST = (3, 5), (0, 1, 2, 4, 6, 7)
 LIST = 40
@@ -66,16 +66,15 @@
 
 
 def forward_kernel(info, proj, *refs):
-    late = 9 - EARLY
+    late = len(ORDER) - EARLY
     sides, (w, facts_t, tiles_own, tiles_sib, out, panel, acc) = (refs[:late], refs[late : 2 * late]), refs[2 * late :]
     fact_pos = info[PLACE]
     for side, pieces in enumerate(sides):
         for at, shift in enumerate(ORDER[:EARLY]):
             panel[side * 8 + ((fact_pos + shift) & 7)] = proj[side * EARLY + at]
-        blocks = [x[...] for x in pieces[:-2]] + [jnp.concatenate([pieces[-2][...], pieces[-1][...]], axis=0)]
-        for shift, rows in zip(ORDER[EARLY:] + (4,), blocks):
+        for shift, rows in zip(ORDER[EARLY:], pieces):
             h = (fact_pos + shift) & 7
-            value = jnp.dot(rows, w[info[KIND + side * 8 + h]], preferred_element_type=F32)
+            value = jnp.dot(rows[...], w[info[KIND + side * 8 + h]], preferred_element_type=F32)
             panel[side * 8 + h] = value.astype(BF16)
     acc[...] = jnp.zeros_like(acc)
     for side, tiles in enumerate((tiles_own, tiles_sib)):
@@ -154,7 +153,7 @@
 
 
 def slice_kernel(info, kept, given, from_below, from_above, from_far, *refs):
-    pieces, (tab, gsum, self_piece, tacc) = refs[:18], refs[18:]
+    pieces, (tab, gsum, self_piece, tacc) = refs[:16], refs[16:]
     fact_pos, core = info[PLACE], info[PLACE + 2]
     total = kept[...]
     for arrived in (given, from_below, from_above, from_far):
@@ -165,16 +164,11 @@
     tacc[...] = jnp.zeros_like(tacc)
     for side in range(2):
         column = 8 * (core if side == 0 else 1 - core)
-        for at, shift in enumerate(ORDER + (4,)):
+        for at, shift in enumerate(ORDER):
             h = (fact_pos + shift) & 7
             kind = info[KIND + side * 8 + h]
-            grad = gsum[column + h]
-            if shift == 4:
-                low, high = pieces[side * 9 + 7], pieces[side * 9 + 8]
-                rows = jnp.concatenate([low[...], high[...]], axis=0)
-            else:
-                rows = pieces[side * 9 + at][...]
-            tacc[kind] += jnp.dot(grad, rows, preferred_element_type=F32)
+            rows = pieces[side * 8 + at][...]
+            tacc[kind] += jnp.dot(gsum[column + h], rows, preferred_element_type=F32)
     for q in range(4):
         for t in range(3):
             at = q * 96 + t * 32
@@ -191,20 +185,19 @@
         out[z, 64:96, :] = piece
 
 
-def rows_kernel(info, kept, given, w, grad_dims):
-    even = info[PLACE + 2] == 0
-    kind = info[KIND + info[PLACE]]
-    mine, other = kept[...].astype(F32).reshape(256, 128), given[...].astype(F32).reshape(256, 128)
-    turned = jnp.concatenate([jnp.where(even, mine, other), jnp.where(even, other, mine)], axis=0)
-    grad_dims[...] = lax.dot_general(
-        turned.T.astype(BF16), w[kind], (((1,), (1,)), ((), ())), preferred_element_type=F32
-    )
-
-
-def final_kernel(info, own, sib, grad_self, grad_tab):
+def final_kernel(info, own, sib, kept, given, w, grad_dims, grad_self, grad_tab):
     even = info[PLACE + 2] == 0
     scale = F32(32768.0**-0.5)
     q = pl.program_id(0)
+
+    @pl.when(q == 0)
+    def _():
+        mine, other = kept[...].astype(F32).reshape(256, 128), given[...].astype(F32).reshape(256, 128)
+        turned = jnp.concatenate([jnp.where(even, mine, other), jnp.where(even, other, mine)], axis=0)
+        weight = w[info[KIND + info[PLACE]]]
+        grad_dims[...] = lax.dot_general(
+            turned.T.astype(BF16), weight, (((1,), (1,)), ((), ())), preferred_element_type=F32
+        )
 
     def both_cores(chip, z):
         mine, other = own[chip, z].astype(F32) * scale, sib[chip, z].astype(F32) * scale
@@ -268,15 +261,16 @@
     )(place, links_own, links_sib, block_table)
     tiles_sib = swap(tiles)
 
-    pieces, up, down = [dims], dims, dims
-    for step in range(3):
-        if step == 1:
-            up, down, info = lax.optimization_barrier((up, down, info))
-        up, down = shift(up, 1), shift(down, -1)
-        pieces += [up, down]
+    up, down = shift(dims, 1), shift(dims, -1)
+    far, up, down, info = lax.optimization_barrier((dims, up, down, info))
+    far = shift(far, 4)
+    pieces = [dims, up, down]
+    up, down = shift(up, 1), shift(down, -1)
+    pieces += [up, down]
+    up, down = lax.optimization_barrier((up, down))
+    late = [far, shift(up, 1), shift(down, -1)]
     pieces_sib = [swap(x) for x in pieces]
-    far = [shift(up[: rows // 2], 1), shift(down[rows // 2 :], -1)]
-    early = pieces[:EARLY] + pieces_sib[:EARLY]
+    early = pieces + pieces_sib
     proj, facts_t = call(
         project_kernel,
         (jax.ShapeDtypeStruct((len(early), rows, width), BF16), jax.ShapeDtypeStruct((width, block), BF16)),
@@ -284,16 +278,16 @@
         flops=2 * len(early) * rows * width * width,
         moved=4 << 20,
     )(info, w_tables, facts, *early)
-    *far, proj = lax.optimization_barrier((*far, proj))
-    pieces, pieces_sib = pieces + far, pieces_sib + [swap(x) for x in far]
+    *late, proj = lax.optimization_barrier((*late, proj))
+    late_sib = [swap(x) for x in late]
     partial = call(
         forward_kernel,
         jax.ShapeDtypeStruct((chips, 544, 128), BF16),
-        [SMEM] + [VMEM] * (5 + 2 * (9 - EARLY)),
+        [SMEM] + [VMEM] * (5 + 2 * len(late)),
         [pltpu.VMEM((2 * n_fact, rows, width), BF16), pltpu.VMEM((chips + 1, block, width), F32)],
         flops=2 * slots * block * block * width,
         moved=8 << 20,
-    )(info, proj, *pieces[EARLY:], *pieces_sib[EARLY:], w_tables, facts_t, tiles, tiles_sib)
+    )(info, proj, *late, *late_sib, w_tables, facts_t, tiles, tiles_sib)
     parts = by_chip(partial)
 
     fact_out, spread, facts_t = call(
@@ -332,7 +326,7 @@
     down = shift((keep[5] + give[5].astype(F32)).astype(BF16), -1)
     give_rest, up, down = lax.optimization_barrier((give_rest, up, down))
     give |= {k: give_rest[at] for at, k in enumerate(REST)}
-    far = shift((keep[4] + give[4].astype(F32)).astype(BF16), 4)
+    far_sum = shift((keep[4] + give[4].astype(F32)).astype(BF16), 4)
     for k in (2, 1):
         up, down = lax.optimization_barrier((partial_sum(k, up), partial_sum(8 - k, down)))
         up, down = shift(up, 1), shift(down, -1)
@@ -344,11 +338,11 @@
             jax.ShapeDtypeStruct((2 * n_fact, 32, 128), BF16),
             jax.ShapeDtypeStruct((8, 128), F32),
         ),
-        [SMEM] + [VMEM] * 23,
+        [SMEM] + [VMEM] * 21,
         [pltpu.VMEM((3, 32, width), F32)],
         flops=4 * n_fact * 32 * 128 * width,
         moved=3 << 20,
-    )(info, keep[0], give[0], up, down, far, *pieces, *pieces_sib)
+    )(info, keep[0], give[0], up, down, far_sum, *pieces, *late, *pieces_sib, *late_sib)
     tab = by_chip(tab.reshape(chips, 24, 128))
     packed = call(
         pack_kernel, jax.ShapeDtypeStruct((n_fact, 96, 128), BF16), [SMEM] + [VMEM] * 3, moved=1 << 19
@@ -357,25 +351,23 @@
     pieces_own = by_chip(jnp.broadcast_to(packed[None, :, 64:, :], (chips, n_fact, 32, 128)))
     given = swap(packed[:, 32:64, :])
 
-    grad_dims = call(
-        rows_kernel,
-        jax.ShapeDtypeStruct((rows, width), F32),
-        [SMEM] + [VMEM] * 3,
-        flops=2 * rows * width * width,
-        moved=2 << 20,
-    )(info, packed[:, :32, :], given, w_tables)
-    grad_self, grad_tab = pl.pallas_call(
+    grad_dims, grad_self, grad_tab = pl.pallas_call(
         final_kernel,
-        out_shape=(jax.ShapeDtypeStruct((width, width), F32), jax.ShapeDtypeStruct((3, width, width), F32)),
+        out_shape=(
+            jax.ShapeDtypeStruct((rows, width), F32),
+            jax.ShapeDtypeStruct((width, width), F32),
+            jax.ShapeDtypeStruct((3, width, width), F32),
+        ),
         grid=(4,),
-        in_specs=[SMEM, VMEM, VMEM],
+        in_specs=[SMEM] + [VMEM] * 5,
         out_specs=(
+            pl.BlockSpec((rows, width), lambda q: (0, 0)),
             pl.BlockSpec((width, 128), lambda q: (0, q)),
             pl.BlockSpec((3, 128, width), lambda q: (0, q, 0)),
         ),
         compiler_params=PARAMS,
-        cost_estimate=pl.CostEstimate(flops=0, bytes_accessed=8 << 20, transcendentals=0),
-    )(info, pieces_own, swap(pieces_own))
+        cost_estimate=pl.CostEstimate(flops=2 * rows * width * width, bytes_accessed=8 << 20, transcendentals=0),
+    )(info, pieces_own, swap(pieces_own), packed[:, :32, :], given, w_tables)
     return (fact_out, grad_dims, grad_self, grad_tab)
 
 

time: 193 us -> 193 us (level)
  waiting for transfers between devices: 18.7 us -> 23.4 us
  starting transfers between devices: 47.8 us -> 45.7 us
  blocking collectives: 107 us -> 105 us
    ppermute x15 -> x14, waiting for transfers between devices: 13.2 us -> 18.1 us  [shift(): lax.ppermute(x, 'fact', [(i, (i + by) % n_fact) for i in range(n_fact)])]
    all_to_all x4, blocking collectives: 94.7 us -> 91.8 us  [by_chip(): return lax.all_to_all(x, 'dim', 0, 0, tiled=True, axis_index_groups=same)]
    ppermute x15 -> x14, starting transfers between devices: 23 us -> 21.5 us  [shift(): lax.ppermute(x, 'fact', [(i, (i + by) % n_fact) for i in range(n_fact)])]
    pallas_call x2 -> x1, Pallas kernels: 4.84 us -> 3.69 us  [body(): pl.pallas_call(final_kernel, out_shape=(jax.ShapeDtypeStruct((rows, width...]
    ppermute x15 -> x14, starting transfers between devices: 24.9 us -> 24.2 us  [swap(): return lax.ppermute(x, 'dim', pair)]
    ppermute x15 -> x14, waiting for transfers between devices: 5.5 us -> 5.33 us  [swap(): return lax.ppermute(x, 'dim', pair)]
  transfers between devices with their start and end apart: 30 -> 28, of which waited for: 12 -> 14; matrix products, arithmetic and copies ran while one was open for 1% -> 1% of each run, Pallas kernels for 2% -> 2%
where the time goes in v11:
time: 193 us
  blocking collectives  105 us (54%)
  starting transfers between devices  45.7 us (24%)
  waiting for transfers between devices  23.4 us (12%)
  Pallas kernels  15.8 us (8%)
    all_to_all x4, blocking collectives, by_chip(): return lax.all_to_all(x, 'dim', 0, 0, tiled=True, axis_index_groups=same)  91.8 us
    ppermute x14, starting transfers between devices, swap(): return lax.ppermute(x, 'dim', pair)  24.2 us
    ppermute x14, starting transfers between devices, shift(): lax.ppermute(x, 'fact', [(i, (i + by) % n_fact) for i in range(n_fact)])  21.5 us
    ppermute x14, waiting for transfers between devices, shift(): lax.ppermute(x, 'fact', [(i, (i + by) % n_fact) for i in range(n_fact)])  18.1 us
    all_to_all x1, blocking collectives, by_fact(): return lax.all_to_all(x, 'fact', 0, 0, tiled=True)  13 us
    ppermute x14, waiting for transfers between devices, swap(): return lax.ppermute(x, 'dim', pair)  5.33 us
  transfers between devices with their start and end apart: 28, of which 14 were waited for; matrix products, arithmetic and copies ran while one was open for 1% of the time, Pallas kernels for 2%

profile of v11, /device:TPU:1, one launch (start us, length us, event | category | flops | bytes accessed | tf_op | source)
XLA Modules:
  0.0 193.1 jit_solution(10562656502274870650)
XLA Ops:
  0.6 3.3 %collective-permute-start.16 = (bf16[32,128,128]{2,1,0:T(8,128)(2,1)}, bf16[32,128,128]{2,1,0:T(8,128)(2,1)S(1)}, u32[]{:S(2)}, u32[]{:S(2)}) collective-permute-start(bf16[32,128,128]{2,1,0:T(8,128)(2,1)} %tiles_own.1), channel_id=1, source_target_pairs={{0,1},{1,0},{2,3},{3,2},{4,5},{5,4},{6,7},{7,6},{8,9},{9,8},{10,11... | collective-permute-start | bytes 3145736 | tf_op jit(solution)/shard_map/ppermute | solution.py:240
  4.1 3.8 %collective-permute-start.1 = (bf16[128,512]{1,0:T(8,128)(2,1)}, bf16[128,512]{1,0:T(8,128)(2,1)S(1)}, u32[]{:S(2)}, u32[]{:S(2)}) collective-permute-start(bf16[128,512]{1,0:T(8,128)(2,1)} %refs_0_.3), channel_id=1, source_target_pairs={{0,224},{32,0},{64,32},{96,64},{128,96},{160,128},{192,160},{224,1... | collective-permute-start | bytes 393224 | tf_op jit(solution)/shard_map/ppermute | solution.py:243
  8.6 0.7 concatenate.3.links_own
  9.2 0.7 collective-permute-start.2
  10.0 0.7 collective-permute-done.2.links_sib
  10.8 0.7 copy-done.6
  11.4 1.5 shard_map.120.info
  13.0 0.7 collective-permute-done.refs_1_
  13.7 2.7 %collective-permute-start.5 = (bf16[128,512]{1,0:T(8,128)(2,1)S(1)}, bf16[128,512]{1,0:T(8,128)(2,1)S(1)}, u32[]{:S(2)}, u32[]{:S(2)}) collective-permute-start(bf16[128,512]{1,0:T(8,128)(2,1)S(1)} %collective-permute-done.1.refs_2_), channel_id=1, source_target_pairs={{0,224},{32,0},{64,32},{96,64},{128,96},{160,128},{192,160},{224,1... | collective-permute-start | bytes 393224 | tf_op jit(solution)/shard_map/ppermute | solution.py:243
  16.3 2.1 %collective-permute-start.9 = (bf16[128,512]{1,0:T(8,128)(2,1)S(1)}, bf16[128,512]{1,0:T(8,128)(2,1)S(1)}, u32[]{:S(2)}, u32[]{:S(2)}) collective-permute-start(bf16[128,512]{1,0:T(8,128)(2,1)S(1)} %collective-permute-done.refs_1_), channel_id=1, source_target_pairs={{0,1},{1,0},{2,3},{3,2},{4,5},{5,4},{6,7},{7,6},{8,9},{9,8},{10,11... | collective-permute-start | bytes 393224 | tf_op jit(solution)/shard_map/ppermute | solution.py:240
  18.5 0.2 collective-permute-done.4.refs_3_
  18.7 2.7 %collective-permute-start.11 = (bf16[128,512]{1,0:T(8,128)(2,1)S(1)}, bf16[128,512]{1,0:T(8,128)(2,1)S(1)}, u32[]{:S(2)}, u32[]{:S(2)}) collective-permute-start(bf16[128,512]{1,0:T(8,128)(2,1)S(1)} %collective-permute-done.4.refs_3_), channel_id=1, source_target_pairs={{0,1},{1,0},{2,3},{3,2},{4,5},{5,4},{6,7},{7,6},{8,9},{9,8},{10,11... | collective-permute-start | bytes 393224 | tf_op jit(solution)/shard_map/ppermute | solution.py:240
  21.4 1.9 %collective-permute-start.3 = (bf16[128,512]{1,0:T(8,128)(2,1)S(1)}, bf16[128,512]{1,0:T(8,128)(2,1)S(1)}, u32[]{:S(2)}, u32[]{:S(2)}) collective-permute-start(bf16[128,512]{1,0:T(8,128)(2,1)S(1)} %copy-done.3), channel_id=1, source_target_pairs={{0,128},{32,160},{64,192},{96,224},{128,0},{160,32},{192,64},{224,... | collective-permute-start | bytes 393224 | tf_op jit(solution)/shard_map/ppermute | solution.py:243
  23.4 0.7 collective-permute-start.6
  24.0 2.0 %collective-permute-start.7 = (bf16[128,512]{1,0:T(8,128)(2,1)S(1)}, bf16[128,512]{1,0:T(8,128)(2,1)S(1)}, u32[]{:S(2)}, u32[]{:S(2)}) collective-permute-start(bf16[128,512]{1,0:T(8,128)(2,1)S(1)} %collective-permute-done.5.refs_4_), channel_id=1, source_target_pairs={{0,224},{32,0},{64,32},{96,64},{128,96},{160,128},{192,160},{224,1... | collective-permute-start | bytes 393224 | tf_op jit(solution)/shard_map/ppermute | solution.py:243
  26.1 1.4 shard_map.121
  27.5 3.0 %collective-permute-done.3.refs_0_.refs_5_ = bf16[128,512]{1,0:T(8,128)(2,1)S(1)} collective-permute-done((bf16[128,512]{1,0:T(8,128)(2,1)S(1)}, bf16[128,512]{1,0:T(8,128)(2,1)S(1)}, u32[]{:S(2)}, u32[]{:S(2)}) %collective-permute-start.3) | collective-permute-done | bytes 131104 | tf_op jit(solution)/shard_map/ppermute | solution.py:243
  30.5 3.1 %collective-permute-done.6.refs_1_.refs_6_ = bf16[128,512]{1,0:T(8,128)(2,1)S(1)} collective-permute-done((bf16[128,512]{1,0:T(8,128)(2,1)S(1)}, bf16[128,512]{1,0:T(8,128)(2,1)S(1)}, u32[]{:S(2)}, u32[]{:S(2)}) %collective-permute-start.6) | collective-permute-done | bytes 131104 | tf_op jit(solution)/shard_map/ppermute | solution.py:243
  33.5 1.4 collective-permute-start.13
  35.0 0.4 collective-permute-start.15
  35.5 0.5 collective-permute-done.13.refs_3_.refs_13_
  35.9 0.4 collective-permute-done.14.refs_4_.refs_14_
  36.3 0.2 collective-permute-done.15.refs_5_.refs_15_
  36.5 3.1 %shard_map.122 = bf16[16,544,128]{2,1,0:T(8,128)(2,1)S(1)} custom-call(s32[128]{0:T(128)S(1)} %shard_map.120.info, bf16[10,128,512]{2,1,0:T(8,128)(2,1)S(1)} %get-tuple-element.44.proj, bf16[128,512]{1,0:T(8,128)(2,1)S(1)} %collective-permute-done.3.refs_0_.refs_5_, bf16[128,512]{1,0:T(8,128)(2,1)S(1)} %collective-permute-done.6.refs_1_.refs_6_, ...), custom_call_target="tpu_custom_call" | custom-call | flops 536870912 | bytes 8388608 | tf_op jit(solution)/shard_map/pallas_call | solution.py:283
  39.6 37.0 %all_to_all.25.parts = bf16[16,544,128]{2,1,0:T(8,128)(2,1)S(1)} all-to-all(bf16[16,544,128]{2,1,0:T(8,128)(2,1)S(1)} %shard_map.122), channel_id=1, replica_groups={{0,2,4,6,8,10,12,14,16,18,20,22,24,26,28,30},{1,3,5,7,9,11,13,15,17,19,..., dimensions={0} | all-to-all | bytes 4456448 | tf_op jit(solution)/shard_map/all_to_all | solution.py:246
  76.6 1.2 shard_map.123
  77.7 29.9 %all_to_all.26.grads = bf16[16,512,128]{2,1,0:T(8,128)(2,1)S(1)} all-to-all(bf16[16,512,128]{2,1,0:T(8,128)(2,1)S(1)} %get-tuple-element.50), channel_id=1, replica_groups={{0,2,4,6,8,10,12,14,16,18,20,22,24,26,28,30},{1,3,5,7,9,11,13,15,17,19,..., dimensions={0} | all-to-all | bytes 4194304 | tf_op jit(solution)/shard_map/all_to_all | solution.py:246
  107.6 3.3 %shard_map.124 = (f32[8,528,128]{2,1,0:T(8,128)S(1)}, bf16[2,528,128]{2,1,0:T(8,128)(2,1)S(1)}, bf16[6,528,128]{2,1,0:T(8,128)(2,1)S(1)}) custom-call(s32[128]{0:T(128)S(1)} %shard_map.120.info, bf16[16,512,128]{2,1,0:T(8,128)(2,1)S(1)} %all_to_all.26.grads, bf16[16,32,128]{2,1,0:T(8,128)(2,1)S(1)} %get-tuple-element.51.facts_t, ...), custom_call_target="tpu_custom_call" | custom-call | flops 536870912 | bytes 9437184 | tf_op jit(solution)/shard_map/pallas_call | solution.py:306
  110.9 2.7 %collective-permute-start.17 = (bf16[2,528,128]{2,1,0:T(8,128)(2,1)S(1)}, bf16[2,528,128]{2,1,0:T(8,128)(2,1)S(1)}, u32[]{:S(2)}, u32[]{:S(2)}) collective-permute-start(bf16[2,528,128]{2,1,0:T(8,128)(2,1)S(1)} %get-tuple-element.53), channel_id=1, source_target_pairs={{0,1},{1,0},{2,3},{3,2},{4,5},{5,4},{6,7},{7,6},{8,9},{9,8},{10,11... | collective-permute-start | bytes 811016 | tf_op jit(solution)/shard_map/ppermute | solution.py:240
  113.6 1.2 collective-permute-done.17
  114.8 0.4 collective-permute-start.18
  115.2 2.0 %collective-permute-start.20 = (bf16[528,128]{1,0:T(8,128)(2,1)S(1)}, bf16[528,128]{1,0:T(8,128)(2,1)S(1)}, u32[]{:S(2)}, u32[]{:S(2)}) collective-permute-start(bf16[528,128]{1,0:T(8,128)(2,1)S(1)} %get-tuple-element.74), channel_id=1, source_target_pairs={{0,224},{32,0},{64,32},{96,64},{128,96},{160,128},{192,160},{224,1... | collective-permute-start | bytes 405512 | tf_op jit(solution)/shard_map/ppermute | solution.py:243
  117.2 3.1 %collective-permute-done.20 = bf16[528,128]{1,0:T(8,128)(2,1)S(1)} collective-permute-done((bf16[528,128]{1,0:T(8,128)(2,1)S(1)}, bf16[528,128]{1,0:T(8,128)(2,1)S(1)}, u32[]{:S(2)}, u32[]{:S(2)}) %collective-permute-start.20) | collective-permute-done | bytes 135200 | tf_op jit(solution)/shard_map/ppermute | solution.py:243
  120.4 2.8 %collective-permute-done.19 = bf16[528,128]{1,0:T(8,128)(2,1)S(1)} collective-permute-done((bf16[528,128]{1,0:T(8,128)(2,1)S(1)}, bf16[528,128]{1,0:T(8,128)(2,1)S(1)}, u32[]{:S(2)}, u32[]{:S(2)}) %collective-permute-start.19) | collective-permute-done | bytes 135200 | tf_op jit(solution)/shard_map/ppermute | solution.py:243
  123.4 2.7 %collective-permute-start.22 = (bf16[528,128]{1,0:T(8,128)(2,1)S(1)}, bf16[528,128]{1,0:T(8,128)(2,1)S(1)}, u32[]{:S(2)}, u32[]{:S(2)}) collective-permute-start(bf16[528,128]{1,0:T(8,128)(2,1)S(1)} %get-tuple-element.61), channel_id=1, source_target_pairs={{0,224},{32,0},{64,32},{96,64},{128,96},{160,128},{192,160},{224,1... | collective-permute-start | bytes 405512 | tf_op jit(solution)/shard_map/ppermute | solution.py:243
  126.1 2.9 %collective-permute-start.25 = (bf16[528,128]{1,0:T(8,128)(2,1)S(1)}, bf16[528,128]{1,0:T(8,128)(2,1)S(1)}, u32[]{:S(2)}, u32[]{:S(2)}) collective-permute-start(bf16[528,128]{1,0:T(8,128)(2,1)S(1)} %get-tuple-element.76), channel_id=1, source_target_pairs={{0,128},{32,160},{64,192},{96,224},{128,0},{160,32},{192,64},{224,... | collective-permute-start | bytes 405512 | tf_op jit(solution)/shard_map/ppermute | solution.py:243
  129.2 2.7 %collective-permute-start.24 = (bf16[528,128]{1,0:T(8,128)(2,1)S(1)}, bf16[528,128]{1,0:T(8,128)(2,1)S(1)}, u32[]{:S(2)}, u32[]{:S(2)}) collective-permute-start(bf16[528,128]{1,0:T(8,128)(2,1)S(1)} %get-tuple-element.63), channel_id=1, source_target_pairs={{0,224},{32,0},{64,32},{96,64},{128,96},{160,128},{192,160},{224,1... | collective-permute-start | bytes 405512 | tf_op jit(solution)/shard_map/ppermute | solution.py:243
  131.9 4.9 %collective-permute-done.25.from_far = bf16[528,128]{1,0:T(8,128)(2,1)S(1)} collective-permute-done((bf16[528,128]{1,0:T(8,128)(2,1)S(1)}, bf16[528,128]{1,0:T(8,128)(2,1)S(1)}, u32[]{:S(2)}, u32[]{:S(2)}) %collective-permute-start.25) | collective-permute-done | bytes 135200 | tf_op jit(solution)/shard_map/ppermute | solution.py:243
  136.7 0.3 collective-permute-done.24.from_above
  137.0 1.1 shard_map.125
  138.1 10.2 %all_to_all.27.parts = bf16[16,24,128]{2,1,0:T(8,128)(2,1)S(1)} all-to-all(bf16[16,24,128]{2,1,0:T(8,128)(2,1)S(1)} %bitcast.34), channel_id=1, replica_groups={{0,2,4,6,8,10,12,14,16,18,20,22,24,26,28,30},{1,3,5,7,9,11,13,15,17,19,..., dimensions={0} | all-to-all | bytes 196608 | tf_op jit(solution)/shard_map/all_to_all | solution.py:246
  148.3 0.6 shard_map.126
  148.9 13.0 %all_to_all.28 = bf16[8,96,128]{2,1,0:T(8,128)(2,1)S(1)} all-to-all(bf16[8,96,128]{2,1,0:T(8,128)(2,1)S(1)} %shard_map.126), channel_id=1, replica_groups=mesh['fact'=8,'dim'=32] {'fact'}, dimensions={0} | all-to-all | bytes 393216 | tf_op jit(solution)/shard_map/all_to_all | solution.py:249
  161.9 0.2 broadcast_in_dim.5
  162.1 14.7 %all_to_all.29.own = bf16[16,8,32,128]{3,2,1,0:T(8,128)(2,1)S(1)} all-to-all(bf16[16,8,32,128]{3,2,1,0:T(8,128)(2,1)S(1)} %broadcast_in_dim.5), channel_id=1, replica_groups={{0,2,4,6,8,10,12,14,16,18,20,22,24,26,28,30},{1,3,5,7,9,11,13,15,17,19,..., dimensions={0} | all-to-all | bytes 2097152 | tf_op jit(solution)/shard_map/all_to_all | solution.py:246
  176.8 10.3 %collective-permute-start.26 = (bf16[16,8,32,128]{3,2,1,0:T(8,128)(2,1)S(1)}, bf16[16,8,32,128]{3,2,1,0:T(8,128)(2,1)S(1)}, u32[]{:S(2)}, u32[]{:S(2)}) collective-permute-start(bf16[16,8,32,128]{3,2,1,0:T(8,128)(2,1)S(1)} %all_to_all.29.own), channel_id=1, source_target_pairs={{0,1},{1,0},{2,3},{3,2},{4,5},{5,4},{6,7},{7,6},{8,9},{9,8},{10,11... | collective-permute-start | bytes 3145736 | tf_op jit(solution)/shard_map/ppermute | solution.py:240
  187.1 2.4 %collective-permute-done.27.given = bf16[8,32,128]{2,1,0:T(8,128)(2,1)S(1)} collective-permute-done((bf16[8,32,128]{2,1,0:T(8,128)(2,1)S(1)}, bf16[8,32,128]{2,1,0:T(8,128)(2,1)S(1)}, u32[]{:S(2)}, u32[]{:S(2)}) %collective-permute-start.27) | collective-permute-done | bytes 65568 | tf_op jit(solution)/shard_map/ppermute | solution.py:240
  189.4 3.7 %shard_map.127 = (f32[128,512]{1,0:T(8,128)}, f32[512,512]{1,0:T(8,128)}, f32[3,512,512]{2,1,0:T(8,128)}) custom-call(s32[128]{0:T(128)S(1)} %shard_map.120.info, bf16[16,8,32,128]{3,2,1,0:T(8,128)(2,1)S(1)} %all_to_all.29.own, bf16[16,8,32,128]{3,2,1,0:T(8,128)(2,1)S(1)} %collective-permute-done.26.sib, bf16[8,32,128]{2,1,0:T(8,128)(2,1)S(1)} %get-tuple-element.79.kept, ...), custom_call_target="tpu_custom_call" | custom-call | flops 67108864 | bytes 8388608 | tf_op jit(solution)/shard_map/pallas_call | solution.py:354
  (44 shorter events, 0.9 us)
Async XLA Ops:
  0.6 35.9 %collective-permute-start.16 = (bf16[32,128,128]{2,1,0:T(8,128)(2,1)}, bf16[32,128,128]{2,1,0:T(8,128)(2,1)S(1)}, u32[]{:S(2)}, u32[]{:S(2)}) collective-permute-start(bf16[32,128,128]{2,1,0:T(8,128)(2,1)} %tiles_own.1), channel_id=1, source_target_pairs={{0,1},{1,0},{2,3},{3,2},{4,5},{5,4},{6,7},{7,6},{8,9},{9,8},{10,11... | collective-permute-start | bytes 3145736 | tf_op jit(solution)/shard_map/ppermute | solution.py:240
  4.0 14.5 %collective-permute-start.8 = (bf16[128,512]{1,0:T(8,128)(2,1)}, bf16[128,512]{1,0:T(8,128)(2,1)S(1)}, u32[]{:S(2)}, u32[]{:S(2)}) collective-permute-start(bf16[128,512]{1,0:T(8,128)(2,1)} %refs_0_.3), channel_id=1, source_target_pairs={{0,1},{1,0},{2,3},{3,2},{4,5},{5,4},{6,7},{7,6},{8,9},{9,8},{10,11... | collective-permute-start | bytes 393224 | tf_op jit(solution)/shard_map/ppermute | solution.py:240
  4.1 8.9 %collective-permute-start.1 = (bf16[128,512]{1,0:T(8,128)(2,1)}, bf16[128,512]{1,0:T(8,128)(2,1)S(1)}, u32[]{:S(2)}, u32[]{:S(2)}) collective-permute-start(bf16[128,512]{1,0:T(8,128)(2,1)} %refs_0_.3), channel_id=1, source_target_pairs={{0,224},{32,0},{64,32},{96,64},{128,96},{160,128},{192,160},{224,1... | collective-permute-start | bytes 393224 | tf_op jit(solution)/shard_map/ppermute | solution.py:243
  7.9 5.8 %collective-permute-start = (bf16[128,512]{1,0:T(8,128)(2,1)}, bf16[128,512]{1,0:T(8,128)(2,1)S(1)}, u32[]{:S(2)}, u32[]{:S(2)}) collective-permute-start(bf16[128,512]{1,0:T(8,128)(2,1)} %refs_0_.3), channel_id=1, source_target_pairs={{0,32},{32,64},{64,96},{96,128},{128,160},{160,192},{192,224},{224... | collective-permute-start | bytes 393224 | tf_op jit(solution)/shard_map/ppermute | solution.py:243
  9.2 1.5 collective-permute-start.2
  10.0 11.4 %copy-start.3 = (bf16[128,512]{1,0:T(8,128)(2,1)S(1)}, bf16[128,512]{1,0:T(8,128)(2,1)}, u32[]{:S(2)}) copy-start(bf16[128,512]{1,0:T(8,128)(2,1)} %refs_0_.3) | copy-start | bytes 393220
  10.0 16.1 %copy-start = (bf16[3,512,512]{2,1,0:T(8,128)(2,1)S(1)}, bf16[3,512,512]{2,1,0:T(8,128)(2,1)}, u32[]{:S(2)}) copy-start(bf16[3,512,512]{2,1,0:T(8,128)(2,1)} %w.5) | copy-start | bytes 4718596
  10.0 16.1 %copy-start.2 = (bf16[128,512]{1,0:T(8,128)(2,1)S(1)}, bf16[128,512]{1,0:T(8,128)(2,1)}, u32[]{:S(2)}) copy-start(bf16[128,512]{1,0:T(8,128)(2,1)} %facts.3) | copy-start | bytes 393220
  10.8 0.7 copy-start.6
  13.0 23.5 %copy-start.1 = (bf16[32,128,128]{2,1,0:T(8,128)(2,1)S(1)}, bf16[32,128,128]{2,1,0:T(8,128)(2,1)}, u32[]{:S(2)}) copy-start(bf16[32,128,128]{2,1,0:T(8,128)(2,1)} %tiles_own.1) | copy-start | bytes 3145732
  13.7 5.0 %collective-permute-start.4 = (bf16[128,512]{1,0:T(8,128)(2,1)S(1)}, bf16[128,512]{1,0:T(8,128)(2,1)S(1)}, u32[]{:S(2)}, u32[]{:S(2)}) collective-permute-start(bf16[128,512]{1,0:T(8,128)(2,1)S(1)} %collective-permute-done.refs_1_), channel_id=1, source_target_pairs={{0,32},{32,64},{64,96},{96,128},{128,160},{160,192},{192,224},{224... | collective-permute-start | bytes 393224 | tf_op jit(solution)/shard_map/ppermute | solution.py:243
  13.7 7.7 %collective-permute-start.5 = (bf16[128,512]{1,0:T(8,128)(2,1)S(1)}, bf16[128,512]{1,0:T(8,128)(2,1)S(1)}, u32[]{:S(2)}, u32[]{:S(2)}) collective-permute-start(bf16[128,512]{1,0:T(8,128)(2,1)S(1)} %collective-permute-done.1.refs_2_), channel_id=1, source_target_pairs={{0,224},{32,0},{64,32},{96,64},{128,96},{160,128},{192,160},{224,1... | collective-permute-start | bytes 393224 | tf_op jit(solution)/shard_map/ppermute | solution.py:243
  16.3 5.1 %collective-permute-start.9 = (bf16[128,512]{1,0:T(8,128)(2,1)S(1)}, bf16[128,512]{1,0:T(8,128)(2,1)S(1)}, u32[]{:S(2)}, u32[]{:S(2)}) collective-permute-start(bf16[128,512]{1,0:T(8,128)(2,1)S(1)} %collective-permute-done.refs_1_), channel_id=1, source_target_pairs={{0,1},{1,0},{2,3},{3,2},{4,5},{5,4},{6,7},{7,6},{8,9},{9,8},{10,11... | collective-permute-start | bytes 393224 | tf_op jit(solution)/shard_map/ppermute | solution.py:240
  18.5 4.9 %collective-permute-start.10 = (bf16[128,512]{1,0:T(8,128)(2,1)S(1)}, bf16[128,512]{1,0:T(8,128)(2,1)S(1)}, u32[]{:S(2)}, u32[]{:S(2)}) collective-permute-start(bf16[128,512]{1,0:T(8,128)(2,1)S(1)} %collective-permute-done.1.refs_2_), channel_id=1, source_target_pairs={{0,1},{1,0},{2,3},{3,2},{4,5},{5,4},{6,7},{7,6},{8,9},{9,8},{10,11... | collective-permute-start | bytes 393224 | tf_op jit(solution)/shard_map/ppermute | solution.py:240
  18.7 5.3 %collective-permute-start.11 = (bf16[128,512]{1,0:T(8,128)(2,1)S(1)}, bf16[128,512]{1,0:T(8,128)(2,1)S(1)}, u32[]{:S(2)}, u32[]{:S(2)}) collective-permute-start(bf16[128,512]{1,0:T(8,128)(2,1)S(1)} %collective-permute-done.4.refs_3_), channel_id=1, source_target_pairs={{0,1},{1,0},{2,3},{3,2},{4,5},{5,4},{6,7},{7,6},{8,9},{9,8},{10,11... | collective-permute-start | bytes 393224 | tf_op jit(solution)/shard_map/ppermute | solution.py:240
  21.4 4.6 %collective-permute-start.12 = (bf16[128,512]{1,0:T(8,128)(2,1)S(1)}, bf16[128,512]{1,0:T(8,128)(2,1)S(1)}, u32[]{:S(2)}, u32[]{:S(2)}) collective-permute-start(bf16[128,512]{1,0:T(8,128)(2,1)S(1)} %collective-permute-done.5.refs_4_), channel_id=1, source_target_pairs={{0,1},{1,0},{2,3},{3,2},{4,5},{5,4},{6,7},{7,6},{8,9},{9,8},{10,11... | collective-permute-start | bytes 393224 | tf_op jit(solution)/shard_map/ppermute | solution.py:240
  21.4 9.0 %collective-permute-start.3 = (bf16[128,512]{1,0:T(8,128)(2,1)S(1)}, bf16[128,512]{1,0:T(8,128)(2,1)S(1)}, u32[]{:S(2)}, u32[]{:S(2)}) collective-permute-start(bf16[128,512]{1,0:T(8,128)(2,1)S(1)} %copy-done.3), channel_id=1, source_target_pairs={{0,128},{32,160},{64,192},{96,224},{128,0},{160,32},{192,64},{224,... | collective-permute-start | bytes 393224 | tf_op jit(solution)/shard_map/ppermute | solution.py:243
  23.4 10.2 %collective-permute-start.6 = (bf16[128,512]{1,0:T(8,128)(2,1)S(1)}, bf16[128,512]{1,0:T(8,128)(2,1)S(1)}, u32[]{:S(2)}, u32[]{:S(2)}) collective-permute-start(bf16[128,512]{1,0:T(8,128)(2,1)S(1)} %collective-permute-done.4.refs_3_), channel_id=1, source_target_pairs={{0,32},{32,64},{64,96},{96,128},{128,160},{160,192},{192,224},{224... | collective-permute-start | bytes 393224 | tf_op jit(solution)/shard_map/ppermute | solution.py:243
  24.0 9.5 %collective-permute-start.7 = (bf16[128,512]{1,0:T(8,128)(2,1)S(1)}, bf16[128,512]{1,0:T(8,128)(2,1)S(1)}, u32[]{:S(2)}, u32[]{:S(2)}) collective-permute-start(bf16[128,512]{1,0:T(8,128)(2,1)S(1)} %collective-permute-done.5.refs_4_), channel_id=1, source_target_pairs={{0,224},{32,0},{64,32},{96,64},{128,96},{160,128},{192,160},{224,1... | collective-permute-start | bytes 393224 | tf_op jit(solution)/shard_map/ppermute | solution.py:243
  33.5 2.4 %collective-permute-start.13 = (bf16[128,512]{1,0:T(8,128)(2,1)S(1)}, bf16[128,512]{1,0:T(8,128)(2,1)S(1)}, u32[]{:S(2)}, u32[]{:S(2)}) collective-permute-start(bf16[128,512]{1,0:T(8,128)(2,1)S(1)} %collective-permute-done.3.refs_0_.refs_5_), channel_id=1, source_target_pairs={{0,1},{1,0},{2,3},{3,2},{4,5},{5,4},{6,7},{7,6},{8,9},{9,8},{10,11... | collective-permute-start | bytes 393224 | tf_op jit(solution)/shard_map/ppermute | solution.py:240
  34.9 1.3 collective-permute-start.14
  35.0 1.4 collective-permute-start.15
  39.5 37.0 %copy-start.4 = (bf16[512,512]{1,0:T(8,128)(2,1)S(1)}, bf16[512,512]{1,0:T(8,128)(2,1)}, u32[]{:S(2)}) copy-start(bf16[512,512]{1,0:T(8,128)(2,1)} %w.4) | copy-start | bytes 1572868
  39.6 37.0 %copy-start.5 = (bf16[128,512]{1,0:T(8,128)(2,1)S(1)}, bf16[128,512]{1,0:T(8,128)(2,1)}, u32[]{:S(2)}) copy-start(bf16[128,512]{1,0:T(8,128)(2,1)} %cot.1) | copy-start | bytes 393220
  110.9 3.9 %collective-permute-start.17 = (bf16[2,528,128]{2,1,0:T(8,128)(2,1)S(1)}, bf16[2,528,128]{2,1,0:T(8,128)(2,1)S(1)}, u32[]{:S(2)}, u32[]{:S(2)}) collective-permute-start(bf16[2,528,128]{2,1,0:T(8,128)(2,1)S(1)} %get-tuple-element.53), channel_id=1, source_target_pairs={{0,1},{1,0},{2,3},{3,2},{4,5},{5,4},{6,7},{7,6},{8,9},{9,8},{10,11... | collective-permute-start | bytes 811016 | tf_op jit(solution)/shard_map/ppermute | solution.py:240
  114.8 8.4 %collective-permute-start.18 = (bf16[6,528,128]{2,1,0:T(8,128)(2,1)S(1)}, bf16[6,528,128]{2,1,0:T(8,128)(2,1)S(1)}, u32[]{:S(2)}, u32[]{:S(2)}) collective-permute-start(bf16[6,528,128]{2,1,0:T(8,128)(2,1)S(1)} %get-tuple-element.55), channel_id=1, source_target_pairs={{0,1},{1,0},{2,3},{3,2},{4,5},{5,4},{6,7},{7,6},{8,9},{9,8},{10,11... | collective-permute-start | bytes 2433032 | tf_op jit(solution)/shard_map/ppermute | solution.py:240
  115.2 5.1 %collective-permute-start.20 = (bf16[528,128]{1,0:T(8,128)(2,1)S(1)}, bf16[528,128]{1,0:T(8,128)(2,1)S(1)}, u32[]{:S(2)}, u32[]{:S(2)}) collective-permute-start(bf16[528,128]{1,0:T(8,128)(2,1)S(1)} %get-tuple-element.74), channel_id=1, source_target_pairs={{0,224},{32,0},{64,32},{96,64},{128,96},{160,128},{192,160},{224,1... | collective-permute-start | bytes 405512 | tf_op jit(solution)/shard_map/ppermute | solution.py:243
  117.2 5.9 %collective-permute-start.19 = (bf16[528,128]{1,0:T(8,128)(2,1)S(1)}, bf16[528,128]{1,0:T(8,128)(2,1)S(1)}, u32[]{:S(2)}, u32[]{:S(2)}) collective-permute-start(bf16[528,128]{1,0:T(8,128)(2,1)S(1)} %get-tuple-element.75), channel_id=1, source_target_pairs={{0,32},{32,64},{64,96},{96,128},{128,160},{160,192},{192,224},{224... | collective-permute-start | bytes 405512 | tf_op jit(solution)/shard_map/ppermute | solution.py:243
  123.3 5.7 %collective-permute-start.21 = (bf16[528,128]{1,0:T(8,128)(2,1)S(1)}, bf16[528,128]{1,0:T(8,128)(2,1)S(1)}, u32[]{:S(2)}, u32[]{:S(2)}) collective-permute-start(bf16[528,128]{1,0:T(8,128)(2,1)S(1)} %get-tuple-element.60), channel_id=1, source_target_pairs={{0,32},{32,64},{64,96},{96,128},{128,160},{160,192},{192,224},{224... | collective-permute-start | bytes 405512 | tf_op jit(solution)/shard_map/ppermute | solution.py:243
  123.4 5.6 %collective-permute-start.22 = (bf16[528,128]{1,0:T(8,128)(2,1)S(1)}, bf16[528,128]{1,0:T(8,128)(2,1)S(1)}, u32[]{:S(2)}, u32[]{:S(2)}) collective-permute-start(bf16[528,128]{1,0:T(8,128)(2,1)S(1)} %get-tuple-element.61), channel_id=1, source_target_pairs={{0,224},{32,0},{64,32},{96,64},{128,96},{160,128},{192,160},{224,1... | collective-permute-start | bytes 405512 | tf_op jit(solution)/shard_map/ppermute | solution.py:243
  126.1 10.6 %collective-permute-start.25 = (bf16[528,128]{1,0:T(8,128)(2,1)S(1)}, bf16[528,128]{1,0:T(8,128)(2,1)S(1)}, u32[]{:S(2)}, u32[]{:S(2)}) collective-permute-start(bf16[528,128]{1,0:T(8,128)(2,1)S(1)} %get-tuple-element.76), channel_id=1, source_target_pairs={{0,128},{32,160},{64,192},{96,224},{128,0},{160,32},{192,64},{224,... | collective-permute-start | bytes 405512 | tf_op jit(solution)/shard_map/ppermute | solution.py:243
  129.1 7.6 %collective-permute-start.23 = (bf16[528,128]{1,0:T(8,128)(2,1)S(1)}, bf16[528,128]{1,0:T(8,128)(2,1)S(1)}, u32[]{:S(2)}, u32[]{:S(2)}) collective-permute-start(bf16[528,128]{1,0:T(8,128)(2,1)S(1)} %get-tuple-element.62), channel_id=1, source_target_pairs={{0,32},{32,64},{64,96},{96,128},{128,160},{160,192},{192,224},{224... | collective-permute-start | bytes 405512 | tf_op jit(solution)/shard_map/ppermute | solution.py:243
  129.2 7.8 %collective-permute-start.24 = (bf16[528,128]{1,0:T(8,128)(2,1)S(1)}, bf16[528,128]{1,0:T(8,128)(2,1)S(1)}, u32[]{:S(2)}, u32[]{:S(2)}) collective-permute-start(bf16[528,128]{1,0:T(8,128)(2,1)S(1)} %get-tuple-element.63), channel_id=1, source_target_pairs={{0,224},{32,0},{64,32},{96,64},{128,96},{160,128},{192,160},{224,1... | collective-permute-start | bytes 405512 | tf_op jit(solution)/shard_map/ppermute | solution.py:243
  176.8 12.6 %collective-permute-start.26 = (bf16[16,8,32,128]{3,2,1,0:T(8,128)(2,1)S(1)}, bf16[16,8,32,128]{3,2,1,0:T(8,128)(2,1)S(1)}, u32[]{:S(2)}, u32[]{:S(2)}) collective-permute-start(bf16[16,8,32,128]{3,2,1,0:T(8,128)(2,1)S(1)} %all_to_all.29.own), channel_id=1, source_target_pairs={{0,1},{1,0},{2,3},{3,2},{4,5},{5,4},{6,7},{7,6},{8,9},{9,8},{10,11... | collective-permute-start | bytes 3145736 | tf_op jit(solution)/shard_map/ppermute | solution.py:240
  187.1 2.4 %collective-permute-start.27 = (bf16[8,32,128]{2,1,0:T(8,128)(2,1)S(1)}, bf16[8,32,128]{2,1,0:T(8,128)(2,1)S(1)}, u32[]{:S(2)}, u32[]{:S(2)}) collective-permute-start(bf16[8,32,128]{2,1,0:T(8,128)(2,1)S(1)} %get-tuple-element.78), channel_id=1, source_target_pairs={{0,1},{1,0},{2,3},{3,2},{4,5},{5,4},{6,7},{7,6},{8,9},{9,8},{10,11... | collective-permute-start | bytes 196616 | tf_op jit(solution)/shard_map/ppermute | solution.py:240

commit v12 on v10

--- a/solution.py
+++ b/solution.py
@@ -191,20 +191,19 @@
         out[z, 64:96, :] = piece
 
 
-def rows_kernel(info, kept, given, w, grad_dims):
-    even = info[PLACE + 2] == 0
-    kind = info[KIND + info[PLACE]]
-    mine, other = kept[...].astype(F32).reshape(256, 128), given[...].astype(F32).reshape(256, 128)
-    turned = jnp.concatenate([jnp.where(even, mine, other), jnp.where(even, other, mine)], axis=0)
-    grad_dims[...] = lax.dot_general(
-        turned.T.astype(BF16), w[kind], (((1,), (1,)), ((), ())), preferred_element_type=F32
-    )
-
-
-def final_kernel(info, own, sib, grad_self, grad_tab):
+def final_kernel(info, own, sib, kept, given, w, grad_dims, grad_self, grad_tab):
     even = info[PLACE + 2] == 0
     scale = F32(32768.0**-0.5)
     q = pl.program_id(0)
+
+    @pl.when(q == 0)
+    def _():
+        mine, other = kept[...].astype(F32).reshape(256, 128), given[...].astype(F32).reshape(256, 128)
+        turned = jnp.concatenate([jnp.where(even, mine, other), jnp.where(even, other, mine)], axis=0)
+        weight = w[info[KIND + info[PLACE]]]
+        grad_dims[...] = lax.dot_general(
+            turned.T.astype(BF16), weight, (((1,), (1,)), ((), ())), preferred_element_type=F32
+        )
 
     def both_cores(chip, z):
         mine, other = own[chip, z].astype(F32) * scale, sib[chip, z].astype(F32) * scale
@@ -357,25 +356,23 @@
     pieces_own = by_chip(jnp.broadcast_to(packed[None, :, 64:, :], (chips, n_fact, 32, 128)))
     given = swap(packed[:, 32:64, :])
 
-    grad_dims = call(
-        rows_kernel,
-        jax.ShapeDtypeStruct((rows, width), F32),
-        [SMEM] + [VMEM] * 3,
-        flops=2 * rows * width * width,
-        moved=2 << 20,
-    )(info, packed[:, :32, :], given, w_tables)
-    grad_self, grad_tab = pl.pallas_call(
+    grad_dims, grad_self, grad_tab = pl.pallas_call(
         final_kernel,
-        out_shape=(jax.ShapeDtypeStruct((width, width), F32), jax.ShapeDtypeStruct((3, width, width), F32)),
+        out_shape=(
+            jax.ShapeDtypeStruct((rows, width), F32),
+            jax.ShapeDtypeStruct((width, width), F32),
+            jax.ShapeDtypeStruct((3, width, width), F32),
+        ),
         grid=(4,),
-        in_specs=[SMEM, VMEM, VMEM],
+        in_specs=[SMEM] + [VMEM] * 5,
         out_specs=(
+            pl.BlockSpec((rows, width), lambda q: (0, 0)),
             pl.BlockSpec((width, 128), lambda q: (0, q)),
             pl.BlockSpec((3, 128, width), lambda q: (0, q, 0)),
         ),
         compiler_params=PARAMS,
-        cost_estimate=pl.CostEstimate(flops=0, bytes_accessed=8 << 20, transcendentals=0),
-    )(info, pieces_own, swap(pieces_own))
+        cost_estimate=pl.CostEstimate(flops=2 * rows * width * width, bytes_accessed=8 << 20, transcendentals=0),
+    )(info, pieces_own, swap(pieces_own), packed[:, :32, :], given, w_tables)
     return (fact_out, grad_dims, grad_self, grad_tab)
 
 

time: 193 us -> 192 us (level)
  blocking collectives: 107 us -> 104 us
  starting transfers between devices: 47.8 us -> 50.8 us
    all_to_all x4, blocking collectives: 94.7 us -> 88.6 us  [by_chip(): return lax.all_to_all(x, 'dim', 0, 0, tiled=True, axis_index_groups=same)]
    ppermute x15, starting transfers between devices: 23 us -> 27.6 us  [shift(): lax.ppermute(x, 'fact', [(i, (i + by) % n_fact) for i in range(n_fact)])]
    all_to_all x1, blocking collectives: 12.5 us -> 15 us  [by_fact(): return lax.all_to_all(x, 'fact', 0, 0, tiled=True)]
    pallas_call x2 -> x1, Pallas kernels: 4.84 us -> 3.69 us  [body(): pl.pallas_call(final_kernel, out_shape=(jax.ShapeDtypeStruct((rows, width...]
  transfers between devices with their start and end apart: 30 -> 30, of which waited for: 12 -> 11; matrix products, arithmetic and copies ran while one was open for 1% -> 1% of each run, Pallas kernels for 2% -> 2%
where the time goes in v12:
time: 192 us
  blocking collectives  104 us (54%)
  starting transfers between devices  50.8 us (26%)
  waiting for transfers between devices  18.8 us (10%)
  Pallas kernels  15.8 us (8%)
    all_to_all x4, blocking collectives, by_chip(): return lax.all_to_all(x, 'dim', 0, 0, tiled=True, axis_index_groups=same)  88.6 us
    ppermute x15, starting transfers between devices, shift(): lax.ppermute(x, 'fact', [(i, (i + by) % n_fact) for i in range(n_fact)])  27.6 us
    ppermute x15, starting transfers between devices, swap(): return lax.ppermute(x, 'dim', pair)  23.2 us
    all_to_all x1, blocking collectives, by_fact(): return lax.all_to_all(x, 'fact', 0, 0, tiled=True)  15 us
    ppermute x15, waiting for transfers between devices, shift(): lax.ppermute(x, 'fact', [(i, (i + by) % n_fact) for i in range(n_fact)])  13.3 us
    ppermute x15, waiting for transfers between devices, swap(): return lax.ppermute(x, 'dim', pair)  5.5 us
  transfers between devices with their start and end apart: 30, of which 11 were waited for; matrix products, arithmetic and copies ran while one was open for 1% of the time, Pallas kernels for 2%

profile of v12, /device:TPU:1, one launch (start us, length us, event | category | flops | bytes accessed | tf_op | source)
XLA Modules:
  0.0 192.5 jit_solution(9520761535996696771)
XLA Ops:
  0.6 3.3 %collective-permute-start.18 = (bf16[32,128,128]{2,1,0:T(8,128)(2,1)}, bf16[32,128,128]{2,1,0:T(8,128)(2,1)S(1)}, u32[]{:S(2)}, u32[]{:S(2)}) collective-permute-start(bf16[32,128,128]{2,1,0:T(8,128)(2,1)} %tiles_own.1), channel_id=1, source_target_pairs={{0,1},{1,0},{2,3},{3,2},{4,5},{5,4},{6,7},{7,6},{8,9},{9,8},{10,11... | collective-permute-start | bytes 3145736 | tf_op jit(solution)/shard_map/ppermute | solution.py:246
  4.0 3.9 %collective-permute-start.1 = (bf16[128,512]{1,0:T(8,128)(2,1)}, bf16[128,512]{1,0:T(8,128)(2,1)S(1)}, u32[]{:S(2)}, u32[]{:S(2)}) collective-permute-start(bf16[128,512]{1,0:T(8,128)(2,1)} %refs_0_.3), channel_id=1, source_target_pairs={{0,224},{32,0},{64,32},{96,64},{128,96},{160,128},{192,160},{224,1... | collective-permute-start | bytes 393224 | tf_op jit(solution)/shard_map/ppermute | solution.py:249
  8.5 0.7 concatenate.3.links_own
  9.2 0.4 collective-permute-start.2
  9.6 0.7 collective-permute-done.2.links_sib
  10.3 0.7 copy-done.6
  11.0 1.5 shard_map.120.info
  12.6 1.4 collective-permute-done.refs_1_
  14.0 2.7 %collective-permute-start.6 = (bf16[128,512]{1,0:T(8,128)(2,1)S(1)}, bf16[128,512]{1,0:T(8,128)(2,1)S(1)}, u32[]{:S(2)}, u32[]{:S(2)}) collective-permute-start(bf16[128,512]{1,0:T(8,128)(2,1)S(1)} %collective-permute-done.1.refs_2_), channel_id=1, source_target_pairs={{0,224},{32,0},{64,32},{96,64},{128,96},{160,128},{192,160},{224,1... | collective-permute-start | bytes 393224 | tf_op jit(solution)/shard_map/ppermute | solution.py:249
  16.6 1.7 collective-permute-start.9
  18.4 0.6 collective-permute-done.3.refs_3_
  19.0 2.7 %collective-permute-start.7 = (bf16[128,512]{1,0:T(8,128)(2,1)S(1)}, bf16[128,512]{1,0:T(8,128)(2,1)S(1)}, u32[]{:S(2)}, u32[]{:S(2)}) collective-permute-start(bf16[128,512]{1,0:T(8,128)(2,1)S(1)} %collective-permute-done.6.refs_4_), channel_id=1, source_target_pairs={{0,224},{32,0},{64,32},{96,64},{128,96},{160,128},{192,160},{224,1... | collective-permute-start | bytes 393224 | tf_op jit(solution)/shard_map/ppermute | solution.py:249
  21.7 2.9 %collective-permute-start.11 = (bf16[128,512]{1,0:T(8,128)(2,1)S(1)}, bf16[128,512]{1,0:T(8,128)(2,1)S(1)}, u32[]{:S(2)}, u32[]{:S(2)}) collective-permute-start(bf16[128,512]{1,0:T(8,128)(2,1)S(1)} %collective-permute-done.1.refs_2_), channel_id=1, source_target_pairs={{0,1},{1,0},{2,3},{3,2},{4,5},{5,4},{6,7},{7,6},{8,9},{9,8},{10,11... | collective-permute-start | bytes 393224 | tf_op jit(solution)/shard_map/ppermute | solution.py:246
  24.6 2.9 %collective-permute-start.12 = (bf16[128,512]{1,0:T(8,128)(2,1)S(1)}, bf16[128,512]{1,0:T(8,128)(2,1)S(1)}, u32[]{:S(2)}, u32[]{:S(2)}) collective-permute-start(bf16[128,512]{1,0:T(8,128)(2,1)S(1)} %collective-permute-done.3.refs_3_), channel_id=1, source_target_pairs={{0,1},{1,0},{2,3},{3,2},{4,5},{5,4},{6,7},{7,6},{8,9},{9,8},{10,11... | collective-permute-start | bytes 393224 | tf_op jit(solution)/shard_map/ppermute | solution.py:246
  27.6 3.0 %collective-permute-start.8 = (bf16[64,512]{1,0:T(8,128)(2,1)S(1)}, bf16[64,512]{1,0:T(8,128)(2,1)S(1)}, u32[]{:S(2)}, u32[]{:S(2)}) collective-permute-start(bf16[64,512]{1,0:T(8,128)(2,1)S(1)} %slice.85), channel_id=1, source_target_pairs={{0,224},{32,0},{64,32},{96,64},{128,96},{160,128},{192,160},{224,1... | collective-permute-start | bytes 196616 | tf_op jit(solution)/shard_map/ppermute | solution.py:249
  30.7 0.7 collective-permute-start.14
  31.4 0.3 collective-permute-start.15
  31.6 1.4 shard_map.121
  33.1 0.5 collective-permute-start.16
  33.7 0.8 collective-permute-done.16.refs_6_.refs_16_
  34.5 0.4 collective-permute-done.17.refs_7_.refs_17_
  34.9 3.0 %shard_map.122 = bf16[16,544,128]{2,1,0:T(8,128)(2,1)S(1)} custom-call(s32[128]{0:T(128)S(1)} %shard_map.120.info, bf16[10,128,512]{2,1,0:T(8,128)(2,1)S(1)} %get-tuple-element.37.proj, bf16[128,512]{1,0:T(8,128)(2,1)S(1)} %collective-permute-done.4.refs_0_.refs_5_, bf16[128,512]{1,0:T(8,128)(2,1)S(1)} %collective-permute-done.7.refs_1_.refs_6_, ...), custom_call_target="tpu_custom_call" | custom-call | flops 536870912 | bytes 8388608 | tf_op jit(solution)/shard_map/pallas_call | solution.py:288
  38.0 35.3 %all_to_all.25.parts = bf16[16,544,128]{2,1,0:T(8,128)(2,1)S(1)} all-to-all(bf16[16,544,128]{2,1,0:T(8,128)(2,1)S(1)} %shard_map.122), channel_id=1, replica_groups={{0,2,4,6,8,10,12,14,16,18,20,22,24,26,28,30},{1,3,5,7,9,11,13,15,17,19,..., dimensions={0} | all-to-all | bytes 4456448 | tf_op jit(solution)/shard_map/all_to_all | solution.py:252
  73.3 1.2 shard_map.123
  74.4 28.9 %all_to_all.26.grads = bf16[16,512,128]{2,1,0:T(8,128)(2,1)S(1)} all-to-all(bf16[16,512,128]{2,1,0:T(8,128)(2,1)S(1)} %get-tuple-element.42), channel_id=1, replica_groups={{0,2,4,6,8,10,12,14,16,18,20,22,24,26,28,30},{1,3,5,7,9,11,13,15,17,19,..., dimensions={0} | all-to-all | bytes 4194304 | tf_op jit(solution)/shard_map/all_to_all | solution.py:252
  103.3 3.3 %shard_map.124 = (f32[8,528,128]{2,1,0:T(8,128)S(1)}, bf16[2,528,128]{2,1,0:T(8,128)(2,1)S(1)}, bf16[6,528,128]{2,1,0:T(8,128)(2,1)S(1)}) custom-call(s32[128]{0:T(128)S(1)} %shard_map.120.info, bf16[16,512,128]{2,1,0:T(8,128)(2,1)S(1)} %all_to_all.26.grads, bf16[16,32,128]{2,1,0:T(8,128)(2,1)S(1)} %get-tuple-element.43.facts_t, ...), custom_call_target="tpu_custom_call" | custom-call | flops 536870912 | bytes 9437184 | tf_op jit(solution)/shard_map/pallas_call | solution.py:311
  106.6 3.6 %collective-permute-start.19 = (bf16[2,528,128]{2,1,0:T(8,128)(2,1)S(1)}, bf16[2,528,128]{2,1,0:T(8,128)(2,1)S(1)}, u32[]{:S(2)}, u32[]{:S(2)}) collective-permute-start(bf16[2,528,128]{2,1,0:T(8,128)(2,1)S(1)} %get-tuple-element.45), channel_id=1, source_target_pairs={{0,1},{1,0},{2,3},{3,2},{4,5},{5,4},{6,7},{7,6},{8,9},{9,8},{10,11... | collective-permute-start | bytes 811016 | tf_op jit(solution)/shard_map/ppermute | solution.py:246
  110.3 1.2 collective-permute-done.19
  111.4 0.4 collective-permute-start.20
  111.9 4.5 %collective-permute-start.22 = (bf16[528,128]{1,0:T(8,128)(2,1)S(1)}, bf16[528,128]{1,0:T(8,128)(2,1)S(1)}, u32[]{:S(2)}, u32[]{:S(2)}) collective-permute-start(bf16[528,128]{1,0:T(8,128)(2,1)S(1)} %get-tuple-element.66), channel_id=1, source_target_pairs={{0,224},{32,0},{64,32},{96,64},{128,96},{160,128},{192,160},{224,1... | collective-permute-start | bytes 405512 | tf_op jit(solution)/shard_map/ppermute | solution.py:249
  116.4 2.8 %collective-permute-done.22 = bf16[528,128]{1,0:T(8,128)(2,1)S(1)} collective-permute-done((bf16[528,128]{1,0:T(8,128)(2,1)S(1)}, bf16[528,128]{1,0:T(8,128)(2,1)S(1)}, u32[]{:S(2)}, u32[]{:S(2)}) %collective-permute-start.22) | collective-permute-done | bytes 135200 | tf_op jit(solution)/shard_map/ppermute | solution.py:249
  119.2 3.1 %collective-permute-done.21 = bf16[528,128]{1,0:T(8,128)(2,1)S(1)} collective-permute-done((bf16[528,128]{1,0:T(8,128)(2,1)S(1)}, bf16[528,128]{1,0:T(8,128)(2,1)S(1)}, u32[]{:S(2)}, u32[]{:S(2)}) %collective-permute-start.21) | collective-permute-done | bytes 135200 | tf_op jit(solution)/shard_map/ppermute | solution.py:249
  122.3 0.1 fusion.1
  122.5 2.7 %collective-permute-start.24 = (bf16[528,128]{1,0:T(8,128)(2,1)S(1)}, bf16[528,128]{1,0:T(8,128)(2,1)S(1)}, u32[]{:S(2)}, u32[]{:S(2)}) collective-permute-start(bf16[528,128]{1,0:T(8,128)(2,1)S(1)} %get-tuple-element.53), channel_id=1, source_target_pairs={{0,224},{32,0},{64,32},{96,64},{128,96},{160,128},{192,160},{224,1... | collective-permute-start | bytes 405512 | tf_op jit(solution)/shard_map/ppermute | solution.py:249
  125.2 5.3 %collective-permute-start.27 = (bf16[528,128]{1,0:T(8,128)(2,1)S(1)}, bf16[528,128]{1,0:T(8,128)(2,1)S(1)}, u32[]{:S(2)}, u32[]{:S(2)}) collective-permute-start(bf16[528,128]{1,0:T(8,128)(2,1)S(1)} %get-tuple-element.68), channel_id=1, source_target_pairs={{0,128},{32,160},{64,192},{96,224},{128,0},{160,32},{192,64},{224,... | collective-permute-start | bytes 405512 | tf_op jit(solution)/shard_map/ppermute | solution.py:249
  130.5 0.1 fusion
  130.7 2.7 %collective-permute-start.26 = (bf16[528,128]{1,0:T(8,128)(2,1)S(1)}, bf16[528,128]{1,0:T(8,128)(2,1)S(1)}, u32[]{:S(2)}, u32[]{:S(2)}) collective-permute-start(bf16[528,128]{1,0:T(8,128)(2,1)S(1)} %get-tuple-element.55), channel_id=1, source_target_pairs={{0,224},{32,0},{64,32},{96,64},{128,96},{160,128},{192,160},{224,1... | collective-permute-start | bytes 405512 | tf_op jit(solution)/shard_map/ppermute | solution.py:249
  133.4 3.1 %collective-permute-done.27.from_far = bf16[528,128]{1,0:T(8,128)(2,1)S(1)} collective-permute-done((bf16[528,128]{1,0:T(8,128)(2,1)S(1)}, bf16[528,128]{1,0:T(8,128)(2,1)S(1)}, u32[]{:S(2)}, u32[]{:S(2)}) %collective-permute-start.27) | collective-permute-done | bytes 135200 | tf_op jit(solution)/shard_map/ppermute | solution.py:249
  136.5 2.2 %collective-permute-done.25.from_below = bf16[528,128]{1,0:T(8,128)(2,1)S(1)} collective-permute-done((bf16[528,128]{1,0:T(8,128)(2,1)S(1)}, bf16[528,128]{1,0:T(8,128)(2,1)S(1)}, u32[]{:S(2)}, u32[]{:S(2)}) %collective-permute-start.25) | collective-permute-done | bytes 135200 | tf_op jit(solution)/shard_map/ppermute | solution.py:249
  138.7 1.1 shard_map.125
  139.8 9.2 %all_to_all.27.parts = bf16[16,24,128]{2,1,0:T(8,128)(2,1)S(1)} all-to-all(bf16[16,24,128]{2,1,0:T(8,128)(2,1)S(1)} %bitcast.34), channel_id=1, replica_groups={{0,2,4,6,8,10,12,14,16,18,20,22,24,26,28,30},{1,3,5,7,9,11,13,15,17,19,..., dimensions={0} | all-to-all | bytes 196608 | tf_op jit(solution)/shard_map/all_to_all | solution.py:252
  149.0 0.6 shard_map.126
  149.6 15.0 %all_to_all.28 = bf16[8,96,128]{2,1,0:T(8,128)(2,1)S(1)} all-to-all(bf16[8,96,128]{2,1,0:T(8,128)(2,1)S(1)} %shard_map.126), channel_id=1, replica_groups=mesh['fact'=8,'dim'=32] {'fact'}, dimensions={0} | all-to-all | bytes 393216 | tf_op jit(solution)/shard_map/all_to_all | solution.py:255
  164.6 0.2 broadcast_in_dim.5
  164.8 15.1 %all_to_all.29.own = bf16[16,8,32,128]{3,2,1,0:T(8,128)(2,1)S(1)} all-to-all(bf16[16,8,32,128]{3,2,1,0:T(8,128)(2,1)S(1)} %broadcast_in_dim.5), channel_id=1, replica_groups={{0,2,4,6,8,10,12,14,16,18,20,22,24,26,28,30},{1,3,5,7,9,11,13,15,17,19,..., dimensions={0} | all-to-all | bytes 2097152 | tf_op jit(solution)/shard_map/all_to_all | solution.py:252
  180.0 6.4 %collective-permute-start.28 = (bf16[16,8,32,128]{3,2,1,0:T(8,128)(2,1)S(1)}, bf16[16,8,32,128]{3,2,1,0:T(8,128)(2,1)S(1)}, u32[]{:S(2)}, u32[]{:S(2)}) collective-permute-start(bf16[16,8,32,128]{3,2,1,0:T(8,128)(2,1)S(1)} %all_to_all.29.own), channel_id=1, source_target_pairs={{0,1},{1,0},{2,3},{3,2},{4,5},{5,4},{6,7},{7,6},{8,9},{9,8},{10,11... | collective-permute-start | bytes 3145736 | tf_op jit(solution)/shard_map/ppermute | solution.py:246
  186.4 2.4 %collective-permute-done.29.given = bf16[8,32,128]{2,1,0:T(8,128)(2,1)S(1)} collective-permute-done((bf16[8,32,128]{2,1,0:T(8,128)(2,1)S(1)}, bf16[8,32,128]{2,1,0:T(8,128)(2,1)S(1)}, u32[]{:S(2)}, u32[]{:S(2)}) %collective-permute-start.29) | collective-permute-done | bytes 65568 | tf_op jit(solution)/shard_map/ppermute | solution.py:246
  188.8 3.7 %shard_map.127 = (f32[128,512]{1,0:T(8,128)}, f32[512,512]{1,0:T(8,128)}, f32[3,512,512]{2,1,0:T(8,128)}) custom-call(s32[128]{0:T(128)S(1)} %shard_map.120.info, bf16[16,8,32,128]{3,2,1,0:T(8,128)(2,1)S(1)} %all_to_all.29.own, bf16[16,8,32,128]{3,2,1,0:T(8,128)(2,1)S(1)} %collective-permute-done.28.sib, bf16[8,32,128]{2,1,0:T(8,128)(2,1)S(1)} %get-tuple-element.71.kept, ...), custom_call_target="tpu_custom_call" | custom-call | flops 67108864 | bytes 8388608 | tf_op jit(solution)/shard_map/pallas_call | solution.py:359
  (50 shorter events, 0.6 us)
Async XLA Ops:
  0.6 34.3 %collective-permute-start.18 = (bf16[32,128,128]{2,1,0:T(8,128)(2,1)}, bf16[32,128,128]{2,1,0:T(8,128)(2,1)S(1)}, u32[]{:S(2)}, u32[]{:S(2)}) collective-permute-start(bf16[32,128,128]{2,1,0:T(8,128)(2,1)} %tiles_own.1), channel_id=1, source_target_pairs={{0,1},{1,0},{2,3},{3,2},{4,5},{5,4},{6,7},{7,6},{8,9},{9,8},{10,11... | collective-permute-start | bytes 3145736 | tf_op jit(solution)/shard_map/ppermute | solution.py:246
  4.0 8.6 %collective-permute-start.1 = (bf16[128,512]{1,0:T(8,128)(2,1)}, bf16[128,512]{1,0:T(8,128)(2,1)S(1)}, u32[]{:S(2)}, u32[]{:S(2)}) collective-permute-start(bf16[128,512]{1,0:T(8,128)(2,1)} %refs_0_.3), channel_id=1, source_target_pairs={{0,224},{32,0},{64,32},{96,64},{128,96},{160,128},{192,160},{224,1... | collective-permute-start | bytes 393224 | tf_op jit(solution)/shard_map/ppermute | solution.py:249
  7.8 6.1 %collective-permute-start = (bf16[128,512]{1,0:T(8,128)(2,1)}, bf16[128,512]{1,0:T(8,128)(2,1)S(1)}, u32[]{:S(2)}, u32[]{:S(2)}) collective-permute-start(bf16[128,512]{1,0:T(8,128)(2,1)} %refs_0_.3), channel_id=1, source_target_pairs={{0,32},{32,64},{64,96},{96,128},{128,160},{160,192},{192,224},{224... | collective-permute-start | bytes 393224 | tf_op jit(solution)/shard_map/ppermute | solution.py:249
  9.2 1.2 collective-permute-start.2
  9.6 7.1 %copy-start.3 = (bf16[128,512]{1,0:T(8,128)(2,1)S(1)}, bf16[128,512]{1,0:T(8,128)(2,1)}, u32[]{:S(2)}) copy-start(bf16[128,512]{1,0:T(8,128)(2,1)} %refs_0_.3) | copy-start | bytes 393220
  9.6 22.1 %copy-start = (bf16[3,512,512]{2,1,0:T(8,128)(2,1)S(1)}, bf16[3,512,512]{2,1,0:T(8,128)(2,1)}, u32[]{:S(2)}) copy-start(bf16[3,512,512]{2,1,0:T(8,128)(2,1)} %w.5) | copy-start | bytes 4718596
  9.6 22.1 %copy-start.2 = (bf16[128,512]{1,0:T(8,128)(2,1)S(1)}, bf16[128,512]{1,0:T(8,128)(2,1)}, u32[]{:S(2)}) copy-start(bf16[128,512]{1,0:T(8,128)(2,1)} %facts.3) | copy-start | bytes 393220
  10.3 0.7 copy-start.6
  12.5 22.4 %copy-start.1 = (bf16[32,128,128]{2,1,0:T(8,128)(2,1)S(1)}, bf16[32,128,128]{2,1,0:T(8,128)(2,1)}, u32[]{:S(2)}) copy-start(bf16[32,128,128]{2,1,0:T(8,128)(2,1)} %tiles_own.1) | copy-start | bytes 3145732
  14.0 5.0 %collective-permute-start.3 = (bf16[128,512]{1,0:T(8,128)(2,1)S(1)}, bf16[128,512]{1,0:T(8,128)(2,1)S(1)}, u32[]{:S(2)}, u32[]{:S(2)}) collective-permute-start(bf16[128,512]{1,0:T(8,128)(2,1)S(1)} %collective-permute-done.refs_1_), channel_id=1, source_target_pairs={{0,32},{32,64},{64,96},{96,128},{128,160},{160,192},{192,224},{224... | collective-permute-start | bytes 393224 | tf_op jit(solution)/shard_map/ppermute | solution.py:249
  14.0 5.0 %collective-permute-start.6 = (bf16[128,512]{1,0:T(8,128)(2,1)S(1)}, bf16[128,512]{1,0:T(8,128)(2,1)S(1)}, u32[]{:S(2)}, u32[]{:S(2)}) collective-permute-start(bf16[128,512]{1,0:T(8,128)(2,1)S(1)} %collective-permute-done.1.refs_2_), channel_id=1, source_target_pairs={{0,224},{32,0},{64,32},{96,64},{128,96},{160,128},{192,160},{224,1... | collective-permute-start | bytes 393224 | tf_op jit(solution)/shard_map/ppermute | solution.py:249
  16.6 7.9 %collective-permute-start.9 = (bf16[128,512]{1,0:T(8,128)(2,1)S(1)}, bf16[128,512]{1,0:T(8,128)(2,1)S(1)}, u32[]{:S(2)}, u32[]{:S(2)}) collective-permute-start(bf16[128,512]{1,0:T(8,128)(2,1)S(1)} %copy-done.3), channel_id=1, source_target_pairs={{0,1},{1,0},{2,3},{3,2},{4,5},{5,4},{6,7},{7,6},{8,9},{9,8},{10,11... | collective-permute-start | bytes 393224 | tf_op jit(solution)/shard_map/ppermute | solution.py:246
  19.0 5.6 %collective-permute-start.4 = (bf16[128,512]{1,0:T(8,128)(2,1)S(1)}, bf16[128,512]{1,0:T(8,128)(2,1)S(1)}, u32[]{:S(2)}, u32[]{:S(2)}) collective-permute-start(bf16[128,512]{1,0:T(8,128)(2,1)S(1)} %collective-permute-done.3.refs_3_), channel_id=1, source_target_pairs={{0,32},{32,64},{64,96},{96,128},{128,160},{160,192},{192,224},{224... | collective-permute-start | bytes 393224 | tf_op jit(solution)/shard_map/ppermute | solution.py:249
  19.0 8.5 %collective-permute-start.7 = (bf16[128,512]{1,0:T(8,128)(2,1)S(1)}, bf16[128,512]{1,0:T(8,128)(2,1)S(1)}, u32[]{:S(2)}, u32[]{:S(2)}) collective-permute-start(bf16[128,512]{1,0:T(8,128)(2,1)S(1)} %collective-permute-done.6.refs_4_), channel_id=1, source_target_pairs={{0,224},{32,0},{64,32},{96,64},{128,96},{160,128},{192,160},{224,1... | collective-permute-start | bytes 393224 | tf_op jit(solution)/shard_map/ppermute | solution.py:249
  21.7 5.9 %collective-permute-start.11 = (bf16[128,512]{1,0:T(8,128)(2,1)S(1)}, bf16[128,512]{1,0:T(8,128)(2,1)S(1)}, u32[]{:S(2)}, u32[]{:S(2)}) collective-permute-start(bf16[128,512]{1,0:T(8,128)(2,1)S(1)} %collective-permute-done.1.refs_2_), channel_id=1, source_target_pairs={{0,1},{1,0},{2,3},{3,2},{4,5},{5,4},{6,7},{7,6},{8,9},{9,8},{10,11... | collective-permute-start | bytes 393224 | tf_op jit(solution)/shard_map/ppermute | solution.py:246
  24.6 3.1 %collective-permute-start.10 = (bf16[128,512]{1,0:T(8,128)(2,1)S(1)}, bf16[128,512]{1,0:T(8,128)(2,1)S(1)}, u32[]{:S(2)}, u32[]{:S(2)}) collective-permute-start(bf16[128,512]{1,0:T(8,128)(2,1)S(1)} %collective-permute-done.refs_1_), channel_id=1, source_target_pairs={{0,1},{1,0},{2,3},{3,2},{4,5},{5,4},{6,7},{7,6},{8,9},{9,8},{10,11... | collective-permute-start | bytes 393224 | tf_op jit(solution)/shard_map/ppermute | solution.py:246
  24.6 6.1 %collective-permute-start.12 = (bf16[128,512]{1,0:T(8,128)(2,1)S(1)}, bf16[128,512]{1,0:T(8,128)(2,1)S(1)}, u32[]{:S(2)}, u32[]{:S(2)}) collective-permute-start(bf16[128,512]{1,0:T(8,128)(2,1)S(1)} %collective-permute-done.3.refs_3_), channel_id=1, source_target_pairs={{0,1},{1,0},{2,3},{3,2},{4,5},{5,4},{6,7},{7,6},{8,9},{9,8},{10,11... | collective-permute-start | bytes 393224 | tf_op jit(solution)/shard_map/ppermute | solution.py:246
  27.5 3.9 %collective-permute-start.13 = (bf16[128,512]{1,0:T(8,128)(2,1)S(1)}, bf16[128,512]{1,0:T(8,128)(2,1)S(1)}, u32[]{:S(2)}, u32[]{:S(2)}) collective-permute-start(bf16[128,512]{1,0:T(8,128)(2,1)S(1)} %collective-permute-done.6.refs_4_), channel_id=1, source_target_pairs={{0,1},{1,0},{2,3},{3,2},{4,5},{5,4},{6,7},{7,6},{8,9},{9,8},{10,11... | collective-permute-start | bytes 393224 | tf_op jit(solution)/shard_map/ppermute | solution.py:246
  27.5 5.5 %collective-permute-start.5 = (bf16[64,512]{1,0:T(8,128)(2,1)S(1)}, bf16[64,512]{1,0:T(8,128)(2,1)S(1)}, u32[]{:S(2)}, u32[]{:S(2)}) collective-permute-start(bf16[64,512]{1,0:T(8,128)(2,1)S(1)} %slice.84), channel_id=1, source_target_pairs={{0,32},{32,64},{64,96},{96,128},{128,160},{160,192},{192,224},{224... | collective-permute-start | bytes 196616 | tf_op jit(solution)/shard_map/ppermute | solution.py:249
  27.6 5.4 %collective-permute-start.8 = (bf16[64,512]{1,0:T(8,128)(2,1)S(1)}, bf16[64,512]{1,0:T(8,128)(2,1)S(1)}, u32[]{:S(2)}, u32[]{:S(2)}) collective-permute-start(bf16[64,512]{1,0:T(8,128)(2,1)S(1)} %slice.85), channel_id=1, source_target_pairs={{0,224},{32,0},{64,32},{96,64},{128,96},{160,128},{192,160},{224,1... | collective-permute-start | bytes 196616 | tf_op jit(solution)/shard_map/ppermute | solution.py:249
  30.7 4.2 %collective-permute-start.14 = (bf16[128,512]{1,0:T(8,128)(2,1)S(1)}, bf16[128,512]{1,0:T(8,128)(2,1)S(1)}, u32[]{:S(2)}, u32[]{:S(2)}) collective-permute-start(bf16[128,512]{1,0:T(8,128)(2,1)S(1)} %collective-permute-done.4.refs_0_.refs_5_), channel_id=1, source_target_pairs={{0,1},{1,0},{2,3},{3,2},{4,5},{5,4},{6,7},{7,6},{8,9},{9,8},{10,11... | collective-permute-start | bytes 393224 | tf_op jit(solution)/shard_map/ppermute | solution.py:246
  31.4 3.5 %collective-permute-start.15 = (bf16[128,512]{1,0:T(8,128)(2,1)S(1)}, bf16[128,512]{1,0:T(8,128)(2,1)S(1)}, u32[]{:S(2)}, u32[]{:S(2)}) collective-permute-start(bf16[128,512]{1,0:T(8,128)(2,1)S(1)} %collective-permute-done.7.refs_1_.refs_6_), channel_id=1, source_target_pairs={{0,1},{1,0},{2,3},{3,2},{4,5},{5,4},{6,7},{7,6},{8,9},{9,8},{10,11... | collective-permute-start | bytes 393224 | tf_op jit(solution)/shard_map/ppermute | solution.py:246
  33.1 1.4 collective-permute-start.16
  33.6 1.3 collective-permute-start.17
  37.9 35.3 %copy-start.4 = (bf16[512,512]{1,0:T(8,128)(2,1)S(1)}, bf16[512,512]{1,0:T(8,128)(2,1)}, u32[]{:S(2)}) copy-start(bf16[512,512]{1,0:T(8,128)(2,1)} %w.4) | copy-start | bytes 1572868
  38.0 35.3 %copy-start.5 = (bf16[128,512]{1,0:T(8,128)(2,1)S(1)}, bf16[128,512]{1,0:T(8,128)(2,1)}, u32[]{:S(2)}) copy-start(bf16[128,512]{1,0:T(8,128)(2,1)} %cot.1) | copy-start | bytes 393220
  106.6 4.8 %collective-permute-start.19 = (bf16[2,528,128]{2,1,0:T(8,128)(2,1)S(1)}, bf16[2,528,128]{2,1,0:T(8,128)(2,1)S(1)}, u32[]{:S(2)}, u32[]{:S(2)}) collective-permute-start(bf16[2,528,128]{2,1,0:T(8,128)(2,1)S(1)} %get-tuple-element.45), channel_id=1, source_target_pairs={{0,1},{1,0},{2,3},{3,2},{4,5},{5,4},{6,7},{7,6},{8,9},{9,8},{10,11... | collective-permute-start | bytes 811016 | tf_op jit(solution)/shard_map/ppermute | solution.py:246
  111.4 10.9 %collective-permute-start.20 = (bf16[6,528,128]{2,1,0:T(8,128)(2,1)S(1)}, bf16[6,528,128]{2,1,0:T(8,128)(2,1)S(1)}, u32[]{:S(2)}, u32[]{:S(2)}) collective-permute-start(bf16[6,528,128]{2,1,0:T(8,128)(2,1)S(1)} %get-tuple-element.47), channel_id=1, source_target_pairs={{0,1},{1,0},{2,3},{3,2},{4,5},{5,4},{6,7},{7,6},{8,9},{9,8},{10,11... | collective-permute-start | bytes 2433032 | tf_op jit(solution)/shard_map/ppermute | solution.py:246
  111.9 7.3 %collective-permute-start.22 = (bf16[528,128]{1,0:T(8,128)(2,1)S(1)}, bf16[528,128]{1,0:T(8,128)(2,1)S(1)}, u32[]{:S(2)}, u32[]{:S(2)}) collective-permute-start(bf16[528,128]{1,0:T(8,128)(2,1)S(1)} %get-tuple-element.66), channel_id=1, source_target_pairs={{0,224},{32,0},{64,32},{96,64},{128,96},{160,128},{192,160},{224,1... | collective-permute-start | bytes 405512 | tf_op jit(solution)/shard_map/ppermute | solution.py:249
  116.4 5.9 %collective-permute-start.21 = (bf16[528,128]{1,0:T(8,128)(2,1)S(1)}, bf16[528,128]{1,0:T(8,128)(2,1)S(1)}, u32[]{:S(2)}, u32[]{:S(2)}) collective-permute-start(bf16[528,128]{1,0:T(8,128)(2,1)S(1)} %get-tuple-element.67), channel_id=1, source_target_pairs={{0,32},{32,64},{64,96},{96,128},{128,160},{160,192},{192,224},{224... | collective-permute-start | bytes 405512 | tf_op jit(solution)/shard_map/ppermute | solution.py:249
  122.4 8.1 %collective-permute-start.23 = (bf16[528,128]{1,0:T(8,128)(2,1)S(1)}, bf16[528,128]{1,0:T(8,128)(2,1)S(1)}, u32[]{:S(2)}, u32[]{:S(2)}) collective-permute-start(bf16[528,128]{1,0:T(8,128)(2,1)S(1)} %get-tuple-element.52), channel_id=1, source_target_pairs={{0,32},{32,64},{64,96},{96,128},{128,160},{160,192},{192,224},{224... | collective-permute-start | bytes 405512 | tf_op jit(solution)/shard_map/ppermute | solution.py:249
  122.5 8.0 %collective-permute-start.24 = (bf16[528,128]{1,0:T(8,128)(2,1)S(1)}, bf16[528,128]{1,0:T(8,128)(2,1)S(1)}, u32[]{:S(2)}, u32[]{:S(2)}) collective-permute-start(bf16[528,128]{1,0:T(8,128)(2,1)S(1)} %get-tuple-element.53), channel_id=1, source_target_pairs={{0,224},{32,0},{64,32},{96,64},{128,96},{160,128},{192,160},{224,1... | collective-permute-start | bytes 405512 | tf_op jit(solution)/shard_map/ppermute | solution.py:249
  125.2 11.3 %collective-permute-start.27 = (bf16[528,128]{1,0:T(8,128)(2,1)S(1)}, bf16[528,128]{1,0:T(8,128)(2,1)S(1)}, u32[]{:S(2)}, u32[]{:S(2)}) collective-permute-start(bf16[528,128]{1,0:T(8,128)(2,1)S(1)} %get-tuple-element.68), channel_id=1, source_target_pairs={{0,128},{32,160},{64,192},{96,224},{128,0},{160,32},{192,64},{224,... | collective-permute-start | bytes 405512 | tf_op jit(solution)/shard_map/ppermute | solution.py:249
  130.6 8.1 %collective-permute-start.25 = (bf16[528,128]{1,0:T(8,128)(2,1)S(1)}, bf16[528,128]{1,0:T(8,128)(2,1)S(1)}, u32[]{:S(2)}, u32[]{:S(2)}) collective-permute-start(bf16[528,128]{1,0:T(8,128)(2,1)S(1)} %get-tuple-element.54), channel_id=1, source_target_pairs={{0,32},{32,64},{64,96},{96,128},{128,160},{160,192},{192,224},{224... | collective-permute-start | bytes 405512 | tf_op jit(solution)/shard_map/ppermute | solution.py:249
  130.7 8.0 %collective-permute-start.26 = (bf16[528,128]{1,0:T(8,128)(2,1)S(1)}, bf16[528,128]{1,0:T(8,128)(2,1)S(1)}, u32[]{:S(2)}, u32[]{:S(2)}) collective-permute-start(bf16[528,128]{1,0:T(8,128)(2,1)S(1)} %get-tuple-element.55), channel_id=1, source_target_pairs={{0,224},{32,0},{64,32},{96,64},{128,96},{160,128},{192,160},{224,1... | collective-permute-start | bytes 405512 | tf_op jit(solution)/shard_map/ppermute | solution.py:249
  180.0 8.8 %collective-permute-start.28 = (bf16[16,8,32,128]{3,2,1,0:T(8,128)(2,1)S(1)}, bf16[16,8,32,128]{3,2,1,0:T(8,128)(2,1)S(1)}, u32[]{:S(2)}, u32[]{:S(2)}) collective-permute-start(bf16[16,8,32,128]{3,2,1,0:T(8,128)(2,1)S(1)} %all_to_all.29.own), channel_id=1, source_target_pairs={{0,1},{1,0},{2,3},{3,2},{4,5},{5,4},{6,7},{7,6},{8,9},{9,8},{10,11... | collective-permute-start | bytes 3145736 | tf_op jit(solution)/shard_map/ppermute | solution.py:246
  186.4 2.4 %collective-permute-start.29 = (bf16[8,32,128]{2,1,0:T(8,128)(2,1)S(1)}, bf16[8,32,128]{2,1,0:T(8,128)(2,1)S(1)}, u32[]{:S(2)}, u32[]{:S(2)}) collective-permute-start(bf16[8,32,128]{2,1,0:T(8,128)(2,1)S(1)} %get-tuple-element.70), channel_id=1, source_target_pairs={{0,1},{1,0},{2,3},{3,2},{4,5},{5,4},{6,7},{7,6},{8,9},{9,8},{10,11... | collective-permute-start | bytes 196616 | tf_op jit(solution)/shard_map/ppermute | solution.py:246

commit v13 on v12

--- a/solution.py
+++ b/solution.py
@@ -10,7 +10,7 @@
 VMEM = pl.BlockSpec(memory_space=pltpu.VMEM)
 SMEM = pl.BlockSpec(memory_space=pltpu.SMEM)
 PARAMS = pltpu.CompilerParams(vmem_limit_bytes=24 * 1024 * 1024)
-UNROLL = 4
+UNROLL = 8
 
 
 ORDER = (0, -1, 1, -2, 2, -3, 3)

time: 192 us -> 191 us (level)
  starting transfers between devices: 50.8 us -> 47.3 us
    all_to_all x4, blocking collectives: 88.6 us -> 92.9 us  [by_chip(): return lax.all_to_all(x, 'dim', 0, 0, tiled=True, axis_index_groups=same)]
    ppermute x15, starting transfers between devices: 27.6 us -> 23.4 us  [shift(): lax.ppermute(x, 'fact', [(i, (i + by) % n_fact) for i in range(n_fact)])]
    all_to_all x1, blocking collectives: 15 us -> 12.2 us  [by_fact(): return lax.all_to_all(x, 'fact', 0, 0, tiled=True)]
  transfers between devices with their start and end apart: 30 -> 30, of which waited for: 11 -> 12; matrix products, arithmetic and copies ran while one was open for 1% -> 1% of each run, Pallas kernels for 2% -> 2%
where the time goes in v13:
time: 191 us
  blocking collectives  105 us (55%)
  starting transfers between devices  47.3 us (25%)
  waiting for transfers between devices  19.4 us (10%)
  Pallas kernels  15.5 us (8%)
    all_to_all x4, blocking collectives, by_chip(): return lax.all_to_all(x, 'dim', 0, 0, tiled=True, axis_index_groups=same)  92.9 us
    ppermute x15, starting transfers between devices, swap(): return lax.ppermute(x, 'dim', pair)  23.9 us
    ppermute x15, starting transfers between devices, shift(): lax.ppermute(x, 'fact', [(i, (i + by) % n_fact) for i in range(n_fact)])  23.4 us
    ppermute x15, waiting for transfers between devices, shift(): lax.ppermute(x, 'fact', [(i, (i + by) % n_fact) for i in range(n_fact)])  13.8 us
    all_to_all x1, blocking collectives, by_fact(): return lax.all_to_all(x, 'fact', 0, 0, tiled=True)  12.2 us
    ppermute x15, waiting for transfers between devices, swap(): return lax.ppermute(x, 'dim', pair)  5.5 us
  transfers between devices with their start and end apart: 30, of which 12 were waited for; matrix products, arithmetic and copies ran while one was open for 1% of the time, Pallas kernels for 2%

profile of v13, /device:TPU:1, one launch (start us, length us, event | category | flops | bytes accessed | tf_op | source)
XLA Modules:
  0.0 190.8 jit_solution(18383276627309911793)
XLA Ops:
  0.6 3.3 %collective-permute-start.18 = (bf16[32,128,128]{2,1,0:T(8,128)(2,1)}, bf16[32,128,128]{2,1,0:T(8,128)(2,1)S(1)}, u32[]{:S(2)}, u32[]{:S(2)}) collective-permute-start(bf16[32,128,128]{2,1,0:T(8,128)(2,1)} %tiles_own.1), channel_id=1, source_target_pairs={{0,1},{1,0},{2,3},{3,2},{4,5},{5,4},{6,7},{7,6},{8,9},{9,8},{10,11... | collective-permute-start | bytes 3145736 | tf_op jit(solution)/shard_map/ppermute | solution.py:246
  4.0 3.9 %collective-permute-start.1 = (bf16[128,512]{1,0:T(8,128)(2,1)}, bf16[128,512]{1,0:T(8,128)(2,1)S(1)}, u32[]{:S(2)}, u32[]{:S(2)}) collective-permute-start(bf16[128,512]{1,0:T(8,128)(2,1)} %refs_0_.3), channel_id=1, source_target_pairs={{0,224},{32,0},{64,32},{96,64},{128,96},{160,128},{192,160},{224,1... | collective-permute-start | bytes 393224 | tf_op jit(solution)/shard_map/ppermute | solution.py:249
  8.5 0.7 concatenate.3.links_own
  9.2 0.4 collective-permute-start.2
  9.6 0.7 collective-permute-done.2.links_sib
  10.3 0.7 copy-done.6
  11.0 1.5 shard_map.120.info
  12.6 1.4 collective-permute-done.refs_1_
  14.0 2.7 %collective-permute-start.6 = (bf16[128,512]{1,0:T(8,128)(2,1)S(1)}, bf16[128,512]{1,0:T(8,128)(2,1)S(1)}, u32[]{:S(2)}, u32[]{:S(2)}) collective-permute-start(bf16[128,512]{1,0:T(8,128)(2,1)S(1)} %collective-permute-done.1.refs_2_), channel_id=1, source_target_pairs={{0,224},{32,0},{64,32},{96,64},{128,96},{160,128},{192,160},{224,1... | collective-permute-start | bytes 393224 | tf_op jit(solution)/shard_map/ppermute | solution.py:249
  16.6 1.7 collective-permute-start.9
  18.4 0.6 collective-permute-done.3.refs_3_
  19.0 2.7 %collective-permute-start.7 = (bf16[128,512]{1,0:T(8,128)(2,1)S(1)}, bf16[128,512]{1,0:T(8,128)(2,1)S(1)}, u32[]{:S(2)}, u32[]{:S(2)}) collective-permute-start(bf16[128,512]{1,0:T(8,128)(2,1)S(1)} %collective-permute-done.6.refs_4_), channel_id=1, source_target_pairs={{0,224},{32,0},{64,32},{96,64},{128,96},{160,128},{192,160},{224,1... | collective-permute-start | bytes 393224 | tf_op jit(solution)/shard_map/ppermute | solution.py:249
  21.7 2.9 %collective-permute-start.11 = (bf16[128,512]{1,0:T(8,128)(2,1)S(1)}, bf16[128,512]{1,0:T(8,128)(2,1)S(1)}, u32[]{:S(2)}, u32[]{:S(2)}) collective-permute-start(bf16[128,512]{1,0:T(8,128)(2,1)S(1)} %collective-permute-done.1.refs_2_), channel_id=1, source_target_pairs={{0,1},{1,0},{2,3},{3,2},{4,5},{5,4},{6,7},{7,6},{8,9},{9,8},{10,11... | collective-permute-start | bytes 393224 | tf_op jit(solution)/shard_map/ppermute | solution.py:246
  24.6 2.9 %collective-permute-start.12 = (bf16[128,512]{1,0:T(8,128)(2,1)S(1)}, bf16[128,512]{1,0:T(8,128)(2,1)S(1)}, u32[]{:S(2)}, u32[]{:S(2)}) collective-permute-start(bf16[128,512]{1,0:T(8,128)(2,1)S(1)} %collective-permute-done.3.refs_3_), channel_id=1, source_target_pairs={{0,1},{1,0},{2,3},{3,2},{4,5},{5,4},{6,7},{7,6},{8,9},{9,8},{10,11... | collective-permute-start | bytes 393224 | tf_op jit(solution)/shard_map/ppermute | solution.py:246
  27.6 3.0 %collective-permute-start.8 = (bf16[64,512]{1,0:T(8,128)(2,1)S(1)}, bf16[64,512]{1,0:T(8,128)(2,1)S(1)}, u32[]{:S(2)}, u32[]{:S(2)}) collective-permute-start(bf16[64,512]{1,0:T(8,128)(2,1)S(1)} %slice.85), channel_id=1, source_target_pairs={{0,224},{32,0},{64,32},{96,64},{128,96},{160,128},{192,160},{224,1... | collective-permute-start | bytes 196616 | tf_op jit(solution)/shard_map/ppermute | solution.py:249
  30.7 0.7 collective-permute-start.14
  31.4 0.3 collective-permute-start.15
  31.6 1.4 shard_map.121
  33.1 0.5 collective-permute-start.16
  33.7 0.8 collective-permute-done.16.refs_6_.refs_16_
  34.5 0.4 collective-permute-done.17.refs_7_.refs_17_
  34.9 2.9 %shard_map.122 = bf16[16,544,128]{2,1,0:T(8,128)(2,1)S(1)} custom-call(s32[128]{0:T(128)S(1)} %shard_map.120.info, bf16[10,128,512]{2,1,0:T(8,128)(2,1)S(1)} %get-tuple-element.37.proj, bf16[128,512]{1,0:T(8,128)(2,1)S(1)} %collective-permute-done.4.refs_0_.refs_5_, bf16[128,512]{1,0:T(8,128)(2,1)S(1)} %collective-permute-done.7.refs_1_.refs_6_, ...), custom_call_target="tpu_custom_call" | custom-call | flops 536870912 | bytes 8388608 | tf_op jit(solution)/shard_map/pallas_call | solution.py:288
  37.8 36.2 %all_to_all.25.parts = bf16[16,544,128]{2,1,0:T(8,128)(2,1)S(1)} all-to-all(bf16[16,544,128]{2,1,0:T(8,128)(2,1)S(1)} %shard_map.122), channel_id=1, replica_groups={{0,2,4,6,8,10,12,14,16,18,20,22,24,26,28,30},{1,3,5,7,9,11,13,15,17,19,..., dimensions={0} | all-to-all | bytes 4456448 | tf_op jit(solution)/shard_map/all_to_all | solution.py:252
  74.0 1.2 shard_map.123
  75.2 30.2 %all_to_all.26.grads = bf16[16,512,128]{2,1,0:T(8,128)(2,1)S(1)} all-to-all(bf16[16,512,128]{2,1,0:T(8,128)(2,1)S(1)} %get-tuple-element.42), channel_id=1, replica_groups={{0,2,4,6,8,10,12,14,16,18,20,22,24,26,28,30},{1,3,5,7,9,11,13,15,17,19,..., dimensions={0} | all-to-all | bytes 4194304 | tf_op jit(solution)/shard_map/all_to_all | solution.py:252
  105.4 3.2 %shard_map.124 = (f32[8,528,128]{2,1,0:T(8,128)S(1)}, bf16[2,528,128]{2,1,0:T(8,128)(2,1)S(1)}, bf16[6,528,128]{2,1,0:T(8,128)(2,1)S(1)}) custom-call(s32[128]{0:T(128)S(1)} %shard_map.120.info, bf16[16,512,128]{2,1,0:T(8,128)(2,1)S(1)} %all_to_all.26.grads, bf16[16,32,128]{2,1,0:T(8,128)(2,1)S(1)} %get-tuple-element.43.facts_t, ...), custom_call_target="tpu_custom_call" | custom-call | flops 536870912 | bytes 9437184 | tf_op jit(solution)/shard_map/pallas_call | solution.py:311
  108.6 2.3 %collective-permute-start.19 = (bf16[2,528,128]{2,1,0:T(8,128)(2,1)S(1)}, bf16[2,528,128]{2,1,0:T(8,128)(2,1)S(1)}, u32[]{:S(2)}, u32[]{:S(2)}) collective-permute-start(bf16[2,528,128]{2,1,0:T(8,128)(2,1)S(1)} %get-tuple-element.45), channel_id=1, source_target_pairs={{0,1},{1,0},{2,3},{3,2},{4,5},{5,4},{6,7},{7,6},{8,9},{9,8},{10,11... | collective-permute-start | bytes 811016 | tf_op jit(solution)/shard_map/ppermute | solution.py:246
  110.9 1.2 collective-permute-done.19
  112.1 0.4 collective-permute-start.20
  112.6 3.3 %collective-permute-start.22 = (bf16[528,128]{1,0:T(8,128)(2,1)S(1)}, bf16[528,128]{1,0:T(8,128)(2,1)S(1)}, u32[]{:S(2)}, u32[]{:S(2)}) collective-permute-start(bf16[528,128]{1,0:T(8,128)(2,1)S(1)} %get-tuple-element.66), channel_id=1, source_target_pairs={{0,224},{32,0},{64,32},{96,64},{128,96},{160,128},{192,160},{224,1... | collective-permute-start | bytes 405512 | tf_op jit(solution)/shard_map/ppermute | solution.py:249
  115.8 2.8 %collective-permute-done.22 = bf16[528,128]{1,0:T(8,128)(2,1)S(1)} collective-permute-done((bf16[528,128]{1,0:T(8,128)(2,1)S(1)}, bf16[528,128]{1,0:T(8,128)(2,1)S(1)}, u32[]{:S(2)}, u32[]{:S(2)}) %collective-permute-start.22) | collective-permute-done | bytes 135200 | tf_op jit(solution)/shard_map/ppermute | solution.py:249
  118.7 3.1 %collective-permute-done.21 = bf16[528,128]{1,0:T(8,128)(2,1)S(1)} collective-permute-done((bf16[528,128]{1,0:T(8,128)(2,1)S(1)}, bf16[528,128]{1,0:T(8,128)(2,1)S(1)}, u32[]{:S(2)}, u32[]{:S(2)}) %collective-permute-start.21) | collective-permute-done | bytes 135200 | tf_op jit(solution)/shard_map/ppermute | solution.py:249
  122.0 2.7 %collective-permute-start.24 = (bf16[528,128]{1,0:T(8,128)(2,1)S(1)}, bf16[528,128]{1,0:T(8,128)(2,1)S(1)}, u32[]{:S(2)}, u32[]{:S(2)}) collective-permute-start(bf16[528,128]{1,0:T(8,128)(2,1)S(1)} %get-tuple-element.53), channel_id=1, source_target_pairs={{0,224},{32,0},{64,32},{96,64},{128,96},{160,128},{192,160},{224,1... | collective-permute-start | bytes 405512 | tf_op jit(solution)/shard_map/ppermute | solution.py:249
  124.7 1.1 collective-permute-start.27
  125.8 1.5 collective-permute-done.23
  127.3 0.1 fusion
  127.6 3.8 %collective-permute-start.26 = (bf16[528,128]{1,0:T(8,128)(2,1)S(1)}, bf16[528,128]{1,0:T(8,128)(2,1)S(1)}, u32[]{:S(2)}, u32[]{:S(2)}) collective-permute-start(bf16[528,128]{1,0:T(8,128)(2,1)S(1)} %get-tuple-element.55), channel_id=1, source_target_pairs={{0,224},{32,0},{64,32},{96,64},{128,96},{160,128},{192,160},{224,1... | collective-permute-start | bytes 405512 | tf_op jit(solution)/shard_map/ppermute | solution.py:249
  131.4 3.2 %collective-permute-done.27.from_far = bf16[528,128]{1,0:T(8,128)(2,1)S(1)} collective-permute-done((bf16[528,128]{1,0:T(8,128)(2,1)S(1)}, bf16[528,128]{1,0:T(8,128)(2,1)S(1)}, u32[]{:S(2)}, u32[]{:S(2)}) %collective-permute-start.27) | collective-permute-done | bytes 135200 | tf_op jit(solution)/shard_map/ppermute | solution.py:249
  134.6 1.2 collective-permute-done.25.from_below
  135.8 1.1 shard_map.125
  136.8 11.8 %all_to_all.27.parts = bf16[16,24,128]{2,1,0:T(8,128)(2,1)S(1)} all-to-all(bf16[16,24,128]{2,1,0:T(8,128)(2,1)S(1)} %bitcast.34), channel_id=1, replica_groups={{0,2,4,6,8,10,12,14,16,18,20,22,24,26,28,30},{1,3,5,7,9,11,13,15,17,19,..., dimensions={0} | all-to-all | bytes 196608 | tf_op jit(solution)/shard_map/all_to_all | solution.py:252
  148.6 0.6 shard_map.126
  149.2 12.2 %all_to_all.28 = bf16[8,96,128]{2,1,0:T(8,128)(2,1)S(1)} all-to-all(bf16[8,96,128]{2,1,0:T(8,128)(2,1)S(1)} %shard_map.126), channel_id=1, replica_groups=mesh['fact'=8,'dim'=32] {'fact'}, dimensions={0} | all-to-all | bytes 393216 | tf_op jit(solution)/shard_map/all_to_all | solution.py:255
  161.4 0.2 broadcast_in_dim.5
  161.6 14.7 %all_to_all.29.own = bf16[16,8,32,128]{3,2,1,0:T(8,128)(2,1)S(1)} all-to-all(bf16[16,8,32,128]{3,2,1,0:T(8,128)(2,1)S(1)} %broadcast_in_dim.5), channel_id=1, replica_groups={{0,2,4,6,8,10,12,14,16,18,20,22,24,26,28,30},{1,3,5,7,9,11,13,15,17,19,..., dimensions={0} | all-to-all | bytes 2097152 | tf_op jit(solution)/shard_map/all_to_all | solution.py:252
  176.3 8.3 %collective-permute-start.28 = (bf16[16,8,32,128]{3,2,1,0:T(8,128)(2,1)S(1)}, bf16[16,8,32,128]{3,2,1,0:T(8,128)(2,1)S(1)}, u32[]{:S(2)}, u32[]{:S(2)}) collective-permute-start(bf16[16,8,32,128]{3,2,1,0:T(8,128)(2,1)S(1)} %all_to_all.29.own), channel_id=1, source_target_pairs={{0,1},{1,0},{2,3},{3,2},{4,5},{5,4},{6,7},{7,6},{8,9},{9,8},{10,11... | collective-permute-start | bytes 3145736 | tf_op jit(solution)/shard_map/ppermute | solution.py:246
  184.7 2.4 %collective-permute-done.29.given = bf16[8,32,128]{2,1,0:T(8,128)(2,1)S(1)} collective-permute-done((bf16[8,32,128]{2,1,0:T(8,128)(2,1)S(1)}, bf16[8,32,128]{2,1,0:T(8,128)(2,1)S(1)}, u32[]{:S(2)}, u32[]{:S(2)}) %collective-permute-start.29) | collective-permute-done | bytes 65568 | tf_op jit(solution)/shard_map/ppermute | solution.py:246
  187.1 3.7 %shard_map.127 = (f32[128,512]{1,0:T(8,128)}, f32[512,512]{1,0:T(8,128)}, f32[3,512,512]{2,1,0:T(8,128)}) custom-call(s32[128]{0:T(128)S(1)} %shard_map.120.info, bf16[16,8,32,128]{3,2,1,0:T(8,128)(2,1)S(1)} %all_to_all.29.own, bf16[16,8,32,128]{3,2,1,0:T(8,128)(2,1)S(1)} %collective-permute-done.28.sib, bf16[8,32,128]{2,1,0:T(8,128)(2,1)S(1)} %get-tuple-element.71.kept, ...), custom_call_target="tpu_custom_call" | custom-call | flops 67108864 | bytes 8388608 | tf_op jit(solution)/shard_map/pallas_call | solution.py:359
  (50 shorter events, 0.7 us)
Async XLA Ops:
  0.6 34.3 %collective-permute-start.18 = (bf16[32,128,128]{2,1,0:T(8,128)(2,1)}, bf16[32,128,128]{2,1,0:T(8,128)(2,1)S(1)}, u32[]{:S(2)}, u32[]{:S(2)}) collective-permute-start(bf16[32,128,128]{2,1,0:T(8,128)(2,1)} %tiles_own.1), channel_id=1, source_target_pairs={{0,1},{1,0},{2,3},{3,2},{4,5},{5,4},{6,7},{7,6},{8,9},{9,8},{10,11... | collective-permute-start | bytes 3145736 | tf_op jit(solution)/shard_map/ppermute | solution.py:246
  4.0 8.6 %collective-permute-start.1 = (bf16[128,512]{1,0:T(8,128)(2,1)}, bf16[128,512]{1,0:T(8,128)(2,1)S(1)}, u32[]{:S(2)}, u32[]{:S(2)}) collective-permute-start(bf16[128,512]{1,0:T(8,128)(2,1)} %refs_0_.3), channel_id=1, source_target_pairs={{0,224},{32,0},{64,32},{96,64},{128,96},{160,128},{192,160},{224,1... | collective-permute-start | bytes 393224 | tf_op jit(solution)/shard_map/ppermute | solution.py:249
  7.8 6.1 %collective-permute-start = (bf16[128,512]{1,0:T(8,128)(2,1)}, bf16[128,512]{1,0:T(8,128)(2,1)S(1)}, u32[]{:S(2)}, u32[]{:S(2)}) collective-permute-start(bf16[128,512]{1,0:T(8,128)(2,1)} %refs_0_.3), channel_id=1, source_target_pairs={{0,32},{32,64},{64,96},{96,128},{128,160},{160,192},{192,224},{224... | collective-permute-start | bytes 393224 | tf_op jit(solution)/shard_map/ppermute | solution.py:249
  9.2 1.2 collective-permute-start.2
  9.6 7.1 %copy-start.3 = (bf16[128,512]{1,0:T(8,128)(2,1)S(1)}, bf16[128,512]{1,0:T(8,128)(2,1)}, u32[]{:S(2)}) copy-start(bf16[128,512]{1,0:T(8,128)(2,1)} %refs_0_.3) | copy-start | bytes 393220
  9.6 22.1 %copy-start = (bf16[3,512,512]{2,1,0:T(8,128)(2,1)S(1)}, bf16[3,512,512]{2,1,0:T(8,128)(2,1)}, u32[]{:S(2)}) copy-start(bf16[3,512,512]{2,1,0:T(8,128)(2,1)} %w.5) | copy-start | bytes 4718596
  9.6 22.1 %copy-start.2 = (bf16[128,512]{1,0:T(8,128)(2,1)S(1)}, bf16[128,512]{1,0:T(8,128)(2,1)}, u32[]{:S(2)}) copy-start(bf16[128,512]{1,0:T(8,128)(2,1)} %facts.3) | copy-start | bytes 393220
  10.3 0.7 copy-start.6
  12.5 22.4 %copy-start.1 = (bf16[32,128,128]{2,1,0:T(8,128)(2,1)S(1)}, bf16[32,128,128]{2,1,0:T(8,128)(2,1)}, u32[]{:S(2)}) copy-start(bf16[32,128,128]{2,1,0:T(8,128)(2,1)} %tiles_own.1) | copy-start | bytes 3145732
  14.0 5.0 %collective-permute-start.3 = (bf16[128,512]{1,0:T(8,128)(2,1)S(1)}, bf16[128,512]{1,0:T(8,128)(2,1)S(1)}, u32[]{:S(2)}, u32[]{:S(2)}) collective-permute-start(bf16[128,512]{1,0:T(8,128)(2,1)S(1)} %collective-permute-done.refs_1_), channel_id=1, source_target_pairs={{0,32},{32,64},{64,96},{96,128},{128,160},{160,192},{192,224},{224... | collective-permute-start | bytes 393224 | tf_op jit(solution)/shard_map/ppermute | solution.py:249
  14.0 5.0 %collective-permute-start.6 = (bf16[128,512]{1,0:T(8,128)(2,1)S(1)}, bf16[128,512]{1,0:T(8,128)(2,1)S(1)}, u32[]{:S(2)}, u32[]{:S(2)}) collective-permute-start(bf16[128,512]{1,0:T(8,128)(2,1)S(1)} %collective-permute-done.1.refs_2_), channel_id=1, source_target_pairs={{0,224},{32,0},{64,32},{96,64},{128,96},{160,128},{192,160},{224,1... | collective-permute-start | bytes 393224 | tf_op jit(solution)/shard_map/ppermute | solution.py:249
  16.6 7.9 %collective-permute-start.9 = (bf16[128,512]{1,0:T(8,128)(2,1)S(1)}, bf16[128,512]{1,0:T(8,128)(2,1)S(1)}, u32[]{:S(2)}, u32[]{:S(2)}) collective-permute-start(bf16[128,512]{1,0:T(8,128)(2,1)S(1)} %copy-done.3), channel_id=1, source_target_pairs={{0,1},{1,0},{2,3},{3,2},{4,5},{5,4},{6,7},{7,6},{8,9},{9,8},{10,11... | collective-permute-start | bytes 393224 | tf_op jit(solution)/shard_map/ppermute | solution.py:246
  19.0 5.6 %collective-permute-start.4 = (bf16[128,512]{1,0:T(8,128)(2,1)S(1)}, bf16[128,512]{1,0:T(8,128)(2,1)S(1)}, u32[]{:S(2)}, u32[]{:S(2)}) collective-permute-start(bf16[128,512]{1,0:T(8,128)(2,1)S(1)} %collective-permute-done.3.refs_3_), channel_id=1, source_target_pairs={{0,32},{32,64},{64,96},{96,128},{128,160},{160,192},{192,224},{224... | collective-permute-start | bytes 393224 | tf_op jit(solution)/shard_map/ppermute | solution.py:249
  19.0 8.5 %collective-permute-start.7 = (bf16[128,512]{1,0:T(8,128)(2,1)S(1)}, bf16[128,512]{1,0:T(8,128)(2,1)S(1)}, u32[]{:S(2)}, u32[]{:S(2)}) collective-permute-start(bf16[128,512]{1,0:T(8,128)(2,1)S(1)} %collective-permute-done.6.refs_4_), channel_id=1, source_target_pairs={{0,224},{32,0},{64,32},{96,64},{128,96},{160,128},{192,160},{224,1... | collective-permute-start | bytes 393224 | tf_op jit(solution)/shard_map/ppermute | solution.py:249
  21.7 5.9 %collective-permute-start.11 = (bf16[128,512]{1,0:T(8,128)(2,1)S(1)}, bf16[128,512]{1,0:T(8,128)(2,1)S(1)}, u32[]{:S(2)}, u32[]{:S(2)}) collective-permute-start(bf16[128,512]{1,0:T(8,128)(2,1)S(1)} %collective-permute-done.1.refs_2_), channel_id=1, source_target_pairs={{0,1},{1,0},{2,3},{3,2},{4,5},{5,4},{6,7},{7,6},{8,9},{9,8},{10,11... | collective-permute-start | bytes 393224 | tf_op jit(solution)/shard_map/ppermute | solution.py:246
  24.6 3.1 %collective-permute-start.10 = (bf16[128,512]{1,0:T(8,128)(2,1)S(1)}, bf16[128,512]{1,0:T(8,128)(2,1)S(1)}, u32[]{:S(2)}, u32[]{:S(2)}) collective-permute-start(bf16[128,512]{1,0:T(8,128)(2,1)S(1)} %collective-permute-done.refs_1_), channel_id=1, source_target_pairs={{0,1},{1,0},{2,3},{3,2},{4,5},{5,4},{6,7},{7,6},{8,9},{9,8},{10,11... | collective-permute-start | bytes 393224 | tf_op jit(solution)/shard_map/ppermute | solution.py:246
  24.6 6.1 %collective-permute-start.12 = (bf16[128,512]{1,0:T(8,128)(2,1)S(1)}, bf16[128,512]{1,0:T(8,128)(2,1)S(1)}, u32[]{:S(2)}, u32[]{:S(2)}) collective-permute-start(bf16[128,512]{1,0:T(8,128)(2,1)S(1)} %collective-permute-done.3.refs_3_), channel_id=1, source_target_pairs={{0,1},{1,0},{2,3},{3,2},{4,5},{5,4},{6,7},{7,6},{8,9},{9,8},{10,11... | collective-permute-start | bytes 393224 | tf_op jit(solution)/shard_map/ppermute | solution.py:246
  27.5 3.9 %collective-permute-start.13 = (bf16[128,512]{1,0:T(8,128)(2,1)S(1)}, bf16[128,512]{1,0:T(8,128)(2,1)S(1)}, u32[]{:S(2)}, u32[]{:S(2)}) collective-permute-start(bf16[128,512]{1,0:T(8,128)(2,1)S(1)} %collective-permute-done.6.refs_4_), channel_id=1, source_target_pairs={{0,1},{1,0},{2,3},{3,2},{4,5},{5,4},{6,7},{7,6},{8,9},{9,8},{10,11... | collective-permute-start | bytes 393224 | tf_op jit(solution)/shard_map/ppermute | solution.py:246
  27.5 5.5 %collective-permute-start.5 = (bf16[64,512]{1,0:T(8,128)(2,1)S(1)}, bf16[64,512]{1,0:T(8,128)(2,1)S(1)}, u32[]{:S(2)}, u32[]{:S(2)}) collective-permute-start(bf16[64,512]{1,0:T(8,128)(2,1)S(1)} %slice.84), channel_id=1, source_target_pairs={{0,32},{32,64},{64,96},{96,128},{128,160},{160,192},{192,224},{224... | collective-permute-start | bytes 196616 | tf_op jit(solution)/shard_map/ppermute | solution.py:249
  27.6 5.4 %collective-permute-start.8 = (bf16[64,512]{1,0:T(8,128)(2,1)S(1)}, bf16[64,512]{1,0:T(8,128)(2,1)S(1)}, u32[]{:S(2)}, u32[]{:S(2)}) collective-permute-start(bf16[64,512]{1,0:T(8,128)(2,1)S(1)} %slice.85), channel_id=1, source_target_pairs={{0,224},{32,0},{64,32},{96,64},{128,96},{160,128},{192,160},{224,1... | collective-permute-start | bytes 196616 | tf_op jit(solution)/shard_map/ppermute | solution.py:249
  30.7 4.2 %collective-permute-start.14 = (bf16[128,512]{1,0:T(8,128)(2,1)S(1)}, bf16[128,512]{1,0:T(8,128)(2,1)S(1)}, u32[]{:S(2)}, u32[]{:S(2)}) collective-permute-start(bf16[128,512]{1,0:T(8,128)(2,1)S(1)} %collective-permute-done.4.refs_0_.refs_5_), channel_id=1, source_target_pairs={{0,1},{1,0},{2,3},{3,2},{4,5},{5,4},{6,7},{7,6},{8,9},{9,8},{10,11... | collective-permute-start | bytes 393224 | tf_op jit(solution)/shard_map/ppermute | solution.py:246
  31.4 3.5 %collective-permute-start.15 = (bf16[128,512]{1,0:T(8,128)(2,1)S(1)}, bf16[128,512]{1,0:T(8,128)(2,1)S(1)}, u32[]{:S(2)}, u32[]{:S(2)}) collective-permute-start(bf16[128,512]{1,0:T(8,128)(2,1)S(1)} %collective-permute-done.7.refs_1_.refs_6_), channel_id=1, source_target_pairs={{0,1},{1,0},{2,3},{3,2},{4,5},{5,4},{6,7},{7,6},{8,9},{9,8},{10,11... | collective-permute-start | bytes 393224 | tf_op jit(solution)/shard_map/ppermute | solution.py:246
  33.1 1.4 collective-permute-start.16
  33.6 1.3 collective-permute-start.17
  37.8 36.3 %copy-start.4 = (bf16[512,512]{1,0:T(8,128)(2,1)S(1)}, bf16[512,512]{1,0:T(8,128)(2,1)}, u32[]{:S(2)}) copy-start(bf16[512,512]{1,0:T(8,128)(2,1)} %w.4) | copy-start | bytes 1572868
  37.8 36.3 %copy-start.5 = (bf16[128,512]{1,0:T(8,128)(2,1)S(1)}, bf16[128,512]{1,0:T(8,128)(2,1)}, u32[]{:S(2)}) copy-start(bf16[128,512]{1,0:T(8,128)(2,1)} %cot.1) | copy-start | bytes 393220
  108.6 3.5 %collective-permute-start.19 = (bf16[2,528,128]{2,1,0:T(8,128)(2,1)S(1)}, bf16[2,528,128]{2,1,0:T(8,128)(2,1)S(1)}, u32[]{:S(2)}, u32[]{:S(2)}) collective-permute-start(bf16[2,528,128]{2,1,0:T(8,128)(2,1)S(1)} %get-tuple-element.45), channel_id=1, source_target_pairs={{0,1},{1,0},{2,3},{3,2},{4,5},{5,4},{6,7},{7,6},{8,9},{9,8},{10,11... | collective-permute-start | bytes 811016 | tf_op jit(solution)/shard_map/ppermute | solution.py:246
  112.1 9.6 %collective-permute-start.20 = (bf16[6,528,128]{2,1,0:T(8,128)(2,1)S(1)}, bf16[6,528,128]{2,1,0:T(8,128)(2,1)S(1)}, u32[]{:S(2)}, u32[]{:S(2)}) collective-permute-start(bf16[6,528,128]{2,1,0:T(8,128)(2,1)S(1)} %get-tuple-element.47), channel_id=1, source_target_pairs={{0,1},{1,0},{2,3},{3,2},{4,5},{5,4},{6,7},{7,6},{8,9},{9,8},{10,11... | collective-permute-start | bytes 2433032 | tf_op jit(solution)/shard_map/ppermute | solution.py:246
  112.6 6.1 %collective-permute-start.22 = (bf16[528,128]{1,0:T(8,128)(2,1)S(1)}, bf16[528,128]{1,0:T(8,128)(2,1)S(1)}, u32[]{:S(2)}, u32[]{:S(2)}) collective-permute-start(bf16[528,128]{1,0:T(8,128)(2,1)S(1)} %get-tuple-element.66), channel_id=1, source_target_pairs={{0,224},{32,0},{64,32},{96,64},{128,96},{160,128},{192,160},{224,1... | collective-permute-start | bytes 405512 | tf_op jit(solution)/shard_map/ppermute | solution.py:249
  115.8 5.9 %collective-permute-start.21 = (bf16[528,128]{1,0:T(8,128)(2,1)S(1)}, bf16[528,128]{1,0:T(8,128)(2,1)S(1)}, u32[]{:S(2)}, u32[]{:S(2)}) collective-permute-start(bf16[528,128]{1,0:T(8,128)(2,1)S(1)} %get-tuple-element.67), channel_id=1, source_target_pairs={{0,32},{32,64},{64,96},{96,128},{128,160},{160,192},{192,224},{224... | collective-permute-start | bytes 405512 | tf_op jit(solution)/shard_map/ppermute | solution.py:249
  121.9 5.5 %collective-permute-start.23 = (bf16[528,128]{1,0:T(8,128)(2,1)S(1)}, bf16[528,128]{1,0:T(8,128)(2,1)S(1)}, u32[]{:S(2)}, u32[]{:S(2)}) collective-permute-start(bf16[528,128]{1,0:T(8,128)(2,1)S(1)} %get-tuple-element.52), channel_id=1, source_target_pairs={{0,32},{32,64},{64,96},{96,128},{128,160},{160,192},{192,224},{224... | collective-permute-start | bytes 405512 | tf_op jit(solution)/shard_map/ppermute | solution.py:249
  122.0 5.4 %collective-permute-start.24 = (bf16[528,128]{1,0:T(8,128)(2,1)S(1)}, bf16[528,128]{1,0:T(8,128)(2,1)S(1)}, u32[]{:S(2)}, u32[]{:S(2)}) collective-permute-start(bf16[528,128]{1,0:T(8,128)(2,1)S(1)} %get-tuple-element.53), channel_id=1, source_target_pairs={{0,224},{32,0},{64,32},{96,64},{128,96},{160,128},{192,160},{224,1... | collective-permute-start | bytes 405512 | tf_op jit(solution)/shard_map/ppermute | solution.py:249
  124.7 9.9 %collective-permute-start.27 = (bf16[528,128]{1,0:T(8,128)(2,1)S(1)}, bf16[528,128]{1,0:T(8,128)(2,1)S(1)}, u32[]{:S(2)}, u32[]{:S(2)}) collective-permute-start(bf16[528,128]{1,0:T(8,128)(2,1)S(1)} %get-tuple-element.68), channel_id=1, source_target_pairs={{0,128},{32,160},{64,192},{96,224},{128,0},{160,32},{192,64},{224,... | collective-permute-start | bytes 405512 | tf_op jit(solution)/shard_map/ppermute | solution.py:249
  127.5 8.3 %collective-permute-start.25 = (bf16[528,128]{1,0:T(8,128)(2,1)S(1)}, bf16[528,128]{1,0:T(8,128)(2,1)S(1)}, u32[]{:S(2)}, u32[]{:S(2)}) collective-permute-start(bf16[528,128]{1,0:T(8,128)(2,1)S(1)} %get-tuple-element.54), channel_id=1, source_target_pairs={{0,32},{32,64},{64,96},{96,128},{128,160},{160,192},{192,224},{224... | collective-permute-start | bytes 405512 | tf_op jit(solution)/shard_map/ppermute | solution.py:249
  127.6 8.2 %collective-permute-start.26 = (bf16[528,128]{1,0:T(8,128)(2,1)S(1)}, bf16[528,128]{1,0:T(8,128)(2,1)S(1)}, u32[]{:S(2)}, u32[]{:S(2)}) collective-permute-start(bf16[528,128]{1,0:T(8,128)(2,1)S(1)} %get-tuple-element.55), channel_id=1, source_target_pairs={{0,224},{32,0},{64,32},{96,64},{128,96},{160,128},{192,160},{224,1... | collective-permute-start | bytes 405512 | tf_op jit(solution)/shard_map/ppermute | solution.py:249
  176.3 10.7 %collective-permute-start.28 = (bf16[16,8,32,128]{3,2,1,0:T(8,128)(2,1)S(1)}, bf16[16,8,32,128]{3,2,1,0:T(8,128)(2,1)S(1)}, u32[]{:S(2)}, u32[]{:S(2)}) collective-permute-start(bf16[16,8,32,128]{3,2,1,0:T(8,128)(2,1)S(1)} %all_to_all.29.own), channel_id=1, source_target_pairs={{0,1},{1,0},{2,3},{3,2},{4,5},{5,4},{6,7},{7,6},{8,9},{9,8},{10,11... | collective-permute-start | bytes 3145736 | tf_op jit(solution)/shard_map/ppermute | solution.py:246
  184.7 2.4 %collective-permute-start.29 = (bf16[8,32,128]{2,1,0:T(8,128)(2,1)S(1)}, bf16[8,32,128]{2,1,0:T(8,128)(2,1)S(1)}, u32[]{:S(2)}, u32[]{:S(2)}) collective-permute-start(bf16[8,32,128]{2,1,0:T(8,128)(2,1)S(1)} %get-tuple-element.70), channel_id=1, source_target_pairs={{0,1},{1,0},{2,3},{3,2},{4,5},{5,4},{6,7},{7,6},{8,9},{9,8},{10,11... | collective-permute-start | bytes 196616 | tf_op jit(solution)/shard_map/ppermute | solution.py:246
